TPU v7x, 32 devices: a whole 2x2x4 slice. The times are simulated.
32 devices in a mesh: ep: 8 (over y, x, core), tp: 4 (over z).
Axes of the slice: x: 2, y: 2, z: 4, core: 2. Of those that a mesh axis runs over, the one named last changes fastest.
Arguments:
- hidden_in: bfloat16 [2048, 2048], P('ep'), may hold values from -6 to 6
- expert_ids: int32 [2048, 8], P('ep'), may hold values from 0 to 31, all different within a row; in each aligned block of 256 rows (0 to 255, 256 to 511, ...) at most 128 rows name the same one
- attention_gain: bfloat16 [2048], P('ep'), may hold values from 0.5 to 1.5
- query_gain: bfloat16 [128], P('ep'), may hold values from 0.5 to 1.5
- key_gain: bfloat16 [128], P('ep'), may hold values from 0.5 to 1.5
- query_weight: bfloat16 [2048, 4096], P('ep', 'tp'), may hold values from -0.125 to 0.125
- key_matrix: bfloat16 [2048, 512], P('ep', 'tp'), may hold values from -0.125 to 0.125
- value_matrix: bfloat16 [2048, 512], P('ep', 'tp'), may hold values from -0.125 to 0.125
- output_weight: bfloat16 [4096, 2048], P('tp'), may hold values from -1.5 to 1.5
- expert_gain: bfloat16 [2048], P('ep'), may hold values from 0.5 to 1.5
- router_weight: bfloat16 [2048, 32], P('ep'), may hold values from -0.0625 to 0.0625
- gate_up_weight: bfloat16 [32, 2048, 1536], P('ep', None, 'tp'), may hold values from -0.125 to 0.125
- down_weight: bfloat16 [32, 768, 2048], P('ep', 'tp'), may hold values from -1.75 to 1.75
- output_grad: bfloat16 [2048, 2048], P('ep'), may hold values from -6 to 6
Outputs:
- block_out: bfloat16 [2048, 2048], P('ep')
- input_grad: float32 [2048, 2048], P('ep')
- attention_gain_grad: float32 [2048], P('ep')
- query_gain_grad: float32 [128], P('ep')
- key_gain_grad: float32 [128], P('ep')
- query_weight_grad: float32 [2048, 4096], P('ep', 'tp')
- key_weight_grad: float32 [2048, 512], P('ep', 'tp')
- value_weight_grad: float32 [2048, 512], P('ep', 'tp')
- output_weight_grad: float32 [4096, 2048], P('tp')
- expert_gain_grad: float32 [2048], P('ep')
- router_weight_grad: float32 [2048, 32], P('ep')
- gate_up_weight_grad: float32 [32, 2048, 1536], P('ep', None, 'tp')
- down_weight_grad: float32 [32, 768, 2048], P('ep', 'tp')
Inputs may be any that keep to these rules, and one draw needn't show every extreme that they name: `expert_ids`: each row names 8 different experts. Among the tokens of one index of ep (aligned blocks of 256 rows) no expert is named by more than 128 rows, a bound that some block reaches.
All inputs are finite; a program needn't handle non-finite values.
Results may differ from a plain program's by a relative error of at most 0.024.
Values may be sent and summed in bfloat16 or wider, within the bound.
No kernel may reach another device: no remote copies, remote signals or barrier semaphores. Data moves between devices by JAX's collectives and lax.ppermute only.
A program may use at most 320 MiB of HBM per device.

v0:
```python
import math

import jax
import jax.numpy as jnp
from jax import lax
from jax.sharding import PartitionSpec as P

HEAD_SIZE = 128
TOP = 8
PAIR = 64


EPSILON = 1e-06
THETA = 1000000.0


def norm_rows(value_rows, norm_gain):
    return (
        value_rows
        * lax.rsqrt(jnp.mean(value_rows * value_rows, axis=-1, keepdims=True) + EPSILON)
        * norm_gain
    )


def norm_back(value_rows, norm_gain, upstream):
    scaling = lax.rsqrt(jnp.mean(value_rows * value_rows, axis=-1, keepdims=True) + EPSILON)
    normal = value_rows * scaling
    weighted = upstream * norm_gain
    inward = scaling * (weighted - normal * jnp.mean(weighted * normal, axis=-1, keepdims=True))
    return (inward, upstream * normal)


def rope_tables(positions, head_size):
    halfway = head_size // 2
    inverse = THETA ** (-(jnp.arange(halfway, dtype=jnp.float32) * 2.0) / head_size)
    angles = positions.astype(jnp.float32)[:, None] * inverse[None, :]
    return (jnp.cos(angles)[:, None, :], jnp.sin(angles)[:, None, :])


def rotate(value_rows, cosine, sine_table):
    halfway = value_rows.shape[-1] // 2
    first_half = value_rows[..., :halfway]
    second_half = value_rows[..., halfway:]
    return jnp.concatenate(
        [
            first_half * cosine - second_half * sine_table,
            second_half * cosine + first_half * sine_table,
        ],
        axis=-1,
    )


def rotate_back(upstream, cosine, sine_table):
    halfway = upstream.shape[-1] // 2
    first_half = upstream[..., :halfway]
    second_half = upstream[..., halfway:]
    return jnp.concatenate(
        [
            first_half * cosine + second_half * sine_table,
            second_half * cosine - first_half * sine_table,
        ],
        axis=-1,
    )


def slot_index(chosen_ids, expert_count, capacity):
    onehot = (chosen_ids[:, None] == jnp.arange(expert_count, dtype=jnp.int32)[None, :]).astype(
        jnp.int32
    )
    earlier = jnp.cumsum(onehot, axis=0) - onehot
    return chosen_ids * capacity + jnp.sum(earlier * onehot, axis=1)


def send_rows(row_block):
    return lax.all_to_all(row_block, "ep", split_axis=0, concat_axis=0, tiled=True)


def return_rows(producer, quarter, owners):
    summed = lax.psum_scatter(
        producer(jnp.int32(0), quarter * lax.axis_size("tp")), "tp", scatter_dimension=0, tiled=True
    )
    rounded = summed.astype(jnp.bfloat16).reshape(summed.shape[0], owners, -1)
    returned = lax.all_to_all(rounded, "ep", split_axis=1, concat_axis=1, tiled=True)
    return returned.reshape(summed.shape[0], -1)


def shards(
    hidden_in,
    expert_ids,
    attention_gain,
    query_gain,
    key_gain,
    query_weight,
    key_matrix,
    value_matrix,
    output_weight,
    expert_gain,
    router_weight,
    gate_up_weight,
    down_weight,
    output_grad,
):
    tokens = hidden_in.shape[0]
    features = hidden_in.shape[1]
    owners = lax.axis_size("ep")
    tensor_parts = lax.axis_size("tp")
    local_experts = gate_up_weight.shape[0]
    expert_count = local_experts * owners
    capacity = 2 * tokens * TOP // expert_count
    quarter = features // tensor_parts
    tensor_index = lax.axis_index("tp")
    ff_local = gate_up_weight.shape[2] // 2
    groups = ff_local // PAIR
    gathered = (
        lax.all_gather(attention_gain, "ep", axis=0, tiled=True),
        lax.all_gather(query_gain, "ep", axis=0, tiled=True),
        lax.all_gather(key_gain, "ep", axis=0, tiled=True),
        lax.all_gather(expert_gain, "ep", axis=0, tiled=True),
        lax.all_gather(query_weight, "ep", axis=0, tiled=True),
        lax.all_gather(key_matrix, "ep", axis=0, tiled=True),
        lax.all_gather(value_matrix, "ep", axis=0, tiled=True),
        lax.all_gather(router_weight, "ep", axis=0, tiled=True),
    )
    attn_gain_full = gathered[0].astype(jnp.float32)
    query_gain_full = gathered[1].astype(jnp.float32)
    key_gain_full = gathered[2].astype(jnp.float32)
    mlp_gain_full = gathered[3].astype(jnp.float32)
    query_full = gathered[4]
    key_full = gathered[5]
    value_full = gathered[6]
    router_full = gathered[7]
    hidden_f = hidden_in.astype(jnp.float32)
    normed_low = norm_rows(hidden_f, attn_gain_full).astype(jnp.bfloat16)
    query_heads = query_full.shape[1] // HEAD_SIZE
    key_heads = key_full.shape[1] // HEAD_SIZE
    heads_per_group = query_heads // key_heads
    query_raw = jnp.dot(normed_low, query_full, preferred_element_type=jnp.float32).reshape(
        tokens, query_heads, HEAD_SIZE
    )
    key_raw = jnp.dot(normed_low, key_full, preferred_element_type=jnp.float32).reshape(
        tokens, key_heads, HEAD_SIZE
    )
    value_low = jnp.dot(normed_low, value_full, preferred_element_type=jnp.float32).astype(
        jnp.bfloat16
    )
    positions = jnp.arange(tokens, dtype=jnp.int32)
    cosine, sine_table = rope_tables(positions, HEAD_SIZE)
    query_low = rotate(norm_rows(query_raw, query_gain_full), cosine, sine_table).astype(
        jnp.bfloat16
    )
    all_keys = rotate(norm_rows(key_raw, key_gain_full), cosine, sine_table).astype(jnp.bfloat16)
    all_values = value_low.reshape(tokens, key_heads, HEAD_SIZE)
    allowed = jnp.arange(tokens)[None, :] <= jnp.arange(tokens)[:, None]
    grouped_queries = query_low.reshape(tokens, key_heads, heads_per_group, HEAD_SIZE)

    def score_block():
        raw_scores = jnp.einsum(
            "ikgd,jkd->kgij", grouped_queries, all_keys, preferred_element_type=jnp.float32
        ) / math.sqrt(HEAD_SIZE)
        return jnp.where(allowed, raw_scores, -jnp.inf)

    scores = score_block()
    row_max = jnp.max(scores, axis=-1, keepdims=True)
    weights = jnp.exp(scores - row_max)
    row_total = jnp.sum(weights, axis=-1, keepdims=True)
    probs = weights / row_total
    log_total = row_max + jnp.log(row_total)
    attention_output = (
        jnp.einsum(
            "kgij,jkd->ikgd",
            probs.astype(jnp.bfloat16),
            all_values,
            preferred_element_type=jnp.float32,
        )
        .astype(jnp.bfloat16)
        .reshape(tokens, query_heads * HEAD_SIZE)
    )
    head_part = jnp.dot(attention_output, output_weight, preferred_element_type=jnp.float32)
    attended = lax.psum(head_part, "tp")
    resid = hidden_f + attended
    routed_low = norm_rows(resid, mlp_gain_full).astype(jnp.bfloat16)
    logits = jnp.dot(routed_low, router_full, preferred_element_type=jnp.float32)
    logit_max = jnp.max(logits, axis=-1, keepdims=True)
    exponent = jnp.exp(logits - logit_max)
    router = exponent / jnp.sum(exponent, axis=-1, keepdims=True)
    chosen = jnp.take_along_axis(router, expert_ids, axis=1)
    chosen_total = jnp.sum(chosen, axis=1, keepdims=True)
    gates = chosen / chosen_total
    pair_count = tokens * TOP
    slots = slot_index(expert_ids.reshape(-1), expert_count, capacity)
    table = (
        jnp.full((expert_count * capacity,), pair_count, jnp.int32)
        .at[slots]
        .set(jnp.arange(pair_count, dtype=jnp.int32))
    )
    live_slots = table < pair_count
    clipped = jnp.minimum(table, pair_count - 1)
    source_token = clipped // TOP
    send_block = jnp.where(
        live_slots[:, None], routed_low[source_token], jnp.zeros((), jnp.bfloat16)
    ).reshape(owners, local_experts * capacity, features)
    received = send_rows(send_block).reshape(owners, local_experts, capacity, features)
    both = jnp.einsum(
        "pecd,edn->pecn", received, gate_up_weight, preferred_element_type=jnp.float32
    )
    parted = both.reshape(owners, local_experts, capacity, groups, 2, PAIR)
    activation = parted[:, :, :, :, 0, :].reshape(owners, local_experts, capacity, ff_local)
    upper = parted[:, :, :, :, 1, :].reshape(owners, local_experts, capacity, ff_local)
    sigmoid_act = jax.nn.sigmoid(activation)
    inner = (activation * sigmoid_act * upper).astype(jnp.bfloat16)

    def expert_output(start, count):
        return jnp.einsum(
            "pecf,efd->dpec", inner, down_weight, preferred_element_type=jnp.float32
        ).reshape(count, -1)

    returned = return_rows(expert_output, quarter, owners)
    picked = returned[:, slots].reshape(quarter, tokens, TOP).astype(jnp.float32)
    mixture_part = jnp.sum(picked * gates[None, :, :], axis=2)
    mixture = (
        lax.all_gather(mixture_part.astype(jnp.bfloat16), "tp", axis=0, tiled=True)
        .astype(mixture_part.dtype)
        .T
    )
    block_out = (resid + mixture).astype(jnp.bfloat16)
    grad_out = output_grad.astype(jnp.float32)
    own_columns = lax.dynamic_slice_in_dim(grad_out, tensor_index * quarter, quarter, 1)
    gate_part = jnp.einsum("id,dik->ik", own_columns, picked, precision=lax.Precision.HIGHEST)
    gate_flat = gates.reshape(-1)
    grad_block = (
        jnp.where(live_slots[:, None], grad_out[source_token] * gate_flat[clipped][:, None], 0.0)
        .astype(jnp.bfloat16)
        .reshape(owners, local_experts * capacity, features)
    )
    grad_received = send_rows(grad_block).reshape(owners, local_experts, capacity, features)
    down_grad = jnp.einsum(
        "pecf,pecd->efd", inner, grad_received, preferred_element_type=jnp.float32
    )
    grad_inner = jnp.einsum(
        "pecd,efd->pecf", grad_received, down_weight, preferred_element_type=jnp.float32
    )
    grad_act = (grad_inner * upper * sigmoid_act * (1.0 + activation * (1.0 - sigmoid_act))).astype(
        jnp.bfloat16
    )
    grad_upper = (grad_inner * activation * sigmoid_act).astype(jnp.bfloat16)
    joined = jnp.stack(
        [
            grad_act.reshape(owners, local_experts, capacity, groups, PAIR),
            grad_upper.reshape(owners, local_experts, capacity, groups, PAIR),
        ],
        axis=4,
    ).reshape(owners, local_experts, capacity, 2 * ff_local)
    gate_up_grad = jnp.einsum(
        "pecd,pecn->edn", received, joined, preferred_element_type=jnp.float32
    )

    def row_gradient(start, count):
        total = jnp.einsum(
            "pecn,edn->dpec", joined, gate_up_weight, preferred_element_type=jnp.float32
        )
        return total.reshape(count, -1)

    grad_returned = return_rows(row_gradient, quarter, owners)
    grad_share = jnp.sum(
        grad_returned[:, slots].reshape(quarter, tokens, TOP).astype(jnp.float32), axis=2
    )
    grad_columns, gate_parts = (
        lax.all_gather(grad_share, "tp", axis=0, tiled=True),
        lax.all_gather(gate_part.reshape(1, pair_count), "tp", axis=0, tiled=True),
    )
    grad_gates = jnp.sum(gate_parts, axis=0).reshape(tokens, TOP)
    grad_chosen = (grad_gates - jnp.sum(grad_gates * gates, axis=1, keepdims=True)) / chosen_total
    expert_onehot = (
        expert_ids[:, :, None] == jnp.arange(expert_count, dtype=jnp.int32)[None, None, :]
    ).astype(jnp.float32)
    grad_router = jnp.sum(expert_onehot * grad_chosen[:, :, None], axis=1)
    grad_logits = (
        router * (grad_router - jnp.sum(router * grad_router, axis=1, keepdims=True))
    ).astype(jnp.bfloat16)
    router_grad = jnp.dot(routed_low.T, grad_logits, preferred_element_type=jnp.float32)
    grad_routed = grad_columns.T + jnp.dot(
        grad_logits, router_full.T, preferred_element_type=jnp.float32
    )
    grad_resid_norm, mlp_terms = norm_back(resid, mlp_gain_full, grad_routed)
    mlp_gain_grad = jnp.sum(mlp_terms, axis=0)
    grad_resid = grad_out + grad_resid_norm
    grad_attended = grad_resid.astype(jnp.bfloat16)
    output_local = jnp.dot(attention_output.T, grad_attended, preferred_element_type=jnp.float32)
    output_weight_grad = lax.psum(output_local.astype(jnp.bfloat16), "ep").astype(jnp.float32)
    grad_mixed = (
        jnp.dot(grad_attended, output_weight.T, preferred_element_type=jnp.float32)
        .astype(jnp.bfloat16)
        .reshape(tokens, key_heads, heads_per_group, HEAD_SIZE)
    )
    probs_again = jnp.exp(score_block() - log_total)
    grad_probs = jnp.einsum(
        "ikgd,jkd->kgij", grad_mixed, all_values, preferred_element_type=jnp.float32
    )
    grad_values = jnp.einsum(
        "kgij,ikgd->jkd",
        probs_again.astype(jnp.bfloat16),
        grad_mixed,
        preferred_element_type=jnp.float32,
    )
    grad_scores = (
        probs_again * (grad_probs - jnp.sum(probs_again * grad_probs, axis=-1, keepdims=True))
    ).astype(jnp.bfloat16)
    grad_queries = jnp.einsum(
        "kgij,jkd->ikgd", grad_scores, all_keys, preferred_element_type=jnp.float32
    ) / math.sqrt(HEAD_SIZE)
    grad_keys = jnp.einsum(
        "kgij,ikgd->jkd", grad_scores, grouped_queries, preferred_element_type=jnp.float32
    ) / math.sqrt(HEAD_SIZE)
    grad_value_low = grad_values.reshape(tokens, -1).astype(jnp.bfloat16)
    grad_query_rot = rotate_back(
        grad_queries.reshape(tokens, query_heads, HEAD_SIZE), cosine, sine_table
    )
    grad_query_raw, query_terms = norm_back(query_raw, query_gain_full, grad_query_rot)
    grad_key_rot = rotate_back(grad_keys, cosine, sine_table)
    grad_key_raw, key_terms = norm_back(key_raw, key_gain_full, grad_key_rot)
    grad_query_low = grad_query_raw.reshape(tokens, -1).astype(jnp.bfloat16)
    grad_key_low = grad_key_raw.reshape(tokens, -1).astype(jnp.bfloat16)
    query_grad_w = jnp.dot(normed_low.T, grad_query_low, preferred_element_type=jnp.float32)
    key_grad_w = jnp.dot(normed_low.T, grad_key_low, preferred_element_type=jnp.float32)
    value_grad_w = jnp.dot(normed_low.T, grad_value_low, preferred_element_type=jnp.float32)
    feature_part = jnp.dot(grad_query_low, query_full.T, preferred_element_type=jnp.float32)
    feature_part = feature_part + jnp.dot(
        grad_key_low, key_full.T, preferred_element_type=jnp.float32
    )
    feature_part = feature_part + jnp.dot(
        grad_value_low, value_full.T, preferred_element_type=jnp.float32
    )
    grad_normed, query_gain_grad, key_gain_grad = (
        lax.psum(feature_part.astype(jnp.bfloat16), "tp").astype(jnp.float32),
        lax.psum(jnp.sum(query_terms, axis=(0, 1)).astype(jnp.bfloat16), "tp").astype(jnp.float32),
        lax.psum(jnp.sum(key_terms, axis=(0, 1)).astype(jnp.bfloat16), "tp").astype(jnp.float32),
    )
    grad_input_norm, attn_terms = norm_back(hidden_f, attn_gain_full, grad_normed)
    input_grad = grad_resid + grad_input_norm
    attn_gain_grad = jnp.sum(attn_terms, axis=0)
    shared = (
        lax.psum_scatter(
            attn_gain_grad.astype(jnp.bfloat16), "ep", scatter_dimension=0, tiled=True
        ).astype(jnp.float32),
        lax.psum_scatter(
            query_gain_grad.astype(jnp.bfloat16), "ep", scatter_dimension=0, tiled=True
        ).astype(jnp.float32),
        lax.psum_scatter(
            key_gain_grad.astype(jnp.bfloat16), "ep", scatter_dimension=0, tiled=True
        ).astype(jnp.float32),
        lax.psum_scatter(
            mlp_gain_grad.astype(jnp.bfloat16), "ep", scatter_dimension=0, tiled=True
        ).astype(jnp.float32),
        lax.psum_scatter(
            query_grad_w.astype(jnp.bfloat16), "ep", scatter_dimension=0, tiled=True
        ).astype(jnp.float32),
        lax.psum_scatter(
            key_grad_w.astype(jnp.bfloat16), "ep", scatter_dimension=0, tiled=True
        ).astype(jnp.float32),
        lax.psum_scatter(
            value_grad_w.astype(jnp.bfloat16), "ep", scatter_dimension=0, tiled=True
        ).astype(jnp.float32),
        lax.psum_scatter(
            router_grad.astype(jnp.bfloat16), "ep", scatter_dimension=0, tiled=True
        ).astype(jnp.float32),
    )
    return (
        block_out,
        input_grad,
        shared[0],
        shared[1],
        shared[2],
        shared[4],
        shared[5],
        shared[6],
        output_weight_grad,
        shared[3],
        shared[7],
        gate_up_grad,
        down_grad,
    )


def solution(mesh):
    in_specs = (
        P("ep", None),
        P("ep", None),
        P("ep"),
        P("ep"),
        P("ep"),
        P("ep", "tp"),
        P("ep", "tp"),
        P("ep", "tp"),
        P("tp", None),
        P("ep"),
        P("ep", None),
        P("ep", None, "tp"),
        P("ep", "tp", None),
        P("ep", None),
    )
    out_specs = (
        P("ep", None),
        P("ep", None),
        P("ep"),
        P("ep"),
        P("ep"),
        P("ep", "tp"),
        P("ep", "tp"),
        P("ep", "tp"),
        P("tp", None),
        P("ep"),
        P("ep", None),
        P("ep", None, "tp"),
        P("ep", "tp", None),
    )
    return jax.shard_map(shards, mesh=mesh, in_specs=in_specs, out_specs=out_specs, check_vma=False)
```

profile of v0, /device:TPU:8, one launch (start us, length us, event | category | flops | bytes accessed | tf_op | source)
XLA Modules:
  0.0 2418.7 jit_solution(12247308480619502063)
XLA Ops:
  21.4 13.3 all-reduce.7
  35.4 12.0 all_gather.35
  87.6 15.9 reduce-window.6
  120.1 42.1 %all-reduce.13.cloned.1.call-done = f32[256,2048]{1,0:T(8,128)} async-done(((f32[256,2048]{1,0:T(8,128)}), f32[256,2048]{1,0:T(8,128)}) %all-reduce.13.cloned.1.call-update) | async-done | bytes 2097168 | tf_op jit(solution)/shard_map/psum | solution.py:179
  167.0 32.7 %gather_fusion = bf16[4096,2048]{1,0:T(8,128)(2,1)} fusion(bf16[256,2048]{1,0:T(8,128)(2,1)} %multiply_convert_fusion.1, s32[4096]{0:T(1024)S(1)} %get-tuple-element.52), kind=kCustom, calls=%fused_computation | custom fusion | bytes 33570816 | tf_op jit(solution)/shard_map/gather | solution.py:200
  208.0 187.7 %all_to_all.20 = bf16[8,512,2048]{2,1,0:T(8,128)(2,1)} all-to-all(bf16[8,512,2048]{2,1,0:T(8,128)(2,1)S(1)} %broadcast_select_fusion), channel_id=1, replica_groups=mesh['ep'=8,'tp'=4] {'ep'}, dimensions={0} | all-to-all | bytes 33554432 | tf_op jit(solution)/shard_map/all_to_all | solution.py:75
  395.7 15.8 fusion.23
  425.3 13.1 convolution_bitcast_fusion
  438.5 23.1 copy.215
  461.6 547.6 %reduce-scatter.7.cloned.1.call-done = f32[512,4096]{0,1:T(8,128)} async-done(((f32[2048,4096]{0,1:T(8,128)}), f32[512,4096]{0,1:T(8,128)}) %reduce-scatter.7.cloned.1.call-update) | async-done | bytes 8388624 | tf_op jit(solution)/shard_map/reduce_scatter | solution.py:79
  1022.9 33.3 %gather_fusion.2 = f32[4096,2048]{1,0:T(8,128)} fusion(f32[256,2048]{1,0:T(8,128)} %convert_element_type.245, s32[4096]{0:T(1024)S(1)} %get-tuple-element.52), kind=kCustom, calls=%fused_computation.2 | custom fusion | bytes 67125248 | tf_op jit(solution)/shard_map/gather | solution.py:231
  1056.2 16.0 all_gather.40
  1075.6 16.8 gather_fusion.5
  1094.2 12.0 gather_fusion.1
  1109.0 15.9 all-gather.2
  1125.3 23.0 gather_fusion.3
  1148.4 12.6 select_convert_fusion
  1161.0 188.0 %all_to_all.21 = bf16[8,512,2048]{2,1,0:T(8,128)(2,1)} all-to-all(bf16[8,512,2048]{2,1,0:T(8,128)(2,1)S(1)} %select_convert_fusion), channel_id=1, replica_groups=mesh['ep'=8,'tp'=4] {'ep'}, dimensions={0} | all-to-all | bytes 33554432 | tf_op jit(solution)/shard_map/all_to_all | solution.py:75
  1348.9 11.7 fusion.14
  1365.5 18.5 convolution_bitcast_fusion.1
  1383.9 23.1 copy.224
  1407.1 548.0 %reduce-scatter.9.cloned.1.call-done = f32[512,4096]{0,1:T(8,128)} async-done(((f32[2048,4096]{0,1:T(8,128)}), f32[512,4096]{0,1:T(8,128)}) %reduce-scatter.9.cloned.1.call-update) | async-done | bytes 8388624 | tf_op jit(solution)/shard_map/reduce_scatter | solution.py:79
  1959.0 53.5 %all_to_all.22 = bf16[512,8,512]{0,2,1:T(8,128)(2,1)} all-to-all(bf16[512,8,512]{0,2,1:T(8,128)(2,1)S(1)} %bitcast.278), channel_id=1, replica_groups=mesh['ep'=8,'tp'=4] {'ep'}, dimensions={1} | all-to-all | bytes 8388608 | tf_op jit(solution)/shard_map/all_to_all | solution.py:83
  2012.5 12.0 gather_fusion.4
  2035.8 38.6 %all-gather.11.cloned.1.call-done = f32[2048,256]{0,1:T(8,128)} async-done(((f32[512,256]{0,1:T(8,128)}), f32[2048,256]{0,1:T(8,128)}) %all-gather.11.cloned.1.call-update) | async-done | bytes 2097168 | tf_op jit(solution)/shard_map/all_gather | solution.py:268
  2079.3 25.5 %all-gather.9.cloned.1.call-done = bf16[2048,256]{0,1:T(8,128)(2,1)} async-done(((bf16[512,256]{0,1:T(8,128)(2,1)}), bf16[2048,256]{0,1:T(8,128)(2,1)}) %all-gather.9.cloned.1.call-update) | async-done | bytes 1048592 | tf_op jit(solution)/shard_map/all_gather | solution.py:221
  2166.9 17.3 convolution_bitcast_fusion.2
  2185.7 47.3 %all-reduce.15.cloned.1.call-done = bf16[256,2048]{1,0:T(8,128)(2,1)} async-done(((bf16[256,2048]{1,0:T(8,128)(2,1)}), bf16[256,2048]{1,0:T(8,128)(2,1)}) %all-reduce.15.cloned.1.call-update) | async-done | bytes 1048592 | tf_op jit(solution)/shard_map/psum | solution.py:334
  2235.4 13.9 all-reduce.6
  2249.4 20.2 reduce-scatter.13.cloned.1.call-done
  2285.8 69.1 %all-reduce.17.cloned.1.call-done = bf16[1024,2048]{1,0:T(8,128)(2,1)} async-done(((bf16[1024,2048]{1,0:T(8,128)(2,1)}), bf16[1024,2048]{1,0:T(8,128)(2,1)}) %all-reduce.17.cloned.1.call-update) | async-done | bytes 4194320 | tf_op jit(solution)/shard_map/psum | solution.py:289
  2361.5 48.0 %reduce-scatter.11.cloned.1.call-done = bf16[256,1024]{1,0:T(8,128)(2,1)} async-done(((bf16[2048,1024]{1,0:T(8,128)(2,1)}), bf16[256,1024]{1,0:T(8,128)(2,1)}) %reduce-scatter.11.cloned.1.call-update) | async-done | bytes 524304 | tf_op jit(solution)/shard_map/reduce_scatter | solution.py:354
  (336 shorter events, 233.8 us)
Async XLA Ops:
  7.2 418.2 %copy-start = (bf16[4,192,2048]{2,1,0:T(8,128)(2,1)S(1)}, bf16[4,192,2048]{2,1,0:T(8,128)(2,1)}, u32[]{:S(2)}) copy-start(bf16[4,192,2048]{2,1,0:T(8,128)(2,1)} %param.26) | copy-start | bytes 9437188
  7.2 55.3 %all-gather.7.cloned.1.call-start = ((), (), s32[]{:S(2)}) async-start(), calls=%async_computation.10 | async-start | bytes 4718592 | tf_op jit(solution)/shard_map/all_gather | solution.py:119
  7.9 154.3 %all-reduce.13.cloned.1.call-start = ((), (), s32[]{:S(2)}) async-start(), calls=%async_computation.11 | async-start | bytes 4194304 | tf_op jit(solution)/shard_map/psum | solution.py:179
  17.7 44.8 %copy-start.38 = (f32[8,1,256]{2,1,0:T(1,128)}, f32[8,1,256]{2,1,0:T(1,128)S(1)}, u32[]{:S(2)}) copy-start(f32[8,1,256]{2,1,0:T(1,128)S(1)} %convert_element_type.285) | copy-start | bytes 24580
  34.7 23.8 copy-start.4
  34.7 33.3 %copy-start.73 = (f32[128]{0:T(128)}, f32[128]{0:T(128)S(1)}, u32[]{:S(2)}) copy-start(f32[128]{0:T(128)S(1)} %convert_element_type.231) | copy-start | bytes 1540
  34.7 25.5 %copy-start.69 = (f32[128]{0:T(128)}, f32[128]{0:T(128)S(1)}, u32[]{:S(2)}) copy-start(f32[128]{0:T(128)S(1)} %convert_element_type.229) | copy-start | bytes 1540
  34.7 27.2 %copy-start.71 = (f32[64]{0:T(128)}, f32[64]{0:T(128)S(1)}, u32[]{:S(2)}) copy-start(f32[64]{0:T(128)S(1)} %multiply_power_fusion) | copy-start | bytes 772
  34.8 27.1 %copy-start.67 = (f32[256]{0:T(256)}, f32[256]{0:T(256)S(1)}, u32[]{:S(2)}) copy-start(f32[256]{0:T(256)S(1)} %iota_convert_fusion) | copy-start | bytes 3076
  76.9 932.3 %reduce-scatter.7.cloned.1.call-start = ((), (), s32[]{:S(2)}) async-start(), calls=%async_computation.12 | async-start | bytes 41943040 | tf_op jit(solution)/shard_map/reduce_scatter | solution.py:79
  86.9 77.6 %copy-start.45 = (f32[8,1,256]{2,1,0:T(1,128)}, f32[8,1,256]{2,1,0:T(1,128)S(1)}, u32[]{:S(2)}) copy-start(f32[8,1,256]{2,1,0:T(1,128)S(1)} %convert_element_type.286) | copy-start | bytes 24580
  119.5 80.2 %copy-start.52 = (pred[8,512]{1,0:T(8,128)(4,1)}, pred[8,512]{1,0:T(8,128)(4,1)S(1)}, u32[]{:S(2)}) copy-start(pred[8,512]{1,0:T(8,128)(4,1)S(1)} %broadcast_in_dim.40) | copy-start | bytes 12292
  164.5 35.2 %copy-start.65 = (f32[256]{0:T(256)}, f32[256]{0:T(256)S(1)}, u32[]{:S(2)}) copy-start(f32[256]{0:T(256)S(1)} %add_rsqrt_fusion.1) | copy-start | bytes 3076
  1015.1 79.1 %all-to-all-start.1 = ((bf16[512,8,512]{0,2,1:T(8,128)(2,1)}), bf16[512,8,512]{0,2,1:T(8,128)(2,1)}, u32[]{:S(2)}, u32[]{:S(2)}) async-start(bf16[512,8,512]{0,2,1:T(8,128)(2,1)} %bitcast.277), calls=%async_computation.2 | async-start | bytes 8388608 | tf_op jit(solution)/shard_map/all_to_all | solution.py:83
  1019.6 935.4 %reduce-scatter.9.cloned.1.call-start = ((), (), s32[]{:S(2)}) async-start(), calls=%async_computation.14 | async-start | bytes 41943040 | tf_op jit(solution)/shard_map/reduce_scatter | solution.py:79
  1022.9 33.3 %copy-start.63 = (bf16[256,32]{0,1:T(8,128)(2,1)S(1)}, bf16[256,32]{0,1:T(8,128)(2,1)}, u32[]{:S(2)}) copy-start(bf16[256,32]{0,1:T(8,128)(2,1)} %param.24) | copy-start | bytes 49156
  1022.9 51.0 %copy-start.57 = (s32[2048,1]{0,1:T(1,128)S(1)}, s32[2048,1]{0,1:T(1,128)}, u32[]{:S(2)}) copy-start(s32[2048,1]{0,1:T(1,128)} %copy-done.56) | copy-start | bytes 24580
  1106.2 19.2 copy-start.51
  1125.3 23.1 copy-start.53
  1161.0 188.0 %copy-start.10 = (f32[8,4,128,3,1,64]{2,5,3,0,1,4:T(8,128)S(1)}, f32[8,4,128,3,1,64]{2,5,3,0,1,4:T(8,128)}, u32[]{:S(2)}) copy-start(f32[8,4,128,3,1,64]{2,5,3,0,1,4:T(8,128)} %copy-done.9) | copy-start | bytes 9437188
  1407.0 667.4 %all-gather.11.cloned.1.call-start = ((), (), s32[]{:S(2)}) async-start(), calls=%async_computation.15 | async-start | bytes 2621440 | tf_op jit(solution)/shard_map/all_gather | solution.py:268
  2028.3 46.2 %copy-start.46 = (f32[8,1,256]{2,1,0:T(1,128)S(1)}, f32[8,1,256]{2,1,0:T(1,128)}, u32[]{:S(2)}) copy-start(f32[8,1,256]{2,1,0:T(1,128)} %copy-done.45) | copy-start | bytes 24580
  2028.3 46.2 %copy-start.66 = (f32[256]{0:T(256)S(1)}, f32[256]{0:T(256)}, u32[]{:S(2)}) copy-start(f32[256]{0:T(256)} %copy-done.65) | copy-start | bytes 3076
  2028.3 76.5 %all-gather.9.cloned.1.call-start = ((), (), s32[]{:S(2)}) async-start(), calls=%async_computation.13 | async-start | bytes 1310720 | tf_op jit(solution)/shard_map/all_gather | solution.py:221
  2032.0 123.8 %reduce-scatter.17.cloned.1.call-start = ((), (), s32[]{:S(2)}) async-start(), calls=%async_computation.21 | async-start | bytes 147456 | tf_op jit(solution)/shard_map/reduce_scatter | solution.py:363
  2035.8 148.5 %reduce-scatter.15.cloned.1.call-start = ((), (), s32[]{:S(2)}) async-start(), calls=%async_computation.19 | async-start | bytes 589824 | tf_op jit(solution)/shard_map/reduce_scatter | solution.py:360
  2133.5 99.5 %all-reduce.15.cloned.1.call-start = ((), (), s32[]{:S(2)}) async-start(), calls=%async_computation.16 | async-start | bytes 2097152 | tf_op jit(solution)/shard_map/psum | solution.py:334
  2141.7 128.0 %reduce-scatter.13.cloned.1.call-start = ((), (), s32[]{:S(2)}) async-start(), calls=%async_computation.18 | async-start | bytes 589824 | tf_op jit(solution)/shard_map/reduce_scatter | solution.py:357
  2144.4 210.5 %all-reduce.17.cloned.1.call-start = ((), (), s32[]{:S(2)}) async-start(), calls=%async_computation.20 | async-start | bytes 8388608 | tf_op jit(solution)/shard_map/psum | solution.py:289
  2149.7 259.9 %reduce-scatter.11.cloned.1.call-start = ((), (), s32[]{:S(2)}) async-start(), calls=%async_computation.17 | async-start | bytes 4718592 | tf_op jit(solution)/shard_map/reduce_scatter | solution.py:354
  2184.2 51.2 %copy-start.64 = (bf16[2048]{0:T(1024)(128)(2,1)S(1)}, bf16[2048]{0:T(1024)(128)(2,1)}, u32[]{:S(2)}) copy-start(bf16[2048]{0:T(1024)(128)(2,1)} %get-tuple-element.13) | copy-start | bytes 12292
  2184.2 51.2 %copy-start.77 = (bf16[128]{0:T(256)(128)(2,1)S(1)}, bf16[128]{0:T(256)(128)(2,1)}, u32[]{:S(2)}) copy-start(bf16[128]{0:T(256)(128)(2,1)} %get-tuple-element.17) | copy-start | bytes 772
  (63 other events, 187.1 us)
Sparse Core Ops, SparseCore 0:
  9.9 39.9 all-gather.6
  77.0 85.2 all-reduce.12
  461.7 547.3 reduce-scatter.6
  1407.2 547.8 reduce-scatter.8
  2028.4 46.0 all-gather.10
  2076.5 28.2 all-gather.8
  2108.1 32.8 reduce-scatter.16
  2144.1 34.1 reduce-scatter.14
  2181.3 51.6 all-reduce.14
  2235.9 33.6 reduce-scatter.12
  2273.9 80.9 all-reduce.16
  2358.1 51.3 reduce-scatter.10
where the time goes:
time: 2430 us; the launch traced here: 2420 us
  waiting for transfers between devices  1390 us (57%)
  blocking collectives  536 us (22%)
  local copies, waits for them, and re-layouts  233 us (10%)
  matrix products  132 us (5%)
  other arithmetic  109 us (4%)
    reduce_scatter x2, waiting for transfers between devices, return_rows(): lax.psum_scatter(producer(jnp.int32(0), quarter * lax.axis_size('tp')), '...  1100 us
    all_to_all x2, blocking collectives, send_rows(): lax.all_to_all(row_block, 'ep', split_axis=0, concat_axis=0, tiled=True)  376 us
    psum x1, waiting for transfers between devices, shards(): lax.psum(output_local.astype(jnp.bfloat16), 'ep').astype(jnp.float32)  69.1 us
    all_to_all x1, blocking collectives, return_rows(): lax.all_to_all(rounded, 'ep', split_axis=1, concat_axis=1, tiled=True)  53.5 us
  transfers between devices with their start and end apart: 13, of which 9 were waited for; matrix products, arithmetic and copies ran while one was open for 8% of the time, Pallas kernels for 0%

commit v1 on v0

v1 whole, which is shorter than its diff:
```python
import functools
import math

import jax
import jax.numpy as jnp
from jax import lax
from jax.experimental import pallas as pl
from jax.experimental.pallas import tpu as pltpu
from jax.sharding import PartitionSpec as P

HEAD_SIZE = 128
TOP = 8
PAIR = 64
LANES = 128

EPSILON = 1e-06
THETA = 1000000.0
F32 = jnp.float32
BF16 = jnp.bfloat16


def norm_rows(value_rows, norm_gain):
    return (
        value_rows
        * lax.rsqrt(jnp.mean(value_rows * value_rows, axis=-1, keepdims=True) + EPSILON)
        * norm_gain
    )


def norm_back(value_rows, norm_gain, upstream):
    scaling = lax.rsqrt(jnp.mean(value_rows * value_rows, axis=-1, keepdims=True) + EPSILON)
    normal = value_rows * scaling
    weighted = upstream * norm_gain
    inward = scaling * (weighted - normal * jnp.mean(weighted * normal, axis=-1, keepdims=True))
    return (inward, upstream * normal)


def rope_tables(positions, head_size):
    halfway = head_size // 2
    inverse = THETA ** (-(jnp.arange(halfway, dtype=jnp.float32) * 2.0) / head_size)
    angles = positions.astype(jnp.float32)[:, None] * inverse[None, :]
    return (jnp.cos(angles)[:, None, :], jnp.sin(angles)[:, None, :])


def rotate(value_rows, cosine, sine_table):
    halfway = value_rows.shape[-1] // 2
    first_half = value_rows[..., :halfway]
    second_half = value_rows[..., halfway:]
    return jnp.concatenate(
        [
            first_half * cosine - second_half * sine_table,
            second_half * cosine + first_half * sine_table,
        ],
        axis=-1,
    )


def rotate_back(upstream, cosine, sine_table):
    halfway = upstream.shape[-1] // 2
    first_half = upstream[..., :halfway]
    second_half = upstream[..., halfway:]
    return jnp.concatenate(
        [
            first_half * cosine + second_half * sine_table,
            second_half * cosine - first_half * sine_table,
        ],
        axis=-1,
    )


SWAPPED = 8


def swap(value, axis, mask):
    count = lax.axis_size(axis)
    return lax.ppermute(value, axis, [(i, i ^ mask) for i in range(count)])


def link_bits(reverse):
    count = lax.axis_size("ep")
    bits = [1 << i for i in range(1, count.bit_length() - 1)]
    return bits[::-1] if reverse else bits


def gather_half(value, reverse):
    blocks = {0: value}
    for bit in link_bits(reverse):
        blocks.update({m | bit: swap(v, "ep", bit) for m, v in blocks.items()})
    blocks.update({m | 1: swap(v, "ep", 1) for m, v in blocks.items()})
    return [blocks[m] for m in range(lax.axis_size("ep"))]


def gather_blocks(value):
    if lax.axis_size("ep") > SWAPPED:
        return lax.all_gather(value, "ep", axis=0, tiled=True)
    half = value.shape[0] // 2
    upper = gather_half(value[:half], False)
    lower = gather_half(value[half:], True)
    return jnp.concatenate([v for pair in zip(upper, lower) for v in pair], axis=0)


def plus(left, right):
    return (left.astype(F32) + right.astype(F32)).astype(BF16)


def scatter_half(blocks, reverse):
    for bit in link_bits(reverse):
        blocks = {
            m: plus(v, swap(blocks[m | bit], "ep", bit)) for m, v in blocks.items() if not m & bit
        }
    return blocks[0]


def scatter_blocks(value):
    count = lax.axis_size("ep")
    if count > SWAPPED:
        return [lax.psum_scatter(value, "ep", scatter_dimension=0, tiled=True)]
    rows = value.shape[0] // count
    half = rows // 2
    piece = lambda m, h: value[m * rows + h * half : m * rows + (h + 1) * half]
    halves = []
    for h in range(2):
        blocks = {
            m: plus(piece(m, h), swap(piece(m | 1, h), "ep", 1)) for m in range(0, count, 2)
        }
        halves.append(scatter_half(blocks, h == 1))
    return halves


def sum_chunks(value):
    parts = lax.axis_size("tp")
    mine = lax.axis_index("tp")
    rows = value.shape[0] // parts
    take = lambda i: lax.dynamic_slice_in_dim(value, i * rows, rows, 0)
    total = take(mine).astype(F32)
    for mask in range(1, parts):
        total = total + swap(take(mine ^ mask), "tp", mask).astype(F32)
    return total


def spread_chunks(chunk):
    parts = lax.axis_size("tp")
    mine = lax.axis_index("tp")
    rows = chunk.shape[0]
    result = jnp.zeros((parts * rows,) + chunk.shape[1:], chunk.dtype)
    for mask in range(parts):
        piece = swap(chunk, "tp", mask) if mask else chunk
        result = lax.dynamic_update_slice_in_dim(result, piece, (mine ^ mask) * rows, 0)
    return result


def sum_tp(value):
    return spread_chunks(sum_chunks(value).astype(BF16))


def reorder(value, axis):
    count = lax.axis_size("ep")
    if count > SWAPPED:
        return value
    mine = lax.axis_index("ep")
    size = value.shape[axis] // count
    return jnp.concatenate(
        [lax.dynamic_slice_in_dim(value, (mine ^ m) * size, size, axis) for m in range(count)],
        axis=axis,
    )


def expert_kernel(
    base_ref, x_ref, g_ref, ids_ref, router_ref, wgu_ref, wd_ref, dx_ref, joined_ref, hidden_ref
):
    rows = x_ref.shape[0]
    features = x_ref.shape[1]
    expert_count = router_ref.shape[1]
    hidden_count = wd_ref.shape[0]
    extra = dx_ref.shape[1] - features
    base = base_ref[0]
    local = base_ref.shape[0] - 1
    x = x_ref[...]
    logits = jnp.dot(x, router_ref[...], preferred_element_type=F32)
    lane = lax.broadcasted_iota(jnp.int32, (rows, expert_count), 1)
    named = ids_ref[:, 0:1] == lane
    for k in range(1, TOP):
        named = named | (ids_ref[:, k : k + 1] == lane)
    exponent = jnp.exp(logits - jnp.max(logits, axis=1, keepdims=True))
    router = exponent / jnp.sum(exponent, axis=1, keepdims=True)
    chosen = jnp.where(named, router, 0.0)
    gates = chosen / jnp.sum(chosen, axis=1, keepdims=True)
    gate = [
        jnp.sum(jnp.where(lane == base + j, gates, 0.0), axis=1, keepdims=True)
        for j in range(local)
    ]
    act = jnp.dot(x, wgu_ref[...], preferred_element_type=F32)
    back = lax.dot_general(
        g_ref[...], wd_ref[...], (((1,), (1,)), ((), ())), preferred_element_type=F32
    )
    left = lax.broadcasted_iota(jnp.int32, (rows, LANES), 1) < PAIR
    per_expert = hidden_count // local // PAIR
    gate_sum = [jnp.zeros((rows, LANES), F32) for _ in range(local)]
    for p in range(hidden_count // LANES):
        one, two = 2 * p // per_expert, (2 * p + 1) // per_expert
        first = act[:, 2 * p * LANES : (2 * p + 1) * LANES]
        second = act[:, (2 * p + 1) * LANES : (2 * p + 2) * LANES]
        g = jnp.where(left, first, pltpu.roll(second, PAIR, 1))
        u = jnp.where(left, pltpu.roll(first, PAIR, 1), second)
        gh = back[:, p * LANES : (p + 1) * LANES]
        if one == two:
            scale = jnp.broadcast_to(gate[one], (rows, LANES))
        else:
            scale = jnp.where(left, gate[one], gate[two])
        sig = 1.0 / (1.0 + jnp.exp(-g))
        silu = g * sig
        hid = silu * u
        product = hid * gh
        if one == two:
            gate_sum[one] += product
        else:
            gate_sum[one] += jnp.where(left, product, 0.0)
            gate_sum[two] += jnp.where(left, 0.0, product)
        hidden_ref[:, p * LANES : (p + 1) * LANES] = (hid * scale).astype(BF16)
        gs = gh * scale
        dg = gs * u * sig * (1.0 + g * (1.0 - sig))
        du = gs * silu
        joined_ref[:, 2 * p * LANES : (2 * p + 1) * LANES] = jnp.where(
            left, dg, pltpu.roll(du, PAIR, 1)
        ).astype(BF16)
        joined_ref[:, (2 * p + 1) * LANES : (2 * p + 2) * LANES] = jnp.where(
            left, pltpu.roll(dg, PAIR, 1), du
        ).astype(BF16)
    dx = lax.dot_general(
        joined_ref[...], wgu_ref[...], (((1,), (1,)), ((), ())), preferred_element_type=F32
    )
    dx_ref[:, :features] = dx.astype(BF16)
    wide = lax.broadcasted_iota(jnp.int32, (rows, extra), 1)
    tail = jnp.zeros((rows, extra), F32)
    for j in range(local):
        total = jnp.sum(gate_sum[j], axis=1, keepdims=True)
        high = total.astype(BF16).astype(F32)
        tail = jnp.where(wide == base + j, high, tail)
        tail = jnp.where(wide == expert_count + base + j, total - high, tail)
    dx_ref[:, features:] = tail.astype(BF16)


def run_experts(x, g, ids, router, wgu, wd, local):
    tokens, features = x.shape
    tile = 256
    expert_count = router.shape[1]
    extra = -(-2 * expert_count // LANES) * LANES
    base = jnp.full((local + 1,), lax.axis_index("ep") * local, jnp.int32)
    whole = lambda v: pl.BlockSpec(v.shape, lambda i, s: (0, 0), pipeline_mode=pl.Buffered(1))
    by_rows = lambda width: pl.BlockSpec((tile, width), lambda i, s: (i, 0))
    return pl.pallas_call(
        expert_kernel,
        grid_spec=pltpu.PrefetchScalarGridSpec(
            num_scalar_prefetch=1,
            grid=(tokens // tile,),
            in_specs=[
                by_rows(features),
                by_rows(features),
                by_rows(TOP),
                whole(router),
                whole(wgu),
                whole(wd),
            ],
            out_specs=[by_rows(features + extra), by_rows(wgu.shape[1]), by_rows(wd.shape[0])],
        ),
        out_shape=[
            jax.ShapeDtypeStruct((tokens, features + extra), BF16),
            jax.ShapeDtypeStruct((tokens, wgu.shape[1]), BF16),
            jax.ShapeDtypeStruct((tokens, wd.shape[0]), BF16),
        ],
        compiler_params=pltpu.CompilerParams(vmem_limit_bytes=48 * 1024 * 1024),
        cost_estimate=pl.CostEstimate(
            flops=2 * tokens * features * (2 * wgu.shape[1] + wd.shape[0]),
            bytes_accessed=2 * tokens * features * 3 + 2 * features * 2 * wgu.shape[1],
            transcendentals=tokens * wd.shape[0],
        ),
    )(base, x, g, ids, router, wgu, wd)


def shards(
    hidden_in,
    expert_ids,
    attention_gain,
    query_gain,
    key_gain,
    query_weight,
    key_matrix,
    value_matrix,
    output_weight,
    expert_gain,
    router_weight,
    gate_up_weight,
    down_weight,
    output_grad,
):
    tokens, features = hidden_in.shape
    owners = lax.axis_size("ep")
    local_experts = gate_up_weight.shape[0]
    expert_count = local_experts * owners
    everyone = lambda v: lax.all_gather(v, "ep", axis=0, tiled=True)

    weights = jnp.concatenate([query_weight, key_matrix, value_matrix], axis=1)
    weights_rel = gather_blocks(weights)
    packed = everyone(
        jnp.concatenate([router_weight, attention_gain[:, None], expert_gain[:, None]], axis=1)
    )
    router_full = packed[:, :expert_count]
    attn_gain_full = packed[:, expert_count].astype(F32)
    mlp_gain_full = packed[:, expert_count + 1].astype(F32)
    head_gains = everyone(jnp.stack([query_gain, key_gain], axis=1)).astype(F32)
    query_gain_full = head_gains[:, 0]
    key_gain_full = head_gains[:, 1]
    ids_rel = gather_blocks(expert_ids)
    grads_rel = gather_blocks(output_grad)
    wgu = gate_up_weight.transpose(1, 0, 2).reshape(features, -1)
    wd = down_weight.reshape(-1, features)

    hidden_f = hidden_in.astype(F32)
    normed_low = norm_rows(hidden_f, attn_gain_full).astype(BF16)
    normed_rel = reorder(normed_low, 1)
    query_width = query_weight.shape[1]
    key_width = key_matrix.shape[1]
    query_heads = query_width // HEAD_SIZE
    key_heads = key_width // HEAD_SIZE
    heads_per_group = query_heads // key_heads
    raw = jnp.dot(normed_rel, weights_rel, preferred_element_type=F32)
    query_raw = raw[:, :query_width].reshape(tokens, query_heads, HEAD_SIZE)
    key_raw = raw[:, query_width : query_width + key_width].reshape(tokens, key_heads, HEAD_SIZE)
    value_low = raw[:, query_width + key_width :].astype(BF16)
    positions = jnp.arange(tokens, dtype=jnp.int32)
    cosine, sine_table = rope_tables(positions, HEAD_SIZE)
    query_low = rotate(norm_rows(query_raw, query_gain_full), cosine, sine_table).astype(BF16)
    all_keys = rotate(norm_rows(key_raw, key_gain_full), cosine, sine_table).astype(BF16)
    all_values = value_low.reshape(tokens, key_heads, HEAD_SIZE)
    allowed = jnp.arange(tokens)[None, :] <= jnp.arange(tokens)[:, None]
    grouped_queries = query_low.reshape(tokens, key_heads, heads_per_group, HEAD_SIZE)

    def score_block():
        raw_scores = jnp.einsum(
            "ikgd,jkd->kgij", grouped_queries, all_keys, preferred_element_type=F32
        ) / math.sqrt(HEAD_SIZE)
        return jnp.where(allowed, raw_scores, -jnp.inf)

    scores = score_block()
    row_max = jnp.max(scores, axis=-1, keepdims=True)
    exps = jnp.exp(scores - row_max)
    row_total = jnp.sum(exps, axis=-1, keepdims=True)
    probs = exps / row_total
    log_total = row_max + jnp.log(row_total)
    attention_output = (
        jnp.einsum("kgij,jkd->ikgd", probs.astype(BF16), all_values, preferred_element_type=F32)
        .astype(BF16)
        .reshape(tokens, query_heads * HEAD_SIZE)
    )
    head_part = jnp.dot(attention_output, output_weight, preferred_element_type=F32)
    attended = sum_tp(head_part.astype(BF16)).astype(F32)
    resid = hidden_f + attended
    routed_low = norm_rows(resid, mlp_gain_full).astype(BF16)
    routed_rel = gather_blocks(routed_low)
    logits = jnp.dot(routed_low, router_full, preferred_element_type=F32)
    logit_max = jnp.max(logits, axis=-1, keepdims=True)
    exponent = jnp.exp(logits - logit_max)
    router = exponent / jnp.sum(exponent, axis=-1, keepdims=True)
    every_expert = jnp.arange(expert_count, dtype=jnp.int32)
    named = jnp.any(expert_ids[:, :, None] == every_expert[None, None, :], axis=1)
    chosen = jnp.where(named, router, 0.0)
    chosen_total = jnp.sum(chosen, axis=1, keepdims=True)
    gates = chosen / chosen_total

    grad_parts, joined, hidden = run_experts(
        routed_rel, grads_rel, ids_rel, router_full, wgu, wd, local_experts
    )
    returned = sum_tp(jnp.concatenate(scatter_blocks(grad_parts), axis=0))

    mixture_parts = jnp.dot(hidden, wd, preferred_element_type=F32).astype(BF16)
    mixture = sum_tp(jnp.concatenate(scatter_blocks(mixture_parts), axis=0))
    block_out = (resid + mixture.astype(F32)).astype(BF16)
    down_grad = lax.dot_general(
        hidden, grads_rel, (((0,), (0,)), ((), ())), preferred_element_type=F32
    ).reshape(down_weight.shape)
    gate_up_grad = jnp.einsum(
        "td,ten->edn",
        routed_rel,
        joined.reshape(joined.shape[0], local_experts, -1),
        preferred_element_type=F32,
    )

    grad_out = output_grad.astype(F32)
    tail = returned[:, features:].astype(F32)
    grad_gates = tail[:, :expert_count] + tail[:, expert_count : 2 * expert_count]
    grad_gates = jnp.where(named, grad_gates, 0.0)
    grad_router = jnp.where(
        named,
        (grad_gates - jnp.sum(grad_gates * gates, axis=1, keepdims=True)) / chosen_total,
        0.0,
    )
    grad_logits = (
        router * (grad_router - jnp.sum(router * grad_router, axis=1, keepdims=True))
    ).astype(BF16)
    router_grad = jnp.dot(routed_low.T, grad_logits, preferred_element_type=F32)
    grad_routed = returned[:, :features].astype(F32) + jnp.dot(
        grad_logits, router_full.T, preferred_element_type=F32
    )
    grad_resid_norm, mlp_terms = norm_back(resid, mlp_gain_full, grad_routed)
    mlp_gain_grad = jnp.sum(mlp_terms, axis=0)
    grad_resid = grad_out + grad_resid_norm
    grad_attended = grad_resid.astype(BF16)
    output_local = jnp.dot(
        reorder(attention_output, 1).T, grad_attended, preferred_element_type=F32
    ).astype(BF16)
    output_rows = jnp.concatenate(scatter_blocks(output_local), axis=0)
    output_weight_grad = reorder(gather_blocks(output_rows), 0).astype(F32)
    grad_mixed = (
        jnp.dot(grad_attended, output_weight.T, preferred_element_type=F32)
        .astype(BF16)
        .reshape(tokens, key_heads, heads_per_group, HEAD_SIZE)
    )
    probs_again = jnp.exp(score_block() - log_total)
    grad_probs = jnp.einsum("ikgd,jkd->kgij", grad_mixed, all_values, preferred_element_type=F32)
    grad_values = jnp.einsum(
        "kgij,ikgd->jkd", probs_again.astype(BF16), grad_mixed, preferred_element_type=F32
    )
    grad_scores = (
        probs_again * (grad_probs - jnp.sum(probs_again * grad_probs, axis=-1, keepdims=True))
    ).astype(BF16)
    grad_queries = jnp.einsum(
        "kgij,jkd->ikgd", grad_scores, all_keys, preferred_element_type=F32
    ) / math.sqrt(HEAD_SIZE)
    grad_keys = jnp.einsum(
        "kgij,ikgd->jkd", grad_scores, grouped_queries, preferred_element_type=F32
    ) / math.sqrt(HEAD_SIZE)
    grad_query_rot = rotate_back(
        grad_queries.reshape(tokens, query_heads, HEAD_SIZE), cosine, sine_table
    )
    grad_query_raw, query_terms = norm_back(query_raw, query_gain_full, grad_query_rot)
    grad_key_rot = rotate_back(grad_keys, cosine, sine_table)
    grad_key_raw, key_terms = norm_back(key_raw, key_gain_full, grad_key_rot)
    grad_raw = jnp.concatenate(
        [
            grad_query_raw.reshape(tokens, -1).astype(BF16),
            grad_key_raw.reshape(tokens, -1).astype(BF16),
            grad_values.reshape(tokens, -1).astype(BF16),
        ],
        axis=1,
    )
    weights_grad = jnp.dot(normed_rel.T, grad_raw, preferred_element_type=F32).astype(BF16)
    weights_rows = jnp.concatenate(scatter_blocks(weights_grad), axis=0).astype(F32)
    feature_part = lax.dot_general(
        grad_raw, weights_rel, (((1,), (1,)), ((), ())), preferred_element_type=F32
    ).astype(BF16)
    grad_normed = reorder(sum_tp(feature_part), 1).astype(F32)
    grad_input_norm, attn_terms = norm_back(hidden_f, attn_gain_full, grad_normed)
    input_grad = grad_resid + grad_input_norm
    attn_gain_grad = jnp.sum(attn_terms, axis=0)
    small = lax.psum_scatter(
        jnp.concatenate(
            [router_grad, attn_gain_grad[:, None], mlp_gain_grad[:, None]], axis=1
        ).astype(BF16),
        "ep",
        scatter_dimension=0,
        tiled=True,
    ).astype(F32)
    head_grads = jnp.stack(
        [jnp.sum(query_terms, axis=(0, 1)), jnp.sum(key_terms, axis=(0, 1))], axis=1
    )
    head_grads = lax.psum(head_grads.astype(BF16), ("ep", "tp")).astype(F32)
    share = HEAD_SIZE // owners
    head_grads = lax.dynamic_slice_in_dim(head_grads, lax.axis_index("ep") * share, share, 0)
    return (
        block_out,
        input_grad,
        small[:, expert_count],
        head_grads[:, 0],
        head_grads[:, 1],
        weights_rows[:, :query_width],
        weights_rows[:, query_width : query_width + key_width],
        weights_rows[:, query_width + key_width :],
        output_weight_grad,
        small[:, expert_count + 1],
        small[:, :expert_count],
        gate_up_grad,
        down_grad,
    )


def solution(mesh):
    in_specs = (
        P("ep", None),
        P("ep", None),
        P("ep"),
        P("ep"),
        P("ep"),
        P("ep", "tp"),
        P("ep", "tp"),
        P("ep", "tp"),
        P("tp", None),
        P("ep"),
        P("ep", None),
        P("ep", None, "tp"),
        P("ep", "tp", None),
        P("ep", None),
    )
    out_specs = (
        P("ep", None),
        P("ep", None),
        P("ep"),
        P("ep"),
        P("ep"),
        P("ep", "tp"),
        P("ep", "tp"),
        P("ep", "tp"),
        P("tp", None),
        P("ep"),
        P("ep", None),
        P("ep", None, "tp"),
        P("ep", "tp", None),
    )
    return jax.shard_map(shards, mesh=mesh, in_specs=in_specs, out_specs=out_specs, check_vma=False)
```

time: 2430 us -> 804 us (0.33)
  waiting for transfers between devices: 1390 us -> 300 us
  blocking collectives: 536 us -> 62.6 us
  local copies, waits for them, and re-layouts: 233 us -> 129 us
  starting transfers between devices: 5.4 us -> 99.8 us
  matrix products: 132 us -> 66.9 us
  Pallas kernels: 0 us -> 50.5 us
  other arithmetic: 109 us -> 67.7 us
    reduce_scatter x6 -> x1, waiting for transfers between devices: 1160 us -> 15 us  [shards(): lax.psum_scatter(jnp.concatenate([router_grad, attn_gain_grad[:, None], m...]
    all_to_all x3 -> x0, blocking collectives: 429 us -> none  [the longest x2 376 us: send_rows(): lax.all_to_all(row_block, 'ep', split_axis=0, concat_axis=0, tiled=True)]
    ppermute x0 -> x150, waiting for transfers between devices: none -> 285 us  [swap(): return lax.ppermute(value, axis, [(i, i ^ mask) for i in range(count)])]
    psum x3 -> x0, waiting for transfers between devices: 158 us -> none  [the longest x1 69.1 us: shards(): lax.psum(output_local.astype(jnp.bfloat16), 'ep').astype(jnp.float32)]
    gather x10 -> x0, local copies, waits for them, and re-layouts: 132 us -> none  [the longest x1 33.3 us: shards(): grad_out[source_token] * gate_flat[clipped][:, None]]
    ppermute x0 -> x150, starting transfers between devices: none -> 99.7 us  [swap(): return lax.ppermute(value, axis, [(i, i ^ mask) for i in range(count)])]
    dot_general x24 -> x14, matrix products: 128 us -> 61.7 us  [the longest x1 17.1 us: shards(): jnp.einsum('td,ten->edn', routed_rel, joined.reshape(joined.shape[0], loc...]
    all_gather x3 -> x0, waiting for transfers between devices: 64.2 us -> none  [the longest x1 38.6 us: shards(): lax.all_gather(grad_share, 'tp', axis=0, tiled=True)]
  transfers between devices with their start and end apart: 13 -> 151, of which waited for: 9 -> 58; matrix products, arithmetic and copies ran while one was open for 8% -> 26% of each run, Pallas kernels for 0% -> 0%
where the time goes in v1:
time: 804 us; the launch traced here: 793 us
  waiting for transfers between devices  300 us (37%)
  local copies, waits for them, and re-layouts  129 us (16%)
  starting transfers between devices  99.8 us (12%)
  other arithmetic  67.7 us (8%)
  matrix products  66.9 us (8%)
  blocking collectives  62.6 us (8%)
  Pallas kernels  50.5 us (6%)
  between operations  16.3 us (2%)
    ppermute x150, waiting for transfers between devices, swap(): return lax.ppermute(value, axis, [(i, i ^ mask) for i in range(count)])  285 us
    ppermute x150, starting transfers between devices, swap(): return lax.ppermute(value, axis, [(i, i ^ mask) for i in range(count)])  99.7 us
    unnamed x250, local copies, waits for them, and re-layouts  83 us
    pallas_call x1, Pallas kernels, run_experts(): pl.pallas_call(expert_kernel, grid_spec=pltpu.PrefetchScalarGridSpec(num_...  50.5 us
    psum x1, blocking collectives, shards(): head_grads = lax.psum(head_grads.astype(BF16), ('ep', 'tp')).astype(F32)  37.9 us
    convert_element_type x17, other arithmetic, plus(): return (left.astype(F32) + right.astype(F32)).astype(BF16)  28.7 us
    all_gather x2, blocking collectives, shards(): everyone = lambda v: lax.all_gather(v, 'ep', axis=0, tiled=True)  24.7 us
    dot_general x1, matrix products, shards(): jnp.einsum('td,ten->edn', routed_rel, joined.reshape(joined.shape[0], loc...  17.1 us
  transfers between devices with their start and end apart: 151, of which 58 were waited for; matrix products, arithmetic and copies ran while one was open for 26% of the time, Pallas kernels for 0%

profile of v1, /device:TPU:8, one launch (start us, length us, event | category | flops | bytes accessed | tf_op | source)
XLA Modules:
  0.0 793.0 jit_solution(13083772688918040259)
XLA Ops:
  20.6 15.4 %all_gather.6 = bf16[2048,34]{1,0:T(8,128)(2,1)S(1)} all-gather(bf16[256,34]{1,0:T(8,128)(2,1)S(1)} %copy.155), channel_id=1, replica_groups=mesh['ep'=8,'tp'=4] {'ep'}, dimensions={0}, use_global_device_ids=true | all-gather | bytes 156672 | tf_op jit(solution)/shard_map/all_gather | solution.py:300
  37.0 9.3 %all-gather = bf16[8,16,2]{1,2,0:T(2,128)(2,1)S(1)} all-gather(bf16[1,16,2]{1,2,0:T(2,128)(2,1)S(1)} %maximum_bitcast_fusion.3), channel_id=1, replica_groups=mesh['ep'=8,'tp'=4] {'ep'}, dimensions={0}, use_global_device_ids=true | all-gather | bytes 576 | tf_op jit(solution)/shard_map/all_gather | solution.py:300
  53.8 6.2 copy.198
  103.7 9.1 %collective-permute-done.36 = bf16[128,2048]{1,0:T(8,128)(2,1)} collective-permute-done((bf16[128,2048]{1,0:T(8,128)(2,1)}, bf16[128,2048]{1,0:T(8,128)(2,1)}, u32[]{:S(2)}, u32[]{:S(2)}) %collective-permute-start.36) | collective-permute-done | bytes 524320 | tf_op jit(solution)/shard_map/ppermute | solution.py:76
  114.7 8.4 %collective-permute-done.37 = bf16[128,2048]{1,0:T(8,128)(2,1)} collective-permute-done((bf16[128,2048]{1,0:T(8,128)(2,1)}, bf16[128,2048]{1,0:T(8,128)(2,1)}, u32[]{:S(2)}, u32[]{:S(2)}) %collective-permute-start.37) | collective-permute-done | bytes 524320 | tf_op jit(solution)/shard_map/ppermute | solution.py:76
  132.7 13.8 %collective-permute-done.10 = bf16[128,1280]{1,0:T(8,128)(2,1)S(1)} collective-permute-done((bf16[128,1280]{1,0:T(8,128)(2,1)}, bf16[128,1280]{1,0:T(8,128)(2,1)S(1)}, u32[]{:S(2)}, u32[]{:S(2)}) %collective-permute-start.10) | collective-permute-done | bytes 327712 | tf_op jit(solution)/shard_map/ppermute | solution.py:76
  211.6 13.5 %collective-permute-done.18 = bf16[64,2048]{1,0:T(8,128)(2,1)S(1)} collective-permute-done((bf16[64,2048]{1,0:T(8,128)(2,1)S(1)}, bf16[64,2048]{1,0:T(8,128)(2,1)S(1)}, u32[]{:S(2)}, u32[]{:S(2)}) %collective-permute-start.18) | collective-permute-done | bytes 262176 | tf_op jit(solution)/shard_map/ppermute | solution.py:76
  225.2 6.5 collective-permute-done.19
  243.6 6.2 collective-permute-done.22
  253.2 7.4 collective-permute-done.23
  286.9 50.5 %shard_map.237 = (bf16[2048,2176]{1,0:T(8,128)(2,1)}, bf16[2048,1536]{1,0:T(8,128)(2,1)}, bf16[2048,768]{1,0:T(8,128)(2,1)S(1)}) custom-call(s32[5]{0:T(128)S(1)} %broadcast_in_dim.34.base_ref, bf16[2048,2048]{1,0:T(8,128)(2,1)} %constant_dynamic-update-slice_fusion.28.x_ref, bf16[2048,2048]{1,0:T(8,128)(2,1)} %constant_dynamic-update-slice_fusion.43.g_ref, ...), custom_call_target="tpu_custom_call" | custom-call | flops 32212254720 | bytes 37748736 | tf_op jit(solution)/shard_map/pallas_call | solution.py:251
  337.5 9.2 %convolution_convert_fusion.1 = bf16[2048,2048]{1,0:T(8,128)(2,1)S(1)} fusion(bf16[2048,768]{1,0:T(8,128)(2,1)S(1)} %get-tuple-element.16, bf16[768,2048]{1,0:T(8,128)(2,1)} %bitcast.213), kind=kOutput, calls=%fused_computation.3 | convolution fusion | flops 6446645248 | bytes 14680064 | tf_op jit(solution)/shard_map/dot_general | solution.py:375
  357.0 10.8 %fusion.96 = f32[768,2048]{1,0:T(8,128)} fusion(bf16[2048,768]{1,0:T(8,128)(2,1)S(1)} %get-tuple-element.16, bf16[2048,2048]{1,0:T(8,128)(2,1)} %constant_dynamic-update-slice_fusion.43.g_ref), kind=kOutput, calls=%fused_computation.400 | convolution fusion | flops 6442450944 | bytes 17825792 | tf_op jit(solution)/shard_map/dot_general | solution.py:378
  367.8 9.0 %copy.194 = bf16[2048,1536]{0,1:T(8,128)(2,1)} copy(bf16[2048,1536]{1,0:T(8,128)(2,1)} %get-tuple-element.18) | data formatting | bytes 12582912 | tf_op jit(solution)/shard_map/reshape | solution.py:384
  384.1 9.5 %collective-permute-done.71 = bf16[128,2048]{1,0:T(8,128)(2,1)S(1)} collective-permute-done((bf16[128,2048]{1,0:T(8,128)(2,1)}, bf16[128,2048]{1,0:T(8,128)(2,1)S(1)}, u32[]{:S(2)}, u32[]{:S(2)}) %collective-permute-start.71) | collective-permute-done | bytes 524320 | tf_op jit(solution)/shard_map/ppermute | solution.py:76
  399.5 8.4 %collective-permute-done.91 = bf16[128,2176]{1,0:T(8,128)(2,1)S(1)} collective-permute-done((bf16[128,2176]{1,0:T(8,128)(2,1)S(1)}, bf16[128,2176]{1,0:T(8,128)(2,1)S(1)}, u32[]{:S(2)}, u32[]{:S(2)}) %collective-permute-start.91) | collective-permute-done | bytes 557088 | tf_op jit(solution)/shard_map/ppermute | solution.py:76
  412.8 17.1 %fusion.2 = f32[4,2048,384]{1,2,0:T(8,128)} fusion(bf16[2048,4,384]{0,2,1:T(8,128)(2,1)S(1)} %bitcast.193, bf16[2048,2048]{1,0:T(8,128)(2,1)} %constant_dynamic-update-slice_fusion.28.x_ref), kind=kOutput, calls=%fused_computation.4 | convolution fusion | flops 12884901888 | bytes 27262976 | tf_op jit(solution)/shard_map/td,ten->edn/dot_general | solution.py:381
  429.8 12.6 %copy.180 = f32[4,2048,384]{2,1,0:T(8,128)} copy(f32[4,2048,384]{1,2,0:T(8,128)} %fusion.2) | data formatting | bytes 25165824
  449.9 7.5 collective-permute-done.64
  475.3 11.0 %collective-permute-done.78 = bf16[64,2048]{1,0:T(8,128)(2,1)S(1)} collective-permute-done((bf16[64,2048]{1,0:T(8,128)(2,1)S(1)}, bf16[64,2048]{1,0:T(8,128)(2,1)S(1)}, u32[]{:S(2)}, u32[]{:S(2)}) %collective-permute-start.78) | collective-permute-done | bytes 262176 | tf_op jit(solution)/shard_map/ppermute | solution.py:76
  486.3 7.4 collective-permute-done.77
  502.2 14.8 %collective-permute-done.97 = bf16[64,2176]{1,0:T(8,128)(2,1)S(1)} collective-permute-done((bf16[64,2176]{1,0:T(8,128)(2,1)S(1)}, bf16[64,2176]{1,0:T(8,128)(2,1)S(1)}, u32[]{:S(2)}, u32[]{:S(2)}) %collective-permute-start.97) | collective-permute-done | bytes 278560 | tf_op jit(solution)/shard_map/ppermute | solution.py:76
  522.6 18.7 %collective-permute-done.81 = bf16[64,2048]{1,0:T(8,128)(2,1)S(1)} collective-permute-done((bf16[64,2048]{1,0:T(8,128)(2,1)S(1)}, bf16[64,2048]{1,0:T(8,128)(2,1)S(1)}, u32[]{:S(2)}, u32[]{:S(2)}) %collective-permute-start.81) | collective-permute-done | bytes 262176 | tf_op jit(solution)/shard_map/ppermute | solution.py:76
  546.1 7.0 collective-permute-done.101
  590.9 37.9 %psum.7 = bf16[128,2]{0,1:T(2,128)(2,1)S(1)} all-reduce(bf16[128,2]{0,1:T(2,128)(2,1)S(1)} %pad_maximum_fusion.10), channel_id=1, replica_groups=mesh['ep'=8,'tp'=4] {'ep','tp'}, use_global_device_ids=true, to_apply=%region_23.24 | all-reduce | flops 256 | bytes 1024 | tf_op jit(solution)/shard_map/psum | solution.py:466
  642.2 9.0 %collective-permute-done.103 = bf16[64,2048]{1,0:T(8,128)(2,1)S(1)} collective-permute-done((bf16[64,2048]{1,0:T(8,128)(2,1)S(1)}, bf16[64,2048]{1,0:T(8,128)(2,1)S(1)}, u32[]{:S(2)}, u32[]{:S(2)}) %collective-permute-start.103) | collective-permute-done | bytes 262176 | tf_op jit(solution)/shard_map/ppermute | solution.py:76
  658.7 8.1 %collective-permute-done.105 = bf16[64,2048]{1,0:T(8,128)(2,1)S(1)} collective-permute-done((bf16[64,2048]{1,0:T(8,128)(2,1)S(1)}, bf16[64,2048]{1,0:T(8,128)(2,1)S(1)}, u32[]{:S(2)}, u32[]{:S(2)}) %collective-permute-start.105) | collective-permute-done | bytes 262176 | tf_op jit(solution)/shard_map/ppermute | solution.py:76
  671.1 9.5 %collective-permute-done.107 = bf16[64,2048]{1,0:T(8,128)(2,1)S(1)} collective-permute-done((bf16[64,2048]{1,0:T(8,128)(2,1)S(1)}, bf16[64,2048]{1,0:T(8,128)(2,1)S(1)}, u32[]{:S(2)}, u32[]{:S(2)}) %collective-permute-start.107) | collective-permute-done | bytes 262176 | tf_op jit(solution)/shard_map/ppermute | solution.py:76
  693.2 6.4 collective-permute-done.113
  702.5 15.0 %reduce-scatter.2.cloned.1.call-done = bf16[256,34]{0,1:T(8,128)(2,1)} async-done(((bf16[2048,34]{0,1:T(8,128)(2,1)}), bf16[256,34]{0,1:T(8,128)(2,1)}) %reduce-scatter.2.cloned.1.call-update) | async-done | bytes 17424 | tf_op jit(solution)/shard_map/reduce_scatter | solution.py:455
  752.8 5.7 collective-permute-done.120
  767.6 8.4 %collective-permute-done.146 = bf16[64,2048]{1,0:T(8,128)(2,1)S(1)} collective-permute-done((bf16[64,2048]{1,0:T(8,128)(2,1)S(1)}, bf16[64,2048]{1,0:T(8,128)(2,1)S(1)}, u32[]{:S(2)}, u32[]{:S(2)}) %collective-permute-start.146) | collective-permute-done | bytes 262176 | tf_op jit(solution)/shard_map/ppermute | solution.py:76
  (680 shorter events, 387.6 us)
Async XLA Ops:
  7.2 710.3 %reduce-scatter.2.cloned.1.call-start = ((), (), s32[]{:S(2)}) async-start(), calls=%async_computation.1 | async-start | bytes 184320 | tf_op jit(solution)/shard_map/reduce_scatter | solution.py:455
  13.3 78.1 %collective-permute-start = (bf16[128,1280]{1,0:T(8,128)(2,1)}, bf16[128,1280]{1,0:T(8,128)(2,1)S(1)}, u32[]{:S(2)}, u32[]{:S(2)}) collective-permute-start(bf16[128,1280]{1,0:T(8,128)(2,1)} %get-tuple-element.207), channel_id=1, source_target_pairs={{0,4},{4,0},{8,12},{12,8},{16,20},{20,16},{24,28},{28,24},{1,5},{5... | collective-permute-start | bytes 983048 | tf_op jit(solution)/shard_map/ppermute | solution.py:76
  13.3 82.2 %collective-permute-start.2 = (bf16[128,1280]{1,0:T(8,128)(2,1)}, bf16[128,1280]{1,0:T(8,128)(2,1)}, u32[]{:S(2)}, u32[]{:S(2)}) collective-permute-start(bf16[128,1280]{1,0:T(8,128)(2,1)} %get-tuple-element.207), channel_id=1, source_target_pairs={{0,8},{4,12},{8,0},{12,4},{16,24},{20,28},{24,16},{28,20},{1,9},{5... | collective-permute-start | bytes 983048 | tf_op jit(solution)/shard_map/ppermute | solution.py:76
  14.8 78.9 %collective-permute-start.1 = (bf16[128,1280]{1,0:T(8,128)(2,1)}, bf16[128,1280]{1,0:T(8,128)(2,1)}, u32[]{:S(2)}, u32[]{:S(2)}) collective-permute-start(bf16[128,1280]{1,0:T(8,128)(2,1)} %get-tuple-element.206), channel_id=1, source_target_pairs={{0,4},{4,0},{8,12},{12,8},{16,20},{20,16},{24,28},{28,24},{1,5},{5... | collective-permute-start | bytes 983048 | tf_op jit(solution)/shard_map/ppermute | solution.py:76
  15.0 82.7 %collective-permute-start.3 = (bf16[128,1280]{1,0:T(8,128)(2,1)}, bf16[128,1280]{1,0:T(8,128)(2,1)}, u32[]{:S(2)}, u32[]{:S(2)}) collective-permute-start(bf16[128,1280]{1,0:T(8,128)(2,1)} %get-tuple-element.206), channel_id=1, source_target_pairs={{0,8},{4,12},{8,0},{12,4},{16,24},{20,28},{24,16},{28,20},{1,9},{5... | collective-permute-start | bytes 983048 | tf_op jit(solution)/shard_map/ppermute | solution.py:76
  16.3 44.5 %collective-permute-start.48 = (s32[128,8]{0,1:T(8,128)S(1)}, s32[128,8]{0,1:T(8,128)S(1)}, u32[]{:S(2)}, u32[]{:S(2)}) collective-permute-start(s32[128,8]{0,1:T(8,128)S(1)} %get-tuple-element.221), channel_id=1, source_target_pairs={{0,4},{4,0},{8,12},{12,8},{16,20},{20,16},{24,28},{28,24},{1,5},{5... | collective-permute-start | bytes 12296 | tf_op jit(solution)/shard_map/ppermute | solution.py:76
  90.6 35.7 %collective-permute-start.6 = (bf16[128,1280]{1,0:T(8,128)(2,1)}, bf16[128,1280]{1,0:T(8,128)(2,1)}, u32[]{:S(2)}, u32[]{:S(2)}) collective-permute-start(bf16[128,1280]{1,0:T(8,128)(2,1)} %get-tuple-element.207), channel_id=1, source_target_pairs={{0,16},{4,20},{8,24},{12,28},{16,0},{20,4},{24,8},{28,12},{1,17},{... | collective-permute-start | bytes 983048 | tf_op jit(solution)/shard_map/ppermute | solution.py:76
  91.4 36.3 %collective-permute-start.7 = (bf16[128,1280]{1,0:T(8,128)(2,1)}, bf16[128,1280]{1,0:T(8,128)(2,1)S(1)}, u32[]{:S(2)}, u32[]{:S(2)}) collective-permute-start(bf16[128,1280]{1,0:T(8,128)(2,1)} %get-tuple-element.206), channel_id=1, source_target_pairs={{0,16},{4,20},{8,24},{12,28},{16,0},{20,4},{24,8},{28,12},{1,17},{... | collective-permute-start | bytes 983048 | tf_op jit(solution)/shard_map/ppermute | solution.py:76
  102.3 47.8 %collective-permute-start.40 = (bf16[128,2048]{1,0:T(8,128)(2,1)}, bf16[128,2048]{1,0:T(8,128)(2,1)}, u32[]{:S(2)}, u32[]{:S(2)}) collective-permute-start(bf16[128,2048]{1,0:T(8,128)(2,1)} %get-tuple-element.198), channel_id=1, source_target_pairs={{0,16},{4,20},{8,24},{12,28},{16,0},{20,4},{24,8},{28,12},{1,17},{... | collective-permute-start | bytes 1572872 | tf_op jit(solution)/shard_map/ppermute | solution.py:76
  132.7 43.5 %collective-permute-start.38 = (bf16[128,2048]{1,0:T(8,128)(2,1)}, bf16[128,2048]{1,0:T(8,128)(2,1)}, u32[]{:S(2)}, u32[]{:S(2)}) collective-permute-start(bf16[128,2048]{1,0:T(8,128)(2,1)} %collective-permute-done.36), channel_id=1, source_target_pairs={{0,4},{4,0},{8,12},{12,8},{16,20},{20,16},{24,28},{28,24},{1,5},{5... | collective-permute-start | bytes 1572872 | tf_op jit(solution)/shard_map/ppermute | solution.py:76
  150.1 41.4 %collective-permute-start.44 = (bf16[128,2048]{1,0:T(8,128)(2,1)}, bf16[128,2048]{1,0:T(8,128)(2,1)}, u32[]{:S(2)}, u32[]{:S(2)}) collective-permute-start(bf16[128,2048]{1,0:T(8,128)(2,1)} %collective-permute-done.36), channel_id=1, source_target_pairs={{0,16},{4,20},{8,24},{12,28},{16,0},{20,4},{24,8},{28,12},{1,17},{... | collective-permute-start | bytes 1572872 | tf_op jit(solution)/shard_map/ppermute | solution.py:76
  150.6 36.0 %collective-permute-start.42 = (bf16[128,2048]{1,0:T(8,128)(2,1)}, bf16[128,2048]{1,0:T(8,128)(2,1)}, u32[]{:S(2)}, u32[]{:S(2)}) collective-permute-start(bf16[128,2048]{1,0:T(8,128)(2,1)} %collective-permute-done.40), channel_id=1, source_target_pairs={{0,4},{4,0},{8,12},{12,8},{16,20},{20,16},{24,28},{28,24},{1,5},{5... | collective-permute-start | bytes 1572872 | tf_op jit(solution)/shard_map/ppermute | solution.py:76
  150.8 39.1 %collective-permute-start.43 = (bf16[128,2048]{1,0:T(8,128)(2,1)}, bf16[128,2048]{1,0:T(8,128)(2,1)}, u32[]{:S(2)}, u32[]{:S(2)}) collective-permute-start(bf16[128,2048]{1,0:T(8,128)(2,1)} %collective-permute-done.41), channel_id=1, source_target_pairs={{0,4},{4,0},{8,12},{12,8},{16,20},{20,16},{24,28},{28,24},{1,5},{5... | collective-permute-start | bytes 1572872 | tf_op jit(solution)/shard_map/ppermute | solution.py:76
  191.4 45.8 %collective-permute-start.46 = (bf16[128,2048]{1,0:T(8,128)(2,1)}, bf16[128,2048]{1,0:T(8,128)(2,1)}, u32[]{:S(2)}, u32[]{:S(2)}) collective-permute-start(bf16[128,2048]{1,0:T(8,128)(2,1)} %collective-permute-done.44), channel_id=1, source_target_pairs={{0,4},{4,0},{8,12},{12,8},{16,20},{20,16},{24,28},{28,24},{1,5},{5... | collective-permute-start | bytes 1572872 | tf_op jit(solution)/shard_map/ppermute | solution.py:76
  206.2 33.5 %collective-permute-start.47 = (bf16[128,2048]{1,0:T(8,128)(2,1)}, bf16[128,2048]{1,0:T(8,128)(2,1)}, u32[]{:S(2)}, u32[]{:S(2)}) collective-permute-start(bf16[128,2048]{1,0:T(8,128)(2,1)} %collective-permute-done.45), channel_id=1, source_target_pairs={{0,4},{4,0},{8,12},{12,8},{16,20},{20,16},{24,28},{28,24},{1,5},{5... | collective-permute-start | bytes 1572872 | tf_op jit(solution)/shard_map/ppermute | solution.py:76
  398.9 46.8 %collective-permute-start.85 = (bf16[128,2176]{1,0:T(8,128)(2,1)}, bf16[128,2176]{1,0:T(8,128)(2,1)}, u32[]{:S(2)}, u32[]{:S(2)}) collective-permute-start(bf16[128,2176]{1,0:T(8,128)(2,1)} %get-tuple-element.129), channel_id=1, source_target_pairs={{0,4},{4,0},{8,12},{12,8},{16,20},{20,16},{24,28},{28,24},{1,5},{5... | collective-permute-start | bytes 1671176 | tf_op jit(solution)/shard_map/ppermute | solution.py:76
  398.9 65.5 %collective-permute-start.82 = (bf16[128,2176]{1,0:T(8,128)(2,1)}, bf16[128,2176]{1,0:T(8,128)(2,1)}, u32[]{:S(2)}, u32[]{:S(2)}) collective-permute-start(bf16[128,2176]{1,0:T(8,128)(2,1)} %get-tuple-element.131), channel_id=1, source_target_pairs={{0,4},{4,0},{8,12},{12,8},{16,20},{20,16},{24,28},{28,24},{1,5},{5... | collective-permute-start | bytes 1671176 | tf_op jit(solution)/shard_map/ppermute | solution.py:76
  399.4 43.1 %collective-permute-start.65 = (bf16[128,2048]{1,0:T(8,128)(2,1)}, bf16[128,2048]{1,0:T(8,128)(2,1)}, u32[]{:S(2)}, u32[]{:S(2)}) collective-permute-start(bf16[128,2048]{1,0:T(8,128)(2,1)} %get-tuple-element.142), channel_id=1, source_target_pairs={{0,4},{4,0},{8,12},{12,8},{16,20},{20,16},{24,28},{28,24},{1,5},{5... | collective-permute-start | bytes 1572872 | tf_op jit(solution)/shard_map/ppermute | solution.py:76
  407.8 34.6 %collective-permute-start.67 = (bf16[128,2048]{1,0:T(8,128)(2,1)}, bf16[128,2048]{1,0:T(8,128)(2,1)}, u32[]{:S(2)}, u32[]{:S(2)}) collective-permute-start(bf16[128,2048]{1,0:T(8,128)(2,1)} %get-tuple-element.135), channel_id=1, source_target_pairs={{0,8},{4,12},{8,0},{12,4},{16,24},{20,28},{24,16},{28,20},{1,9},{5... | collective-permute-start | bytes 1572872 | tf_op jit(solution)/shard_map/ppermute | solution.py:76
  412.2 34.0 %collective-permute-start.87 = (bf16[128,2176]{1,0:T(8,128)(2,1)}, bf16[128,2176]{1,0:T(8,128)(2,1)}, u32[]{:S(2)}, u32[]{:S(2)}) collective-permute-start(bf16[128,2176]{1,0:T(8,128)(2,1)} %get-tuple-element.122), channel_id=1, source_target_pairs={{0,8},{4,12},{8,0},{12,4},{16,24},{20,28},{24,16},{28,20},{1,9},{5... | collective-permute-start | bytes 1671176 | tf_op jit(solution)/shard_map/ppermute | solution.py:76
  475.3 41.6 %collective-permute-start.97 = (bf16[64,2176]{1,0:T(8,128)(2,1)S(1)}, bf16[64,2176]{1,0:T(8,128)(2,1)S(1)}, u32[]{:S(2)}, u32[]{:S(2)}) collective-permute-start(bf16[64,2176]{1,0:T(8,128)(2,1)S(1)} %get-tuple-element.189), channel_id=1, source_target_pairs={{0,2},{1,3},{2,0},{3,1},{4,6},{5,7},{6,4},{7,5},{8,10},{9,11},{10,... | collective-permute-start | bytes 835592 | tf_op jit(solution)/shard_map/ppermute | solution.py:76
  486.3 30.6 %collective-permute-start.96 = (bf16[64,2176]{1,0:T(8,128)(2,1)S(1)}, bf16[64,2176]{1,0:T(8,128)(2,1)S(1)}, u32[]{:S(2)}, u32[]{:S(2)}) collective-permute-start(bf16[64,2176]{1,0:T(8,128)(2,1)S(1)} %get-tuple-element.188), channel_id=1, source_target_pairs={{0,1},{1,0},{2,3},{3,2},{4,5},{5,4},{6,7},{7,6},{8,9},{9,8},{10,11... | collective-permute-start | bytes 835592 | tf_op jit(solution)/shard_map/ppermute | solution.py:76
  500.8 40.5 %collective-permute-start.81 = (bf16[64,2048]{1,0:T(8,128)(2,1)S(1)}, bf16[64,2048]{1,0:T(8,128)(2,1)S(1)}, u32[]{:S(2)}, u32[]{:S(2)}) collective-permute-start(bf16[64,2048]{1,0:T(8,128)(2,1)S(1)} %get-tuple-element.116), channel_id=1, source_target_pairs={{0,3},{1,2},{2,1},{3,0},{4,7},{5,6},{6,5},{7,4},{8,11},{9,10},{10,... | collective-permute-start | bytes 786440 | tf_op jit(solution)/shard_map/ppermute | solution.py:76
  520.8 32.3 %collective-permute-start.101 = (bf16[64,2176]{1,0:T(8,128)(2,1)S(1)}, bf16[64,2176]{1,0:T(8,128)(2,1)S(1)}, u32[]{:S(2)}, u32[]{:S(2)}) collective-permute-start(bf16[64,2176]{1,0:T(8,128)(2,1)S(1)} %get-tuple-element.114), channel_id=1, source_target_pairs={{0,3},{1,2},{2,1},{3,0},{4,7},{5,6},{6,5},{7,4},{8,11},{9,10},{10,... | collective-permute-start | bytes 835592 | tf_op jit(solution)/shard_map/ppermute | solution.py:76
  589.5 52.5 %collective-permute-start.104 = (bf16[64,2048]{1,0:T(8,128)(2,1)}, bf16[64,2048]{1,0:T(8,128)(2,1)}, u32[]{:S(2)}, u32[]{:S(2)}) collective-permute-start(bf16[64,2048]{1,0:T(8,128)(2,1)} %get-tuple-element.192), channel_id=1, source_target_pairs={{0,3},{1,2},{2,1},{3,0},{4,7},{5,6},{6,5},{7,4},{8,11},{9,10},{10,... | collective-permute-start | bytes 786440 | tf_op jit(solution)/shard_map/ppermute | solution.py:76
  642.0 50.9 %collective-permute-start.111 = (bf16[128,1280]{1,0:T(8,128)(2,1)}, bf16[128,1280]{1,0:T(8,128)(2,1)S(1)}, u32[]{:S(2)}, u32[]{:S(2)}) collective-permute-start(bf16[128,1280]{1,0:T(8,128)(2,1)} %get-tuple-element.156), channel_id=1, source_target_pairs={{0,4},{4,0},{8,12},{12,8},{16,20},{20,16},{24,28},{28,24},{1,5},{5... | collective-permute-start | bytes 983048 | tf_op jit(solution)/shard_map/ppermute | solution.py:76
  651.1 35.6 %collective-permute-start.132 = (bf16[64,2048]{1,0:T(8,128)(2,1)}, bf16[64,2048]{1,0:T(8,128)(2,1)}, u32[]{:S(2)}, u32[]{:S(2)}) collective-permute-start(bf16[64,2048]{1,0:T(8,128)(2,1)} %get-tuple-element.162), channel_id=1, source_target_pairs={{0,4},{4,0},{8,12},{12,8},{16,20},{20,16},{24,28},{28,24},{1,5},{5... | collective-permute-start | bytes 786440 | tf_op jit(solution)/shard_map/ppermute | solution.py:76
  652.1 34.7 %collective-permute-start.125 = (bf16[64,2048]{1,0:T(8,128)(2,1)}, bf16[64,2048]{1,0:T(8,128)(2,1)}, u32[]{:S(2)}, u32[]{:S(2)}) collective-permute-start(bf16[64,2048]{1,0:T(8,128)(2,1)} %get-tuple-element.165), channel_id=1, source_target_pairs={{0,4},{4,0},{8,12},{12,8},{16,20},{20,16},{24,28},{28,24},{1,5},{5... | collective-permute-start | bytes 786440 | tf_op jit(solution)/shard_map/ppermute | solution.py:76
  686.8 45.5 %collective-permute-start.108 = (bf16[128,1280]{1,0:T(8,128)(2,1)S(1)}, bf16[128,1280]{1,0:T(8,128)(2,1)S(1)}, u32[]{:S(2)}, u32[]{:S(2)}) collective-permute-start(bf16[128,1280]{1,0:T(8,128)(2,1)S(1)} %copy-done.35), channel_id=1, source_target_pairs={{0,4},{4,0},{8,12},{12,8},{16,20},{20,16},{24,28},{28,24},{1,5},{5... | collective-permute-start | bytes 983048 | tf_op jit(solution)/shard_map/ppermute | solution.py:76
  686.9 45.5 %collective-permute-start.119 = (bf16[128,1280]{1,0:T(8,128)(2,1)S(1)}, bf16[128,1280]{1,0:T(8,128)(2,1)S(1)}, u32[]{:S(2)}, u32[]{:S(2)}) collective-permute-start(bf16[128,1280]{1,0:T(8,128)(2,1)S(1)} %copy-done.34), channel_id=1, source_target_pairs={{0,4},{4,0},{8,12},{12,8},{16,20},{20,16},{24,28},{28,24},{1,5},{5... | collective-permute-start | bytes 983048 | tf_op jit(solution)/shard_map/ppermute | solution.py:76
  687.4 32.8 %collective-permute-start.122 = (bf16[64,2048]{1,0:T(8,128)(2,1)}, bf16[64,2048]{1,0:T(8,128)(2,1)}, u32[]{:S(2)}, u32[]{:S(2)}) collective-permute-start(bf16[64,2048]{1,0:T(8,128)(2,1)} %get-tuple-element.167), channel_id=1, source_target_pairs={{0,4},{4,0},{8,12},{12,8},{16,20},{20,16},{24,28},{28,24},{1,5},{5... | collective-permute-start | bytes 786440 | tf_op jit(solution)/shard_map/ppermute | solution.py:76
  732.3 50.5 %collective-permute-start.115 = (bf16[128,1280]{1,0:T(8,128)(2,1)S(1)}, bf16[128,1280]{1,0:T(8,128)(2,1)S(1)}, u32[]{:S(2)}, u32[]{:S(2)}) collective-permute-start(bf16[128,1280]{1,0:T(8,128)(2,1)S(1)} %get-tuple-element.154), channel_id=1, source_target_pairs={{0,4},{4,0},{8,12},{12,8},{16,20},{20,16},{24,28},{28,24},{1,5},{5... | collective-permute-start | bytes 983048 | tf_op jit(solution)/shard_map/ppermute | solution.py:76
  (193 other events, 3064.2 us)
Sparse Core Ops, SparseCore 0:
  686.9 30.6 reduce-scatter.1

commit v2 on v1

v2 whole, which is shorter than its diff:
```python
import functools
import math

import jax
import jax.numpy as jnp
from jax import lax
from jax.experimental import pallas as pl
from jax.experimental.pallas import tpu as pltpu
from jax.sharding import PartitionSpec as P

HEAD_SIZE = 128
TOP = 8
PAIR = 64
LANES = 128

EPSILON = 1e-06
THETA = 1000000.0
F32 = jnp.float32
BF16 = jnp.bfloat16


def norm_rows(value_rows, norm_gain):
    return (
        value_rows
        * lax.rsqrt(jnp.mean(value_rows * value_rows, axis=-1, keepdims=True) + EPSILON)
        * norm_gain
    )


def norm_back(value_rows, norm_gain, upstream):
    scaling = lax.rsqrt(jnp.mean(value_rows * value_rows, axis=-1, keepdims=True) + EPSILON)
    normal = value_rows * scaling
    weighted = upstream * norm_gain
    inward = scaling * (weighted - normal * jnp.mean(weighted * normal, axis=-1, keepdims=True))
    return (inward, upstream * normal)


def rope_tables(positions, head_size):
    halfway = head_size // 2
    inverse = THETA ** (-(jnp.arange(halfway, dtype=jnp.float32) * 2.0) / head_size)
    angles = positions.astype(jnp.float32)[:, None] * inverse[None, :]
    return (jnp.cos(angles)[:, None, :], jnp.sin(angles)[:, None, :])


def rotate(value_rows, cosine, sine_table):
    halfway = value_rows.shape[-1] // 2
    first_half = value_rows[..., :halfway]
    second_half = value_rows[..., halfway:]
    return jnp.concatenate(
        [
            first_half * cosine - second_half * sine_table,
            second_half * cosine + first_half * sine_table,
        ],
        axis=-1,
    )


def rotate_back(upstream, cosine, sine_table):
    halfway = upstream.shape[-1] // 2
    first_half = upstream[..., :halfway]
    second_half = upstream[..., halfway:]
    return jnp.concatenate(
        [
            first_half * cosine + second_half * sine_table,
            second_half * cosine - first_half * sine_table,
        ],
        axis=-1,
    )


SWAPPED = 8


def swap(value, axis, mask):
    count = lax.axis_size(axis)
    return lax.ppermute(value, axis, [(i, i ^ mask) for i in range(count)])


def join(*values):
    return lax.optimization_barrier(values)


ORDER = (0, 2, 4, 6, 1, 3, 5, 7)


def plus(*values):
    total = values[0].astype(F32)
    for v in values[1:]:
        total = total + v.astype(F32)
    return total.astype(BF16)


def absolute():
    return lax.axis_size("ep") > SWAPPED


def gather_hops(value):
    if absolute():
        return [lax.all_gather(value, "ep", axis=0, tiled=True)]
    return [swap(value, "ep", m) for m in ORDER[1:4]]


def gather_near(value, hops):
    if absolute():
        return hops[0][: hops[0].shape[0] // 2]
    return jnp.concatenate([value] + hops, axis=0)


def gather_core(near, hops):
    if absolute():
        return hops[0][hops[0].shape[0] // 2 :]
    return swap(near, "ep", 1)


def scatter_swap(send):
    return send if absolute() else swap(send, "ep", 1)


def scatter_sums(keep, come):
    if absolute():
        return [jnp.concatenate([keep, come], axis=0)]
    rows = keep.shape[0] // 4
    return [
        plus(keep[i * rows : (i + 1) * rows], come[i * rows : (i + 1) * rows]) for i in range(4)
    ]


def scatter_hops(sums):
    if absolute():
        return [lax.psum_scatter(sums[0], "ep", scatter_dimension=0, tiled=True)]
    return [swap(v, "ep", m) for v, m in zip(sums[1:], ORDER[1:4])]


def scatter_total(sums, hops):
    return hops[0] if absolute() else plus(sums[0], *hops)


def chunk_of(value, index):
    rows = value.shape[0] // lax.axis_size("tp")
    return lax.dynamic_slice_in_dim(value, index * rows, rows, 0)


def reduce_hops(value):
    mine = lax.axis_index("tp")
    return [swap(chunk_of(value, mine ^ m), "tp", m) for m in range(1, lax.axis_size("tp"))]


def reduce_total(value, hops):
    return plus(chunk_of(value, lax.axis_index("tp")), *hops)


def spread_hops(chunk):
    return [swap(chunk, "tp", m) for m in range(1, lax.axis_size("tp"))]


def spread_total(chunk, hops):
    mine = lax.axis_index("tp")
    rows = chunk.shape[0]
    result = jnp.zeros(((len(hops) + 1) * rows,) + chunk.shape[1:], chunk.dtype)
    for m, piece in enumerate([chunk] + hops):
        result = lax.dynamic_update_slice_in_dim(result, piece, (mine ^ m) * rows, 0)
    return result


def pick_blocks(value, axis):
    count = lax.axis_size("ep")
    if count > SWAPPED:
        return value
    mine = lax.axis_index("ep")
    size = value.shape[axis] // count
    return jnp.concatenate(
        [lax.dynamic_slice_in_dim(value, (mine ^ m) * size, size, axis) for m in ORDER],
        axis=axis,
    )


def put_blocks(value, axis):
    count = lax.axis_size("ep")
    if count > SWAPPED:
        return value
    mine = lax.axis_index("ep")
    size = value.shape[axis] // count
    place = lambda m: (m // 2 + (m % 2) * (count // 2)) * size
    return jnp.concatenate(
        [lax.dynamic_slice_in_dim(value, place(mine ^ b), size, axis) for b in range(count)],
        axis=axis,
    )


def expert_kernel(
    base_ref, x_ref, g_ref, ids_ref, router_ref, wgu_ref, wd_ref, *rest
):
    dx_ref, joined_ref, hidden_ref = rest[-3:]
    rows = x_ref.shape[0]
    features = x_ref.shape[1]
    expert_count = router_ref.shape[1]
    hidden_count = wd_ref.shape[0]
    extra = dx_ref.shape[1] - features
    base = base_ref[0]
    local = base_ref.shape[0] - 1
    x = x_ref[...]
    logits = jnp.dot(x, router_ref[...], preferred_element_type=F32)
    lane = lax.broadcasted_iota(jnp.int32, (rows, expert_count), 1)
    named = ids_ref[:, 0:1] == lane
    for k in range(1, TOP):
        named = named | (ids_ref[:, k : k + 1] == lane)
    exponent = jnp.exp(logits - jnp.max(logits, axis=1, keepdims=True))
    router = exponent / jnp.sum(exponent, axis=1, keepdims=True)
    chosen = jnp.where(named, router, 0.0)
    gates = chosen / jnp.sum(chosen, axis=1, keepdims=True)
    gate = [
        jnp.sum(jnp.where(lane == base + j, gates, 0.0), axis=1, keepdims=True)
        for j in range(local)
    ]
    left = lax.broadcasted_iota(jnp.int32, (rows, LANES), 1) < PAIR
    per_expert = hidden_count // local // PAIR
    gate_sum = [jnp.zeros((rows, LANES), F32) for _ in range(local)]
    group = 3

    def products(q):
        wide = group * LANES
        act = jnp.dot(
            x, wgu_ref[:, 2 * q * wide : 2 * (q + 1) * wide], preferred_element_type=F32
        )
        back = lax.dot_general(
            g_ref[...],
            wd_ref[q * wide : (q + 1) * wide, :],
            (((1,), (1,)), ((), ())),
            preferred_element_type=F32,
        )
        return act, back

    def elementwise(q, act, back):
        for i in range(group):
            p = q * group + i
            one, two = 2 * p // per_expert, (2 * p + 1) // per_expert
            first = act[:, 2 * i * LANES : (2 * i + 1) * LANES]
            second = act[:, (2 * i + 1) * LANES : (2 * i + 2) * LANES]
            g = jnp.where(left, first, pltpu.roll(second, PAIR, 1))
            u = jnp.where(left, pltpu.roll(first, PAIR, 1), second)
            gh = back[:, i * LANES : (i + 1) * LANES]
            if one == two:
                scale = jnp.broadcast_to(gate[one], (rows, LANES))
            else:
                scale = jnp.where(left, gate[one], gate[two])
            sig = lax.logistic(g)
            silu = g * sig
            hid = silu * u
            product = hid * gh
            if one == two:
                gate_sum[one] += product
            else:
                gate_sum[one] += jnp.where(left, product, 0.0)
                gate_sum[two] += jnp.where(left, 0.0, product)
            hidden_ref[:, p * LANES : (p + 1) * LANES] = (hid * scale).astype(BF16)
            gs = gh * scale
            dg = gs * u * sig * (1.0 + g * (1.0 - sig))
            du = gs * silu
            joined_ref[:, 2 * p * LANES : (2 * p + 1) * LANES] = jnp.where(
                left, dg, pltpu.roll(du, PAIR, 1)
            ).astype(BF16)
            joined_ref[:, (2 * p + 1) * LANES : (2 * p + 2) * LANES] = jnp.where(
                left, pltpu.roll(dg, PAIR, 1), du
            ).astype(BF16)

    count = hidden_count // LANES // group
    waiting = []
    for q in range(count):
        waiting.append((q, *products(q)))
        if q:
            elementwise(*waiting.pop(0))
    elementwise(*waiting.pop(0))
    dx = lax.dot_general(
        joined_ref[...], wgu_ref[...], (((1,), (1,)), ((), ())), preferred_element_type=F32
    )
    dx_ref[:, :features] = dx.astype(BF16)
    wide = lax.broadcasted_iota(jnp.int32, (rows, extra), 1)
    tail = jnp.zeros((rows, extra), F32)
    for j in range(local):
        total = jnp.sum(gate_sum[j], axis=1, keepdims=True)
        high = total.astype(BF16).astype(F32)
        tail = jnp.where(wide == base + j, high, tail)
        tail = jnp.where(wide == expert_count + base + j, total - high, tail)
    dx_ref[:, features:] = tail.astype(BF16)


def run_experts(x, g, ids, router, wgu, wd, local, piece, pieces, earlier=None):
    tokens, features = x.shape
    tile = 256
    steps = tokens // tile
    expert_count = router.shape[1]
    extra = -(-2 * expert_count // LANES) * LANES
    base = jnp.full((local + 1,), lax.axis_index("ep") * local, jnp.int32)
    whole = lambda v: pl.BlockSpec(v.shape, lambda i, s: (0, 0), pipeline_mode=pl.Buffered(1))
    by_rows = lambda width, skip=0: pl.BlockSpec((tile, width), lambda i, s: (i + skip, 0))
    in_specs = [
        by_rows(features),
        by_rows(features),
        by_rows(TOP),
        whole(router),
        whole(wgu),
        whole(wd),
    ]
    operands = [base, x, g, ids, router, wgu, wd]
    aliases = {}
    if earlier:
        in_specs += [pl.BlockSpec(memory_space=pl.ANY)] * 2
        operands += list(earlier)
        aliases = {7: 1, 8: 2}
    return pl.pallas_call(
        expert_kernel,
        grid_spec=pltpu.PrefetchScalarGridSpec(
            num_scalar_prefetch=1,
            grid=(steps,),
            in_specs=in_specs,
            out_specs=[
                by_rows(features + extra),
                by_rows(wgu.shape[1], piece * steps),
                by_rows(wd.shape[0], piece * steps),
            ],
        ),
        out_shape=[
            jax.ShapeDtypeStruct((tokens, features + extra), BF16),
            jax.ShapeDtypeStruct((pieces * tokens, wgu.shape[1]), BF16),
            jax.ShapeDtypeStruct((pieces * tokens, wd.shape[0]), BF16),
        ],
        input_output_aliases=aliases,
        compiler_params=pltpu.CompilerParams(vmem_limit_bytes=36 * 1024 * 1024),
        cost_estimate=pl.CostEstimate(
            flops=2 * tokens * features * (2 * wgu.shape[1] + wd.shape[0]),
            bytes_accessed=2 * tokens * features * 3 + 2 * features * 2 * wgu.shape[1],
            transcendentals=tokens * wd.shape[0],
        ),
    )(*operands)


def rows_product(pieces, whole):
    rows = pieces[0].shape[0]
    total = None
    for i, v in enumerate(pieces):
        part = lax.dot_general(
            v[...],
            whole[i * rows : (i + 1) * rows, :],
            (((0,), (0,)), ((), ())),
            preferred_element_type=F32,
        )
        total = part if total is None else total + part
    return total


def gate_up_kernel(*refs):
    *pieces, joined_ref, result_ref = refs
    total = rows_product(pieces, joined_ref)
    width = result_ref.shape[2]
    for e in range(result_ref.shape[0]):
        result_ref[e] = total[:, e * width : (e + 1) * width]


def gate_up_product(pieces, joined, shape):
    rows, features = pieces[0].shape
    tile = 256
    return pl.pallas_call(
        gate_up_kernel,
        grid=(features // tile,),
        in_specs=[pl.BlockSpec((rows, tile), lambda i: (0, i)) for _ in pieces]
        + [pl.BlockSpec(joined.shape, lambda i: (0, 0), pipeline_mode=pl.Buffered(1))],
        out_specs=pl.BlockSpec((shape[0], tile, shape[2]), lambda i: (0, i, 0)),
        out_shape=jax.ShapeDtypeStruct(shape, F32),
        compiler_params=pltpu.CompilerParams(vmem_limit_bytes=56 * 1024 * 1024),
        cost_estimate=pl.CostEstimate(
            flops=2 * joined.shape[0] * features * joined.shape[1],
            bytes_accessed=2 * joined.shape[0] * features + 2 * joined.size + 4 * math.prod(shape),
            transcendentals=0,
        ),
    )(*pieces, joined)


def down_kernel(hidden_ref, *refs):
    *pieces, result_ref = refs
    rows = pieces[0].shape[0]
    total = None
    for i, v in enumerate(pieces):
        part = lax.dot_general(
            hidden_ref[i * rows : (i + 1) * rows, :],
            v[...],
            (((0,), (0,)), ((), ())),
            preferred_element_type=F32,
        )
        total = part if total is None else total + part
    result_ref[...] = total


def down_product(hidden, pieces):
    rows, features = pieces[0].shape
    tile = 256
    whole = pl.BlockSpec((rows, features), lambda i: (0, 0), pipeline_mode=pl.Buffered(1))
    return pl.pallas_call(
        down_kernel,
        grid=(hidden.shape[1] // tile,),
        in_specs=[pl.BlockSpec((hidden.shape[0], tile), lambda i: (0, i))] + [whole] * len(pieces),
        out_specs=pl.BlockSpec((tile, features), lambda i: (i, 0)),
        out_shape=jax.ShapeDtypeStruct((hidden.shape[1], features), F32),
        compiler_params=pltpu.CompilerParams(vmem_limit_bytes=56 * 1024 * 1024),
        cost_estimate=pl.CostEstimate(
            flops=2 * hidden.size * features,
            bytes_accessed=2 * hidden.size
            + 2 * hidden.shape[0] * features
            + 4 * hidden.shape[1] * features,
            transcendentals=0,
        ),
    )(hidden, *pieces)


def shards(
    hidden_in,
    expert_ids,
    attention_gain,
    query_gain,
    key_gain,
    query_weight,
    key_matrix,
    value_matrix,
    output_weight,
    expert_gain,
    router_weight,
    gate_up_weight,
    down_weight,
    output_grad,
):
    tokens, features = hidden_in.shape
    owners = lax.axis_size("ep")
    local_experts = gate_up_weight.shape[0]
    expert_count = local_experts * owners
    everyone = lambda v: lax.all_gather(v, "ep", axis=0, tiled=True)

    rows_a = tokens // 2
    halves = lambda v: (v[:rows_a], v[rows_a:])

    weights = jnp.concatenate([query_weight, key_matrix, value_matrix], axis=1)
    hops = gather_hops(weights)
    head_share = query_gain.shape[0]
    head_gains = jnp.pad(
        jnp.stack([query_gain, key_gain], axis=1),
        ((0, router_weight.shape[0] - head_share), (0, 0)),
    )
    packed = everyone(
        jnp.concatenate(
            [router_weight, attention_gain[:, None], expert_gain[:, None], head_gains], axis=1
        )
    )
    router_full = packed[:, :expert_count]
    attn_gain_full = packed[:, expert_count].astype(F32)
    mlp_gain_full = packed[:, expert_count + 1].astype(F32)
    head_gains = (
        packed[:, expert_count + 2 :]
        .reshape(owners, -1, 2)[:, :head_share]
        .reshape(HEAD_SIZE, 2)
        .astype(F32)
    )
    query_gain_full = head_gains[:, 0]
    key_gain_full = head_gains[:, 1]
    wgu = gate_up_weight.transpose(1, 0, 2).reshape(features, -1)
    wd = down_weight.reshape(-1, features)
    hidden_f = hidden_in.astype(F32)
    normed_low = norm_rows(hidden_f, attn_gain_full).astype(BF16)
    normed_rel = pick_blocks(normed_low, 1)
    positions = jnp.arange(tokens, dtype=jnp.int32)
    cosine, sine_table = rope_tables(positions, HEAD_SIZE)
    hops, normed_rel, wgu, cosine, sine_table, router_full, output_grad = join(
        hops, normed_rel, wgu, cosine, sine_table, router_full, output_grad
    )

    near = gather_near(weights, hops)
    weights_rel = [near, gather_core(near, hops)]
    grad_halves = halves(output_grad)
    grad_hops = [gather_hops(v) for v in grad_halves]
    query_width = query_weight.shape[1]
    key_width = key_matrix.shape[1]
    query_heads = query_width // HEAD_SIZE
    key_heads = key_width // HEAD_SIZE
    heads_per_group = query_heads // key_heads
    split = features // 2
    raw = jnp.dot(normed_rel[:, :split], weights_rel[0], preferred_element_type=F32) + jnp.dot(
        normed_rel[:, split:], weights_rel[1], preferred_element_type=F32
    )
    query_raw = raw[:, :query_width].reshape(tokens, query_heads, HEAD_SIZE)
    key_raw = raw[:, query_width : query_width + key_width].reshape(tokens, key_heads, HEAD_SIZE)
    value_low = raw[:, query_width + key_width :].astype(BF16)
    query_low = rotate(norm_rows(query_raw, query_gain_full), cosine, sine_table).astype(BF16)
    all_keys = rotate(norm_rows(key_raw, key_gain_full), cosine, sine_table).astype(BF16)
    all_values = value_low.reshape(tokens, key_heads, HEAD_SIZE)
    allowed = jnp.arange(tokens)[None, :] <= jnp.arange(tokens)[:, None]
    grouped_queries = query_low.reshape(tokens, key_heads, heads_per_group, HEAD_SIZE)

    def score_block():
        raw_scores = jnp.einsum(
            "ikgd,jkd->kgij", grouped_queries, all_keys, preferred_element_type=F32
        ) / math.sqrt(HEAD_SIZE)
        return jnp.where(allowed, raw_scores, -jnp.inf)

    scores = score_block()
    row_max = jnp.max(scores, axis=-1, keepdims=True)
    exps = jnp.exp(scores - row_max)
    row_total = jnp.sum(exps, axis=-1, keepdims=True)
    probs = exps / row_total
    log_total = row_max + jnp.log(row_total)
    attention_output = (
        jnp.einsum("kgij,jkd->ikgd", probs.astype(BF16), all_values, preferred_element_type=F32)
        .astype(BF16)
        .reshape(tokens, query_heads * HEAD_SIZE)
    )
    head_parts = [
        jnp.dot(v, output_weight, preferred_element_type=F32).astype(BF16)
        for v in halves(attention_output)
    ]
    head_parts, grad_hops[0] = join(head_parts, grad_hops[0])

    grad_near = [gather_near(grad_halves[0], grad_hops[0])]
    grad_core = [gather_core(grad_near[0], grad_hops[0])]
    ids_hops = gather_hops(expert_ids)
    hops = reduce_hops(head_parts[0])
    hops, ids_hops = join(hops, ids_hops)

    ids_near = gather_near(expert_ids, ids_hops)
    ids_core = gather_core(ids_near, ids_hops)
    chunk = reduce_total(head_parts[0], hops)
    hops_b, hops, grad_core[0], grad_hops[1], ids_core = join(
        reduce_hops(head_parts[1]), spread_hops(chunk), grad_core[0], grad_hops[1], ids_core
    )

    attended = [spread_total(chunk, hops)]
    chunk = reduce_total(head_parts[1], hops_b)
    hops = spread_hops(chunk)
    grad_near.append(gather_near(grad_halves[1], grad_hops[1]))
    grad_core.append(gather_core(grad_near[1], grad_hops[1]))
    resid_halves = [hidden_f[:rows_a] + attended[0].astype(F32)]
    routed_halves = [norm_rows(resid_halves[0], mlp_gain_full).astype(BF16)]
    hops_a, hops, grad_core[1] = join(gather_hops(routed_halves[0]), hops, grad_core[1])

    attended.append(spread_total(chunk, hops))
    resid_halves.append(hidden_f[rows_a:] + attended[1].astype(F32))
    routed_halves.append(norm_rows(resid_halves[1], mlp_gain_full).astype(BF16))
    near_a = gather_near(routed_halves[0], hops_a)
    core_a = gather_core(near_a, hops_a)
    hops_b = gather_hops(routed_halves[1])
    grad_pieces = [grad_near[0], grad_core[0], grad_near[1], grad_core[1]]
    piece_rows = near_a.shape[0]
    ids_pieces = [
        v.reshape(-1, 2, rows_a, TOP)[:, h].reshape(piece_rows, TOP)
        for h in range(2)
        for v in (ids_near, ids_core)
    ]

    def experts(piece, x, kept=None):
        return run_experts(
            x,
            grad_pieces[piece],
            ids_pieces[piece],
            router_full,
            wgu,
            wd,
            local_experts,
            piece,
            4,
            kept,
        )

    keep_a, *kept = experts(0, near_a)
    send_a, *kept = experts(1, core_a, kept)
    hops_b, send_a, kept = join(hops_b, send_a, kept)

    near_b = gather_near(routed_halves[1], hops_b)
    core_b = gather_core(near_b, hops_b)
    come = scatter_swap(send_a)
    keep_b, *kept = experts(2, near_b, kept)
    come, core_b, keep_b, kept = join(come, core_b, keep_b, kept)

    sums_a = scatter_sums(keep_a, come)
    hops_a = scatter_hops(sums_a)
    send_b, *kept = experts(3, core_b, kept)
    hops_a, send_b, kept = join(hops_a, send_b, kept)
    joined, hidden = kept
    routed_pieces = [near_a, core_a, near_b, core_b]
    resid = jnp.concatenate(resid_halves, axis=0)
    routed_low = jnp.concatenate(routed_halves, axis=0)
    logits = jnp.dot(routed_low, router_full, preferred_element_type=F32)
    logit_max = jnp.max(logits, axis=-1, keepdims=True)
    exponent = jnp.exp(logits - logit_max)
    router = exponent / jnp.sum(exponent, axis=-1, keepdims=True)
    every_expert = jnp.arange(expert_count, dtype=jnp.int32)
    named = jnp.any(expert_ids[:, :, None] == every_expert[None, None, :], axis=1)
    chosen = jnp.where(named, router, 0.0)
    chosen_total = jnp.sum(chosen, axis=1, keepdims=True)
    gates = chosen / chosen_total

    come = scatter_swap(send_b)
    total_a = scatter_total(sums_a, hops_a)
    hops = reduce_hops(total_a)
    mixture_parts = [
        jnp.dot(
            hidden[i * piece_rows : (i + 1) * piece_rows], wd, preferred_element_type=F32
        ).astype(BF16)
        for i in (1, 3, 0, 2)
    ]
    come, hops, mixture_parts = join(come, hops, mixture_parts)

    sums_b = scatter_sums(keep_b, come)
    hops_b = scatter_hops(sums_b)
    chunk = reduce_total(total_a, hops)
    hops_a = spread_hops(chunk)
    mixture_come = [scatter_swap(v) for v in mixture_parts[:2]]
    hops_b, hops_a, mixture_come = join(hops_b, hops_a, mixture_come)

    returned = [spread_total(chunk, hops_a)]
    total_b = scatter_total(sums_b, hops_b)
    hops = reduce_hops(total_b)
    mixture_sums = [scatter_sums(k, c) for k, c in zip(mixture_parts[2:], mixture_come)]
    mixture_hops = [scatter_hops(v) for v in mixture_sums]
    (hops,) = join(hops)
    chunk = reduce_total(total_b, hops)
    hops, mixture_hops[0] = join(spread_hops(chunk), mixture_hops[0])

    returned.append(spread_total(chunk, hops))
    returned = jnp.concatenate(returned, axis=0)
    grad_out = output_grad.astype(F32)
    tail = returned[:, features:].astype(F32)
    grad_gates = tail[:, :expert_count] + tail[:, expert_count : 2 * expert_count]
    grad_gates = jnp.where(named, grad_gates, 0.0)
    grad_router = jnp.where(
        named,
        (grad_gates - jnp.sum(grad_gates * gates, axis=1, keepdims=True)) / chosen_total,
        0.0,
    )
    grad_logits = (
        router * (grad_router - jnp.sum(router * grad_router, axis=1, keepdims=True))
    ).astype(BF16)
    router_grad = jnp.dot(routed_low.T, grad_logits, preferred_element_type=F32)
    grad_routed = returned[:, :features].astype(F32) + jnp.dot(
        grad_logits, router_full.T, preferred_element_type=F32
    )
    grad_resid_norm, mlp_terms = norm_back(resid, mlp_gain_full, grad_routed)
    mlp_gain_grad = jnp.sum(mlp_terms, axis=0)
    grad_resid = grad_out + grad_resid_norm
    grad_attended = grad_resid.astype(BF16)
    mixed_rel = pick_blocks(attention_output, 1)
    output_local = lax.dot_general(
        mixed_rel, grad_attended, (((0,), (0,)), ((), ())), preferred_element_type=F32
    ).astype(BF16)
    output_half = output_local.shape[0] // 2
    output_local, grad_attended, mixture_hops[1] = join(
        output_local, grad_attended, mixture_hops[1]
    )

    come = scatter_swap(output_local[output_half:])
    mixture = jnp.concatenate(
        [scatter_total(v, h) for v, h in zip(mixture_sums, mixture_hops)], axis=0
    )
    grad_mixed = (
        jnp.dot(grad_attended, output_weight.T, preferred_element_type=F32)
        .astype(BF16)
        .reshape(tokens, key_heads, heads_per_group, HEAD_SIZE)
    )
    grad_mixed, come = join(grad_mixed, come)

    output_sums = scatter_sums(output_local[:output_half], come)
    output_hops = scatter_hops(output_sums)
    mixture_hops = reduce_hops(mixture)
    probs_again = jnp.exp(score_block() - log_total)
    grad_probs = jnp.einsum("ikgd,jkd->kgij", grad_mixed, all_values, preferred_element_type=F32)
    grad_values = jnp.einsum(
        "kgij,ikgd->jkd", probs_again.astype(BF16), grad_mixed, preferred_element_type=F32
    )
    grad_scores = (
        probs_again * (grad_probs - jnp.sum(probs_again * grad_probs, axis=-1, keepdims=True))
    ).astype(BF16)
    grad_queries = jnp.einsum(
        "kgij,jkd->ikgd", grad_scores, all_keys, preferred_element_type=F32
    ) / math.sqrt(HEAD_SIZE)
    grad_keys = jnp.einsum(
        "kgij,ikgd->jkd", grad_scores, grouped_queries, preferred_element_type=F32
    ) / math.sqrt(HEAD_SIZE)
    grad_query_rot = rotate_back(
        grad_queries.reshape(tokens, query_heads, HEAD_SIZE), cosine, sine_table
    )
    grad_query_raw, query_terms = norm_back(query_raw, query_gain_full, grad_query_rot)
    grad_key_rot = rotate_back(grad_keys, cosine, sine_table)
    grad_key_raw, key_terms = norm_back(key_raw, key_gain_full, grad_key_rot)
    grad_raw = jnp.concatenate(
        [
            grad_query_raw.reshape(tokens, -1).astype(BF16),
            grad_key_raw.reshape(tokens, -1).astype(BF16),
            grad_values.reshape(tokens, -1).astype(BF16),
        ],
        axis=1,
    )
    over_columns = (((1,), (1,)), ((), ()))
    feature_part = jnp.concatenate(
        [
            lax.dot_general(grad_raw, w, over_columns, preferred_element_type=F32).astype(BF16)
            for w in weights_rel
        ]
        + [jnp.sum(query_terms, axis=1).astype(BF16), jnp.sum(key_terms, axis=1).astype(BF16)],
        axis=1,
    )
    by_feature = jnp.concatenate([router_grad, mlp_gain_grad[:, None]], axis=1).astype(BF16)
    by_feature = jnp.pad(by_feature, ((0, 0), (0, -by_feature.shape[1] % LANES)))
    weights_grad = jnp.concatenate(
        [
            lax.dot_general(
                normed_rel, grad_raw, (((0,), (0,)), ((), ())), preferred_element_type=F32
            ).astype(BF16),
            pick_blocks(by_feature, 0),
        ],
        axis=1,
    )
    feature_part, weights_grad, output_hops, mixture_hops = join(
        feature_part, weights_grad, output_hops, mixture_hops
    )

    come = scatter_swap(weights_grad[split:])
    hops = reduce_hops(feature_part)
    output_share = scatter_total(output_sums, output_hops)
    output_hops = gather_hops(output_share)
    mixture_chunk = reduce_total(mixture, mixture_hops)
    come, hops = join(come, hops)

    weights_sums = scatter_sums(weights_grad[:split], come)
    weights_hops = scatter_hops(weights_sums)
    chunk = reduce_total(feature_part, hops)
    hops = spread_hops(chunk)
    last_joined, last_hidden, chunk = join(joined, hidden, chunk)
    down_grad = down_product(last_hidden, grad_pieces).reshape(down_weight.shape)
    hops, output_hops, down_grad = join(hops, output_hops, down_grad)

    near = gather_near(output_share, output_hops)
    output_weight_grad = put_blocks(
        jnp.concatenate([near, gather_core(near, output_hops)], axis=0), 0
    ).astype(F32)
    mixture_hops = spread_hops(mixture_chunk)
    total = spread_total(chunk, hops)
    grad_normed = put_blocks(total[:, :features], 1).astype(F32)
    head_grads = jnp.sum(total[:, features:].astype(F32), axis=0)
    grad_input_norm, attn_terms = norm_back(hidden_f, attn_gain_full, grad_normed)
    input_grad = grad_resid + grad_input_norm
    late = jnp.concatenate([jnp.sum(attn_terms, axis=0), head_grads])
    weights_hops, late, last_joined = join(weights_hops, late, last_joined)
    late = lax.psum(late, "ep")
    weights_rows = scatter_total(weights_sums, weights_hops).astype(F32)
    early = weights_rows[:, query_width + 2 * key_width :]
    gate_up_grad = gate_up_product(routed_pieces, last_joined, gate_up_weight.shape)
    mixture = spread_total(mixture_chunk, mixture_hops)
    block_out = (resid + mixture.astype(F32)).astype(BF16)
    mine = lax.axis_index("ep")
    own = lambda start, size: lax.dynamic_slice_in_dim(
        late, start + mine * (size // owners), size // owners, 0
    )
    return (
        block_out,
        input_grad,
        own(0, features),
        own(features, HEAD_SIZE),
        own(features + HEAD_SIZE, HEAD_SIZE),
        weights_rows[:, :query_width],
        weights_rows[:, query_width : query_width + key_width],
        weights_rows[:, query_width + key_width : query_width + 2 * key_width],
        output_weight_grad,
        early[:, expert_count],
        early[:, :expert_count],
        gate_up_grad,
        down_grad,
    )


def solution(mesh):
    in_specs = (
        P("ep", None),
        P("ep", None),
        P("ep"),
        P("ep"),
        P("ep"),
        P("ep", "tp"),
        P("ep", "tp"),
        P("ep", "tp"),
        P("tp", None),
        P("ep"),
        P("ep", None),
        P("ep", None, "tp"),
        P("ep", "tp", None),
        P("ep", None),
    )
    out_specs = (
        P("ep", None),
        P("ep", None),
        P("ep"),
        P("ep"),
        P("ep"),
        P("ep", "tp"),
        P("ep", "tp"),
        P("ep", "tp"),
        P("tp", None),
        P("ep"),
        P("ep", None),
        P("ep", None, "tp"),
        P("ep", "tp", None),
    )
    return jax.shard_map(shards, mesh=mesh, in_specs=in_specs, out_specs=out_specs, check_vma=False)
```

time: 804 us -> 617 us (0.77)
  waiting for transfers between devices: 300 us -> 177 us
  local copies, waits for them, and re-layouts: 129 us -> 67 us
  Pallas kernels: 50.5 us -> 91.3 us
  matrix products: 66.9 us -> 39.7 us
  other arithmetic: 67.7 us -> 82.7 us
  between operations: 16.3 us -> 3.49 us
  blocking collectives: 62.6 us -> 53.1 us
    ppermute x150 -> x88, waiting for transfers between devices: 285 us -> 177 us  [swap(): return lax.ppermute(value, axis, [(i, i ^ mask) for i in range(count)])]
    unnamed x250 -> x281, local copies, waits for them, and re-layouts: 83 us -> 30 us
    pallas_call x0 -> x2, Pallas kernels: none -> 31.7 us  [the longest x1 19.2 us: gate_up_product(): pl.pallas_call(gate_up_kernel, grid=(features // tile,), in_specs=[pl.Blo...]
    dot_general x8 -> x12, matrix products: 54.4 us -> 26.7 us  [the longest x4 12.5 us: shards(): jnp.dot(hidden[i * piece_rows:(i + 1) * piece_rows], wd, preferred_elemen...]
    psum x1, blocking collectives: 37.9 us -> 22.3 us  [shards(): late = lax.psum(late, 'ep')]
    concatenate x3 -> x11, other arithmetic: 1.99 us -> 17.5 us  [the longest x6 13.1 us: gather_near(): return jnp.concatenate([value] + hops, axis=0)]
    reduce_scatter x1 -> x0, waiting for transfers between devices: 15 us -> none  [shards(): lax.psum_scatter(jnp.concatenate([router_grad, attn_gain_grad[:, None], m...]
    pallas_call x1 -> x4, Pallas kernels: 50.5 us -> 59.7 us  [run_experts(): pl.pallas_call(expert_kernel, grid_spec=pltpu.PrefetchScalarGridSpec(num_...]
  transfers between devices with their start and end apart: 151 -> 88, of which waited for: 58 -> 34; matrix products, arithmetic and copies ran while one was open for 26% -> 25% of each run, Pallas kernels for 0% -> 15%
where the time goes in v2:
time: 617 us; the launch traced here: 609 us
  waiting for transfers between devices  177 us (29%)
  starting transfers between devices  94.1 us (15%)
  Pallas kernels  91.3 us (15%)
  other arithmetic  82.7 us (13%)
  local copies, waits for them, and re-layouts  67 us (11%)
  blocking collectives  53.1 us (9%)
  matrix products  39.7 us (6%)
    ppermute x88, waiting for transfers between devices, swap(): return lax.ppermute(value, axis, [(i, i ^ mask) for i in range(count)])  177 us
    ppermute x88, starting transfers between devices, swap(): return lax.ppermute(value, axis, [(i, i ^ mask) for i in range(count)])  94.1 us
    pallas_call x4, Pallas kernels, run_experts(): pl.pallas_call(expert_kernel, grid_spec=pltpu.PrefetchScalarGridSpec(num_...  59.7 us
    all_gather x1, blocking collectives, shards(): everyone = lambda v: lax.all_gather(v, 'ep', axis=0, tiled=True)  30.8 us
    unnamed x281, local copies, waits for them, and re-layouts  30 us
    psum x1, blocking collectives, shards(): late = lax.psum(late, 'ep')  22.3 us
    pallas_call x1, Pallas kernels, gate_up_product(): pl.pallas_call(gate_up_kernel, grid=(features // tile,), in_specs=[pl.Blo...  19.2 us
    convert_element_type x11, other arithmetic, plus(): return total.astype(BF16)  19.1 us
  transfers between devices with their start and end apart: 88, of which 34 were waited for; matrix products, arithmetic and copies ran while one was open for 25% of the time, Pallas kernels for 15%

profile of v2, /device:TPU:8, one launch (start us, length us, event | category | flops | bytes accessed | tf_op | source)
XLA Modules:
  0.0 608.7 jit_solution(15494961133162966047)
XLA Ops:
  10.5 30.8 %all_gather.3 = bf16[2048,36]{1,0:T(8,128)(2,1)S(1)} all-gather(bf16[256,36]{1,0:T(8,128)(2,1)S(1)} %copy.185), channel_id=1, replica_groups=mesh['ep'=8,'tp'=4] {'ep'}, dimensions={0}, use_global_device_ids=true | all-gather | bytes 165888 | tf_op jit(solution)/shard_map/all_gather | solution.py:434
  42.8 6.2 %copy.240 = bf16[4,256,8,384]{3,2,0,1:T(8,128)(2,1)} copy(bf16[4,256,8,384]{3,2,1,0:T(8,128)(2,1)} %bitcast.194) | data formatting | bytes 12582912 | tf_op jit(solution)/shard_map/reshape | solution.py:462
  73.3 8.7 %collective-permute-done.5 = bf16[128,2048]{1,0:T(8,128)(2,1)} collective-permute-done((bf16[128,2048]{1,0:T(8,128)(2,1)}, bf16[128,2048]{1,0:T(8,128)(2,1)}, u32[]{:S(2)}, u32[]{:S(2)}) %collective-permute-start.5) | collective-permute-done | bytes 524320 | tf_op jit(solution)/shard_map/ppermute | solution.py:76
  98.2 6.0 collective-permute-done.8
  112.6 8.4 %collective-permute-done.21 = bf16[128,2048]{1,0:T(8,128)(2,1)} collective-permute-done((bf16[128,2048]{1,0:T(8,128)(2,1)}, bf16[128,2048]{1,0:T(8,128)(2,1)}, u32[]{:S(2)}, u32[]{:S(2)}) %collective-permute-start.21) | collective-permute-done | bytes 524320 | tf_op jit(solution)/shard_map/ppermute | solution.py:76
  123.9 3.9 collective-permute-start.16
  158.7 3.6 collective-permute-start.28
  163.7 3.5 collective-permute-done.28
  169.7 6.2 %collective-permute-done.29 = bf16[32,2048]{1,0:T(8,128)(2,1)} collective-permute-done((bf16[32,2048]{1,0:T(8,128)(2,1)}, bf16[32,2048]{1,0:T(8,128)(2,1)}, u32[]{:S(2)}, u32[]{:S(2)}) %collective-permute-start.29) | collective-permute-done | bytes 131104 | tf_op jit(solution)/shard_map/ppermute | solution.py:76
  175.8 3.6 collective-permute-done.25
  186.5 14.3 %shard_map.237 = (bf16[512,2176]{1,0:T(8,128)(2,1)S(1)}, bf16[2048,1536]{1,0:T(8,128)(2,1)}, bf16[2048,768]{1,0:T(8,128)(2,1)S(1)}) custom-call(s32[5]{0:T(128)S(1)} %broadcast_in_dim.34.base_ref, bf16[512,2048]{1,0:T(8,128)(2,1)S(1)} %pad_maximum_fusion.5.x_ref.refs_0_, bf16[512,2048]{1,0:T(8,128)(2,1)S(1)} %pad_maximum_fusion.2.g_ref.refs_0_, ...), custom_call_target="tpu_custom_call" | custom-call | flops 8053063680 | bytes 18874368 | tf_op jit(solution)/shard_map/pallas_call | solution.py:310
  202.2 15.1 %shard_map.238 = (bf16[512,2176]{1,0:T(8,128)(2,1)}, bf16[2048,1536]{1,0:T(8,128)(2,1)}, bf16[2048,768]{1,0:T(8,128)(2,1)S(1)}) custom-call(s32[5]{0:T(128)S(1)} %broadcast_in_dim.34.base_ref, bf16[512,2048]{1,0:T(8,128)(2,1)S(1)} %collective-permute-done.34.x_ref.refs_1_, ...), custom_call_target="tpu_custom_call", output_to_operand_aliasing={{1}: (7, {}), {2}: (8, {})} | custom-call | flops 8053063680 | bytes 18874368 | tf_op jit(solution)/shard_map/pallas_call | solution.py:310
  226.0 15.0 %shard_map.239 = (bf16[512,2176]{1,0:T(8,128)(2,1)S(1)}, bf16[2048,1536]{1,0:T(8,128)(2,1)}, bf16[2048,768]{1,0:T(8,128)(2,1)S(1)}) custom-call(s32[5]{0:T(128)S(1)} %broadcast_in_dim.34.base_ref, bf16[512,2048]{1,0:T(8,128)(2,1)} %pad_maximum_fusion.6.x_ref.refs_2_, ...), custom_call_target="tpu_custom_call", output_to_operand_aliasing={{1}: (7, {}), {2}: (8, {})} | custom-call | flops 8053063680 | bytes 18874368 | tf_op jit(solution)/shard_map/pallas_call | solution.py:310
  246.4 15.2 %shard_map.240 = (bf16[512,2176]{1,0:T(8,128)(2,1)S(1)}, bf16[2048,1536]{1,0:T(8,128)(2,1)}, bf16[2048,768]{1,0:T(8,128)(2,1)S(1)}) custom-call(s32[5]{0:T(128)S(1)} %broadcast_in_dim.34.base_ref, bf16[512,2048]{1,0:T(8,128)(2,1)} %collective-permute-done.36.x_ref.refs_3_, ...), custom_call_target="tpu_custom_call", output_to_operand_aliasing={{1}: (7, {}), {2}: (8, {})} | custom-call | flops 8053063680 | bytes 18874368 | tf_op jit(solution)/shard_map/pallas_call | solution.py:310
  261.7 9.7 %collective-permute-done.38 = bf16[128,2176]{1,0:T(8,128)(2,1)S(1)} collective-permute-done((bf16[128,2176]{1,0:T(8,128)(2,1)S(1)}, bf16[128,2176]{1,0:T(8,128)(2,1)S(1)}, u32[]{:S(2)}, u32[]{:S(2)}) %collective-permute-start.38) | collective-permute-done | bytes 557088 | tf_op jit(solution)/shard_map/ppermute | solution.py:76
  298.3 5.7 collective-permute-done.48
  314.6 14.6 %collective-permute-done.45 = bf16[128,2176]{1,0:T(8,128)(2,1)} collective-permute-done((bf16[128,2176]{1,0:T(8,128)(2,1)}, bf16[128,2176]{1,0:T(8,128)(2,1)}, u32[]{:S(2)}, u32[]{:S(2)}) %collective-permute-start.45) | collective-permute-done | bytes 557088 | tf_op jit(solution)/shard_map/ppermute | solution.py:76
  335.2 3.4 collective-permute-start.53
  356.2 3.7 collective-permute-done.56
  374.1 11.4 %collective-permute-done.62 = bf16[128,2048]{1,0:T(8,128)(2,1)S(1)} collective-permute-done((bf16[128,2048]{1,0:T(8,128)(2,1)S(1)}, bf16[128,2048]{1,0:T(8,128)(2,1)S(1)}, u32[]{:S(2)}, u32[]{:S(2)}) %collective-permute-start.62) | collective-permute-done | bytes 524320 | tf_op jit(solution)/shard_map/ppermute | solution.py:76
  431.7 11.1 %collective-permute-done.70 = bf16[64,2048]{1,0:T(8,128)(2,1)S(1)} collective-permute-done((bf16[64,2048]{1,0:T(8,128)(2,1)S(1)}, bf16[64,2048]{1,0:T(8,128)(2,1)S(1)}, u32[]{:S(2)}, u32[]{:S(2)}) %collective-permute-start.70) | collective-permute-done | bytes 262176 | tf_op jit(solution)/shard_map/ppermute | solution.py:76
  457.4 5.0 collective-permute-done.71
  464.2 6.7 %collective-permute-done.72 = bf16[64,2048]{1,0:T(8,128)(2,1)S(1)} collective-permute-done((bf16[64,2048]{1,0:T(8,128)(2,1)S(1)}, bf16[64,2048]{1,0:T(8,128)(2,1)S(1)}, u32[]{:S(2)}, u32[]{:S(2)}) %collective-permute-start.72) | collective-permute-done | bytes 262176 | tf_op jit(solution)/shard_map/ppermute | solution.py:76
  471.0 18.2 %collective-permute-done.73 = bf16[64,2048]{1,0:T(8,128)(2,1)S(1)} collective-permute-done((bf16[64,2048]{1,0:T(8,128)(2,1)S(1)}, bf16[64,2048]{1,0:T(8,128)(2,1)S(1)}, u32[]{:S(2)}, u32[]{:S(2)}) %collective-permute-start.73) | collective-permute-done | bytes 262176 | tf_op jit(solution)/shard_map/ppermute | solution.py:76
  497.0 4.1 collective-permute-done.77
  501.3 3.6 collective-permute-start.79
  505.0 12.4 %shard_map.241 = f32[768,2048]{1,0:T(8,128)} custom-call(bf16[2048,768]{1,0:T(8,128)(2,1)} %copy-done.9, bf16[512,2048]{1,0:T(8,128)(2,1)} %copy-done.2, bf16[512,2048]{1,0:T(8,128)(2,1)} %collective-permute-done.19.g_ref.refs_1_, bf16[512,2048]{1,0:T(8,128)(2,1)} %pad_maximum_fusion.3.g_ref.refs_2_, bf16[512,2048]{1,0:T(8,128)(2,1)} %collective-permute-done.30.g_ref.refs_3_), custom_call_target="tpu_custom_call" | custom-call | flops 6442450944 | bytes 17825792 | tf_op jit(solution)/shard_map/pallas_call | solution.py:397
  523.3 10.1 %collective-permute-done.80 = bf16[64,2304]{1,0:T(8,128)(2,1)S(1)} collective-permute-done((bf16[64,2304]{1,0:T(8,128)(2,1)S(1)}, bf16[64,2304]{1,0:T(8,128)(2,1)S(1)}, u32[]{:S(2)}, u32[]{:S(2)}) %collective-permute-start.80) | collective-permute-done | bytes 294944 | tf_op jit(solution)/shard_map/ppermute | solution.py:76
  544.8 8.5 %collective-permute-done.85 = bf16[256,1408]{0,1:T(8,128)(2,1)S(1)} collective-permute-done((bf16[256,1408]{0,1:T(8,128)(2,1)S(1)}, bf16[256,1408]{0,1:T(8,128)(2,1)S(1)}, u32[]{:S(2)}, u32[]{:S(2)}) %collective-permute-start.85) | collective-permute-done | bytes 720928 | tf_op jit(solution)/shard_map/ppermute | solution.py:76
  559.0 22.3 %psum.7 = f32[2304]{0:T(1024)S(1)} all-reduce(f32[2304]{0:T(1024)S(1)} %pad_maximum_fusion.20), channel_id=1, replica_groups=mesh['ep'=8,'tp'=4] {'ep'}, use_global_device_ids=true, to_apply=%region_23.24 | all-reduce | flops 2304 | bytes 18432 | tf_op jit(solution)/shard_map/psum | solution.py:747
  582.5 19.2 %shard_map.242 = f32[4,2048,384]{2,1,0:T(8,128)} custom-call(bf16[512,2048]{1,0:T(8,128)(2,1)} %copy-done.3, bf16[512,2048]{1,0:T(8,128)(2,1)} %copy-done.6, bf16[512,2048]{1,0:T(8,128)(2,1)} %pad_maximum_fusion.6.x_ref.refs_2_, bf16[512,2048]{1,0:T(8,128)(2,1)} %collective-permute-done.36.x_ref.refs_3_, bf16[2048,1536]{1,0:T(8,128)(2,1)} %get-tuple-element.263.refs_4_), custom_call_target="tpu_custom_call" | custom-call | flops 12884901888 | bytes 27262976 | tf_op jit(solution)/shard_map/pallas_call | solution.py:362
  604.0 4.4 convert_element_type.752
  (606 shorter events, 290.3 us)
Async XLA Ops:
  3.6 46.6 %collective-permute-start = (bf16[256,1280]{1,0:T(8,128)(2,1)S(1)}, bf16[256,1280]{1,0:T(8,128)(2,1)}, u32[]{:S(2)}, u32[]{:S(2)}) collective-permute-start(bf16[256,1280]{1,0:T(8,128)(2,1)S(1)} %constant_dynamic-update-slice_fusion), channel_id=1, source_target_pairs={{0,8},{4,12},{8,0},{12,4},{16,24},{20,28},{24,16},{28,20},{1,9},{5... | collective-permute-start | bytes 1966088 | tf_op jit(solution)/shard_map/ppermute | solution.py:76
  5.1 45.1 %collective-permute-start.1 = (bf16[256,1280]{1,0:T(8,128)(2,1)S(1)}, bf16[256,1280]{1,0:T(8,128)(2,1)}, u32[]{:S(2)}, u32[]{:S(2)}) collective-permute-start(bf16[256,1280]{1,0:T(8,128)(2,1)S(1)} %constant_dynamic-update-slice_fusion), channel_id=1, source_target_pairs={{0,16},{4,20},{8,24},{12,28},{16,0},{20,4},{24,8},{28,12},{1,17},{... | collective-permute-start | bytes 1966088 | tf_op jit(solution)/shard_map/ppermute | solution.py:76
  6.6 43.6 %collective-permute-start.2 = (bf16[256,1280]{1,0:T(8,128)(2,1)S(1)}, bf16[256,1280]{1,0:T(8,128)(2,1)}, u32[]{:S(2)}, u32[]{:S(2)}) collective-permute-start(bf16[256,1280]{1,0:T(8,128)(2,1)S(1)} %constant_dynamic-update-slice_fusion), channel_id=1, source_target_pairs={{0,24},{4,28},{8,16},{12,20},{16,8},{20,12},{24,0},{28,4},{1,25},{... | collective-permute-start | bytes 1966088 | tf_op jit(solution)/shard_map/ppermute | solution.py:76
  56.3 25.8 %collective-permute-start.5 = (bf16[128,2048]{1,0:T(8,128)(2,1)}, bf16[128,2048]{1,0:T(8,128)(2,1)}, u32[]{:S(2)}, u32[]{:S(2)}) collective-permute-start(bf16[128,2048]{1,0:T(8,128)(2,1)} %get-tuple-element.407), channel_id=1, source_target_pairs={{0,16},{4,20},{8,24},{12,28},{16,0},{20,4},{24,8},{28,12},{1,17},{... | collective-permute-start | bytes 1572872 | tf_op jit(solution)/shard_map/ppermute | solution.py:76
  83.7 55.9 %collective-permute-start.19 = (bf16[512,2048]{1,0:T(8,128)(2,1)S(1)}, bf16[512,2048]{1,0:T(8,128)(2,1)}, u32[]{:S(2)}, u32[]{:S(2)}) collective-permute-start(bf16[512,2048]{1,0:T(8,128)(2,1)S(1)} %pad_maximum_fusion.2.g_ref.refs_0_), channel_id=1, source_target_pairs={{0,4},{4,0},{8,12},{12,8},{16,20},{20,16},{24,28},{28,24},{1,5},{5... | collective-permute-start | bytes 6291464 | tf_op jit(solution)/shard_map/ppermute | solution.py:76
  142.7 36.7 %collective-permute-start.30 = (bf16[512,2048]{1,0:T(8,128)(2,1)}, bf16[512,2048]{1,0:T(8,128)(2,1)}, u32[]{:S(2)}, u32[]{:S(2)}) collective-permute-start(bf16[512,2048]{1,0:T(8,128)(2,1)} %pad_maximum_fusion.3.g_ref.refs_2_), channel_id=1, source_target_pairs={{0,4},{4,0},{8,12},{12,8},{16,20},{20,16},{24,28},{28,24},{1,5},{5... | collective-permute-start | bytes 6291464 | tf_op jit(solution)/shard_map/ppermute | solution.py:76
  154.1 25.4 %collective-permute-start.25 = (bf16[128,2048]{1,0:T(8,128)(2,1)}, bf16[128,2048]{1,0:T(8,128)(2,1)}, u32[]{:S(2)}, u32[]{:S(2)}) collective-permute-start(bf16[128,2048]{1,0:T(8,128)(2,1)} %multiply_convert_fusion.2), channel_id=1, source_target_pairs={{0,16},{4,20},{8,24},{12,28},{16,0},{20,4},{24,8},{28,12},{1,17},{... | collective-permute-start | bytes 1572872 | tf_op jit(solution)/shard_map/ppermute | solution.py:76
  182.9 34.4 %collective-permute-start.31 = (bf16[128,2048]{1,0:T(8,128)(2,1)S(1)}, bf16[128,2048]{1,0:T(8,128)(2,1)S(1)}, u32[]{:S(2)}, u32[]{:S(2)}) collective-permute-start(bf16[128,2048]{1,0:T(8,128)(2,1)S(1)} %multiply_convert_fusion.1), channel_id=1, source_target_pairs={{0,8},{4,12},{8,0},{12,4},{16,24},{20,28},{24,16},{28,20},{1,9},{5... | collective-permute-start | bytes 1572872 | tf_op jit(solution)/shard_map/ppermute | solution.py:76
  184.7 32.6 %collective-permute-start.32 = (bf16[128,2048]{1,0:T(8,128)(2,1)S(1)}, bf16[128,2048]{1,0:T(8,128)(2,1)S(1)}, u32[]{:S(2)}, u32[]{:S(2)}) collective-permute-start(bf16[128,2048]{1,0:T(8,128)(2,1)S(1)} %multiply_convert_fusion.1), channel_id=1, source_target_pairs={{0,16},{4,20},{8,24},{12,28},{16,0},{20,4},{24,8},{28,12},{1,17},{... | collective-permute-start | bytes 1572872 | tf_op jit(solution)/shard_map/ppermute | solution.py:76
  185.0 32.3 %collective-permute-start.33 = (bf16[128,2048]{1,0:T(8,128)(2,1)S(1)}, bf16[128,2048]{1,0:T(8,128)(2,1)S(1)}, u32[]{:S(2)}, u32[]{:S(2)}) collective-permute-start(bf16[128,2048]{1,0:T(8,128)(2,1)S(1)} %multiply_convert_fusion.1), channel_id=1, source_target_pairs={{0,24},{4,28},{8,16},{12,20},{16,8},{20,12},{24,0},{28,4},{1,25},{... | collective-permute-start | bytes 1572872 | tf_op jit(solution)/shard_map/ppermute | solution.py:76
  244.6 26.7 %collective-permute-start.38 = (bf16[128,2176]{1,0:T(8,128)(2,1)S(1)}, bf16[128,2176]{1,0:T(8,128)(2,1)S(1)}, u32[]{:S(2)}, u32[]{:S(2)}) collective-permute-start(bf16[128,2176]{1,0:T(8,128)(2,1)S(1)} %get-tuple-element.381), channel_id=1, source_target_pairs={{0,16},{4,20},{8,24},{12,28},{16,0},{20,4},{24,8},{28,12},{1,17},{... | collective-permute-start | bytes 1671176 | tf_op jit(solution)/shard_map/ppermute | solution.py:76
  245.0 26.4 %collective-permute-start.39 = (bf16[128,2176]{1,0:T(8,128)(2,1)S(1)}, bf16[128,2176]{1,0:T(8,128)(2,1)S(1)}, u32[]{:S(2)}, u32[]{:S(2)}) collective-permute-start(bf16[128,2176]{1,0:T(8,128)(2,1)S(1)} %get-tuple-element.380), channel_id=1, source_target_pairs={{0,24},{4,28},{8,16},{12,20},{16,8},{20,12},{24,0},{28,4},{1,25},{... | collective-permute-start | bytes 1671176 | tf_op jit(solution)/shard_map/ppermute | solution.py:76
  289.8 39.4 %collective-permute-start.50 = (bf16[512,2048]{1,0:T(8,128)(2,1)}, bf16[512,2048]{1,0:T(8,128)(2,1)}, u32[]{:S(2)}, u32[]{:S(2)}) collective-permute-start(bf16[512,2048]{1,0:T(8,128)(2,1)} %convolution_convert_fusion.5), channel_id=1, source_target_pairs={{0,4},{4,0},{8,12},{12,8},{16,20},{20,16},{24,28},{28,24},{1,5},{5... | collective-permute-start | bytes 6291464 | tf_op jit(solution)/shard_map/ppermute | solution.py:76
  289.8 39.4 %collective-permute-start.51 = (bf16[512,2048]{1,0:T(8,128)(2,1)}, bf16[512,2048]{1,0:T(8,128)(2,1)}, u32[]{:S(2)}, u32[]{:S(2)}) collective-permute-start(bf16[512,2048]{1,0:T(8,128)(2,1)} %convolution_convert_fusion.4), channel_id=1, source_target_pairs={{0,4},{4,0},{8,12},{12,8},{16,20},{20,16},{24,28},{28,24},{1,5},{5... | collective-permute-start | bytes 6291464 | tf_op jit(solution)/shard_map/ppermute | solution.py:76
  304.0 25.2 %collective-permute-start.45 = (bf16[128,2176]{1,0:T(8,128)(2,1)}, bf16[128,2176]{1,0:T(8,128)(2,1)}, u32[]{:S(2)}, u32[]{:S(2)}) collective-permute-start(bf16[128,2176]{1,0:T(8,128)(2,1)} %get-tuple-element.378), channel_id=1, source_target_pairs={{0,16},{4,20},{8,24},{12,28},{16,0},{20,4},{24,8},{28,12},{1,17},{... | collective-permute-start | bytes 1671176 | tf_op jit(solution)/shard_map/ppermute | solution.py:76
  331.1 31.8 %collective-permute-start.58 = (bf16[128,2048]{1,0:T(8,128)(2,1)S(1)}, bf16[128,2048]{1,0:T(8,128)(2,1)S(1)}, u32[]{:S(2)}, u32[]{:S(2)}) collective-permute-start(bf16[128,2048]{1,0:T(8,128)(2,1)S(1)} %get-tuple-element.388), channel_id=1, source_target_pairs={{0,8},{4,12},{8,0},{12,4},{16,24},{20,28},{24,16},{28,20},{1,9},{5... | collective-permute-start | bytes 1572872 | tf_op jit(solution)/shard_map/ppermute | solution.py:76
  331.5 32.8 %collective-permute-start.59 = (bf16[128,2048]{1,0:T(8,128)(2,1)S(1)}, bf16[128,2048]{1,0:T(8,128)(2,1)S(1)}, u32[]{:S(2)}, u32[]{:S(2)}) collective-permute-start(bf16[128,2048]{1,0:T(8,128)(2,1)S(1)} %get-tuple-element.387), channel_id=1, source_target_pairs={{0,16},{4,20},{8,24},{12,28},{16,0},{20,4},{24,8},{28,12},{1,17},{... | collective-permute-start | bytes 1572872 | tf_op jit(solution)/shard_map/ppermute | solution.py:76
  390.1 39.1 %collective-permute-start.68 = (bf16[64,2048]{1,0:T(8,128)(2,1)}, bf16[64,2048]{1,0:T(8,128)(2,1)}, u32[]{:S(2)}, u32[]{:S(2)}) collective-permute-start(bf16[64,2048]{1,0:T(8,128)(2,1)} %get-tuple-element.404), channel_id=1, source_target_pairs={{0,1},{1,0},{2,3},{3,2},{4,5},{5,4},{6,7},{7,6},{8,9},{9,8},{10,11... | collective-permute-start | bytes 786440 | tf_op jit(solution)/shard_map/ppermute | solution.py:76
  390.2 41.6 %collective-permute-start.69 = (bf16[64,2048]{1,0:T(8,128)(2,1)}, bf16[64,2048]{1,0:T(8,128)(2,1)}, u32[]{:S(2)}, u32[]{:S(2)}) collective-permute-start(bf16[64,2048]{1,0:T(8,128)(2,1)} %get-tuple-element.405), channel_id=1, source_target_pairs={{0,2},{1,3},{2,0},{3,1},{4,6},{5,7},{6,4},{7,5},{8,10},{9,11},{10,... | collective-permute-start | bytes 786440 | tf_op jit(solution)/shard_map/ppermute | solution.py:76
  420.3 24.9 %collective-permute-start.66 = (bf16[128,2048]{1,0:T(8,128)(2,1)}, bf16[128,2048]{1,0:T(8,128)(2,1)S(1)}, u32[]{:S(2)}, u32[]{:S(2)}) collective-permute-start(bf16[128,2048]{1,0:T(8,128)(2,1)} %get-tuple-element.375), channel_id=1, source_target_pairs={{0,16},{4,20},{8,24},{12,28},{16,0},{20,4},{24,8},{28,12},{1,17},{... | collective-permute-start | bytes 1572872 | tf_op jit(solution)/shard_map/ppermute | solution.py:76
  447.2 53.9 %collective-permute-start.74 = (bf16[1024,1408]{0,1:T(8,128)(2,1)}, bf16[1024,1408]{0,1:T(8,128)(2,1)}, u32[]{:S(2)}, u32[]{:S(2)}) collective-permute-start(bf16[1024,1408]{0,1:T(8,128)(2,1)} %slice.384), channel_id=1, source_target_pairs={{0,4},{4,0},{8,12},{12,8},{16,20},{20,16},{24,28},{28,24},{1,5},{5... | collective-permute-start | bytes 8650760 | tf_op jit(solution)/shard_map/ppermute | solution.py:76
  453.0 36.2 %collective-permute-start.73 = (bf16[64,2048]{1,0:T(8,128)(2,1)S(1)}, bf16[64,2048]{1,0:T(8,128)(2,1)S(1)}, u32[]{:S(2)}, u32[]{:S(2)}) collective-permute-start(bf16[64,2048]{1,0:T(8,128)(2,1)S(1)} %get-tuple-element.354), channel_id=1, source_target_pairs={{0,3},{1,2},{2,1},{3,0},{4,7},{5,6},{6,5},{7,4},{8,11},{9,10},{10,... | collective-permute-start | bytes 786440 | tf_op jit(solution)/shard_map/ppermute | solution.py:76
  453.0 40.4 %collective-permute-start.75 = (bf16[64,2304]{1,0:T(8,128)(2,1)S(1)}, bf16[64,2304]{1,0:T(8,128)(2,1)S(1)}, u32[]{:S(2)}, u32[]{:S(2)}) collective-permute-start(bf16[64,2304]{1,0:T(8,128)(2,1)S(1)} %get-tuple-element.402), channel_id=1, source_target_pairs={{0,1},{1,0},{2,3},{3,2},{4,5},{5,4},{6,7},{7,6},{8,9},{9,8},{10,11... | collective-permute-start | bytes 884744 | tf_op jit(solution)/shard_map/ppermute | solution.py:76
  462.4 33.1 %collective-permute-start.76 = (bf16[64,2304]{1,0:T(8,128)(2,1)S(1)}, bf16[64,2304]{1,0:T(8,128)(2,1)S(1)}, u32[]{:S(2)}, u32[]{:S(2)}) collective-permute-start(bf16[64,2304]{1,0:T(8,128)(2,1)S(1)} %get-tuple-element.401), channel_id=1, source_target_pairs={{0,2},{1,3},{2,0},{3,1},{4,6},{5,7},{6,4},{7,5},{8,10},{9,11},{10,... | collective-permute-start | bytes 884744 | tf_op jit(solution)/shard_map/ppermute | solution.py:76
  470.9 30.1 %collective-permute-start.77 = (bf16[64,2304]{1,0:T(8,128)(2,1)S(1)}, bf16[64,2304]{1,0:T(8,128)(2,1)S(1)}, u32[]{:S(2)}, u32[]{:S(2)}) collective-permute-start(bf16[64,2304]{1,0:T(8,128)(2,1)S(1)} %get-tuple-element.400), channel_id=1, source_target_pairs={{0,3},{1,2},{2,1},{3,0},{4,7},{5,6},{6,5},{7,4},{8,11},{9,10},{10,... | collective-permute-start | bytes 884744 | tf_op jit(solution)/shard_map/ppermute | solution.py:76
  489.2 30.3 %collective-permute-start.81 = (bf16[128,2048]{1,0:T(8,128)(2,1)S(1)}, bf16[128,2048]{1,0:T(8,128)(2,1)}, u32[]{:S(2)}, u32[]{:S(2)}) collective-permute-start(bf16[128,2048]{1,0:T(8,128)(2,1)S(1)} %get-tuple-element.352), channel_id=1, source_target_pairs={{0,8},{4,12},{8,0},{12,4},{16,24},{20,28},{24,16},{28,20},{1,9},{5... | collective-permute-start | bytes 1572872 | tf_op jit(solution)/shard_map/ppermute | solution.py:76
  493.4 26.3 %collective-permute-start.82 = (bf16[128,2048]{1,0:T(8,128)(2,1)S(1)}, bf16[128,2048]{1,0:T(8,128)(2,1)S(1)}, u32[]{:S(2)}, u32[]{:S(2)}) collective-permute-start(bf16[128,2048]{1,0:T(8,128)(2,1)S(1)} %get-tuple-element.352), channel_id=1, source_target_pairs={{0,16},{4,20},{8,24},{12,28},{16,0},{20,4},{24,8},{28,12},{1,17},{... | collective-permute-start | bytes 1572872 | tf_op jit(solution)/shard_map/ppermute | solution.py:76
  495.5 26.0 %collective-permute-start.83 = (bf16[128,2048]{1,0:T(8,128)(2,1)S(1)}, bf16[128,2048]{1,0:T(8,128)(2,1)S(1)}, u32[]{:S(2)}, u32[]{:S(2)}) collective-permute-start(bf16[128,2048]{1,0:T(8,128)(2,1)S(1)} %get-tuple-element.352), channel_id=1, source_target_pairs={{0,24},{4,28},{8,16},{12,20},{16,8},{20,12},{24,0},{28,4},{1,25},{... | collective-permute-start | bytes 1572872 | tf_op jit(solution)/shard_map/ppermute | solution.py:76
  519.8 25.0 %collective-permute-start.84 = (bf16[256,1408]{0,1:T(8,128)(2,1)S(1)}, bf16[256,1408]{0,1:T(8,128)(2,1)S(1)}, u32[]{:S(2)}, u32[]{:S(2)}) collective-permute-start(bf16[256,1408]{0,1:T(8,128)(2,1)S(1)} %get-tuple-element.373), channel_id=1, source_target_pairs={{0,8},{4,12},{8,0},{12,4},{16,24},{20,28},{24,16},{28,20},{1,9},{5... | collective-permute-start | bytes 2162696 | tf_op jit(solution)/shard_map/ppermute | solution.py:76
  521.5 31.8 %collective-permute-start.85 = (bf16[256,1408]{0,1:T(8,128)(2,1)S(1)}, bf16[256,1408]{0,1:T(8,128)(2,1)S(1)}, u32[]{:S(2)}, u32[]{:S(2)}) collective-permute-start(bf16[256,1408]{0,1:T(8,128)(2,1)S(1)} %get-tuple-element.372), channel_id=1, source_target_pairs={{0,16},{4,20},{8,24},{12,28},{16,0},{20,4},{24,8},{28,12},{1,17},{... | collective-permute-start | bytes 2162696 | tf_op jit(solution)/shard_map/ppermute | solution.py:76
  521.9 31.5 %collective-permute-start.86 = (bf16[256,1408]{0,1:T(8,128)(2,1)S(1)}, bf16[256,1408]{0,1:T(8,128)(2,1)S(1)}, u32[]{:S(2)}, u32[]{:S(2)}) collective-permute-start(bf16[256,1408]{0,1:T(8,128)(2,1)S(1)} %get-tuple-element.371), channel_id=1, source_target_pairs={{0,24},{4,28},{8,16},{12,20},{16,8},{20,12},{24,0},{28,4},{1,25},{... | collective-permute-start | bytes 2162696 | tf_op jit(solution)/shard_map/ppermute | solution.py:76
  539.0 62.6 %collective-permute-start.87 = (bf16[512,2048]{1,0:T(8,128)(2,1)}, bf16[512,2048]{1,0:T(8,128)(2,1)}, u32[]{:S(2)}, u32[]{:S(2)}) collective-permute-start(bf16[512,2048]{1,0:T(8,128)(2,1)} %pad_maximum_fusion.7), channel_id=1, source_target_pairs={{0,4},{4,0},{8,12},{12,8},{16,20},{20,16},{24,28},{28,24},{1,5},{5... | collective-permute-start | bytes 6291464 | tf_op jit(solution)/shard_map/ppermute | solution.py:76
  (169 other events, 1734.6 us)

commit v3 on v2

v3 whole, which is shorter than its diff:
```python
import functools
import math

import jax
import jax.numpy as jnp
from jax import lax
from jax.experimental import pallas as pl
from jax.experimental.pallas import tpu as pltpu
from jax.sharding import PartitionSpec as P

HEAD_SIZE = 128
TOP = 8
PAIR = 64
LANES = 128

EPSILON = 1e-06
THETA = 1000000.0
F32 = jnp.float32
BF16 = jnp.bfloat16


def norm_rows(value_rows, norm_gain):
    return (
        value_rows
        * lax.rsqrt(jnp.mean(value_rows * value_rows, axis=-1, keepdims=True) + EPSILON)
        * norm_gain
    )


def norm_back(value_rows, norm_gain, upstream):
    scaling = lax.rsqrt(jnp.mean(value_rows * value_rows, axis=-1, keepdims=True) + EPSILON)
    normal = value_rows * scaling
    weighted = upstream * norm_gain
    inward = scaling * (weighted - normal * jnp.mean(weighted * normal, axis=-1, keepdims=True))
    return (inward, upstream * normal)


def rope_tables(positions, head_size):
    halfway = head_size // 2
    inverse = THETA ** (-(jnp.arange(halfway, dtype=jnp.float32) * 2.0) / head_size)
    angles = positions.astype(jnp.float32)[:, None] * inverse[None, :]
    cosine, sine = jnp.cos(angles), jnp.sin(angles)
    return (
        jnp.concatenate([cosine, cosine], axis=1),
        jnp.concatenate([-sine, sine], axis=1),
    )


SWAPPED = 8


def swap(value, axis, mask):
    count = lax.axis_size(axis)
    return lax.ppermute(value, axis, [(i, i ^ mask) for i in range(count)])


def join(*values):
    return lax.optimization_barrier(values)


ORDER = (0, 2, 4, 6, 1, 3, 5, 7)


def plus(*values):
    total = values[0].astype(F32)
    for v in values[1:]:
        total = total + v.astype(F32)
    return total.astype(values[0].dtype)


def absolute():
    return lax.axis_size("ep") > SWAPPED


def gather_hops(value):
    if absolute():
        return [lax.all_gather(value, "ep", axis=0, tiled=True)]
    return [swap(value, "ep", m) for m in ORDER[1:4]]


def gather_near(value, hops):
    if absolute():
        return hops[0][: hops[0].shape[0] // 2]
    return jnp.concatenate([value] + hops, axis=0)


def gather_core(near, hops):
    if absolute():
        return hops[0][hops[0].shape[0] // 2 :]
    return swap(near, "ep", 1)


def scatter_swap(send):
    return send if absolute() else swap(send, "ep", 1)


def scatter_sums(keep, come):
    if absolute():
        return [jnp.concatenate([keep, come], axis=0)]
    rows = keep.shape[0] // 4
    return [
        plus(keep[i * rows : (i + 1) * rows], come[i * rows : (i + 1) * rows]) for i in range(4)
    ]


def scatter_hops(sums):
    if absolute():
        return [lax.psum_scatter(sums[0], "ep", scatter_dimension=0, tiled=True)]
    return [swap(v, "ep", m) for v, m in zip(sums[1:], ORDER[1:4])]


def scatter_total(sums, hops):
    return hops[0] if absolute() else plus(sums[0], *hops)


def chunk_of(value, index):
    rows = value.shape[0] // lax.axis_size("tp")
    return lax.dynamic_slice_in_dim(value, index * rows, rows, 0)


def reduce_hops(value):
    mine = lax.axis_index("tp")
    return [swap(chunk_of(value, mine ^ m), "tp", m) for m in range(1, lax.axis_size("tp"))]


def reduce_total(value, hops):
    return plus(chunk_of(value, lax.axis_index("tp")), *hops)


def spread_hops(chunk):
    return [swap(chunk, "tp", m) for m in range(1, lax.axis_size("tp"))]


def spread_total(chunk, hops):
    mine = lax.axis_index("tp")
    rows = chunk.shape[0]
    result = jnp.zeros(((len(hops) + 1) * rows,) + chunk.shape[1:], chunk.dtype)
    for m, piece in enumerate([chunk] + hops):
        result = lax.dynamic_update_slice_in_dim(result, piece, (mine ^ m) * rows, 0)
    return result


def places():
    if absolute():
        return [jnp.int32(b) for b in range(lax.axis_size("ep"))]
    return [lax.axis_index("ep") ^ m for m in ORDER]


def pick_blocks(value, axis):
    count = lax.axis_size("ep")
    if count > SWAPPED:
        return value
    mine = lax.axis_index("ep")
    size = value.shape[axis] // count
    return jnp.concatenate(
        [lax.dynamic_slice_in_dim(value, (mine ^ m) * size, size, axis) for m in ORDER],
        axis=axis,
    )


def put_blocks(value, axis):
    count = lax.axis_size("ep")
    if count > SWAPPED:
        return value
    mine = lax.axis_index("ep")
    size = value.shape[axis] // count
    place = lambda m: (m // 2 + (m % 2) * (count // 2)) * size
    return jnp.concatenate(
        [lax.dynamic_slice_in_dim(value, place(mine ^ b), size, axis) for b in range(count)],
        axis=axis,
    )


def expert_kernel(
    local, place_ref, x_ref, g0_ref, g1_ref, ids0_ref, ids1_ref, router_ref, wgu_ref, wd_ref,
    dx_ref, joined_ref, hidden_ref,
):
    rows = x_ref.shape[0]
    features = x_ref.shape[1]
    expert_count = router_ref.shape[1]
    hidden_count = wd_ref.shape[0]
    extra = dx_ref.shape[1] - features
    base = place_ref[0]
    x = x_ref[...]
    upstream = jnp.concatenate([g0_ref[...], g1_ref[...]], axis=0)
    ids = jnp.concatenate([ids0_ref[...], ids1_ref[...]], axis=0)
    logits = jnp.dot(x, router_ref[...], preferred_element_type=F32)
    lane = lax.broadcasted_iota(jnp.int32, (rows, expert_count), 1)
    named = ids[:, 0:1] == lane
    for k in range(1, TOP):
        named = named | (ids[:, k : k + 1] == lane)
    exponent = jnp.exp(logits - jnp.max(logits, axis=1, keepdims=True))
    router = exponent / jnp.sum(exponent, axis=1, keepdims=True)
    chosen = jnp.where(named, router, 0.0)
    gates = chosen / jnp.sum(chosen, axis=1, keepdims=True)
    gate = [
        jnp.sum(jnp.where(lane == base + j, gates, 0.0), axis=1, keepdims=True)
        for j in range(local)
    ]
    left = lax.broadcasted_iota(jnp.int32, (rows, LANES), 1) < PAIR
    per_expert = hidden_count // local // PAIR
    gate_sum = [jnp.zeros((rows, LANES), F32) for _ in range(local)]
    group = 3

    def products(q):
        wide = group * LANES
        act = jnp.dot(
            x, wgu_ref[:, 2 * q * wide : 2 * (q + 1) * wide], preferred_element_type=F32
        )
        back = lax.dot_general(
            upstream,
            wd_ref[q * wide : (q + 1) * wide, :],
            (((1,), (1,)), ((), ())),
            preferred_element_type=F32,
        )
        return act, back

    def elementwise(q, act, back):
        for i in range(group):
            p = q * group + i
            one, two = 2 * p // per_expert, (2 * p + 1) // per_expert
            first = act[:, 2 * i * LANES : (2 * i + 1) * LANES]
            second = act[:, (2 * i + 1) * LANES : (2 * i + 2) * LANES]
            g = jnp.where(left, first, pltpu.roll(second, PAIR, 1))
            u = jnp.where(left, pltpu.roll(first, PAIR, 1), second)
            gh = back[:, i * LANES : (i + 1) * LANES]
            if one == two:
                scale = jnp.broadcast_to(gate[one], (rows, LANES))
            else:
                scale = jnp.where(left, gate[one], gate[two])
            sig = lax.logistic(g)
            silu = g * sig
            hid = silu * u
            product = hid * gh
            if one == two:
                gate_sum[one] += product
            else:
                gate_sum[one] += jnp.where(left, product, 0.0)
                gate_sum[two] += jnp.where(left, 0.0, product)
            hidden_ref[:, p * LANES : (p + 1) * LANES] = (hid * scale).astype(BF16)
            gs = gh * scale
            dg = gs * u * sig * (1.0 + g * (1.0 - sig))
            du = gs * silu
            joined_ref[:, 2 * p * LANES : (2 * p + 1) * LANES] = jnp.where(
                left, dg, pltpu.roll(du, PAIR, 1)
            ).astype(BF16)
            joined_ref[:, (2 * p + 1) * LANES : (2 * p + 2) * LANES] = jnp.where(
                left, pltpu.roll(dg, PAIR, 1), du
            ).astype(BF16)

    count = hidden_count // LANES // group
    waiting = []
    for q in range(count):
        waiting.append((q, *products(q)))
        if q:
            elementwise(*waiting.pop(0))
    elementwise(*waiting.pop(0))
    dx = lax.dot_general(
        joined_ref[...], wgu_ref[...], (((1,), (1,)), ((), ())), preferred_element_type=F32
    )
    dx_ref[:, :features] = dx.astype(BF16)
    wide = lax.broadcasted_iota(jnp.int32, (rows, extra), 1)
    tail = jnp.zeros((rows, extra), F32)
    for j in range(local):
        total = jnp.sum(gate_sum[j], axis=1, keepdims=True)
        high = total.astype(BF16).astype(F32)
        tail = jnp.where(wide == base + j, high, tail)
        tail = jnp.where(wide == expert_count + base + j, total - high, tail)
    dx_ref[:, features:] = tail.astype(BF16)


def run_experts(x, g, ids, where, router, wgu, wd, local):
    tokens, features = x.shape
    tile = 256
    block = tokens // len(where)
    steps = tokens // tile
    expert_count = router.shape[1]
    extra = -(-2 * expert_count // LANES) * LANES
    place = jnp.stack([lax.axis_index("ep") * local] + list(where)).astype(jnp.int32)
    found = lambda width, j: pl.BlockSpec((block, width), lambda i, s: (s[1 + 2 * i + j], 0))
    whole = lambda v: pl.BlockSpec(v.shape, lambda i, s: (0, 0), pipeline_mode=pl.Buffered(1))
    by_rows = lambda width: pl.BlockSpec((tile, width), lambda i, s: (i, 0))
    in_specs = [
        by_rows(features),
        found(features, 0),
        found(features, 1),
        found(TOP, 0),
        found(TOP, 1),
        whole(router),
        whole(wgu),
        whole(wd),
    ]
    operands = [place, x, g, g, ids, ids, router, wgu, wd]
    return pl.pallas_call(
        functools.partial(expert_kernel, local),
        grid_spec=pltpu.PrefetchScalarGridSpec(
            num_scalar_prefetch=1,
            grid=(steps,),
            in_specs=in_specs,
            out_specs=[
                by_rows(features + extra),
                by_rows(wgu.shape[1]),
                by_rows(wd.shape[0]),
            ],
        ),
        out_shape=[
            jax.ShapeDtypeStruct((tokens, features + extra), BF16),
            jax.ShapeDtypeStruct((tokens, wgu.shape[1]), BF16),
            jax.ShapeDtypeStruct((tokens, wd.shape[0]), BF16),
        ],
        compiler_params=pltpu.CompilerParams(vmem_limit_bytes=32 * 1024 * 1024),
        cost_estimate=pl.CostEstimate(
            flops=2 * tokens * features * (2 * wgu.shape[1] + wd.shape[0]),
            bytes_accessed=2 * tokens * features * 3 + 2 * features * 2 * wgu.shape[1],
            transcendentals=tokens * wd.shape[0],
        ),
    )(*operands)


def gate_up_kernel(*refs):
    *operands, result_ref = refs
    count = len(operands) // 2
    total = None
    for x_ref, joined_ref in zip(operands[:count], operands[count:]):
        part = lax.dot_general(
            x_ref[...], joined_ref[...], (((0,), (0,)), ((), ())), preferred_element_type=F32
        )
        total = part if total is None else total + part
    width = result_ref.shape[2]
    for e in range(result_ref.shape[0]):
        result_ref[e] = total[:, e * width : (e + 1) * width]


def gate_up_product(pieces, joined, shape):
    rows, features = pieces[0].shape
    width = joined[0].shape[1]
    tile = 256
    whole = pl.BlockSpec((rows, width), lambda i: (0, 0), pipeline_mode=pl.Buffered(1))
    return pl.pallas_call(
        gate_up_kernel,
        grid=(features // tile,),
        in_specs=[pl.BlockSpec((rows, tile), lambda i: (0, i)) for _ in pieces]
        + [whole for _ in joined],
        out_specs=pl.BlockSpec((shape[0], tile, shape[2]), lambda i: (0, i, 0)),
        out_shape=jax.ShapeDtypeStruct(shape, F32),
        compiler_params=pltpu.CompilerParams(vmem_limit_bytes=56 * 1024 * 1024),
        cost_estimate=pl.CostEstimate(
            flops=2 * len(pieces) * rows * features * width,
            bytes_accessed=2 * len(pieces) * rows * (features + width) + 4 * math.prod(shape),
            transcendentals=0,
        ),
    )(*pieces, *joined)


def down_kernel(place_ref, *refs):
    *pieces, g_ref, result_ref, sorted_ref = refs
    blocks = place_ref.shape[0] // len(pieces)
    block = pieces[0].shape[0] // blocks
    for i, hidden_ref in enumerate(pieces):
        for k in range(blocks):
            start = pl.multiple_of(place_ref[i * blocks + k] * block, block)
            sorted_ref[pl.ds(start, block), :] = hidden_ref[k * block : (k + 1) * block, :]
    result_ref[...] = lax.dot_general(
        sorted_ref[...], g_ref[...], (((0,), (0,)), ((), ())), preferred_element_type=F32
    )


def down_product(hidden, g, where):
    rows, features = g.shape
    width = hidden[0].shape[1]
    tile = 256
    return pl.pallas_call(
        down_kernel,
        grid_spec=pltpu.PrefetchScalarGridSpec(
            num_scalar_prefetch=1,
            grid=(width // tile,),
            in_specs=[pl.BlockSpec((v.shape[0], tile), lambda i, s: (0, i)) for v in hidden]
            + [pl.BlockSpec((rows, features), lambda i, s: (0, 0), pipeline_mode=pl.Buffered(1))],
            out_specs=pl.BlockSpec((tile, features), lambda i, s: (i, 0)),
            scratch_shapes=[pltpu.VMEM((rows, tile), BF16)],
        ),
        out_shape=jax.ShapeDtypeStruct((width, features), F32),
        compiler_params=pltpu.CompilerParams(vmem_limit_bytes=57 * 1024 * 1024),
        cost_estimate=pl.CostEstimate(
            flops=2 * rows * width * features,
            bytes_accessed=2 * rows * (width + features) + 4 * width * features,
            transcendentals=0,
        ),
    )(jnp.stack(where).astype(jnp.int32), *hidden, g)


def mixture_kernel(
    place_ref, upper0_ref, upper1_ref, lower0_ref, lower1_ref, wd_ref, result_ref
):
    early = pl.program_id(0) < pl.num_programs(0) // 2
    rows = jnp.concatenate(
        [
            jnp.where(early, upper0_ref[...], upper1_ref[...]),
            jnp.where(early, lower0_ref[...], lower1_ref[...]),
        ],
        axis=0,
    )
    result_ref[...] = jnp.dot(rows, wd_ref[...], preferred_element_type=F32).astype(BF16)


def mixture_product(hidden, wd, where):
    count = len(where)
    block = 2 * hidden[0].shape[0] // count
    width, features = wd.shape
    first = pl.BlockSpec((block, width), lambda i, s: (jnp.minimum(i, count // 2 - 1), 0))
    second = pl.BlockSpec((block, width), lambda i, s: (jnp.maximum(i - count // 2, 0), 0))
    return pl.pallas_call(
        mixture_kernel,
        grid_spec=pltpu.PrefetchScalarGridSpec(
            num_scalar_prefetch=1,
            grid=(count,),
            in_specs=[first, second, first, second]
            + [pl.BlockSpec((width, features), lambda i, s: (0, 0))],
            out_specs=pl.BlockSpec((2 * block, features), lambda i, s: (s[i], 0)),
        ),
        out_shape=jax.ShapeDtypeStruct((2 * block * count, features), BF16),
        compiler_params=pltpu.CompilerParams(vmem_limit_bytes=24 * 1024 * 1024),
        cost_estimate=pl.CostEstimate(
            flops=4 * block * count * width * features,
            bytes_accessed=4 * block * count * (width + features) + 2 * width * features,
            transcendentals=0,
        ),
    )(jnp.stack(where).astype(jnp.int32), *hidden, wd)


def rotated(value, cosine, sine):
    return value * cosine + pltpu.roll(value, HEAD_SIZE // 2, 1) * sine


def inverse_rms(value):
    return lax.rsqrt(jnp.mean(value * value, axis=1, keepdims=True) + EPSILON)


def head_columns(h):
    return slice(h * HEAD_SIZE, (h + 1) * HEAD_SIZE)


def against(left, right):
    return lax.dot_general(left, right, (((1,), (1,)), ((), ())), preferred_element_type=F32)


def over_rows(left, right):
    return lax.dot_general(left, right, (((0,), (0,)), ((), ())), preferred_element_type=F32)


def causal(rows):
    return lax.broadcasted_iota(jnp.int32, (rows, rows), 1) <= lax.broadcasted_iota(
        jnp.int32, (rows, rows), 0
    )


def attention_kernel(
    key_heads,
    x_ref,
    near_ref,
    core_ref,
    gains_ref,
    cosine_ref,
    sine_ref,
    wo_ref,
    raw_ref,
    low_ref,
    mixed_ref,
    lse_ref,
    upper_ref,
    lower_ref,
):
    rows = x_ref.shape[0]
    split = near_ref.shape[0]
    query_heads = mixed_ref.shape[1] // HEAD_SIZE
    heads = query_heads + key_heads
    raw = jnp.dot(x_ref[:, :split], near_ref[...], preferred_element_type=F32) + jnp.dot(
        x_ref[:, split:], core_ref[...], preferred_element_type=F32
    )
    raw_ref[...] = raw[:, : heads * HEAD_SIZE]
    low_ref[:, heads * HEAD_SIZE :] = raw[:, heads * HEAD_SIZE :].astype(BF16)
    for h in range(heads):
        u = raw[:, head_columns(h)]
        gain = gains_ref[0:1, :] if h < query_heads else gains_ref[1:2, :]
        low_ref[:, head_columns(h)] = rotated(
            u * inverse_rms(u) * gain, cosine_ref[...], sine_ref[...]
        ).astype(BF16)
    allowed = causal(rows)
    for h in range(query_heads):
        k = query_heads + h * key_heads // query_heads
        scores = against(low_ref[:, head_columns(h)], low_ref[:, head_columns(k)]) / math.sqrt(
            HEAD_SIZE
        )
        scores = jnp.where(allowed, scores, -jnp.inf)
        row_max = jnp.max(scores, axis=1, keepdims=True)
        exps = jnp.exp(scores - row_max)
        total = jnp.sum(exps, axis=1, keepdims=True)
        lse_ref[:, h : h + 1] = row_max + jnp.log(total)
        mixed_ref[:, head_columns(h)] = jnp.dot(
            (exps * (1.0 / total)).astype(BF16),
            low_ref[:, head_columns(k + key_heads)],
            preferred_element_type=F32,
        ).astype(BF16)
    part = jnp.dot(mixed_ref[...], wo_ref[...], preferred_element_type=F32)
    upper_ref[...] = part[: rows // 2].astype(BF16)
    lower_ref[...] = part[rows // 2 :].astype(BF16)


def attention(x, near, core, gains, cosine, sine, wo, key_heads):
    rows = x.shape[0]
    width = near.shape[1]
    query_width, features = wo.shape
    shapes = [
        ((rows, query_width + key_heads * HEAD_SIZE), F32),
        ((rows, width), BF16),
        ((rows, query_width), BF16),
        ((rows, query_width // HEAD_SIZE), F32),
        ((rows // 2, features), BF16),
        ((rows // 2, features), BF16),
    ]
    return pl.pallas_call(
        functools.partial(attention_kernel, key_heads),
        out_shape=[jax.ShapeDtypeStruct(*v) for v in shapes],
        compiler_params=pltpu.CompilerParams(vmem_limit_bytes=32 * 1024 * 1024),
        cost_estimate=pl.CostEstimate(
            flops=2 * rows * features * (width + query_width) + 4 * rows * rows * query_width,
            bytes_accessed=2 * features * (width + query_width) + 8 * rows * width,
            transcendentals=rows * rows * query_width // HEAD_SIZE,
        ),
    )(x, near, core, gains, cosine, sine, wo)


def attention_back_kernel(
    key_heads,
    upstream_ref,
    wo_ref,
    raw_ref,
    low_ref,
    lse_ref,
    gains_ref,
    cosine_ref,
    sine_ref,
    x_ref,
    near_ref,
    core_ref,
    beside_ref,
    feature_ref,
    keep_ref,
    send_ref,
    mixed_grad_ref,
    raw_grad_ref,
):
    rows = upstream_ref.shape[0]
    split = near_ref.shape[0]
    width = near_ref.shape[1]
    query_heads = mixed_grad_ref.shape[1] // HEAD_SIZE
    group = query_heads // key_heads
    root = math.sqrt(HEAD_SIZE)
    mixed_grad_ref[...] = against(upstream_ref[...], wo_ref[...]).astype(BF16)
    allowed = causal(rows)
    cosine = cosine_ref[...]
    sine = sine_ref[...]

    def norm_back(h, grad, gain):
        u = raw_ref[:, head_columns(h)]
        scale = inverse_rms(u)
        normal = u * scale
        turned = grad * cosine - pltpu.roll(grad, HEAD_SIZE // 2, 1) * sine
        weighted = turned * gain
        inward = scale * (weighted - normal * jnp.mean(weighted * normal, axis=1, keepdims=True))
        raw_grad_ref[:, head_columns(h)] = inward.astype(BF16)
        return turned * normal

    query_terms = jnp.zeros((rows, HEAD_SIZE), F32)
    key_terms = jnp.zeros((rows, HEAD_SIZE), F32)
    for k in range(key_heads):
        keys = low_ref[:, head_columns(query_heads + k)]
        values = low_ref[:, head_columns(query_heads + key_heads + k)]
        key_grad = jnp.zeros((rows, HEAD_SIZE), F32)
        value_grad = jnp.zeros((rows, HEAD_SIZE), F32)
        for h in range(k * group, (k + 1) * group):
            queries = low_ref[:, head_columns(h)]
            mixed_grad = mixed_grad_ref[:, head_columns(h)]
            scores = against(queries, keys) / root
            probs = jnp.where(allowed, jnp.exp(scores - lse_ref[:, h : h + 1]), 0.0)
            probs_grad = against(mixed_grad, values)
            value_grad += over_rows(probs.astype(BF16), mixed_grad)
            inner = jnp.sum(probs * probs_grad, axis=1, keepdims=True)
            scores_grad = (probs * (probs_grad - inner)).astype(BF16)
            query_grad = jnp.dot(scores_grad, keys, preferred_element_type=F32) / root
            key_grad += over_rows(scores_grad, queries)
            query_terms += norm_back(h, query_grad, gains_ref[0:1, :])
        key_terms += norm_back(query_heads + k, key_grad / root, gains_ref[1:2, :])
        raw_grad_ref[:, head_columns(query_heads + key_heads + k)] = value_grad.astype(BF16)
    raw_grad = raw_grad_ref[...]
    feature_ref[:, :split] = against(raw_grad, near_ref[...]).astype(BF16)
    feature_ref[:, split : 2 * split] = against(raw_grad, core_ref[...]).astype(BF16)
    feature_ref[:, 2 * split : 2 * split + HEAD_SIZE] = query_terms.astype(BF16)
    feature_ref[:, 2 * split + HEAD_SIZE :] = key_terms.astype(BF16)
    keep_ref[:, :width] = over_rows(x_ref[:, :split], raw_grad).astype(BF16)
    send_ref[:, :width] = over_rows(x_ref[:, split:], raw_grad).astype(BF16)
    keep_ref[:, width:] = beside_ref[:split]
    send_ref[:, width:] = beside_ref[split:]


def attention_back(upstream, wo, raw, low, lse, gains, cosine, sine, x, near, core, beside, key_heads):
    rows, features = upstream.shape
    query_width = wo.shape[0]
    split, width = near.shape
    whole = width + beside.shape[1]
    shapes = [
        ((rows, features + 2 * HEAD_SIZE), BF16),
        ((split, whole), BF16),
        ((split, whole), BF16),
    ]
    return pl.pallas_call(
        functools.partial(attention_back_kernel, key_heads),
        out_shape=[jax.ShapeDtypeStruct(*v) for v in shapes],
        scratch_shapes=[pltpu.VMEM((rows, query_width), BF16), pltpu.VMEM((rows, width), BF16)],
        compiler_params=pltpu.CompilerParams(vmem_limit_bytes=40 * 1024 * 1024),
        cost_estimate=pl.CostEstimate(
            flops=2 * rows * features * (2 * width + query_width) + 10 * rows * rows * query_width,
            bytes_accessed=2 * features * (3 * width + query_width) + 8 * rows * width,
            transcendentals=rows * rows * query_width // HEAD_SIZE,
        ),
    )(upstream, wo, raw, low, lse, gains, cosine, sine, x, near, core, beside)


def shards(
    hidden_in,
    expert_ids,
    attention_gain,
    query_gain,
    key_gain,
    query_weight,
    key_matrix,
    value_matrix,
    output_weight,
    expert_gain,
    router_weight,
    gate_up_weight,
    down_weight,
    output_grad,
):
    tokens, features = hidden_in.shape
    owners = lax.axis_size("ep")
    local_experts = gate_up_weight.shape[0]
    expert_count = local_experts * owners
    rows_a = tokens // 2
    halves = lambda v: (v[:rows_a], v[rows_a:])

    head_share = query_gain.shape[0]
    small_rows = max(tokens, router_weight.shape[0])
    padded = lambda v: jnp.pad(v.astype(BF16), ((0, small_rows - v.shape[0]), (0, 0)))
    by_feature = jnp.concatenate(
        [router_weight, attention_gain[:, None], expert_gain[:, None]], axis=1
    )
    small = jnp.concatenate(
        [
            padded(by_feature),
            padded(jnp.stack([query_gain, key_gain], axis=1)),
            padded(expert_ids),
        ],
        axis=1,
    )
    small_hops = gather_hops(small)
    weights = jnp.concatenate([query_weight, key_matrix, value_matrix], axis=1)
    hops = gather_hops(weights)
    near = gather_near(small, small_hops)
    small = put_blocks(jnp.concatenate([near, gather_core(near, small_hops)], axis=0), 0)
    small = small.reshape(owners, small_rows, -1)
    packed = small[:, : router_weight.shape[0], : expert_count + 2].reshape(features, -1)
    router_full = packed[:, :expert_count]
    attn_gain_full = packed[:, expert_count].astype(F32)
    mlp_gain_full = packed[:, expert_count + 1].astype(F32)
    head_gains = (
        small[:, :head_share, expert_count + 2 : expert_count + 4]
        .reshape(HEAD_SIZE, 2)
        .astype(F32)
    )
    gains = head_gains.T
    ids_all = small[:, :tokens, expert_count + 4 :].reshape(-1, TOP).astype(jnp.int32)
    wd = down_weight.reshape(-1, features)
    hidden_f = hidden_in.astype(F32)
    normed_low = norm_rows(hidden_f, attn_gain_full).astype(BF16)
    normed_rel = pick_blocks(normed_low, 1)
    positions = jnp.arange(tokens, dtype=jnp.int32)
    cosine, sine_table = rope_tables(positions, HEAD_SIZE)
    (
        hops,
        normed_rel,
        cosine,
        sine_table,
        gains,
        packed,
        ids_all,
        output_all,
        gate_up_low,
    ) = join(
        hops,
        normed_rel,
        cosine,
        sine_table,
        gains,
        packed,
        ids_all,
        output_grad,
        gate_up_weight,
    )

    near = gather_near(weights, hops)
    weights_rel = [near, gather_core(near, hops)]
    output_all = lax.all_gather(output_all, "ep", axis=0, tiled=True)
    query_width = query_weight.shape[1]
    key_width = key_matrix.shape[1]
    key_heads = key_width // HEAD_SIZE
    split = features // 2
    raw, low, attention_output, lse, *head_parts = attention(
        normed_rel, *weights_rel, gains, cosine, sine_table, output_weight, key_heads
    )
    (head_parts,) = join(head_parts)

    hops = reduce_hops(head_parts[0])
    wgu = gate_up_low.transpose(1, 0, 2).reshape(features, -1)
    hops, wgu = join(hops, wgu)

    chunk = reduce_total(head_parts[0], hops)
    hops, hops_b = join(spread_hops(chunk), reduce_hops(head_parts[1]))

    attended = [spread_total(chunk, hops)]
    chunk = reduce_total(head_parts[1], hops_b)
    hops = spread_hops(chunk)
    resid_halves = [hidden_f[:rows_a] + attended[0].astype(F32)]
    routed_halves = [norm_rows(resid_halves[0], mlp_gain_full).astype(BF16)]
    hops_a, hops = join(gather_hops(routed_halves[0]), hops)

    attended.append(spread_total(chunk, hops))
    resid_halves.append(hidden_f[rows_a:] + attended[1].astype(F32))
    routed_halves.append(norm_rows(resid_halves[1], mlp_gain_full).astype(BF16))
    near_a = gather_near(routed_halves[0], hops_a)
    core_a = gather_core(near_a, hops_a)
    hops_b = gather_hops(routed_halves[1])
    lined = places()
    where = [2 * b + h for h in range(2) for b in lined]

    def experts(piece, x):
        rows = slice(piece * owners // 2, (piece + 1) * owners // 2)
        return run_experts(
            x, output_all, ids_all, where[rows], router_full, wgu, wd, local_experts
        )

    keep_a, joined_0, hidden_0 = experts(0, near_a)
    send_a, joined_1, hidden_1 = experts(1, core_a)
    hops_b, send_a, keep_a = join(hops_b, send_a, keep_a)

    near_b = gather_near(routed_halves[1], hops_b)
    core_b = gather_core(near_b, hops_b)
    come = scatter_swap(send_a)
    keep_b, joined_2, hidden_2 = experts(2, near_b)
    come, core_b, keep_b = join(come, core_b, keep_b)

    sums_a = scatter_sums(keep_a, come)
    hops_a = scatter_hops(sums_a)
    send_b, joined_3, hidden_3 = experts(3, core_b)
    hops_a, send_b = join(hops_a, send_b)
    joined = [joined_0, joined_1, joined_2, joined_3]
    hidden = [hidden_0, hidden_1, hidden_2, hidden_3]
    routed_pieces = [near_a, core_a, near_b, core_b]
    resid = jnp.concatenate(resid_halves, axis=0)
    routed_low = jnp.concatenate(routed_halves, axis=0)
    logits = jnp.dot(routed_low, router_full, preferred_element_type=F32)
    logit_max = jnp.max(logits, axis=-1, keepdims=True)
    exponent = jnp.exp(logits - logit_max)
    router = exponent / jnp.sum(exponent, axis=-1, keepdims=True)
    every_expert = jnp.arange(expert_count, dtype=jnp.int32)
    named = jnp.any(expert_ids[:, :, None] == every_expert[None, None, :], axis=1)
    chosen = jnp.where(named, router, 0.0)
    chosen_total = jnp.sum(chosen, axis=1, keepdims=True)
    gates = chosen / chosen_total

    come = scatter_swap(send_b)
    total_a = scatter_total(sums_a, hops_a)
    hops = reduce_hops(total_a)
    mixture_parts = mixture_product(hidden, wd, lined)
    come, hops, mixture_parts = join(come, hops, mixture_parts)

    sums_b = scatter_sums(keep_b, come)
    hops_b = scatter_hops(sums_b)
    chunk = reduce_total(total_a, hops)
    hops_a = spread_hops(chunk)
    hops_b, hops_a, mixture_parts = join(hops_b, hops_a, mixture_parts)

    mixture = lax.psum_scatter(mixture_parts, "ep", scatter_dimension=0, tiled=True)
    returned = [spread_total(chunk, hops_a)]
    total_b = scatter_total(sums_b, hops_b)
    hops = reduce_hops(total_b)
    (hops,) = join(hops)
    chunk = reduce_total(total_b, hops)
    (hops,) = join(spread_hops(chunk))

    returned.append(spread_total(chunk, hops))
    returned = jnp.concatenate(returned, axis=0)
    grad_out = output_grad.astype(F32)
    tail = returned[:, features:].astype(F32)
    grad_gates = tail[:, :expert_count] + tail[:, expert_count : 2 * expert_count]
    grad_gates = jnp.where(named, grad_gates, 0.0)
    grad_router = jnp.where(
        named,
        (grad_gates - jnp.sum(grad_gates * gates, axis=1, keepdims=True)) / chosen_total,
        0.0,
    )
    grad_logits = (
        router * (grad_router - jnp.sum(router * grad_router, axis=1, keepdims=True))
    ).astype(BF16)
    router_grad = jnp.dot(routed_low.T, grad_logits, preferred_element_type=F32)
    grad_routed = returned[:, :features].astype(F32) + jnp.dot(
        grad_logits, router_full.T, preferred_element_type=F32
    )
    grad_resid_norm, mlp_terms = norm_back(resid, mlp_gain_full, grad_routed)
    mlp_gain_grad = jnp.sum(mlp_terms, axis=0)
    grad_resid = grad_out + grad_resid_norm
    grad_attended = grad_resid.astype(BF16)
    mixed_rel = pick_blocks(attention_output, 1)
    output_local = lax.dot_general(
        mixed_rel, grad_attended, (((0,), (0,)), ((), ())), preferred_element_type=F32
    ).astype(BF16)
    output_half = output_local.shape[0] // 2
    output_local, grad_attended = join(output_local, grad_attended)

    come = scatter_swap(output_local[output_half:])
    by_feature = jnp.concatenate([router_grad, mlp_gain_grad[:, None]], axis=1).astype(BF16)
    by_feature = jnp.pad(by_feature, ((0, 0), (0, -by_feature.shape[1] % LANES)))
    by_feature = pick_blocks(by_feature, 0)
    by_feature, come = join(by_feature, come)

    output_sums = scatter_sums(output_local[:output_half], come)
    output_hops = scatter_hops(output_sums)
    feature_part, weights_keep, weights_send = attention_back(
        grad_attended,
        output_weight,
        raw,
        low,
        lse,
        gains,
        cosine,
        sine_table,
        normed_rel,
        *weights_rel,
        by_feature,
        key_heads,
    )
    feature_part, weights_keep, weights_send, output_hops, last_joined, last_hidden, mixture = (
        join(feature_part, weights_keep, weights_send, output_hops, joined, hidden, mixture)
    )
    mixture = lax.psum(mixture, "tp")

    come = scatter_swap(weights_send)
    hops = reduce_hops(feature_part)
    output_share = scatter_total(output_sums, output_hops)
    output_hops = gather_hops(output_share)
    down_grad = down_product(last_hidden, output_all, where).reshape(down_weight.shape)
    come, hops, down_grad, last_joined = join(come, hops, down_grad, last_joined)

    weights_sums = scatter_sums(weights_keep, come)
    weights_hops = scatter_hops(weights_sums)
    chunk = reduce_total(feature_part, hops)
    hops = spread_hops(chunk)
    gate_up_grad = gate_up_product(routed_pieces, last_joined, gate_up_weight.shape)
    hops, output_hops, gate_up_grad = join(hops, output_hops, gate_up_grad)

    near = gather_near(output_share, output_hops)
    output_core = gather_core(near, output_hops)
    total = spread_total(chunk, hops)
    grad_normed = put_blocks(total[:, :features], 1).astype(F32)
    head_grads = jnp.sum(total[:, features:].astype(F32), axis=0)
    grad_input_norm, attn_terms = norm_back(hidden_f, attn_gain_full, grad_normed)
    input_grad = grad_resid + grad_input_norm
    late = jnp.concatenate(
        [
            jnp.sum(attn_terms, axis=0).reshape(owners, -1),
            head_grads[:HEAD_SIZE].reshape(owners, -1),
            head_grads[HEAD_SIZE:].reshape(owners, -1),
        ],
        axis=1,
    )
    late = pick_blocks(late, 0)
    late_come, output_core, input_grad = join(
        scatter_swap(late[owners // 2 :]), output_core, input_grad
    )
    late_sums = scatter_sums(late[: owners // 2], late_come)
    late_hops = scatter_hops(late_sums)
    output_weight_grad = put_blocks(
        jnp.concatenate([near, output_core], axis=0), 0
    ).astype(F32)
    late_hops, weights_hops, output_weight_grad = join(
        late_hops, weights_hops, output_weight_grad
    )
    late, mixture = join(scatter_total(late_sums, late_hops)[0], mixture)
    weights_rows = scatter_total(weights_sums, weights_hops).astype(F32)
    block_out = (resid + mixture.astype(F32)).astype(BF16)
    early = weights_rows[:, query_width + 2 * key_width :]
    return (
        block_out,
        input_grad,
        late[: features // owners],
        late[features // owners : features // owners + head_share],
        late[features // owners + head_share :],
        weights_rows[:, :query_width],
        weights_rows[:, query_width : query_width + key_width],
        weights_rows[:, query_width + key_width : query_width + 2 * key_width],
        output_weight_grad,
        early[:, expert_count],
        early[:, :expert_count],
        gate_up_grad,
        down_grad,
    )


def solution(mesh):
    in_specs = (
        P("ep", None),
        P("ep", None),
        P("ep"),
        P("ep"),
        P("ep"),
        P("ep", "tp"),
        P("ep", "tp"),
        P("ep", "tp"),
        P("tp", None),
        P("ep"),
        P("ep", None),
        P("ep", None, "tp"),
        P("ep", "tp", None),
        P("ep", None),
    )
    out_specs = (
        P("ep", None),
        P("ep", None),
        P("ep"),
        P("ep"),
        P("ep"),
        P("ep", "tp"),
        P("ep", "tp"),
        P("ep", "tp"),
        P("tp", None),
        P("ep"),
        P("ep", None),
        P("ep", None, "tp"),
        P("ep", "tp", None),
    )
    return jax.shard_map(shards, mesh=mesh, in_specs=in_specs, out_specs=out_specs, check_vma=False)
```

time: 617 us -> 523 us (0.85)
  blocking collectives: 53.1 us -> 0 us
  matrix products: 39.7 us -> 8 us
  other arithmetic: 82.7 us -> 55.3 us
  Pallas kernels: 91.3 us -> 116 us
  waiting for transfers between devices: 177 us -> 159 us
  local copies, waits for them, and re-layouts: 67 us -> 84.5 us
  starting transfers between devices: 94.1 us -> 79.7 us
  between operations: 3.49 us -> 16 us
    dot_general x18 -> x0, matrix products: 32.3 us -> none  [the longest x4 12.5 us: shards(): jnp.dot(hidden[i * piece_rows:(i + 1) * piece_rows], wd, preferred_elemen...]
    all_gather x1 -> x0, blocking collectives: 30.8 us -> none  [shards(): everyone = lambda v: lax.all_gather(v, 'ep', axis=0, tiled=True)]
    pallas_call x5 -> x8, Pallas kernels: 72.1 us -> 96.4 us  [the longest x4 53.2 us: run_experts(): pl.pallas_call(functools.partial(expert_kernel, local), grid_spec=pltpu.P...]
    psum x1 -> x0, blocking collectives: 22.3 us -> none  [shards(): late = lax.psum(late, 'ep')]
    unnamed x281 -> x225, local copies, waits for them, and re-layouts: 30 us -> 51.5 us
    ppermute x88 -> x70, waiting for transfers between devices: 177 us -> 159 us  [swap(): return lax.ppermute(value, axis, [(i, i ^ mask) for i in range(count)])]
    ppermute x88 -> x70, starting transfers between devices: 94.1 us -> 79.2 us  [swap(): return lax.ppermute(value, axis, [(i, i ^ mask) for i in range(count)])]
    convert_element_type x14 -> x9, other arithmetic: 25.1 us -> 19.8 us  [the longest x6 14.6 us: plus(): return total.astype(values[0].dtype)]
  transfers between devices with their start and end apart: 88 -> 73, of which waited for: 34 -> 28; matrix products, arithmetic and copies ran while one was open for 25% -> 20% of each run, Pallas kernels for 15% -> 22%
where the time goes in v3:
time: 523 us; the launch traced here: 518 us
  waiting for transfers between devices  159 us (30%)
  Pallas kernels  116 us (22%)
  local copies, waits for them, and re-layouts  84.5 us (16%)
  starting transfers between devices  79.7 us (15%)
  other arithmetic  55.3 us (11%)
  between operations  16 us (3%)
  matrix products  8 us (2%)
    ppermute x70, waiting for transfers between devices, swap(): return lax.ppermute(value, axis, [(i, i ^ mask) for i in range(count)])  159 us
    ppermute x70, starting transfers between devices, swap(): return lax.ppermute(value, axis, [(i, i ^ mask) for i in range(count)])  79.2 us
    pallas_call x4, Pallas kernels, run_experts(): pl.pallas_call(functools.partial(expert_kernel, local), grid_spec=pltpu.P...  53.2 us
    unnamed x225, local copies, waits for them, and re-layouts  51.5 us
    pallas_call x1, Pallas kernels, gate_up_product(): pl.pallas_call(gate_up_kernel, grid=(features // tile,), in_specs=[pl.Blo...  19.4 us
    convert_element_type x6, other arithmetic, plus(): return total.astype(values[0].dtype)  14.6 us
    pallas_call x1, Pallas kernels, attention_back(): pl.pallas_call(functools.partial(attention_back_kernel, key_heads), out_s...  13.3 us
    pallas_call x1, Pallas kernels, down_product(): pl.pallas_call(down_kernel, grid_spec=pltpu.PrefetchScalarGridSpec(num_sc...  13.2 us
  transfers between devices with their start and end apart: 73, of which 28 were waited for; matrix products, arithmetic and copies ran while one was open for 20% of the time, Pallas kernels for 22%

profile of v3, /device:TPU:8, one launch (start us, length us, event | category | flops | bytes accessed | tf_op | source)
XLA Modules:
  0.0 517.9 jit_solution(12857189603151946233)
XLA Ops:
  27.9 10.2 %collective-permute-done.2 = bf16[256,1280]{1,0:T(8,128)(2,1)} collective-permute-done((bf16[256,1280]{1,0:T(8,128)(2,1)}, bf16[256,1280]{1,0:T(8,128)(2,1)}, u32[]{:S(2)}, u32[]{:S(2)}) %collective-permute-start.2) | collective-permute-done | bytes 655392 | tf_op jit(solution)/shard_map/ppermute | solution.py:54
  38.1 12.0 %collective-permute-done.1 = bf16[256,1280]{1,0:T(8,128)(2,1)} collective-permute-done((bf16[256,1280]{1,0:T(8,128)(2,1)}, bf16[256,1280]{1,0:T(8,128)(2,1)}, u32[]{:S(2)}, u32[]{:S(2)}) %collective-permute-start.1) | collective-permute-done | bytes 655392 | tf_op jit(solution)/shard_map/ppermute | solution.py:54
  53.4 6.4 %copy.58 = bf16[4,256,8,384]{3,2,0,1:T(8,128)(2,1)} copy(bf16[4,256,8,384]{3,2,1,0:T(8,128)(2,1)} %bitcast.74) | data formatting | bytes 12582912 | tf_op jit(solution)/shard_map/reshape | solution.py:724
  59.8 8.2 %shard_map.237 = (f32[256,1152]{1,0:T(8,128)S(1)}, bf16[256,1280]{1,0:T(8,128)(2,1)S(1)}, bf16[256,1024]{1,0:T(8,128)(2,1)S(1)}, f32[256,8]{1,0:T(8,128)S(1)}, b...) custom-call(bf16[256,2048]{1,0:T(8,128)(2,1)S(1)} %dynamic-slice_dynamic-update-slice_fusion.16.x_ref, ...), custom_call_target="tpu_custom_call" | custom-call | flops 2684354560 | bytes 12058624 | tf_op jit(solution)/shard_map/pallas_call | solution.py:521
  76.2 4.7 collective-permute-done.10
  80.9 7.4 %collective-permute-done.9 = bf16[32,2048]{1,0:T(8,128)(2,1)S(1)} collective-permute-done((bf16[32,2048]{1,0:T(8,128)(2,1)S(1)}, bf16[32,2048]{1,0:T(8,128)(2,1)S(1)}, u32[]{:S(2)}, u32[]{:S(2)}) %collective-permute-start.9) | collective-permute-done | bytes 131104 | tf_op jit(solution)/shard_map/ppermute | solution.py:54
  88.4 3.6 collective-permute-start.12
  114.5 3.9 collective-permute-done.21
  124.1 7.9 %collective-permute-done.18 = bf16[128,2048]{1,0:T(8,128)(2,1)S(1)} collective-permute-done((bf16[128,2048]{1,0:T(8,128)(2,1)S(1)}, bf16[128,2048]{1,0:T(8,128)(2,1)S(1)}, u32[]{:S(2)}, u32[]{:S(2)}) %collective-permute-start.18) | collective-permute-done | bytes 524320 | tf_op jit(solution)/shard_map/ppermute | solution.py:54
  150.7 13.5 %shard_map.239 = (bf16[512,2176]{1,0:T(8,128)(2,1)S(1)}, bf16[512,1536]{1,0:T(8,128)(2,1)S(1)}, bf16[512,768]{1,0:T(8,128)(2,1)S(1)}) custom-call(s32[5]{0:T(128)S(1)} %stack.134.place_ref, bf16[512,2048]{1,0:T(8,128)(2,1)} %pad_maximum_fusion.2.x_ref.refs_0_, bf16[2048,2048]{1,0:T(8,128)(2,1)} %all-gather.2.cloned.1.call-done.g0_ref.g1_ref.refs_4_, ...), custom_call_target="tpu_custom_call" | custom-call | flops 8053063680 | bytes 18874368 | tf_op jit(solution)/shard_map/pallas_call | solution.py:294
  167.7 13.6 %shard_map.238 = (bf16[512,2176]{1,0:T(8,128)(2,1)}, bf16[512,1536]{1,0:T(8,128)(2,1)S(1)}, bf16[512,768]{1,0:T(8,128)(2,1)S(1)}) custom-call(s32[5]{0:T(128)S(1)} %stack.129.place_ref, bf16[512,2048]{1,0:T(8,128)(2,1)} %collective-permute-done.26.x_ref.refs_1_, bf16[2048,2048]{1,0:T(8,128)(2,1)} %all-gather.2.cloned.1.call-done.g0_ref.g1_ref.refs_4_, ...), custom_call_target="tpu_custom_call" | custom-call | flops 8053063680 | bytes 18874368 | tf_op jit(solution)/shard_map/pallas_call | solution.py:294
  181.4 4.1 pad_maximum_fusion.3.x_ref.refs_2_
  190.4 12.8 %shard_map.240 = (bf16[512,2176]{1,0:T(8,128)(2,1)S(1)}, bf16[512,1536]{1,0:T(8,128)(2,1)S(1)}, bf16[512,768]{1,0:T(8,128)(2,1)S(1)}) custom-call(s32[5]{0:T(128)S(1)} %stack.139.place_ref, bf16[512,2048]{1,0:T(8,128)(2,1)} %pad_maximum_fusion.3.x_ref.refs_2_, bf16[2048,2048]{1,0:T(8,128)(2,1)} %all-gather.2.cloned.1.call-done.g0_ref.g1_ref.refs_4_, ...), custom_call_target="tpu_custom_call" | custom-call | flops 8053063680 | bytes 18874368 | tf_op jit(solution)/shard_map/pallas_call | solution.py:294
  209.8 13.3 %shard_map.241 = (bf16[512,2176]{1,0:T(8,128)(2,1)}, bf16[512,1536]{1,0:T(8,128)(2,1)S(1)}, bf16[512,768]{1,0:T(8,128)(2,1)S(1)}) custom-call(s32[5]{0:T(128)S(1)} %stack.144.place_ref, bf16[512,2048]{1,0:T(8,128)(2,1)} %collective-permute-done.28.x_ref.refs_3_, bf16[2048,2048]{1,0:T(8,128)(2,1)} %all-gather.2.cloned.1.call-done.g0_ref.g1_ref.refs_4_, ...), custom_call_target="tpu_custom_call" | custom-call | flops 8053063680 | bytes 18874368 | tf_op jit(solution)/shard_map/pallas_call | solution.py:294
  224.3 9.9 %collective-permute-done.30 = bf16[128,2176]{1,0:T(8,128)(2,1)S(1)} collective-permute-done((bf16[128,2176]{1,0:T(8,128)(2,1)S(1)}, bf16[128,2176]{1,0:T(8,128)(2,1)S(1)}, u32[]{:S(2)}, u32[]{:S(2)}) %collective-permute-start.30) | collective-permute-done | bytes 557088 | tf_op jit(solution)/shard_map/ppermute | solution.py:54
  245.3 8.4 %shard_map.242 = bf16[2048,2048]{1,0:T(8,128)(2,1)S(1)} custom-call(s32[8]{0:T(128)S(1)} %stack.153.place_ref, bf16[512,768]{1,0:T(8,128)(2,1)S(1)} %copy-done.27, bf16[512,768]{1,0:T(8,128)(2,1)S(1)} %copy-done.29, bf16[512,768]{1,0:T(8,128)(2,1)S(1)} %copy-done.31, bf16[512,768]{1,0:T(8,128)(2,1)S(1)} %copy-done.33, bf16[768,2048]{1,0:T(8,128)(2,1)S(1)} %bitcast.64), custom_call_target="tpu_custom_call" | custom-call | flops 6442450944 | bytes 14680064 | tf_op jit(solution)/shard_map/pallas_call | solution.py:412
  268.1 3.5 collective-permute-done.40
  273.1 3.5 collective-permute-done.41
  276.7 9.0 %collective-permute-done.37 = bf16[128,2176]{1,0:T(8,128)(2,1)} collective-permute-done((bf16[128,2176]{1,0:T(8,128)(2,1)S(1)}, bf16[128,2176]{1,0:T(8,128)(2,1)}, u32[]{:S(2)}, u32[]{:S(2)}) %collective-permute-start.37) | collective-permute-done | bytes 557088 | tf_op jit(solution)/shard_map/ppermute | solution.py:54
  309.5 7.5 %collective-permute-done.44 = bf16[32,2176]{1,0:T(8,128)(2,1)S(1)} collective-permute-done((bf16[32,2176]{1,0:T(8,128)(2,1)S(1)}, bf16[32,2176]{1,0:T(8,128)(2,1)S(1)}, u32[]{:S(2)}, u32[]{:S(2)}) %collective-permute-start.44) | collective-permute-done | bytes 139296 | tf_op jit(solution)/shard_map/ppermute | solution.py:54
  318.6 3.4 collective-permute-start.46
  323.3 4.2 collective-permute-done.46
  328.7 5.5 %collective-permute-done.47 = bf16[32,2176]{1,0:T(8,128)(2,1)S(1)} collective-permute-done((bf16[32,2176]{1,0:T(8,128)(2,1)S(1)}, bf16[32,2176]{1,0:T(8,128)(2,1)S(1)}, u32[]{:S(2)}, u32[]{:S(2)}) %collective-permute-start.47) | collective-permute-done | bytes 139296 | tf_op jit(solution)/shard_map/ppermute | solution.py:54
  354.3 13.3 %shard_map.243 = (bf16[256,2304]{1,0:T(8,128)(2,1)S(1)}, bf16[1024,1408]{1,0:T(8,128)(2,1)S(1)}, bf16[1024,1408]{1,0:T(8,128)(2,1)}) custom-call(bf16[256,2048]{1,0:T(8,128)(2,1)S(1)} %get-tuple-element.207.upstream_ref, bf16[1024,2048]{1,0:T(8,128)(2,1)} %wo_ref.3, f32[256,1152]{1,0:T(8,128)S(1)} %copy-done.25, bf16[256,1280]{1,0:T(8,128)(2,1)S(1)} %copy-done.35, ...), custom_call_target="tpu_custom_call" | custom-call | flops 4429185024 | bytes 22544384 | tf_op jit(solution)/shard_map/pallas_call | solution.py:616
  369.2 8.5 %collective-permute-done.50 = bf16[128,2048]{1,0:T(8,128)(2,1)} collective-permute-done((bf16[128,2048]{1,0:T(8,128)(2,1)S(1)}, bf16[128,2048]{1,0:T(8,128)(2,1)}, u32[]{:S(2)}, u32[]{:S(2)}) %collective-permute-start.50) | collective-permute-done | bytes 524320 | tf_op jit(solution)/shard_map/ppermute | solution.py:54
  386.7 13.2 %shard_map.244 = f32[768,2048]{1,0:T(8,128)} custom-call(s32[16]{0:T(128)} %stack.154.place_ref, bf16[512,768]{1,0:T(8,128)(2,1)} %copy-done.26, bf16[512,768]{1,0:T(8,128)(2,1)} %copy-done.28, bf16[512,768]{1,0:T(8,128)(2,1)} %copy-done.30, bf16[512,768]{1,0:T(8,128)(2,1)} %copy-done.32, bf16[2048,2048]{1,0:T(8,128)(2,1)} %all-gather.2.cloned.1.call-done.g0_ref.g1_ref.refs_4_), custom_call_target="tpu_custom_call" | custom-call | flops 6442450944 | bytes 17825792 | tf_op jit(solution)/shard_map/pallas_call | solution.py:372
  400.0 18.1 %collective-permute-done.55 = bf16[64,2304]{1,0:T(8,128)(2,1)S(1)} collective-permute-done((bf16[64,2304]{1,0:T(8,128)(2,1)S(1)}, bf16[64,2304]{1,0:T(8,128)(2,1)S(1)}, u32[]{:S(2)}, u32[]{:S(2)}) %collective-permute-start.55) | collective-permute-done | bytes 294944 | tf_op jit(solution)/shard_map/ppermute | solution.py:54
  419.2 6.7 %collective-permute-done.54 = bf16[64,2304]{1,0:T(8,128)(2,1)S(1)} collective-permute-done((bf16[64,2304]{1,0:T(8,128)(2,1)S(1)}, bf16[64,2304]{1,0:T(8,128)(2,1)S(1)}, u32[]{:S(2)}, u32[]{:S(2)}) %collective-permute-start.54) | collective-permute-done | bytes 294944 | tf_op jit(solution)/shard_map/ppermute | solution.py:54
  431.3 19.4 %shard_map.245 = f32[4,2048,384]{2,1,0:T(8,128)} custom-call(bf16[512,2048]{1,0:T(8,128)(2,1)} %pad_maximum_fusion.2.x_ref.refs_0_, bf16[512,2048]{1,0:T(8,128)(2,1)} %collective-permute-done.26.x_ref.refs_1_, bf16[512,2048]{1,0:T(8,128)(2,1)} %pad_maximum_fusion.3.x_ref.refs_2_, bf16[512,2048]{1,0:T(8,128)(2,1)} %collective-permute-done.28.x_ref.refs_3_, ...), custom_call_target="tpu_custom_call" | custom-call | flops 12884901888 | bytes 27262976 | tf_op jit(solution)/shard_map/pallas_call | solution.py:339
  458.7 15.3 %collective-permute-done.58 = bf16[64,2304]{1,0:T(8,128)(2,1)S(1)} collective-permute-done((bf16[64,2304]{1,0:T(8,128)(2,1)S(1)}, bf16[64,2304]{1,0:T(8,128)(2,1)S(1)}, u32[]{:S(2)}, u32[]{:S(2)}) %collective-permute-start.58) | collective-permute-done | bytes 294944 | tf_op jit(solution)/shard_map/ppermute | solution.py:54
  489.0 3.7 fusion.4
  498.6 4.4 convert_element_type.492
  (480 shorter events, 222.7 us)
Async XLA Ops:
  7.2 137.8 %all-gather.2.cloned.1.call-start = ((), (), s32[]{:S(2)}) async-start(), calls=%async_computation.1 | async-start | bytes 9437184 | tf_op jit(solution)/shard_map/all_gather | solution.py:713
  21.7 28.4 %collective-permute-start.1 = (bf16[256,1280]{1,0:T(8,128)(2,1)}, bf16[256,1280]{1,0:T(8,128)(2,1)}, u32[]{:S(2)}, u32[]{:S(2)}) collective-permute-start(bf16[256,1280]{1,0:T(8,128)(2,1)} %constant_dynamic-update-slice_fusion), channel_id=1, source_target_pairs={{0,16},{4,20},{8,24},{12,28},{16,0},{20,4},{24,8},{28,12},{1,17},{... | collective-permute-start | bytes 1966088 | tf_op jit(solution)/shard_map/ppermute | solution.py:54
  23.6 26.7 %collective-permute-start = (bf16[256,1280]{1,0:T(8,128)(2,1)}, bf16[256,1280]{1,0:T(8,128)(2,1)}, u32[]{:S(2)}, u32[]{:S(2)}) collective-permute-start(bf16[256,1280]{1,0:T(8,128)(2,1)} %constant_dynamic-update-slice_fusion), channel_id=1, source_target_pairs={{0,8},{4,12},{8,0},{12,4},{16,24},{20,28},{24,16},{28,20},{1,9},{5... | collective-permute-start | bytes 1966088 | tf_op jit(solution)/shard_map/ppermute | solution.py:54
  50.2 327.4 %reduce-scatter.2.cloned.1.call-start = ((), (), s32[]{:S(2)}) async-start(), calls=%async_computation.2 | async-start | bytes 9437184 | tf_op jit(solution)/shard_map/reduce_scatter | solution.py:793
  74.5 25.2 %collective-permute-start.15 = (bf16[32,2048]{1,0:T(8,128)(2,1)S(1)}, bf16[32,2048]{1,0:T(8,128)(2,1)S(1)}, u32[]{:S(2)}, u32[]{:S(2)}) collective-permute-start(bf16[32,2048]{1,0:T(8,128)(2,1)S(1)} %get-tuple-element.367), channel_id=1, source_target_pairs={{0,2},{1,3},{2,0},{3,1},{4,6},{5,7},{6,4},{7,5},{8,10},{9,11},{10,... | collective-permute-start | bytes 393224 | tf_op jit(solution)/shard_map/ppermute | solution.py:54
  108.1 23.8 %collective-permute-start.18 = (bf16[128,2048]{1,0:T(8,128)(2,1)S(1)}, bf16[128,2048]{1,0:T(8,128)(2,1)S(1)}, u32[]{:S(2)}, u32[]{:S(2)}) collective-permute-start(bf16[128,2048]{1,0:T(8,128)(2,1)S(1)} %multiply_convert_fusion.2), channel_id=1, source_target_pairs={{0,16},{4,20},{8,24},{12,28},{16,0},{20,4},{24,8},{28,12},{1,17},{... | collective-permute-start | bytes 1572872 | tf_op jit(solution)/shard_map/ppermute | solution.py:54
  109.3 22.7 %collective-permute-start.17 = (bf16[128,2048]{1,0:T(8,128)(2,1)S(1)}, bf16[128,2048]{1,0:T(8,128)(2,1)S(1)}, u32[]{:S(2)}, u32[]{:S(2)}) collective-permute-start(bf16[128,2048]{1,0:T(8,128)(2,1)S(1)} %multiply_convert_fusion.2), channel_id=1, source_target_pairs={{0,8},{4,12},{8,0},{12,4},{16,24},{20,28},{24,16},{28,20},{1,9},{5... | collective-permute-start | bytes 1572872 | tf_op jit(solution)/shard_map/ppermute | solution.py:54
  133.4 34.2 %collective-permute-start.26 = (bf16[512,2048]{1,0:T(8,128)(2,1)}, bf16[512,2048]{1,0:T(8,128)(2,1)}, u32[]{:S(2)}, u32[]{:S(2)}) collective-permute-start(bf16[512,2048]{1,0:T(8,128)(2,1)} %pad_maximum_fusion.2.x_ref.refs_0_), channel_id=1, source_target_pairs={{0,4},{4,0},{8,12},{12,8},{16,20},{20,16},{24,28},{28,24},{1,5},{5... | collective-permute-start | bytes 6291464 | tf_op jit(solution)/shard_map/ppermute | solution.py:54
  141.5 39.8 %collective-permute-start.25 = (bf16[128,2048]{1,0:T(8,128)(2,1)}, bf16[128,2048]{1,0:T(8,128)(2,1)}, u32[]{:S(2)}, u32[]{:S(2)}) collective-permute-start(bf16[128,2048]{1,0:T(8,128)(2,1)} %multiply_convert_fusion.1), channel_id=1, source_target_pairs={{0,24},{4,28},{8,16},{12,20},{16,8},{20,12},{24,0},{28,4},{1,25},{... | collective-permute-start | bytes 1572872 | tf_op jit(solution)/shard_map/ppermute | solution.py:54
  143.2 38.1 %collective-permute-start.24 = (bf16[128,2048]{1,0:T(8,128)(2,1)}, bf16[128,2048]{1,0:T(8,128)(2,1)}, u32[]{:S(2)}, u32[]{:S(2)}) collective-permute-start(bf16[128,2048]{1,0:T(8,128)(2,1)} %multiply_convert_fusion.1), channel_id=1, source_target_pairs={{0,16},{4,20},{8,24},{12,28},{16,0},{20,4},{24,8},{28,12},{1,17},{... | collective-permute-start | bytes 1572872 | tf_op jit(solution)/shard_map/ppermute | solution.py:54
  144.4 36.9 %collective-permute-start.23 = (bf16[128,2048]{1,0:T(8,128)(2,1)}, bf16[128,2048]{1,0:T(8,128)(2,1)}, u32[]{:S(2)}, u32[]{:S(2)}) collective-permute-start(bf16[128,2048]{1,0:T(8,128)(2,1)} %multiply_convert_fusion.1), channel_id=1, source_target_pairs={{0,8},{4,12},{8,0},{12,4},{16,24},{20,28},{24,16},{28,20},{1,9},{5... | collective-permute-start | bytes 1572872 | tf_op jit(solution)/shard_map/ppermute | solution.py:54
  208.0 26.1 %collective-permute-start.30 = (bf16[128,2176]{1,0:T(8,128)(2,1)S(1)}, bf16[128,2176]{1,0:T(8,128)(2,1)S(1)}, u32[]{:S(2)}, u32[]{:S(2)}) collective-permute-start(bf16[128,2176]{1,0:T(8,128)(2,1)S(1)} %get-tuple-element.353), channel_id=1, source_target_pairs={{0,16},{4,20},{8,24},{12,28},{16,0},{20,4},{24,8},{28,12},{1,17},{... | collective-permute-start | bytes 1671176 | tf_op jit(solution)/shard_map/ppermute | solution.py:54
  209.3 24.9 %collective-permute-start.29 = (bf16[128,2176]{1,0:T(8,128)(2,1)S(1)}, bf16[128,2176]{1,0:T(8,128)(2,1)S(1)}, u32[]{:S(2)}, u32[]{:S(2)}) collective-permute-start(bf16[128,2176]{1,0:T(8,128)(2,1)S(1)} %get-tuple-element.354), channel_id=1, source_target_pairs={{0,8},{4,12},{8,0},{12,4},{16,24},{20,28},{24,16},{28,20},{1,9},{5... | collective-permute-start | bytes 1671176 | tf_op jit(solution)/shard_map/ppermute | solution.py:54
  234.1 23.0 %collective-permute-start.32 = (bf16[512,2176]{1,0:T(8,128)(2,1)}, bf16[512,2176]{1,0:T(8,128)(2,1)}, u32[]{:S(2)}, u32[]{:S(2)}) collective-permute-start(bf16[512,2176]{1,0:T(8,128)(2,1)} %get-tuple-element.184), channel_id=1, source_target_pairs={{0,4},{4,0},{8,12},{12,8},{16,20},{20,16},{24,28},{28,24},{1,5},{5... | collective-permute-start | bytes 6684680 | tf_op jit(solution)/shard_map/ppermute | solution.py:54
  260.8 24.9 %collective-permute-start.37 = (bf16[128,2176]{1,0:T(8,128)(2,1)S(1)}, bf16[128,2176]{1,0:T(8,128)(2,1)}, u32[]{:S(2)}, u32[]{:S(2)}) collective-permute-start(bf16[128,2176]{1,0:T(8,128)(2,1)S(1)} %get-tuple-element.350), channel_id=1, source_target_pairs={{0,16},{4,20},{8,24},{12,28},{16,0},{20,4},{24,8},{28,12},{1,17},{... | collective-permute-start | bytes 1671176 | tf_op jit(solution)/shard_map/ppermute | solution.py:54
  262.0 23.7 %collective-permute-start.36 = (bf16[128,2176]{1,0:T(8,128)(2,1)S(1)}, bf16[128,2176]{1,0:T(8,128)(2,1)}, u32[]{:S(2)}, u32[]{:S(2)}) collective-permute-start(bf16[128,2176]{1,0:T(8,128)(2,1)S(1)} %get-tuple-element.351), channel_id=1, source_target_pairs={{0,8},{4,12},{8,0},{12,4},{16,24},{20,28},{24,16},{28,20},{1,9},{5... | collective-permute-start | bytes 1671176 | tf_op jit(solution)/shard_map/ppermute | solution.py:54
  285.7 217.4 %all-reduce.4.cloned.1.call-start = ((), (), s32[]{:S(2)}) async-start(), calls=%async_computation.3 | async-start | bytes 2097152 | tf_op jit(solution)/shard_map/psum | solution.py:855
  352.9 24.7 %collective-permute-start.50 = (bf16[128,2048]{1,0:T(8,128)(2,1)S(1)}, bf16[128,2048]{1,0:T(8,128)(2,1)}, u32[]{:S(2)}, u32[]{:S(2)}) collective-permute-start(bf16[128,2048]{1,0:T(8,128)(2,1)S(1)} %get-tuple-element.344), channel_id=1, source_target_pairs={{0,16},{4,20},{8,24},{12,28},{16,0},{20,4},{24,8},{28,12},{1,17},{... | collective-permute-start | bytes 1572872 | tf_op jit(solution)/shard_map/ppermute | solution.py:54
  353.8 23.8 %collective-permute-start.49 = (bf16[128,2048]{1,0:T(8,128)(2,1)S(1)}, bf16[128,2048]{1,0:T(8,128)(2,1)}, u32[]{:S(2)}, u32[]{:S(2)}) collective-permute-start(bf16[128,2048]{1,0:T(8,128)(2,1)S(1)} %get-tuple-element.345), channel_id=1, source_target_pairs={{0,8},{4,12},{8,0},{12,4},{16,24},{20,28},{24,16},{28,20},{1,9},{5... | collective-permute-start | bytes 1572872 | tf_op jit(solution)/shard_map/ppermute | solution.py:54
  377.6 50.0 %collective-permute-start.52 = (bf16[1024,1408]{1,0:T(8,128)(2,1)}, bf16[1024,1408]{1,0:T(8,128)(2,1)}, u32[]{:S(2)}, u32[]{:S(2)}) collective-permute-start(bf16[1024,1408]{1,0:T(8,128)(2,1)} %get-tuple-element.223), channel_id=1, source_target_pairs={{0,4},{4,0},{8,12},{12,8},{16,20},{20,16},{24,28},{28,24},{1,5},{5... | collective-permute-start | bytes 8650760 | tf_op jit(solution)/shard_map/ppermute | solution.py:54
  381.3 69.3 %collective-permute-start.61 = (bf16[128,2048]{1,0:T(8,128)(2,1)S(1)}, bf16[128,2048]{1,0:T(8,128)(2,1)S(1)}, u32[]{:S(2)}, u32[]{:S(2)}) collective-permute-start(bf16[128,2048]{1,0:T(8,128)(2,1)S(1)} %get-tuple-element.324), channel_id=1, source_target_pairs={{0,24},{4,28},{8,16},{12,20},{16,8},{20,12},{24,0},{28,4},{1,25},{... | collective-permute-start | bytes 1572872 | tf_op jit(solution)/shard_map/ppermute | solution.py:54
  382.8 35.3 %collective-permute-start.55 = (bf16[64,2304]{1,0:T(8,128)(2,1)S(1)}, bf16[64,2304]{1,0:T(8,128)(2,1)S(1)}, u32[]{:S(2)}, u32[]{:S(2)}) collective-permute-start(bf16[64,2304]{1,0:T(8,128)(2,1)S(1)} %get-tuple-element.357), channel_id=1, source_target_pairs={{0,3},{1,2},{2,1},{3,0},{4,7},{5,6},{6,5},{7,4},{8,11},{9,10},{10,... | collective-permute-start | bytes 884744 | tf_op jit(solution)/shard_map/ppermute | solution.py:54
  384.3 41.5 %collective-permute-start.54 = (bf16[64,2304]{1,0:T(8,128)(2,1)S(1)}, bf16[64,2304]{1,0:T(8,128)(2,1)S(1)}, u32[]{:S(2)}, u32[]{:S(2)}) collective-permute-start(bf16[64,2304]{1,0:T(8,128)(2,1)S(1)} %get-tuple-element.358), channel_id=1, source_target_pairs={{0,2},{1,3},{2,0},{3,1},{4,6},{5,7},{6,4},{7,5},{8,10},{9,11},{10,... | collective-permute-start | bytes 884744 | tf_op jit(solution)/shard_map/ppermute | solution.py:54
  385.8 41.8 %collective-permute-start.53 = (bf16[64,2304]{1,0:T(8,128)(2,1)S(1)}, bf16[64,2304]{1,0:T(8,128)(2,1)S(1)}, u32[]{:S(2)}, u32[]{:S(2)}) collective-permute-start(bf16[64,2304]{1,0:T(8,128)(2,1)S(1)} %get-tuple-element.359), channel_id=1, source_target_pairs={{0,1},{1,0},{2,3},{3,2},{4,5},{5,4},{6,7},{7,6},{8,9},{9,8},{10,11... | collective-permute-start | bytes 884744 | tf_op jit(solution)/shard_map/ppermute | solution.py:54
  418.0 37.1 %collective-permute-start.60 = (bf16[128,2048]{1,0:T(8,128)(2,1)S(1)}, bf16[128,2048]{1,0:T(8,128)(2,1)S(1)}, u32[]{:S(2)}, u32[]{:S(2)}) collective-permute-start(bf16[128,2048]{1,0:T(8,128)(2,1)S(1)} %get-tuple-element.324), channel_id=1, source_target_pairs={{0,16},{4,20},{8,24},{12,28},{16,0},{20,4},{24,8},{28,12},{1,17},{... | collective-permute-start | bytes 1572872 | tf_op jit(solution)/shard_map/ppermute | solution.py:54
  425.9 30.8 %collective-permute-start.59 = (bf16[128,2048]{1,0:T(8,128)(2,1)S(1)}, bf16[128,2048]{1,0:T(8,128)(2,1)S(1)}, u32[]{:S(2)}, u32[]{:S(2)}) collective-permute-start(bf16[128,2048]{1,0:T(8,128)(2,1)S(1)} %get-tuple-element.324), channel_id=1, source_target_pairs={{0,8},{4,12},{8,0},{12,4},{16,24},{20,28},{24,16},{28,20},{1,9},{5... | collective-permute-start | bytes 1572872 | tf_op jit(solution)/shard_map/ppermute | solution.py:54
  427.8 29.4 %collective-permute-start.57 = (bf16[64,2304]{1,0:T(8,128)(2,1)S(1)}, bf16[64,2304]{1,0:T(8,128)(2,1)S(1)}, u32[]{:S(2)}, u32[]{:S(2)}) collective-permute-start(bf16[64,2304]{1,0:T(8,128)(2,1)S(1)} %get-tuple-element.326), channel_id=1, source_target_pairs={{0,2},{1,3},{2,0},{3,1},{4,6},{5,7},{6,4},{7,5},{8,10},{9,11},{10,... | collective-permute-start | bytes 884744 | tf_op jit(solution)/shard_map/ppermute | solution.py:54
  431.3 27.4 %collective-permute-start.56 = (bf16[64,2304]{1,0:T(8,128)(2,1)S(1)}, bf16[64,2304]{1,0:T(8,128)(2,1)S(1)}, u32[]{:S(2)}, u32[]{:S(2)}) collective-permute-start(bf16[64,2304]{1,0:T(8,128)(2,1)S(1)} %get-tuple-element.326), channel_id=1, source_target_pairs={{0,1},{1,0},{2,3},{3,2},{4,5},{5,4},{6,7},{7,6},{8,9},{9,8},{10,11... | collective-permute-start | bytes 884744 | tf_op jit(solution)/shard_map/ppermute | solution.py:54
  450.7 23.4 %collective-permute-start.58 = (bf16[64,2304]{1,0:T(8,128)(2,1)S(1)}, bf16[64,2304]{1,0:T(8,128)(2,1)S(1)}, u32[]{:S(2)}, u32[]{:S(2)}) collective-permute-start(bf16[64,2304]{1,0:T(8,128)(2,1)S(1)} %get-tuple-element.326), channel_id=1, source_target_pairs={{0,3},{1,2},{2,1},{3,0},{4,7},{5,6},{6,5},{7,4},{8,11},{9,10},{10,... | collective-permute-start | bytes 884744 | tf_op jit(solution)/shard_map/ppermute | solution.py:54
  455.1 41.7 %collective-permute-start.69 = (bf16[256,1408]{1,0:T(8,128)(2,1)}, bf16[256,1408]{1,0:T(8,128)(2,1)}, u32[]{:S(2)}, u32[]{:S(2)}) collective-permute-start(bf16[256,1408]{1,0:T(8,128)(2,1)} %get-tuple-element.346), channel_id=1, source_target_pairs={{0,24},{4,28},{8,16},{12,20},{16,8},{20,12},{24,0},{28,4},{1,25},{... | collective-permute-start | bytes 2162696 | tf_op jit(solution)/shard_map/ppermute | solution.py:54
  456.7 46.4 %collective-permute-start.68 = (bf16[256,1408]{1,0:T(8,128)(2,1)}, bf16[256,1408]{1,0:T(8,128)(2,1)}, u32[]{:S(2)}, u32[]{:S(2)}) collective-permute-start(bf16[256,1408]{1,0:T(8,128)(2,1)} %get-tuple-element.347), channel_id=1, source_target_pairs={{0,16},{4,20},{8,24},{12,28},{16,0},{20,4},{24,8},{28,12},{1,17},{... | collective-permute-start | bytes 2162696 | tf_op jit(solution)/shard_map/ppermute | solution.py:54
  457.2 45.9 %collective-permute-start.67 = (bf16[256,1408]{1,0:T(8,128)(2,1)}, bf16[256,1408]{1,0:T(8,128)(2,1)}, u32[]{:S(2)}, u32[]{:S(2)}) collective-permute-start(bf16[256,1408]{1,0:T(8,128)(2,1)} %get-tuple-element.348), channel_id=1, source_target_pairs={{0,8},{4,12},{8,0},{12,4},{16,24},{20,28},{24,16},{28,20},{1,9},{5... | collective-permute-start | bytes 2162696 | tf_op jit(solution)/shard_map/ppermute | solution.py:54
  (127 other events, 1340.7 us)
Sparse Core Ops, SparseCore 0:
  50.4 54.7 all-gather.1
  285.9 71.0 reduce-scatter.1
  378.5 89.8 all-reduce.3

commit v4 on v3

--- a/solution.py
+++ b/solution.py
@@ -17,6 +17,7 @@
 THETA = 1000000.0
 F32 = jnp.float32
 BF16 = jnp.bfloat16
+SMALL = pl.CostEstimate(flops=0, bytes_accessed=1024, transcendentals=0)
 
 
 def norm_rows(value_rows, norm_gain):
@@ -25,14 +26,6 @@
         * lax.rsqrt(jnp.mean(value_rows * value_rows, axis=-1, keepdims=True) + EPSILON)
         * norm_gain
     )
-
-
-def norm_back(value_rows, norm_gain, upstream):
-    scaling = lax.rsqrt(jnp.mean(value_rows * value_rows, axis=-1, keepdims=True) + EPSILON)
-    normal = value_rows * scaling
-    weighted = upstream * norm_gain
-    inward = scaling * (weighted - normal * jnp.mean(weighted * normal, axis=-1, keepdims=True))
-    return (inward, upstream * normal)
 
 
 def rope_tables(positions, head_size):
@@ -72,6 +65,29 @@
     return lax.axis_size("ep") > SWAPPED
 
 
+def in_hbm(*values):
+    return [pltpu.with_memory_space_constraint(v, pltpu.HBM) for v in values]
+
+
+def stack_kernel(*refs):
+    *pieces, result_ref = refs
+    rows = pieces[0].shape[0]
+    for i, piece in enumerate(pieces):
+        result_ref[i * rows : (i + 1) * rows, :] = piece[...]
+
+
+def stack_rows(pieces):
+    rows = pieces[0].shape[0]
+    return pl.pallas_call(
+        stack_kernel,
+        out_shape=jax.ShapeDtypeStruct(
+            (len(pieces) * rows,) + pieces[0].shape[1:], pieces[0].dtype
+        ),
+        compiler_params=pltpu.CompilerParams(vmem_limit_bytes=16 * 1024 * 1024),
+        cost_estimate=SMALL,
+    )(*pieces)
+
+
 def gather_hops(value):
     if absolute():
         return [lax.all_gather(value, "ep", axis=0, tiled=True)]
@@ -81,7 +97,7 @@
 def gather_near(value, hops):
     if absolute():
         return hops[0][: hops[0].shape[0] // 2]
-    return jnp.concatenate([value] + hops, axis=0)
+    return stack_rows([value] + hops)
 
 
 def gather_core(near, hops):
@@ -278,7 +294,7 @@
     extra = -(-2 * expert_count // LANES) * LANES
     place = jnp.stack([lax.axis_index("ep") * local] + list(where)).astype(jnp.int32)
     found = lambda width, j: pl.BlockSpec((block, width), lambda i, s: (s[1 + 2 * i + j], 0))
-    whole = lambda v: pl.BlockSpec(v.shape, lambda i, s: (0, 0), pipeline_mode=pl.Buffered(1))
+    resident = pl.BlockSpec(memory_space=pltpu.VMEM)
     by_rows = lambda width: pl.BlockSpec((tile, width), lambda i, s: (i, 0))
     in_specs = [
         by_rows(features),
@@ -286,10 +302,11 @@
         found(features, 1),
         found(TOP, 0),
         found(TOP, 1),
-        whole(router),
-        whole(wgu),
-        whole(wd),
+        resident,
+        resident,
+        resident,
     ]
+    (g,) = in_hbm(g)
     operands = [place, x, g, g, ids, ids, router, wgu, wd]
     return pl.pallas_call(
         functools.partial(expert_kernel, local),
@@ -308,12 +325,8 @@
             jax.ShapeDtypeStruct((tokens, wgu.shape[1]), BF16),
             jax.ShapeDtypeStruct((tokens, wd.shape[0]), BF16),
         ],
-        compiler_params=pltpu.CompilerParams(vmem_limit_bytes=32 * 1024 * 1024),
-        cost_estimate=pl.CostEstimate(
-            flops=2 * tokens * features * (2 * wgu.shape[1] + wd.shape[0]),
-            bytes_accessed=2 * tokens * features * 3 + 2 * features * 2 * wgu.shape[1],
-            transcendentals=tokens * wd.shape[0],
-        ),
+        compiler_params=pltpu.CompilerParams(vmem_limit_bytes=24 * 1024 * 1024),
+        cost_estimate=SMALL,
     )(*operands)
 
 
@@ -344,12 +357,8 @@
         out_specs=pl.BlockSpec((shape[0], tile, shape[2]), lambda i: (0, i, 0)),
         out_shape=jax.ShapeDtypeStruct(shape, F32),
         compiler_params=pltpu.CompilerParams(vmem_limit_bytes=56 * 1024 * 1024),
-        cost_estimate=pl.CostEstimate(
-            flops=2 * len(pieces) * rows * features * width,
-            bytes_accessed=2 * len(pieces) * rows * (features + width) + 4 * math.prod(shape),
-            transcendentals=0,
-        ),
-    )(*pieces, *joined)
+        cost_estimate=SMALL,
+    )(*in_hbm(*pieces, *joined))
 
 
 def down_kernel(place_ref, *refs):
@@ -381,12 +390,8 @@
         ),
         out_shape=jax.ShapeDtypeStruct((width, features), F32),
         compiler_params=pltpu.CompilerParams(vmem_limit_bytes=57 * 1024 * 1024),
-        cost_estimate=pl.CostEstimate(
-            flops=2 * rows * width * features,
-            bytes_accessed=2 * rows * (width + features) + 4 * width * features,
-            transcendentals=0,
-        ),
-    )(jnp.stack(where).astype(jnp.int32), *hidden, g)
+        cost_estimate=SMALL,
+    )(jnp.stack(where).astype(jnp.int32), *in_hbm(*hidden, g))
 
 
 def mixture_kernel(
@@ -420,12 +425,8 @@
         ),
         out_shape=jax.ShapeDtypeStruct((2 * block * count, features), BF16),
         compiler_params=pltpu.CompilerParams(vmem_limit_bytes=24 * 1024 * 1024),
-        cost_estimate=pl.CostEstimate(
-            flops=4 * block * count * width * features,
-            bytes_accessed=4 * block * count * (width + features) + 2 * width * features,
-            transcendentals=0,
-        ),
-    )(jnp.stack(where).astype(jnp.int32), *hidden, wd)
+        cost_estimate=SMALL,
+    )(jnp.stack(where).astype(jnp.int32), *in_hbm(*hidden, wd))
 
 
 def rotated(value, cosine, sine):
@@ -459,6 +460,8 @@
     x_ref,
     near_ref,
     core_ref,
+    near_kv_ref,
+    core_kv_ref,
     gains_ref,
     cosine_ref,
     sine_ref,
@@ -474,13 +477,18 @@
     split = near_ref.shape[0]
     query_heads = mixed_ref.shape[1] // HEAD_SIZE
     heads = query_heads + key_heads
-    raw = jnp.dot(x_ref[:, :split], near_ref[...], preferred_element_type=F32) + jnp.dot(
-        x_ref[:, split:], core_ref[...], preferred_element_type=F32
-    )
-    raw_ref[...] = raw[:, : heads * HEAD_SIZE]
-    low_ref[:, heads * HEAD_SIZE :] = raw[:, heads * HEAD_SIZE :].astype(BF16)
+    queries = query_heads * HEAD_SIZE
+    raw_ref[:, :queries] = jnp.dot(
+        x_ref[:, :split], near_ref[...], preferred_element_type=F32
+    ) + jnp.dot(x_ref[:, split:], core_ref[...], preferred_element_type=F32)
+    wide = 2 * key_heads * HEAD_SIZE
+    raw = jnp.dot(
+        x_ref[:, :split], near_kv_ref[:, :wide], preferred_element_type=F32
+    ) + jnp.dot(x_ref[:, split:], core_kv_ref[:, :wide], preferred_element_type=F32)
+    raw_ref[:, queries:] = raw[:, : key_heads * HEAD_SIZE]
+    low_ref[:, heads * HEAD_SIZE :] = raw[:, key_heads * HEAD_SIZE :].astype(BF16)
     for h in range(heads):
-        u = raw[:, head_columns(h)]
+        u = raw_ref[:, head_columns(h)]
         gain = gains_ref[0:1, :] if h < query_heads else gains_ref[1:2, :]
         low_ref[:, head_columns(h)] = rotated(
             u * inverse_rms(u) * gain, cosine_ref[...], sine_ref[...]
@@ -506,10 +514,10 @@
     lower_ref[...] = part[rows // 2 :].astype(BF16)
 
 
-def attention(x, near, core, gains, cosine, sine, wo, key_heads):
+def attention(x, near, core, near_kv, core_kv, gains, cosine, sine, wo, key_heads):
     rows = x.shape[0]
-    width = near.shape[1]
     query_width, features = wo.shape
+    width = query_width + 2 * key_heads * HEAD_SIZE
     shapes = [
         ((rows, query_width + key_heads * HEAD_SIZE), F32),
         ((rows, width), BF16),
@@ -522,16 +530,13 @@
         functools.partial(attention_kernel, key_heads),
         out_shape=[jax.ShapeDtypeStruct(*v) for v in shapes],
         compiler_params=pltpu.CompilerParams(vmem_limit_bytes=32 * 1024 * 1024),
-        cost_estimate=pl.CostEstimate(
-            flops=2 * rows * features * (width + query_width) + 4 * rows * rows * query_width,
-            bytes_accessed=2 * features * (width + query_width) + 8 * rows * width,
-            transcendentals=rows * rows * query_width // HEAD_SIZE,
-        ),
-    )(x, near, core, gains, cosine, sine, wo)
+        cost_estimate=SMALL,
+    )(x, near, core, near_kv, core_kv, gains, cosine, sine, wo)
 
 
 def attention_back_kernel(
     key_heads,
+    place_ref,
     upstream_ref,
     wo_ref,
     raw_ref,
@@ -543,16 +548,18 @@
     x_ref,
     near_ref,
     core_ref,
+    near_kv_ref,
+    core_kv_ref,
     beside_ref,
     feature_ref,
-    keep_ref,
-    send_ref,
+    weights_ref,
     mixed_grad_ref,
     raw_grad_ref,
 ):
     rows = upstream_ref.shape[0]
     split = near_ref.shape[0]
-    width = near_ref.shape[1]
+    width = raw_grad_ref.shape[1]
+    queries_width = near_ref.shape[1]
     query_heads = mixed_grad_ref.shape[1] // HEAD_SIZE
     group = query_heads // key_heads
     root = math.sqrt(HEAD_SIZE)
@@ -593,37 +600,266 @@
         key_terms += norm_back(query_heads + k, key_grad / root, gains_ref[1:2, :])
         raw_grad_ref[:, head_columns(query_heads + key_heads + k)] = value_grad.astype(BF16)
     raw_grad = raw_grad_ref[...]
-    feature_ref[:, :split] = against(raw_grad, near_ref[...]).astype(BF16)
-    feature_ref[:, split : 2 * split] = against(raw_grad, core_ref[...]).astype(BF16)
+    for part, (query_ref, kv_ref) in enumerate(
+        ((near_ref, near_kv_ref), (core_ref, core_kv_ref))
+    ):
+        feature_ref[:, part * split : (part + 1) * split] = (
+            against(raw_grad[:, :queries_width], query_ref[...])
+            + against(raw_grad[:, queries_width:], kv_ref[:, : width - queries_width])
+        ).astype(BF16)
     feature_ref[:, 2 * split : 2 * split + HEAD_SIZE] = query_terms.astype(BF16)
     feature_ref[:, 2 * split + HEAD_SIZE :] = key_terms.astype(BF16)
-    keep_ref[:, :width] = over_rows(x_ref[:, :split], raw_grad).astype(BF16)
-    send_ref[:, :width] = over_rows(x_ref[:, split:], raw_grad).astype(BF16)
-    keep_ref[:, width:] = beside_ref[:split]
-    send_ref[:, width:] = beside_ref[split:]
-
-
-def attention_back(upstream, wo, raw, low, lse, gains, cosine, sine, x, near, core, beside, key_heads):
+    count = place_ref.shape[0]
+    block = 2 * split // count
+    for j in range(count):
+        at = pl.ds(pl.multiple_of(place_ref[j] * block, block), block)
+        if block % LANES == 0:
+            columns = x_ref[:, j * block : (j + 1) * block]
+            weights_ref[at, :width] = over_rows(columns, raw_grad).astype(BF16)
+    if block % LANES:
+        weights_ref[:, :width] = over_rows(x_ref[...], raw_grad).astype(BF16)
+    weights_ref[:, width:] = beside_ref[...]
+
+
+def in_vmem(count):
+    return [pl.BlockSpec()] * count
+
+
+def in_smem():
+    return [pl.BlockSpec(memory_space=pltpu.SMEM)]
+
+
+def attention_back(
+    where, upstream, wo, raw, low, lse, gains, cosine, sine, x, weights, beside, key_heads
+):
     rows, features = upstream.shape
     query_width = wo.shape[0]
-    split, width = near.shape
+    split = weights[0].shape[0]
+    width = low.shape[1]
     whole = width + beside.shape[1]
     shapes = [
         ((rows, features + 2 * HEAD_SIZE), BF16),
-        ((split, whole), BF16),
-        ((split, whole), BF16),
+        ((features, whole), BF16),
     ]
+    operands = [upstream, wo, raw, low, lse, gains, cosine, sine, x, *weights, beside]
     return pl.pallas_call(
         functools.partial(attention_back_kernel, key_heads),
+        in_specs=in_smem() + in_vmem(len(operands)),
+        out_specs=in_vmem(2),
         out_shape=[jax.ShapeDtypeStruct(*v) for v in shapes],
         scratch_shapes=[pltpu.VMEM((rows, query_width), BF16), pltpu.VMEM((rows, width), BF16)],
         compiler_params=pltpu.CompilerParams(vmem_limit_bytes=40 * 1024 * 1024),
-        cost_estimate=pl.CostEstimate(
-            flops=2 * rows * features * (2 * width + query_width) + 10 * rows * rows * query_width,
-            bytes_accessed=2 * features * (3 * width + query_width) + 8 * rows * width,
-            transcendentals=rows * rows * query_width // HEAD_SIZE,
+        cost_estimate=SMALL,
+    )(jnp.stack(where).astype(jnp.int32), *in_hbm(*operands))
+
+
+def chunk_places():
+    return jnp.stack(
+        [lax.axis_index("tp") ^ m for m in range(lax.axis_size("tp"))]
+    ).astype(jnp.int32)
+
+
+def rows_at(index, size):
+    return pl.ds(pl.multiple_of(index * size, size), size)
+
+
+def resid_kernel(place_ref, *refs):
+    *pieces, hidden_ref, gain_ref, resid_ref, routed_ref = refs
+    rows = pieces[0].shape[0]
+    for m, piece in enumerate(pieces):
+        at = rows_at(place_ref[m], rows)
+        resid = hidden_ref[at, :].astype(F32) + piece[...].astype(F32)
+        resid_ref[at, :] = resid
+        routed_ref[at, :] = (resid * inverse_rms(resid) * gain_ref[...]).astype(BF16)
+
+
+def resid_and_routed(pieces, hidden, gain):
+    return pl.pallas_call(
+        resid_kernel,
+        in_specs=in_smem() + in_vmem(len(pieces) + 2),
+        out_specs=in_vmem(2),
+        out_shape=[
+            jax.ShapeDtypeStruct(hidden.shape, F32),
+            jax.ShapeDtypeStruct(hidden.shape, BF16),
+        ],
+        compiler_params=pltpu.CompilerParams(vmem_limit_bytes=16 * 1024 * 1024),
+        cost_estimate=SMALL,
+    )(chunk_places(), *pieces, hidden, gain)
+
+
+def resid_back_kernel(parts, place_ref, column_ref, *refs):
+    pieces = refs[: 2 * parts]
+    (
+        resid_a_ref,
+        resid_b_ref,
+        routed_a_ref,
+        routed_b_ref,
+        ids_ref,
+        router_ref,
+        gain_ref,
+        upstream_ref,
+        mixed_ref,
+        grad_ref,
+        low_ref,
+        beside_ref,
+        keep_ref,
+        send_ref,
+        returned_ref,
+        wide_ref,
+    ) = refs[2 * parts :]
+    rows, features = upstream_ref.shape
+    expert_count = router_ref.shape[1]
+    chunk = pieces[0].shape[0]
+    for h in range(2):
+        for m in range(parts):
+            returned_ref[rows_at(place_ref[m] + h * parts, chunk), :] = pieces[h * parts + m][...]
+    routed = jnp.concatenate([routed_a_ref[...], routed_b_ref[...]], axis=0)
+    resid = jnp.concatenate([resid_a_ref[...], resid_b_ref[...]], axis=0)
+    logits = jnp.dot(routed, router_ref[...], preferred_element_type=F32)
+    lane = lax.broadcasted_iota(jnp.int32, (rows, expert_count), 1)
+    named = ids_ref[:, 0:1] == lane
+    for k in range(1, TOP):
+        named = named | (ids_ref[:, k : k + 1] == lane)
+    exponent = jnp.exp(logits - jnp.max(logits, axis=1, keepdims=True))
+    router = exponent / jnp.sum(exponent, axis=1, keepdims=True)
+    chosen = jnp.where(named, router, 0.0)
+    total = jnp.sum(chosen, axis=1, keepdims=True)
+    gates = chosen / total
+    tail = returned_ref[:, features:].astype(F32)
+    tail = tail + pltpu.roll(tail, tail.shape[1] - expert_count, 1)
+    grad_gates = jnp.where(named, tail[:, :expert_count], 0.0)
+    inner = jnp.sum(grad_gates * gates, axis=1, keepdims=True)
+    grad_router = jnp.where(named, (grad_gates - inner) / total, 0.0)
+    inner = jnp.sum(router * grad_router, axis=1, keepdims=True)
+    grad_logits = (router * (grad_router - inner)).astype(BF16)
+    grad_routed = returned_ref[:, :features].astype(F32) + against(grad_logits, router_ref[...])
+    scale = inverse_rms(resid)
+    normal = resid * scale
+    weighted = grad_routed * gain_ref[...]
+    inner = jnp.mean(weighted * normal, axis=1, keepdims=True)
+    grad = upstream_ref[...].astype(F32) + scale * (weighted - normal * inner)
+    grad_ref[...] = grad
+    low_ref[...] = grad.astype(BF16)
+    half = column_ref.shape[0] // 2
+    for j in range(half):
+        for k, out_ref in ((j, keep_ref), (half + j, send_ref)):
+            columns = pl.ds(pl.multiple_of(column_ref[k] * LANES, LANES), LANES)
+            out_ref[j * LANES : (j + 1) * LANES, :] = over_rows(
+                mixed_ref[:, columns], low_ref[...]
+            ).astype(BF16)
+    wide_ref[...] = jnp.zeros(wide_ref.shape, BF16)
+    wide_ref[:, :expert_count] = grad_logits
+    one = lax.broadcasted_iota(jnp.int32, wide_ref.shape, 1) == expert_count
+    beside_ref[...] = (
+        over_rows(routed, wide_ref[...])
+        + over_rows((grad_routed * normal).astype(BF16), one.astype(F32).astype(BF16))
+    ).astype(BF16)
+
+
+def resid_back(pieces, resid, routed, ids, router, gain, upstream, mixed, columns):
+    parts = len(pieces) // 2
+    rows, features = upstream.shape
+    expert_count = router.shape[1]
+    wide = -(-(expert_count + 1) // LANES) * LANES
+    half = mixed.shape[1] // 2
+    shapes = [
+        ((rows, features), F32),
+        ((rows, features), BF16),
+        ((features, wide), BF16),
+        ((half, features), BF16),
+        ((half, features), BF16),
+    ]
+    operands = [*pieces, *in_hbm(*resid, *routed, ids, router, gain, upstream, mixed)]
+    return pl.pallas_call(
+        functools.partial(resid_back_kernel, parts),
+        in_specs=in_smem() * 2 + in_vmem(len(operands)),
+        out_specs=in_vmem(len(shapes)),
+        out_shape=[jax.ShapeDtypeStruct(*v) for v in shapes],
+        scratch_shapes=[
+            pltpu.VMEM((rows, pieces[0].shape[1]), BF16),
+            pltpu.VMEM((rows, wide), BF16),
+        ],
+        compiler_params=pltpu.CompilerParams(vmem_limit_bytes=40 * 1024 * 1024),
+        cost_estimate=SMALL,
+    )(chunk_places(), jnp.stack(columns).astype(jnp.int32), *operands)
+
+
+def input_kernel(ordered, place_ref, block_ref, *refs):
+    *pieces, hidden_ref, resid_grad_ref, gain_ref, result_ref, late_ref, total_ref = refs
+    features = hidden_ref.shape[1]
+    rows = pieces[0].shape[0]
+    count = block_ref.shape[0]
+    block = features // count
+    for m, piece in enumerate(pieces):
+        total_ref[rows_at(place_ref[m], rows), :] = piece[...]
+    hidden = hidden_ref[...].astype(F32)
+    scale = inverse_rms(hidden)
+    columns = [
+        slice(j * block, (j + 1) * block)
+        if ordered
+        else pl.ds(pl.multiple_of(block_ref[j] * block, block), block)
+        for j in range(count)
+    ]
+    inner = jnp.zeros((hidden.shape[0], 1), F32)
+    for j in range(count):
+        normal = hidden_ref[:, columns[j]].astype(F32) * scale
+        grad = total_ref[:, j * block : (j + 1) * block].astype(F32)
+        terms = grad * normal
+        inner += jnp.sum(terms * gain_ref[:, columns[j]], axis=1, keepdims=True)
+        late_ref[j : j + 1, :block] = jnp.sum(terms, axis=0, keepdims=True)
+    inner = inner * (1.0 / features)
+    for j in range(count):
+        normal = hidden_ref[:, columns[j]].astype(F32) * scale
+        weighted = total_ref[:, j * block : (j + 1) * block].astype(F32) * gain_ref[:, columns[j]]
+        result_ref[:, columns[j]] = resid_grad_ref[:, columns[j]] + scale * (
+            weighted - normal * inner
+        )
+    heads = jnp.sum(total_ref[:, features:].astype(F32), axis=0, keepdims=True)
+    late_ref[:, block:] = jnp.broadcast_to(heads, (count, heads.shape[1]))
+
+
+def input_gradient(pieces, hidden, resid_grad, gain, where):
+    rows, features = hidden.shape
+    count = len(where)
+    extra = pieces[0].shape[1] - features
+    return pl.pallas_call(
+        functools.partial(input_kernel, absolute()),
+        in_specs=in_smem() * 2 + in_vmem(len(pieces) + 3),
+        out_specs=in_vmem(2),
+        out_shape=[
+            jax.ShapeDtypeStruct((rows, features), F32),
+            jax.ShapeDtypeStruct((count, features // count + extra), F32),
+        ],
+        scratch_shapes=[pltpu.VMEM((rows, pieces[0].shape[1]), BF16)],
+        compiler_params=pltpu.CompilerParams(vmem_limit_bytes=24 * 1024 * 1024),
+        cost_estimate=SMALL,
+    )(chunk_places(), jnp.stack(where).astype(jnp.int32), *pieces, *in_hbm(hidden, resid_grad, gain))
+
+
+def widen_kernel(place_ref, near_ref, core_ref, result_ref):
+    early = pl.program_id(0) < pl.num_programs(0) // 2
+    result_ref[...] = jnp.where(early, near_ref[...], core_ref[...]).astype(F32)
+
+
+def widen_blocks(near, core, where):
+    count = len(where)
+    features = near.shape[1]
+    block = 2 * near.shape[0] // count
+    half = count // 2
+    first = pl.BlockSpec((block, features), lambda i, s: (jnp.minimum(i, half - 1), 0))
+    second = pl.BlockSpec((block, features), lambda i, s: (jnp.maximum(i - half, 0), 0))
+    return pl.pallas_call(
+        widen_kernel,
+        grid_spec=pltpu.PrefetchScalarGridSpec(
+            num_scalar_prefetch=1,
+            grid=(count,),
+            in_specs=[first, second],
+            out_specs=pl.BlockSpec((block, features), lambda i, s: (s[i], 0)),
         ),
-    )(upstream, wo, raw, low, lse, gains, cosine, sine, x, near, core, beside)
+        out_shape=jax.ShapeDtypeStruct((block * count, features), F32),
+        compiler_params=pltpu.CompilerParams(vmem_limit_bytes=24 * 1024 * 1024),
+        cost_estimate=SMALL,
+    )(jnp.stack(where).astype(jnp.int32), near, core)
 
 
 def shards(
@@ -647,74 +883,88 @@
     local_experts = gate_up_weight.shape[0]
     expert_count = local_experts * owners
     rows_a = tokens // 2
-    halves = lambda v: (v[:rows_a], v[rows_a:])
 
     head_share = query_gain.shape[0]
-    small_rows = max(tokens, router_weight.shape[0])
+    share = router_weight.shape[0]
+    small_rows = max(tokens, share)
     padded = lambda v: jnp.pad(v.astype(BF16), ((0, small_rows - v.shape[0]), (0, 0)))
-    by_feature = jnp.concatenate(
-        [router_weight, attention_gain[:, None], expert_gain[:, None]], axis=1
-    )
     small = jnp.concatenate(
         [
-            padded(by_feature),
+            padded(router_weight),
+            padded(jnp.stack([attention_gain, expert_gain], axis=1)),
             padded(jnp.stack([query_gain, key_gain], axis=1)),
             padded(expert_ids),
         ],
         axis=1,
     )
-    small_hops = gather_hops(small)
-    weights = jnp.concatenate([query_weight, key_matrix, value_matrix], axis=1)
-    hops = gather_hops(weights)
-    near = gather_near(small, small_hops)
-    small = put_blocks(jnp.concatenate([near, gather_core(near, small_hops)], axis=0), 0)
-    small = small.reshape(owners, small_rows, -1)
-    packed = small[:, : router_weight.shape[0], : expert_count + 2].reshape(features, -1)
-    router_full = packed[:, :expert_count]
-    attn_gain_full = packed[:, expert_count].astype(F32)
-    mlp_gain_full = packed[:, expert_count + 1].astype(F32)
-    head_gains = (
+    small_width = small.shape[1]
+    small = jnp.pad(small, ((0, 0), (0, -small_width % LANES)))
+    packed = jnp.concatenate([key_matrix, value_matrix], axis=1)
+    packed_width = packed.shape[1]
+    together = small_rows == share
+    if together:
+        packed = jnp.concatenate([packed, small], axis=1)
+    packed_hops = gather_hops(packed)
+    hops = gather_hops(query_weight)
+    packed_near = gather_near(packed, packed_hops)
+    packed_core = gather_core(packed_near, packed_hops)
+    if together:
+        small = jnp.concatenate(
+            [packed_near[:, packed_width:], packed_core[:, packed_width:]], axis=0
+        )
+    else:
+        small = lax.all_gather(small, "ep", axis=0, tiled=True)
+    small = put_blocks(small, 0).reshape(owners, small_rows, -1)
+    by_feature = small[:, :share, : expert_count + 2].reshape(features, -1)
+    router_full = by_feature[:, :expert_count]
+    attn_gain_full = by_feature[:, expert_count].astype(F32)[None, :]
+    mlp_gain_full = by_feature[:, expert_count + 1].astype(F32)[None, :]
+    gains = (
         small[:, :head_share, expert_count + 2 : expert_count + 4]
         .reshape(HEAD_SIZE, 2)
         .astype(F32)
-    )
-    gains = head_gains.T
-    ids_all = small[:, :tokens, expert_count + 4 :].reshape(-1, TOP).astype(jnp.int32)
+        .T
+    )
+    ids_all = small[:, :tokens, expert_count + 4 : small_width].reshape(-1, TOP).astype(jnp.int32)
     wd = down_weight.reshape(-1, features)
-    hidden_f = hidden_in.astype(F32)
-    normed_low = norm_rows(hidden_f, attn_gain_full).astype(BF16)
+    normed_low = norm_rows(hidden_in.astype(F32), attn_gain_full).astype(BF16)
     normed_rel = pick_blocks(normed_low, 1)
     positions = jnp.arange(tokens, dtype=jnp.int32)
     cosine, sine_table = rope_tables(positions, HEAD_SIZE)
     (
         hops,
+        packed_core,
         normed_rel,
         cosine,
         sine_table,
         gains,
-        packed,
+        router_full,
+        attn_gain_full,
+        mlp_gain_full,
         ids_all,
         output_all,
         gate_up_low,
     ) = join(
         hops,
+        packed_core,
         normed_rel,
         cosine,
         sine_table,
         gains,
-        packed,
+        router_full,
+        attn_gain_full,
+        mlp_gain_full,
         ids_all,
         output_grad,
         gate_up_weight,
     )
 
-    near = gather_near(weights, hops)
-    weights_rel = [near, gather_core(near, hops)]
+    near = gather_near(query_weight, hops)
+    weights_rel = [near, gather_core(near, hops), packed_near, packed_core]
     output_all = lax.all_gather(output_all, "ep", axis=0, tiled=True)
     query_width = query_weight.shape[1]
     key_width = key_matrix.shape[1]
     key_heads = key_width // HEAD_SIZE
-    split = features // 2
     raw, low, attention_output, lse, *head_parts = attention(
         normed_rel, *weights_rel, gains, cosine, sine_table, output_weight, key_heads
     )
@@ -727,19 +977,14 @@
     chunk = reduce_total(head_parts[0], hops)
     hops, hops_b = join(spread_hops(chunk), reduce_hops(head_parts[1]))
 
-    attended = [spread_total(chunk, hops)]
+    resid_a, routed_a = resid_and_routed([chunk] + hops, hidden_in[:rows_a], mlp_gain_full)
     chunk = reduce_total(head_parts[1], hops_b)
-    hops = spread_hops(chunk)
-    resid_halves = [hidden_f[:rows_a] + attended[0].astype(F32)]
-    routed_halves = [norm_rows(resid_halves[0], mlp_gain_full).astype(BF16)]
-    hops_a, hops = join(gather_hops(routed_halves[0]), hops)
-
-    attended.append(spread_total(chunk, hops))
-    resid_halves.append(hidden_f[rows_a:] + attended[1].astype(F32))
-    routed_halves.append(norm_rows(resid_halves[1], mlp_gain_full).astype(BF16))
-    near_a = gather_near(routed_halves[0], hops_a)
+    hops_a, hops = join(gather_hops(routed_a), spread_hops(chunk))
+
+    resid_b, routed_b = resid_and_routed([chunk] + hops, hidden_in[rows_a:], mlp_gain_full)
+    near_a = gather_near(routed_a, hops_a)
     core_a = gather_core(near_a, hops_a)
-    hops_b = gather_hops(routed_halves[1])
+    hops_b = gather_hops(routed_b)
     lined = places()
     where = [2 * b + h for h in range(2) for b in lined]
 
@@ -753,7 +998,7 @@
     send_a, joined_1, hidden_1 = experts(1, core_a)
     hops_b, send_a, keep_a = join(hops_b, send_a, keep_a)
 
-    near_b = gather_near(routed_halves[1], hops_b)
+    near_b = gather_near(routed_b, hops_b)
     core_b = gather_core(near_b, hops_b)
     come = scatter_swap(send_a)
     keep_b, joined_2, hidden_2 = experts(2, near_b)
@@ -766,17 +1011,6 @@
     joined = [joined_0, joined_1, joined_2, joined_3]
     hidden = [hidden_0, hidden_1, hidden_2, hidden_3]
     routed_pieces = [near_a, core_a, near_b, core_b]
-    resid = jnp.concatenate(resid_halves, axis=0)
-    routed_low = jnp.concatenate(routed_halves, axis=0)
-    logits = jnp.dot(routed_low, router_full, preferred_element_type=F32)
-    logit_max = jnp.max(logits, axis=-1, keepdims=True)
-    exponent = jnp.exp(logits - logit_max)
-    router = exponent / jnp.sum(exponent, axis=-1, keepdims=True)
-    every_expert = jnp.arange(expert_count, dtype=jnp.int32)
-    named = jnp.any(expert_ids[:, :, None] == every_expert[None, None, :], axis=1)
-    chosen = jnp.where(named, router, 0.0)
-    chosen_total = jnp.sum(chosen, axis=1, keepdims=True)
-    gates = chosen / chosen_total
 
     come = scatter_swap(send_b)
     total_a = scatter_total(sums_a, hops_a)
@@ -784,58 +1018,37 @@
     mixture_parts = mixture_product(hidden, wd, lined)
     come, hops, mixture_parts = join(come, hops, mixture_parts)
 
+    mixture = lax.psum_scatter(mixture_parts, "ep", scatter_dimension=0, tiled=True)
     sums_b = scatter_sums(keep_b, come)
     hops_b = scatter_hops(sums_b)
-    chunk = reduce_total(total_a, hops)
-    hops_a = spread_hops(chunk)
-    hops_b, hops_a, mixture_parts = join(hops_b, hops_a, mixture_parts)
-
-    mixture = lax.psum_scatter(mixture_parts, "ep", scatter_dimension=0, tiled=True)
-    returned = [spread_total(chunk, hops_a)]
+    chunk_a = reduce_total(total_a, hops)
+    gate_up_grad = gate_up_product(routed_pieces, joined, gate_up_weight.shape)
+    spread_a, hops_b, gate_up_grad, hidden = join(
+        spread_hops(chunk_a), hops_b, gate_up_grad, hidden
+    )
+
     total_b = scatter_total(sums_b, hops_b)
-    hops = reduce_hops(total_b)
-    (hops,) = join(hops)
-    chunk = reduce_total(total_b, hops)
-    (hops,) = join(spread_hops(chunk))
-
-    returned.append(spread_total(chunk, hops))
-    returned = jnp.concatenate(returned, axis=0)
-    grad_out = output_grad.astype(F32)
-    tail = returned[:, features:].astype(F32)
-    grad_gates = tail[:, :expert_count] + tail[:, expert_count : 2 * expert_count]
-    grad_gates = jnp.where(named, grad_gates, 0.0)
-    grad_router = jnp.where(
-        named,
-        (grad_gates - jnp.sum(grad_gates * gates, axis=1, keepdims=True)) / chosen_total,
-        0.0,
-    )
-    grad_logits = (
-        router * (grad_router - jnp.sum(router * grad_router, axis=1, keepdims=True))
-    ).astype(BF16)
-    router_grad = jnp.dot(routed_low.T, grad_logits, preferred_element_type=F32)
-    grad_routed = returned[:, :features].astype(F32) + jnp.dot(
-        grad_logits, router_full.T, preferred_element_type=F32
-    )
-    grad_resid_norm, mlp_terms = norm_back(resid, mlp_gain_full, grad_routed)
-    mlp_gain_grad = jnp.sum(mlp_terms, axis=0)
-    grad_resid = grad_out + grad_resid_norm
-    grad_attended = grad_resid.astype(BF16)
-    mixed_rel = pick_blocks(attention_output, 1)
-    output_local = lax.dot_general(
-        mixed_rel, grad_attended, (((0,), (0,)), ((), ())), preferred_element_type=F32
-    ).astype(BF16)
-    output_half = output_local.shape[0] // 2
-    output_local, grad_attended = join(output_local, grad_attended)
-
-    come = scatter_swap(output_local[output_half:])
-    by_feature = jnp.concatenate([router_grad, mlp_gain_grad[:, None]], axis=1).astype(BF16)
-    by_feature = jnp.pad(by_feature, ((0, 0), (0, -by_feature.shape[1] % LANES)))
-    by_feature = pick_blocks(by_feature, 0)
-    by_feature, come = join(by_feature, come)
-
-    output_sums = scatter_sums(output_local[:output_half], come)
-    output_hops = scatter_hops(output_sums)
-    feature_part, weights_keep, weights_send = attention_back(
+    (hops,) = join(reduce_hops(total_b))
+    chunk_b = reduce_total(total_b, hops)
+    (spread_b,) = join(spread_hops(chunk_b))
+
+    columns = (
+        [jnp.int32(b) for b in range(attention_output.shape[1] // LANES)] if absolute() else lined
+    )
+    grad_resid, grad_attended, by_feature, output_keep, output_send = resid_back(
+        [chunk_a, *spread_a, chunk_b, *spread_b],
+        [resid_a, resid_b],
+        [routed_a, routed_b],
+        expert_ids,
+        router_full,
+        mlp_gain_full,
+        output_grad,
+        attention_output,
+        columns,
+    )
+
+    feature_part, weights_grad = attention_back(
+        lined,
         grad_attended,
         output_weight,
         raw,
@@ -845,66 +1058,58 @@
         cosine,
         sine_table,
         normed_rel,
-        *weights_rel,
+        weights_rel,
         by_feature,
         key_heads,
     )
-    feature_part, weights_keep, weights_send, output_hops, last_joined, last_hidden, mixture = (
-        join(feature_part, weights_keep, weights_send, output_hops, joined, hidden, mixture)
-    )
-    mixture = lax.psum(mixture, "tp")
-
-    come = scatter_swap(weights_send)
+    come, feature_part, weights_grad = join(
+        scatter_swap(output_send), feature_part, weights_grad
+    )
+
+    weights_rows = lax.psum_scatter(weights_grad, "ep", scatter_dimension=0, tiled=True)
     hops = reduce_hops(feature_part)
+    output_sums = scatter_sums(output_keep, come)
+    output_hops = scatter_hops(output_sums)
+    down_grad = down_product(hidden, output_all, where).reshape(down_weight.shape)
+    hops, output_hops, down_grad, mixture = join(hops, output_hops, down_grad, mixture)
+
+    chunk = reduce_total(feature_part, hops)
     output_share = scatter_total(output_sums, output_hops)
-    output_hops = gather_hops(output_share)
-    down_grad = down_product(last_hidden, output_all, where).reshape(down_weight.shape)
-    come, hops, down_grad, last_joined = join(come, hops, down_grad, last_joined)
-
-    weights_sums = scatter_sums(weights_keep, come)
-    weights_hops = scatter_hops(weights_sums)
-    chunk = reduce_total(feature_part, hops)
-    hops = spread_hops(chunk)
-    gate_up_grad = gate_up_product(routed_pieces, last_joined, gate_up_weight.shape)
-    hops, output_hops, gate_up_grad = join(hops, output_hops, gate_up_grad)
-
+    hops, output_hops, mixture = join(
+        spread_hops(chunk), gather_hops(output_share), mixture
+    )
+
+    mixture_hops = reduce_hops(mixture)
     near = gather_near(output_share, output_hops)
     output_core = gather_core(near, output_hops)
-    total = spread_total(chunk, hops)
-    grad_normed = put_blocks(total[:, :features], 1).astype(F32)
-    head_grads = jnp.sum(total[:, features:].astype(F32), axis=0)
-    grad_input_norm, attn_terms = norm_back(hidden_f, attn_gain_full, grad_normed)
-    input_grad = grad_resid + grad_input_norm
-    late = jnp.concatenate(
-        [
-            jnp.sum(attn_terms, axis=0).reshape(owners, -1),
-            head_grads[:HEAD_SIZE].reshape(owners, -1),
-            head_grads[HEAD_SIZE:].reshape(owners, -1),
-        ],
-        axis=1,
-    )
-    late = pick_blocks(late, 0)
-    late_come, output_core, input_grad = join(
-        scatter_swap(late[owners // 2 :]), output_core, input_grad
-    )
+    input_grad, late = input_gradient(
+        [chunk, *hops], hidden_in, grad_resid, attn_gain_full, lined
+    )
+    late_come = scatter_swap(late[owners // 2 :])
+    output_core, late_come, mixture_hops = join(output_core, late_come, mixture_hops)
+
+    mixture_chunk = reduce_total(mixture, mixture_hops)
+    mixture_hops = spread_hops(mixture_chunk)
     late_sums = scatter_sums(late[: owners // 2], late_come)
     late_hops = scatter_hops(late_sums)
-    output_weight_grad = put_blocks(
-        jnp.concatenate([near, output_core], axis=0), 0
-    ).astype(F32)
-    late_hops, weights_hops, output_weight_grad = join(
-        late_hops, weights_hops, output_weight_grad
-    )
-    late, mixture = join(scatter_total(late_sums, late_hops)[0], mixture)
-    weights_rows = scatter_total(weights_sums, weights_hops).astype(F32)
-    block_out = (resid + mixture.astype(F32)).astype(BF16)
+    output_weight_grad = widen_blocks(near, output_core, lined)
+    late_hops, output_weight_grad, weights_rows, mixture_hops = join(
+        late_hops, output_weight_grad, weights_rows, mixture_hops
+    )
+    weights_rows = weights_rows.astype(F32)
+    late = scatter_total(late_sums, late_hops)[0]
+    head_grads = lax.dynamic_slice_in_dim(
+        late[share:].reshape(2, HEAD_SIZE), lax.axis_index("ep") * head_share, head_share, 1
+    )
     early = weights_rows[:, query_width + 2 * key_width :]
+    mixture = spread_total(mixture_chunk, mixture_hops)
+    block_out = (jnp.concatenate([resid_a, resid_b], axis=0) + mixture.astype(F32)).astype(BF16)
     return (
         block_out,
         input_grad,
-        late[: features // owners],
-        late[features // owners : features // owners + head_share],
-        late[features // owners + head_share :],
+        late[:share],
+        head_grads[0],
+        head_grads[1],
         weights_rows[:, :query_width],
         weights_rows[:, query_width : query_width + key_width],
         weights_rows[:, query_width + key_width : query_width + 2 * key_width],

time: 523 us -> 493 us (0.943)
  other arithmetic: 55.3 us -> 25.6 us
  Pallas kernels: 116 us -> 145 us
  local copies, waits for them, and re-layouts: 84.5 us -> 59.8 us
  matrix products: 8 us -> 0 us
  starting transfers between devices: 79.7 us -> 86.9 us
    pallas_call x1 -> x11, Pallas kernels: 13.3 us -> 40.1 us  [the longest x1 13.1 us: attention_back(): pl.pallas_call(functools.partial(attention_back_kernel, key_heads), in_sp...]
    unnamed x225 -> x136, local copies, waits for them, and re-layouts: 51.5 us -> 40.1 us
    convert_element_type x11 -> x5, other arithmetic: 13.1 us -> 3.64 us  [the longest x1 1.3 us: shards(): (jnp.concatenate([resid_a, resid_b], axis=0) + mixture.astype(F32)).astyp...]
    concatenate x8 -> x2, other arithmetic: 10.1 us -> 1.15 us  [the longest x1 0.9 us: shards(): packed = jnp.concatenate([packed, small], axis=1)]
    dot_general x4 -> x0, matrix products: 8 us -> none  [the longest x1 2.33 us: shards(): lax.dot_general(mixed_rel, grad_attended, (((0,), (0,)), ((), ())), prefe...]
    ppermute x70 -> x72, starting transfers between devices: 79.2 us -> 86.6 us  [swap(): return lax.ppermute(value, axis, [(i, i ^ mask) for i in range(count)])]
    ppermute x70 -> x72, waiting for transfers between devices: 159 us -> 154 us  [swap(): return lax.ppermute(value, axis, [(i, i ^ mask) for i in range(count)])]
    convert_element_type x6 -> x11, other arithmetic: 14.6 us -> 15.7 us  [plus(): return total.astype(values[0].dtype)]
  transfers between devices with their start and end apart: 73 -> 75, of which waited for: 28 -> 38; matrix products, arithmetic and copies ran while one was open for 20% -> 6% of each run, Pallas kernels for 22% -> 30%
where the time goes in v4:
time: 493 us; the launch traced here: 487 us
  waiting for transfers between devices  155 us (31%)
  Pallas kernels  145 us (29%)
  starting transfers between devices  86.9 us (18%)
  local copies, waits for them, and re-layouts  59.8 us (12%)
  other arithmetic  25.6 us (5%)
  between operations  15.6 us (3%)
    ppermute x72, waiting for transfers between devices, swap(): return lax.ppermute(value, axis, [(i, i ^ mask) for i in range(count)])  154 us
    ppermute x72, starting transfers between devices, swap(): return lax.ppermute(value, axis, [(i, i ^ mask) for i in range(count)])  86.6 us
    pallas_call x4, Pallas kernels, run_experts(): pl.pallas_call(functools.partial(expert_kernel, local), grid_spec=pltpu.P...  53.4 us
    unnamed x136, local copies, waits for them, and re-layouts  40.1 us
    pallas_call x1, Pallas kernels, gate_up_product(): pl.pallas_call(gate_up_kernel, grid=(features // tile,), in_specs=[pl.Blo...  19.8 us
    convert_element_type x11, other arithmetic, plus(): return total.astype(values[0].dtype)  15.7 us
    pallas_call x1, Pallas kernels, down_product(): pl.pallas_call(down_kernel, grid_spec=pltpu.PrefetchScalarGridSpec(num_sc...  13.4 us
    pallas_call x1, Pallas kernels, attention_back(): pl.pallas_call(functools.partial(attention_back_kernel, key_heads), in_sp...  13.1 us
  transfers between devices with their start and end apart: 75, of which 38 were waited for; matrix products, arithmetic and copies ran while one was open for 6% of the time, Pallas kernels for 30%

profile of v4, /device:TPU:8, one launch (start us, length us, event | category | flops | bytes accessed | tf_op | source)
XLA Modules:
  0.0 487.2 jit_solution(7238987843011722498)
XLA Ops:
  35.2 11.4 %collective-permute-done.1.refs_2_ = bf16[256,1024]{1,0:T(8,128)(2,1)} collective-permute-done((bf16[256,1024]{1,0:T(8,128)(2,1)}, bf16[256,1024]{1,0:T(8,128)(2,1)}, u32[]{:S(2)}, u32[]{:S(2)}) %collective-permute-start.1) | collective-permute-done | bytes 524320 | tf_op jit(solution)/shard_map/ppermute | solution.py:47
  50.5 7.3 %copy.56 = bf16[4,256,8,384]{3,2,0,1:T(8,128)(2,1)} copy(bf16[4,256,8,384]{3,2,1,0:T(8,128)(2,1)} %bitcast.79) | data formatting | bytes 12582912 | tf_op jit(solution)/shard_map/reshape | solution.py:974
  58.4 7.1 %shard_map.239 = (f32[256,1152]{1,0:T(8,128)S(1)}, bf16[256,1280]{1,0:T(8,128)(2,1)S(1)}, bf16[256,1024]{1,0:T(8,128)(2,1)S(1)}, f32[256,8]{1,0:T(8,128)S(1)}, b...) custom-call(bf16[256,2048]{1,0:T(8,128)(2,1)S(1)} %copy-done.17, bf16[1024,1024]{1,0:T(8,128)(2,1)S(1)} %shard_map.238.near_ref, ...), custom_call_target="tpu_custom_call" | custom-call | bytes 1024 | tf_op jit(solution)/shard_map/pallas_call | solution.py:529
  79.2 6.8 %collective-permute-start.11 = (bf16[32,2048]{1,0:T(8,128)(2,1)S(1)}, bf16[32,2048]{1,0:T(8,128)(2,1)S(1)}, u32[]{:S(2)}, u32[]{:S(2)}) collective-permute-start(bf16[32,2048]{1,0:T(8,128)(2,1)S(1)} %add_convert_fusion.20.refs_0_), channel_id=1, source_target_pairs={{0,1},{1,0},{2,3},{3,2},{4,5},{5,4},{6,7},{7,6},{8,9},{9,8},{10,11... | collective-permute-start | bytes 393224 | tf_op jit(solution)/shard_map/ppermute | solution.py:47
  87.7 9.3 %collective-permute-done.16 = bf16[32,2048]{1,0:T(8,128)(2,1)S(1)} collective-permute-done((bf16[32,2048]{1,0:T(8,128)(2,1)S(1)}, bf16[32,2048]{1,0:T(8,128)(2,1)S(1)}, u32[]{:S(2)}, u32[]{:S(2)}) %collective-permute-start.16) | collective-permute-done | bytes 131104 | tf_op jit(solution)/shard_map/ppermute | solution.py:47
  116.7 3.7 collective-permute-done.22.refs_3_
  120.4 6.2 %collective-permute-done.18.refs_2_ = bf16[128,2048]{1,0:T(8,128)(2,1)S(1)} collective-permute-done((bf16[128,2048]{1,0:T(8,128)(2,1)S(1)}, bf16[128,2048]{1,0:T(8,128)(2,1)S(1)}, u32[]{:S(2)}, u32[]{:S(2)}) %collective-permute-start.18) | collective-permute-done | bytes 524320 | tf_op jit(solution)/shard_map/ppermute | solution.py:47
  141.8 13.8 %shard_map.244 = (bf16[512,2176]{1,0:T(8,128)(2,1)S(1)}, bf16[512,1536]{1,0:T(8,128)(2,1)S(1)}, bf16[512,768]{1,0:T(8,128)(2,1)S(1)}) custom-call(s32[5]{0:T(128)S(1)} %stack.111.place_ref, bf16[512,2048]{1,0:T(8,128)(2,1)} %shard_map.242.x_ref.refs_0_, bf16[2048,2048]{1,0:T(8,128)(2,1)} %all-gather.2.cloned.1.call-done.g0_ref.g1_ref.refs_4_, ...), custom_call_target="tpu_custom_call" | custom-call | bytes 1024 | tf_op jit(solution)/shard_map/pallas_call | solution.py:311
  159.1 13.6 %shard_map.243 = (bf16[512,2176]{1,0:T(8,128)(2,1)}, bf16[512,1536]{1,0:T(8,128)(2,1)S(1)}, bf16[512,768]{1,0:T(8,128)(2,1)S(1)}) custom-call(s32[5]{0:T(128)S(1)} %stack.106.place_ref, bf16[512,2048]{1,0:T(8,128)(2,1)} %collective-permute-done.26.x_ref.refs_1_, bf16[2048,2048]{1,0:T(8,128)(2,1)} %all-gather.2.cloned.1.call-done.g0_ref.g1_ref.refs_4_, ...), custom_call_target="tpu_custom_call" | custom-call | bytes 1024 | tf_op jit(solution)/shard_map/pallas_call | solution.py:311
  172.8 3.9 shard_map.245.x_ref.refs_2_
  181.5 12.7 %shard_map.246 = (bf16[512,2176]{1,0:T(8,128)(2,1)S(1)}, bf16[512,1536]{1,0:T(8,128)(2,1)S(1)}, bf16[512,768]{1,0:T(8,128)(2,1)S(1)}) custom-call(s32[5]{0:T(128)S(1)} %stack.228.place_ref, bf16[512,2048]{1,0:T(8,128)(2,1)} %shard_map.245.x_ref.refs_2_, bf16[2048,2048]{1,0:T(8,128)(2,1)} %all-gather.2.cloned.1.call-done.g0_ref.g1_ref.refs_4_, ...), custom_call_target="tpu_custom_call" | custom-call | bytes 1024 | tf_op jit(solution)/shard_map/pallas_call | solution.py:311
  194.3 4.0 add_convert_fusion.6
  206.6 13.3 %shard_map.247 = (bf16[512,2176]{1,0:T(8,128)(2,1)}, bf16[512,1536]{1,0:T(8,128)(2,1)S(1)}, bf16[512,768]{1,0:T(8,128)(2,1)S(1)}) custom-call(s32[5]{0:T(128)S(1)} %stack.233.place_ref, bf16[512,2048]{1,0:T(8,128)(2,1)} %collective-permute-done.28.x_ref.refs_3_, bf16[2048,2048]{1,0:T(8,128)(2,1)} %all-gather.2.cloned.1.call-done.g0_ref.g1_ref.refs_4_, ...), custom_call_target="tpu_custom_call" | custom-call | bytes 1024 | tf_op jit(solution)/shard_map/pallas_call | solution.py:311
  219.9 6.2 %collective-permute-done.30 = bf16[128,2176]{1,0:T(8,128)(2,1)} collective-permute-done((bf16[128,2176]{1,0:T(8,128)(2,1)}, bf16[128,2176]{1,0:T(8,128)(2,1)}, u32[]{:S(2)}, u32[]{:S(2)}) %collective-permute-start.30) | collective-permute-done | bytes 557088 | tf_op jit(solution)/shard_map/ppermute | solution.py:47
  232.6 10.9 %shard_map.248 = bf16[2048,2048]{1,0:T(8,128)(2,1)S(1)} custom-call(s32[8]{0:T(128)S(1)} %stack.100.place_ref.column_ref.block_ref, bf16[512,768]{1,0:T(8,128)(2,1)} %copy-done.24, bf16[512,768]{1,0:T(8,128)(2,1)} %copy-done.25, bf16[512,768]{1,0:T(8,128)(2,1)} %copy-done.26, bf16[512,768]{1,0:T(8,128)(2,1)} %copy-done.27, bf16[768,2048]{1,0:T(8,128)(2,1)} %bitcast.60), custom_call_target="tpu_custom_call" | custom-call | bytes 1024 | tf_op jit(solution)/shard_map/pallas_call | solution.py:417
  262.0 19.8 %shard_map.249 = f32[4,2048,384]{2,1,0:T(8,128)} custom-call(bf16[512,2048]{1,0:T(8,128)(2,1)} %shard_map.242.x_ref.refs_0_, bf16[512,2048]{1,0:T(8,128)(2,1)} %collective-permute-done.26.x_ref.refs_1_, bf16[512,2048]{1,0:T(8,128)(2,1)} %shard_map.245.x_ref.refs_2_, bf16[512,2048]{1,0:T(8,128)(2,1)} %collective-permute-done.28.x_ref.refs_3_, ...), custom_call_target="tpu_custom_call" | custom-call | bytes 1024 | tf_op jit(solution)/shard_map/pallas_call | solution.py:352
  290.0 5.3 %collective-permute-done.43 = bf16[32,2176]{1,0:T(8,128)(2,1)S(1)} collective-permute-done((bf16[32,2176]{1,0:T(8,128)(2,1)S(1)}, bf16[32,2176]{1,0:T(8,128)(2,1)S(1)}, u32[]{:S(2)}, u32[]{:S(2)}) %collective-permute-start.43) | collective-permute-done | bytes 139296 | tf_op jit(solution)/shard_map/ppermute | solution.py:47
  304.5 5.0 %collective-permute-done.46.refs_6_ = bf16[32,2176]{1,0:T(8,128)(2,1)S(1)} collective-permute-done((bf16[32,2176]{1,0:T(8,128)(2,1)S(1)}, bf16[32,2176]{1,0:T(8,128)(2,1)S(1)}, u32[]{:S(2)}, u32[]{:S(2)}) %collective-permute-start.46) | collective-permute-done | bytes 139296 | tf_op jit(solution)/shard_map/ppermute | solution.py:47
  312.3 7.5 %shard_map.250 = (f32[256,2048]{1,0:T(8,128)S(1)}, bf16[256,2048]{1,0:T(8,128)(2,1)S(1)}, bf16[2048,128]{1,0:T(8,128)(2,1)S(1)}, bf16[512,2048]{1,0:T(8,128)(2,1)S(1)}, bf16[512,2048]{1,0:T(8,128)(2,1)S(1)}) custom-call(s32[4]{0:T(128)S(1)} %pad_add_fusion.place_ref, s32[8]{0:T(128)S(1)} %stack.100.place_ref.column_ref.block_ref, ...), custom_call_target="tpu_custom_call" | custom-call | bytes 1024 | tf_op jit(solution)/shard_map/pallas_call | solution.py:773
  322.9 13.1 %shard_map.251 = (bf16[256,2304]{1,0:T(8,128)(2,1)S(1)}, bf16[2048,1408]{1,0:T(8,128)(2,1)S(1)}) custom-call(s32[8]{0:T(128)S(1)} %stack.100.place_ref.column_ref.block_ref, bf16[256,2048]{1,0:T(8,128)(2,1)} %copy-done.43, bf16[1024,2048]{1,0:T(8,128)(2,1)} %wo_ref.3, f32[256,1152]{1,0:T(8,128)} %copy-done.42, bf16[256,1280]{1,0:T(8,128)(2,1)} %copy-done.44, ...), custom_call_target="tpu_custom_call" | custom-call | bytes 1024 | tf_op jit(solution)/shard_map/pallas_call | solution.py:645
  351.5 13.4 %shard_map.252 = f32[768,2048]{1,0:T(8,128)} custom-call(s32[16]{0:T(128)} %stack.234.place_ref, bf16[512,768]{1,0:T(8,128)(2,1)} %copy-done.24, bf16[512,768]{1,0:T(8,128)(2,1)} %copy-done.25, bf16[512,768]{1,0:T(8,128)(2,1)} %copy-done.26, bf16[512,768]{1,0:T(8,128)(2,1)} %copy-done.27, bf16[2048,2048]{1,0:T(8,128)(2,1)} %all-gather.2.cloned.1.call-done.g0_ref.g1_ref.refs_4_), custom_call_target="tpu_custom_call" | custom-call | bytes 1024 | tf_op jit(solution)/shard_map/pallas_call | solution.py:381
  367.0 7.7 %collective-permute-done.51 = bf16[64,2304]{1,0:T(8,128)(2,1)} collective-permute-done((bf16[64,2304]{1,0:T(8,128)(2,1)}, bf16[64,2304]{1,0:T(8,128)(2,1)}, u32[]{:S(2)}, u32[]{:S(2)}) %collective-permute-start.51) | collective-permute-done | bytes 294944 | tf_op jit(solution)/shard_map/ppermute | solution.py:47
  387.1 16.0 %collective-permute-done.56.refs_2_ = bf16[64,2304]{1,0:T(8,128)(2,1)S(1)} collective-permute-done((bf16[64,2304]{1,0:T(8,128)(2,1)S(1)}, bf16[64,2304]{1,0:T(8,128)(2,1)S(1)}, u32[]{:S(2)}, u32[]{:S(2)}) %collective-permute-start.56) | collective-permute-done | bytes 294944 | tf_op jit(solution)/shard_map/ppermute | solution.py:47
  403.1 6.7 %collective-permute-done.57.refs_3_ = bf16[64,2304]{1,0:T(8,128)(2,1)S(1)} collective-permute-done((bf16[64,2304]{1,0:T(8,128)(2,1)S(1)}, bf16[64,2304]{1,0:T(8,128)(2,1)S(1)}, u32[]{:S(2)}, u32[]{:S(2)}) %collective-permute-start.57) | collective-permute-done | bytes 294944 | tf_op jit(solution)/shard_map/ppermute | solution.py:47
  409.8 4.8 collective-permute-done.60.refs_3_
  418.4 4.6 shard_map.254
  424.2 3.9 collective-permute-done.63
  428.1 7.8 %collective-permute-done.64 = bf16[64,2048]{1,0:T(8,128)(2,1)S(1)} collective-permute-done((bf16[64,2048]{1,0:T(8,128)(2,1)S(1)}, bf16[64,2048]{1,0:T(8,128)(2,1)S(1)}, u32[]{:S(2)}, u32[]{:S(2)}) %collective-permute-start.64) | collective-permute-done | bytes 262176 | tf_op jit(solution)/shard_map/ppermute | solution.py:47
  435.9 5.9 %collective-permute-done.65 = bf16[64,2048]{1,0:T(8,128)(2,1)S(1)} collective-permute-done((bf16[64,2048]{1,0:T(8,128)(2,1)S(1)}, bf16[64,2048]{1,0:T(8,128)(2,1)S(1)}, u32[]{:S(2)}, u32[]{:S(2)}) %collective-permute-start.65) | collective-permute-done | bytes 262176 | tf_op jit(solution)/shard_map/ppermute | solution.py:47
  454.1 5.3 %shard_map.255 = f32[1024,2048]{1,0:T(8,128)} custom-call(s32[8]{0:T(128)S(1)} %stack.100.place_ref.column_ref.block_ref, bf16[512,2048]{1,0:T(8,128)(2,1)S(1)} %shard_map.253.near_ref, bf16[512,2048]{1,0:T(8,128)(2,1)S(1)} %copy-done.33), custom_call_target="tpu_custom_call" | custom-call | bytes 1024 | tf_op jit(solution)/shard_map/pallas_call | solution.py:851
  459.5 5.9 %collective-permute-done.70 = bf16[64,2048]{1,0:T(8,128)(2,1)} collective-permute-done((bf16[64,2048]{1,0:T(8,128)(2,1)}, bf16[64,2048]{1,0:T(8,128)(2,1)}, u32[]{:S(2)}, u32[]{:S(2)}) %collective-permute-start.70) | collective-permute-done | bytes 262176 | tf_op jit(solution)/shard_map/ppermute | solution.py:47
  465.4 4.8 collective-permute-done.71
  (350 shorter events, 203.7 us)
Async XLA Ops:
  7.2 128.9 %all-gather.2.cloned.1.call-start = ((), (), s32[]{:S(2)}) async-start(), calls=%async_computation.2 | async-start | bytes 9437184 | tf_op jit(solution)/shard_map/all_gather | solution.py:964
  16.9 29.7 %collective-permute-start.1 = (bf16[256,1024]{1,0:T(8,128)(2,1)}, bf16[256,1024]{1,0:T(8,128)(2,1)}, u32[]{:S(2)}, u32[]{:S(2)}) collective-permute-start(bf16[256,1024]{1,0:T(8,128)(2,1)} %refs_0_.1), channel_id=1, source_target_pairs={{0,16},{4,20},{8,24},{12,28},{16,0},{20,4},{24,8},{28,12},{1,17},{... | collective-permute-start | bytes 1572872 | tf_op jit(solution)/shard_map/ppermute | solution.py:47
  19.7 26.9 %collective-permute-start.2 = (bf16[256,1024]{1,0:T(8,128)(2,1)}, bf16[256,1024]{1,0:T(8,128)(2,1)}, u32[]{:S(2)}, u32[]{:S(2)}) collective-permute-start(bf16[256,1024]{1,0:T(8,128)(2,1)} %refs_0_.1), channel_id=1, source_target_pairs={{0,24},{4,28},{8,16},{12,20},{16,8},{20,12},{24,0},{28,4},{1,25},{... | collective-permute-start | bytes 1572872 | tf_op jit(solution)/shard_map/ppermute | solution.py:47
  46.6 328.1 %reduce-scatter.3.cloned.1.call-start = ((), (), s32[]{:S(2)}) async-start(), calls=%async_computation.3 | async-start | bytes 9437184 | tf_op jit(solution)/shard_map/reduce_scatter | solution.py:1021
  104.4 22.3 %collective-permute-start.18 = (bf16[128,2048]{1,0:T(8,128)(2,1)S(1)}, bf16[128,2048]{1,0:T(8,128)(2,1)S(1)}, u32[]{:S(2)}, u32[]{:S(2)}) collective-permute-start(bf16[128,2048]{1,0:T(8,128)(2,1)S(1)} %get-tuple-element.165.refs_0_.refs_10_), channel_id=1, source_target_pairs={{0,16},{4,20},{8,24},{12,28},{16,0},{20,4},{24,8},{28,12},{1,17},{... | collective-permute-start | bytes 1572872 | tf_op jit(solution)/shard_map/ppermute | solution.py:47
  105.2 23.1 %collective-permute-start.19 = (bf16[128,2048]{1,0:T(8,128)(2,1)S(1)}, bf16[128,2048]{1,0:T(8,128)(2,1)S(1)}, u32[]{:S(2)}, u32[]{:S(2)}) collective-permute-start(bf16[128,2048]{1,0:T(8,128)(2,1)S(1)} %get-tuple-element.165.refs_0_.refs_10_), channel_id=1, source_target_pairs={{0,24},{4,28},{8,16},{12,20},{16,8},{20,12},{24,0},{28,4},{1,25},{... | collective-permute-start | bytes 1572872 | tf_op jit(solution)/shard_map/ppermute | solution.py:47
  129.7 29.3 %collective-permute-start.26 = (bf16[512,2048]{1,0:T(8,128)(2,1)}, bf16[512,2048]{1,0:T(8,128)(2,1)}, u32[]{:S(2)}, u32[]{:S(2)}) collective-permute-start(bf16[512,2048]{1,0:T(8,128)(2,1)} %shard_map.242.x_ref.refs_0_), channel_id=1, source_target_pairs={{0,4},{4,0},{8,12},{12,8},{16,20},{20,16},{24,28},{28,24},{1,5},{5... | collective-permute-start | bytes 6291464 | tf_op jit(solution)/shard_map/ppermute | solution.py:47
  132.4 40.3 %collective-permute-start.23 = (bf16[128,2048]{1,0:T(8,128)(2,1)}, bf16[128,2048]{1,0:T(8,128)(2,1)}, u32[]{:S(2)}, u32[]{:S(2)}) collective-permute-start(bf16[128,2048]{1,0:T(8,128)(2,1)} %get-tuple-element.170.refs_0_.refs_11_), channel_id=1, source_target_pairs={{0,8},{4,12},{8,0},{12,4},{16,24},{20,28},{24,16},{28,20},{1,9},{5... | collective-permute-start | bytes 1572872 | tf_op jit(solution)/shard_map/ppermute | solution.py:47
  133.1 39.6 %collective-permute-start.24 = (bf16[128,2048]{1,0:T(8,128)(2,1)}, bf16[128,2048]{1,0:T(8,128)(2,1)}, u32[]{:S(2)}, u32[]{:S(2)}) collective-permute-start(bf16[128,2048]{1,0:T(8,128)(2,1)} %get-tuple-element.170.refs_0_.refs_11_), channel_id=1, source_target_pairs={{0,16},{4,20},{8,24},{12,28},{16,0},{20,4},{24,8},{28,12},{1,17},{... | collective-permute-start | bytes 1572872 | tf_op jit(solution)/shard_map/ppermute | solution.py:47
  134.7 38.0 %collective-permute-start.25 = (bf16[128,2048]{1,0:T(8,128)(2,1)}, bf16[128,2048]{1,0:T(8,128)(2,1)}, u32[]{:S(2)}, u32[]{:S(2)}) collective-permute-start(bf16[128,2048]{1,0:T(8,128)(2,1)} %get-tuple-element.170.refs_0_.refs_11_), channel_id=1, source_target_pairs={{0,24},{4,28},{8,16},{12,20},{16,8},{20,12},{24,0},{28,4},{1,25},{... | collective-permute-start | bytes 1572872 | tf_op jit(solution)/shard_map/ppermute | solution.py:47
  172.7 21.5 %collective-permute-start.27 = (bf16[512,2176]{1,0:T(8,128)(2,1)}, bf16[512,2176]{1,0:T(8,128)(2,1)}, u32[]{:S(2)}, u32[]{:S(2)}) collective-permute-start(bf16[512,2176]{1,0:T(8,128)(2,1)} %get-tuple-element.181), channel_id=1, source_target_pairs={{0,4},{4,0},{8,12},{12,8},{16,20},{20,16},{24,28},{28,24},{1,5},{5... | collective-permute-start | bytes 6684680 | tf_op jit(solution)/shard_map/ppermute | solution.py:47
  198.3 21.6 %collective-permute-start.29 = (bf16[128,2176]{1,0:T(8,128)(2,1)}, bf16[128,2176]{1,0:T(8,128)(2,1)}, u32[]{:S(2)}, u32[]{:S(2)}) collective-permute-start(bf16[128,2176]{1,0:T(8,128)(2,1)} %get-tuple-element.330), channel_id=1, source_target_pairs={{0,8},{4,12},{8,0},{12,4},{16,24},{20,28},{24,16},{28,20},{1,9},{5... | collective-permute-start | bytes 1671176 | tf_op jit(solution)/shard_map/ppermute | solution.py:47
  199.1 27.0 %collective-permute-start.30 = (bf16[128,2176]{1,0:T(8,128)(2,1)}, bf16[128,2176]{1,0:T(8,128)(2,1)}, u32[]{:S(2)}, u32[]{:S(2)}) collective-permute-start(bf16[128,2176]{1,0:T(8,128)(2,1)} %get-tuple-element.329), channel_id=1, source_target_pairs={{0,16},{4,20},{8,24},{12,28},{16,0},{20,4},{24,8},{28,12},{1,17},{... | collective-permute-start | bytes 1671176 | tf_op jit(solution)/shard_map/ppermute | solution.py:47
  200.7 25.4 %collective-permute-start.31 = (bf16[128,2176]{1,0:T(8,128)(2,1)}, bf16[128,2176]{1,0:T(8,128)(2,1)}, u32[]{:S(2)}, u32[]{:S(2)}) collective-permute-start(bf16[128,2176]{1,0:T(8,128)(2,1)} %get-tuple-element.328), channel_id=1, source_target_pairs={{0,24},{4,28},{8,16},{12,20},{16,8},{20,12},{24,0},{28,4},{1,25},{... | collective-permute-start | bytes 1671176 | tf_op jit(solution)/shard_map/ppermute | solution.py:47
  247.0 212.5 %reduce-scatter.5.cloned.1.call-start = ((), (), s32[]{:S(2)}) async-start(), calls=%async_computation.4 | async-start | bytes 6488064 | tf_op jit(solution)/shard_map/reduce_scatter | solution.py:1069
  250.3 31.5 %collective-permute-start.39 = (bf16[128,2176]{1,0:T(8,128)(2,1)S(1)}, bf16[128,2176]{1,0:T(8,128)(2,1)S(1)}, u32[]{:S(2)}, u32[]{:S(2)}) collective-permute-start(bf16[128,2176]{1,0:T(8,128)(2,1)S(1)} %get-tuple-element.327), channel_id=1, source_target_pairs={{0,8},{4,12},{8,0},{12,4},{16,24},{20,28},{24,16},{28,20},{1,9},{5... | collective-permute-start | bytes 1671176 | tf_op jit(solution)/shard_map/ppermute | solution.py:47
  251.7 30.2 %collective-permute-start.40 = (bf16[128,2176]{1,0:T(8,128)(2,1)S(1)}, bf16[128,2176]{1,0:T(8,128)(2,1)S(1)}, u32[]{:S(2)}, u32[]{:S(2)}) collective-permute-start(bf16[128,2176]{1,0:T(8,128)(2,1)S(1)} %get-tuple-element.326), channel_id=1, source_target_pairs={{0,16},{4,20},{8,24},{12,28},{16,0},{20,4},{24,8},{28,12},{1,17},{... | collective-permute-start | bytes 1671176 | tf_op jit(solution)/shard_map/ppermute | solution.py:47
  252.5 29.4 %collective-permute-start.41 = (bf16[128,2176]{1,0:T(8,128)(2,1)S(1)}, bf16[128,2176]{1,0:T(8,128)(2,1)S(1)}, u32[]{:S(2)}, u32[]{:S(2)}) collective-permute-start(bf16[128,2176]{1,0:T(8,128)(2,1)S(1)} %get-tuple-element.325), channel_id=1, source_target_pairs={{0,24},{4,28},{8,16},{12,20},{16,8},{20,12},{24,0},{28,4},{1,25},{... | collective-permute-start | bytes 1671176 | tf_op jit(solution)/shard_map/ppermute | solution.py:47
  255.5 26.3 %collective-permute-start.37 = (bf16[32,2176]{1,0:T(8,128)(2,1)S(1)}, bf16[32,2176]{1,0:T(8,128)(2,1)S(1)}, u32[]{:S(2)}, u32[]{:S(2)}) collective-permute-start(bf16[32,2176]{1,0:T(8,128)(2,1)S(1)} %add_convert_fusion.18.refs_0_), channel_id=1, source_target_pairs={{0,2},{1,3},{2,0},{3,1},{4,6},{5,7},{6,4},{7,5},{8,10},{9,11},{10,... | collective-permute-start | bytes 417800 | tf_op jit(solution)/shard_map/ppermute | solution.py:47
  260.4 21.4 %collective-permute-start.38 = (bf16[32,2176]{1,0:T(8,128)(2,1)S(1)}, bf16[32,2176]{1,0:T(8,128)(2,1)S(1)}, u32[]{:S(2)}, u32[]{:S(2)}) collective-permute-start(bf16[32,2176]{1,0:T(8,128)(2,1)S(1)} %add_convert_fusion.18.refs_0_), channel_id=1, source_target_pairs={{0,3},{1,2},{2,1},{3,0},{4,7},{5,6},{6,5},{7,4},{8,11},{9,10},{10,... | collective-permute-start | bytes 417800 | tf_op jit(solution)/shard_map/ppermute | solution.py:47
  342.3 32.4 %collective-permute-start.52 = (bf16[128,2048]{1,0:T(8,128)(2,1)}, bf16[128,2048]{1,0:T(8,128)(2,1)}, u32[]{:S(2)}, u32[]{:S(2)}) collective-permute-start(bf16[128,2048]{1,0:T(8,128)(2,1)} %get-tuple-element.333), channel_id=1, source_target_pairs={{0,8},{4,12},{8,0},{12,4},{16,24},{20,28},{24,16},{28,20},{1,9},{5... | collective-permute-start | bytes 1572872 | tf_op jit(solution)/shard_map/ppermute | solution.py:47
  343.4 31.3 %collective-permute-start.53 = (bf16[128,2048]{1,0:T(8,128)(2,1)}, bf16[128,2048]{1,0:T(8,128)(2,1)}, u32[]{:S(2)}, u32[]{:S(2)}) collective-permute-start(bf16[128,2048]{1,0:T(8,128)(2,1)} %get-tuple-element.332), channel_id=1, source_target_pairs={{0,16},{4,20},{8,24},{12,28},{16,0},{20,4},{24,8},{28,12},{1,17},{... | collective-permute-start | bytes 1572872 | tf_op jit(solution)/shard_map/ppermute | solution.py:47
  344.2 30.5 %collective-permute-start.54 = (bf16[128,2048]{1,0:T(8,128)(2,1)}, bf16[128,2048]{1,0:T(8,128)(2,1)}, u32[]{:S(2)}, u32[]{:S(2)}) collective-permute-start(bf16[128,2048]{1,0:T(8,128)(2,1)} %get-tuple-element.331), channel_id=1, source_target_pairs={{0,24},{4,28},{8,16},{12,20},{16,8},{20,12},{24,0},{28,4},{1,25},{... | collective-permute-start | bytes 1572872 | tf_op jit(solution)/shard_map/ppermute | solution.py:47
  349.6 25.1 %collective-permute-start.51 = (bf16[64,2304]{1,0:T(8,128)(2,1)}, bf16[64,2304]{1,0:T(8,128)(2,1)}, u32[]{:S(2)}, u32[]{:S(2)}) collective-permute-start(bf16[64,2304]{1,0:T(8,128)(2,1)} %get-tuple-element.334), channel_id=1, source_target_pairs={{0,3},{1,2},{2,1},{3,0},{4,7},{5,6},{6,5},{7,4},{8,11},{9,10},{10,... | collective-permute-start | bytes 884744 | tf_op jit(solution)/shard_map/ppermute | solution.py:47
  380.5 29.3 %collective-permute-start.58 = (bf16[128,2048]{1,0:T(8,128)(2,1)S(1)}, bf16[128,2048]{1,0:T(8,128)(2,1)S(1)}, u32[]{:S(2)}, u32[]{:S(2)}) collective-permute-start(bf16[128,2048]{1,0:T(8,128)(2,1)S(1)} %add_convert_fusion.10.refs_0_), channel_id=1, source_target_pairs={{0,8},{4,12},{8,0},{12,4},{16,24},{20,28},{24,16},{28,20},{1,9},{5... | collective-permute-start | bytes 1572872 | tf_op jit(solution)/shard_map/ppermute | solution.py:47
  381.2 28.5 %collective-permute-start.59 = (bf16[128,2048]{1,0:T(8,128)(2,1)S(1)}, bf16[128,2048]{1,0:T(8,128)(2,1)S(1)}, u32[]{:S(2)}, u32[]{:S(2)}) collective-permute-start(bf16[128,2048]{1,0:T(8,128)(2,1)S(1)} %add_convert_fusion.10.refs_0_), channel_id=1, source_target_pairs={{0,16},{4,20},{8,24},{12,28},{16,0},{20,4},{24,8},{28,12},{1,17},{... | collective-permute-start | bytes 1572872 | tf_op jit(solution)/shard_map/ppermute | solution.py:47
  383.3 31.2 %collective-permute-start.60 = (bf16[128,2048]{1,0:T(8,128)(2,1)S(1)}, bf16[128,2048]{1,0:T(8,128)(2,1)S(1)}, u32[]{:S(2)}, u32[]{:S(2)}) collective-permute-start(bf16[128,2048]{1,0:T(8,128)(2,1)S(1)} %add_convert_fusion.10.refs_0_), channel_id=1, source_target_pairs={{0,24},{4,28},{8,16},{12,20},{16,8},{20,12},{24,0},{28,4},{1,25},{... | collective-permute-start | bytes 1572872 | tf_op jit(solution)/shard_map/ppermute | solution.py:47
  386.0 23.7 %collective-permute-start.57 = (bf16[64,2304]{1,0:T(8,128)(2,1)S(1)}, bf16[64,2304]{1,0:T(8,128)(2,1)S(1)}, u32[]{:S(2)}, u32[]{:S(2)}) collective-permute-start(bf16[64,2304]{1,0:T(8,128)(2,1)S(1)} %add_convert_fusion.15.refs_0_), channel_id=1, source_target_pairs={{0,3},{1,2},{2,1},{3,0},{4,7},{5,6},{6,5},{7,4},{8,11},{9,10},{10,... | collective-permute-start | bytes 884744 | tf_op jit(solution)/shard_map/ppermute | solution.py:47
  414.7 27.2 %collective-permute-start.61 = (bf16[512,2048]{1,0:T(8,128)(2,1)S(1)}, bf16[512,2048]{1,0:T(8,128)(2,1)S(1)}, u32[]{:S(2)}, u32[]{:S(2)}) collective-permute-start(bf16[512,2048]{1,0:T(8,128)(2,1)S(1)} %shard_map.253.near_ref), channel_id=1, source_target_pairs={{0,4},{4,0},{8,12},{12,8},{16,20},{20,16},{24,28},{28,24},{1,5},{5... | collective-permute-start | bytes 6291464 | tf_op jit(solution)/shard_map/ppermute | solution.py:47
  418.0 23.8 %collective-permute-start.65 = (bf16[64,2048]{1,0:T(8,128)(2,1)S(1)}, bf16[64,2048]{1,0:T(8,128)(2,1)S(1)}, u32[]{:S(2)}, u32[]{:S(2)}) collective-permute-start(bf16[64,2048]{1,0:T(8,128)(2,1)S(1)} %get-tuple-element.337), channel_id=1, source_target_pairs={{0,3},{1,2},{2,1},{3,0},{4,7},{5,6},{6,5},{7,4},{8,11},{9,10},{10,... | collective-permute-start | bytes 786440 | tf_op jit(solution)/shard_map/ppermute | solution.py:47
  444.1 21.3 %collective-permute-start.70 = (bf16[64,2048]{1,0:T(8,128)(2,1)}, bf16[64,2048]{1,0:T(8,128)(2,1)}, u32[]{:S(2)}, u32[]{:S(2)}) collective-permute-start(bf16[64,2048]{1,0:T(8,128)(2,1)} %get-tuple-element.324), channel_id=1, source_target_pairs={{0,2},{1,3},{2,0},{3,1},{4,6},{5,7},{6,4},{7,5},{8,10},{9,11},{10,... | collective-permute-start | bytes 786440 | tf_op jit(solution)/shard_map/ppermute | solution.py:47
  447.1 23.2 %collective-permute-start.71 = (bf16[64,2048]{1,0:T(8,128)(2,1)}, bf16[64,2048]{1,0:T(8,128)(2,1)}, u32[]{:S(2)}, u32[]{:S(2)}) collective-permute-start(bf16[64,2048]{1,0:T(8,128)(2,1)} %get-tuple-element.324), channel_id=1, source_target_pairs={{0,3},{1,2},{2,1},{3,0},{4,7},{5,6},{6,5},{7,4},{8,11},{9,10},{10,... | collective-permute-start | bytes 786440 | tf_op jit(solution)/shard_map/ppermute | solution.py:47
  (106 other events, 1173.9 us)
Sparse Core Ops, SparseCore 0:
  46.7 54.6 all-gather.1
  247.1 74.9 reduce-scatter.2
  338.6 75.9 reduce-scatter.4

commit v5 on v4

--- a/solution.py
+++ b/solution.py
@@ -83,7 +83,7 @@
         out_shape=jax.ShapeDtypeStruct(
             (len(pieces) * rows,) + pieces[0].shape[1:], pieces[0].dtype
         ),
-        compiler_params=pltpu.CompilerParams(vmem_limit_bytes=16 * 1024 * 1024),
+        compiler_params=pltpu.CompilerParams(vmem_limit_bytes=8 * 1024 * 1024),
         cost_estimate=SMALL,
     )(*pieces)
 
@@ -325,7 +325,7 @@
             jax.ShapeDtypeStruct((tokens, wgu.shape[1]), BF16),
             jax.ShapeDtypeStruct((tokens, wd.shape[0]), BF16),
         ],
-        compiler_params=pltpu.CompilerParams(vmem_limit_bytes=24 * 1024 * 1024),
+        compiler_params=pltpu.CompilerParams(vmem_limit_bytes=20 * 1024 * 1024),
         cost_estimate=SMALL,
     )(*operands)
 
@@ -682,7 +682,7 @@
             jax.ShapeDtypeStruct(hidden.shape, F32),
             jax.ShapeDtypeStruct(hidden.shape, BF16),
         ],
-        compiler_params=pltpu.CompilerParams(vmem_limit_bytes=16 * 1024 * 1024),
+        compiler_params=pltpu.CompilerParams(vmem_limit_bytes=6 * 1024 * 1024),
         cost_estimate=SMALL,
     )(chunk_places(), *pieces, hidden, gain)
 
@@ -1015,18 +1015,17 @@
     come = scatter_swap(send_b)
     total_a = scatter_total(sums_a, hops_a)
     hops = reduce_hops(total_a)
-    mixture_parts = mixture_product(hidden, wd, lined)
-    come, hops, mixture_parts = join(come, hops, mixture_parts)
-
-    mixture = lax.psum_scatter(mixture_parts, "ep", scatter_dimension=0, tiled=True)
+    come, hidden = join(come, hidden)
+
     sums_b = scatter_sums(keep_b, come)
     hops_b = scatter_hops(sums_b)
+    mixture_parts = mixture_product(hidden, wd, lined)
     chunk_a = reduce_total(total_a, hops)
-    gate_up_grad = gate_up_product(routed_pieces, joined, gate_up_weight.shape)
-    spread_a, hops_b, gate_up_grad, hidden = join(
-        spread_hops(chunk_a), hops_b, gate_up_grad, hidden
-    )
-
+    spread_a, hops_b, mixture_parts, joined = join(
+        spread_hops(chunk_a), hops_b, mixture_parts, joined
+    )
+
+    mixture = lax.psum_scatter(mixture_parts, "ep", scatter_dimension=0, tiled=True)
     total_b = scatter_total(sums_b, hops_b)
     (hops,) = join(reduce_hops(total_b))
     chunk_b = reduce_total(total_b, hops)
@@ -1071,25 +1070,28 @@
     output_sums = scatter_sums(output_keep, come)
     output_hops = scatter_hops(output_sums)
     down_grad = down_product(hidden, output_all, where).reshape(down_weight.shape)
-    hops, output_hops, down_grad, mixture = join(hops, output_hops, down_grad, mixture)
+    hops, output_hops, down_grad, mixture, joined = join(
+        hops, output_hops, down_grad, mixture, joined
+    )
 
     chunk = reduce_total(feature_part, hops)
+    hops = spread_hops(chunk)
+    mixture_hops = reduce_hops(mixture)
     output_share = scatter_total(output_sums, output_hops)
-    hops, output_hops, mixture = join(
-        spread_hops(chunk), gather_hops(output_share), mixture
-    )
-
-    mixture_hops = reduce_hops(mixture)
+    gate_up_grad = gate_up_product(routed_pieces, joined, gate_up_weight.shape)
+    hops, gate_up_grad, output_share = join(hops, gate_up_grad, output_share)
+
+    output_hops = gather_hops(output_share)
+    input_grad, late = input_gradient(
+        [chunk, *hops], hidden_in, grad_resid, attn_gain_full, lined
+    )
+    late_come = scatter_swap(late[owners // 2 :])
+    late_come, output_hops, mixture_hops = join(late_come, output_hops, mixture_hops)
+
+    mixture_chunk = reduce_total(mixture, mixture_hops)
+    mixture_hops = spread_hops(mixture_chunk)
     near = gather_near(output_share, output_hops)
     output_core = gather_core(near, output_hops)
-    input_grad, late = input_gradient(
-        [chunk, *hops], hidden_in, grad_resid, attn_gain_full, lined
-    )
-    late_come = scatter_swap(late[owners // 2 :])
-    output_core, late_come, mixture_hops = join(output_core, late_come, mixture_hops)
-
-    mixture_chunk = reduce_total(mixture, mixture_hops)
-    mixture_hops = spread_hops(mixture_chunk)
     late_sums = scatter_sums(late[: owners // 2], late_come)
     late_hops = scatter_hops(late_sums)
     output_weight_grad = widen_blocks(near, output_core, lined)

time: 493 us -> 477 us (0.968)
  waiting for transfers between devices: 155 us -> 139 us
    ppermute x72, waiting for transfers between devices: 154 us -> 139 us  [swap(): return lax.ppermute(value, axis, [(i, i ^ mask) for i in range(count)])]
    unnamed x136 -> x138, local copies, waits for them, and re-layouts: 40.1 us -> 43.6 us
  transfers between devices with their start and end apart: 75 -> 75, of which waited for: 38 -> 35; matrix products, arithmetic and copies ran while one was open for 6% -> 6% of each run, Pallas kernels for 30% -> 30%
where the time goes in v5:
time: 477 us; the launch traced here: 471 us
  Pallas kernels  144 us (30%)
  waiting for transfers between devices  139 us (29%)
  starting transfers between devices  82.8 us (17%)
  local copies, waits for them, and re-layouts  63.8 us (13%)
  other arithmetic  27.1 us (6%)
  between operations  15.6 us (3%)
    ppermute x72, waiting for transfers between devices, swap(): return lax.ppermute(value, axis, [(i, i ^ mask) for i in range(count)])  139 us
    ppermute x72, starting transfers between devices, swap(): return lax.ppermute(value, axis, [(i, i ^ mask) for i in range(count)])  82.3 us
    pallas_call x4, Pallas kernels, run_experts(): pl.pallas_call(functools.partial(expert_kernel, local), grid_spec=pltpu.P...  52.4 us
    unnamed x138, local copies, waits for them, and re-layouts  43.6 us
    pallas_call x1, Pallas kernels, gate_up_product(): pl.pallas_call(gate_up_kernel, grid=(features // tile,), in_specs=[pl.Blo...  19.2 us
    convert_element_type x11, other arithmetic, plus(): return total.astype(values[0].dtype)  16.2 us
    pallas_call x1, Pallas kernels, attention_back(): pl.pallas_call(functools.partial(attention_back_kernel, key_heads), in_sp...  13.3 us
    pallas_call x1, Pallas kernels, down_product(): pl.pallas_call(down_kernel, grid_spec=pltpu.PrefetchScalarGridSpec(num_sc...  13.2 us
  transfers between devices with their start and end apart: 75, of which 35 were waited for; matrix products, arithmetic and copies ran while one was open for 6% of the time, Pallas kernels for 30%

profile of v5, /device:TPU:8, one launch (start us, length us, event | category | flops | bytes accessed | tf_op | source)
XLA Modules:
  0.0 471.4 jit_solution(5722141714355836217)
XLA Ops:
  35.2 11.4 %collective-permute-done.1.refs_2_ = bf16[256,1024]{1,0:T(8,128)(2,1)} collective-permute-done((bf16[256,1024]{1,0:T(8,128)(2,1)}, bf16[256,1024]{1,0:T(8,128)(2,1)}, u32[]{:S(2)}, u32[]{:S(2)}) %collective-permute-start.1) | collective-permute-done | bytes 524320 | tf_op jit(solution)/shard_map/ppermute | solution.py:47
  50.5 7.3 %copy.56 = bf16[4,256,8,384]{3,2,0,1:T(8,128)(2,1)} copy(bf16[4,256,8,384]{3,2,1,0:T(8,128)(2,1)} %bitcast.79) | data formatting | bytes 12582912 | tf_op jit(solution)/shard_map/reshape | solution.py:974
  58.4 7.1 %shard_map.239 = (f32[256,1152]{1,0:T(8,128)S(1)}, bf16[256,1280]{1,0:T(8,128)(2,1)S(1)}, bf16[256,1024]{1,0:T(8,128)(2,1)S(1)}, f32[256,8]{1,0:T(8,128)S(1)}, b...) custom-call(bf16[256,2048]{1,0:T(8,128)(2,1)S(1)} %copy-done.17, bf16[1024,1024]{1,0:T(8,128)(2,1)S(1)} %shard_map.238.near_ref, ...), custom_call_target="tpu_custom_call" | custom-call | bytes 1024 | tf_op jit(solution)/shard_map/pallas_call | solution.py:529
  79.9 6.8 %collective-permute-start.11 = (bf16[32,2048]{1,0:T(8,128)(2,1)S(1)}, bf16[32,2048]{1,0:T(8,128)(2,1)S(1)}, u32[]{:S(2)}, u32[]{:S(2)}) collective-permute-start(bf16[32,2048]{1,0:T(8,128)(2,1)S(1)} %add_convert_fusion.20.refs_0_), channel_id=1, source_target_pairs={{0,1},{1,0},{2,3},{3,2},{4,5},{5,4},{6,7},{7,6},{8,9},{9,8},{10,11... | collective-permute-start | bytes 393224 | tf_op jit(solution)/shard_map/ppermute | solution.py:47
  88.4 9.3 %collective-permute-done.16 = bf16[32,2048]{1,0:T(8,128)(2,1)S(1)} collective-permute-done((bf16[32,2048]{1,0:T(8,128)(2,1)S(1)}, bf16[32,2048]{1,0:T(8,128)(2,1)S(1)}, u32[]{:S(2)}, u32[]{:S(2)}) %collective-permute-start.16) | collective-permute-done | bytes 131104 | tf_op jit(solution)/shard_map/ppermute | solution.py:47
  117.4 3.7 collective-permute-done.22.refs_3_
  121.2 6.2 %collective-permute-done.18.refs_2_ = bf16[128,2048]{1,0:T(8,128)(2,1)S(1)} collective-permute-done((bf16[128,2048]{1,0:T(8,128)(2,1)S(1)}, bf16[128,2048]{1,0:T(8,128)(2,1)S(1)}, u32[]{:S(2)}, u32[]{:S(2)}) %collective-permute-start.18) | collective-permute-done | bytes 524320 | tf_op jit(solution)/shard_map/ppermute | solution.py:47
  142.6 13.8 %shard_map.244 = (bf16[512,2176]{1,0:T(8,128)(2,1)S(1)}, bf16[512,1536]{1,0:T(8,128)(2,1)S(1)}, bf16[512,768]{1,0:T(8,128)(2,1)S(1)}) custom-call(s32[5]{0:T(128)S(1)} %stack.111.place_ref, bf16[512,2048]{1,0:T(8,128)(2,1)} %shard_map.242.x_ref.refs_0_, bf16[2048,2048]{1,0:T(8,128)(2,1)} %all-gather.2.cloned.1.call-done.g0_ref.g1_ref.refs_4_, ...), custom_call_target="tpu_custom_call" | custom-call | bytes 1024 | tf_op jit(solution)/shard_map/pallas_call | solution.py:311
  159.8 13.6 %shard_map.243 = (bf16[512,2176]{1,0:T(8,128)(2,1)}, bf16[512,1536]{1,0:T(8,128)(2,1)S(1)}, bf16[512,768]{1,0:T(8,128)(2,1)S(1)}) custom-call(s32[5]{0:T(128)S(1)} %stack.106.place_ref, bf16[512,2048]{1,0:T(8,128)(2,1)} %collective-permute-done.26.x_ref.refs_1_, bf16[2048,2048]{1,0:T(8,128)(2,1)} %all-gather.2.cloned.1.call-done.g0_ref.g1_ref.refs_4_, ...), custom_call_target="tpu_custom_call" | custom-call | bytes 1024 | tf_op jit(solution)/shard_map/pallas_call | solution.py:311
  173.6 3.8 shard_map.245.x_ref.refs_2_
  182.2 12.7 %shard_map.246 = (bf16[512,2176]{1,0:T(8,128)(2,1)S(1)}, bf16[512,1536]{1,0:T(8,128)(2,1)S(1)}, bf16[512,768]{1,0:T(8,128)(2,1)S(1)}) custom-call(s32[5]{0:T(128)S(1)} %stack.228.place_ref, bf16[512,2048]{1,0:T(8,128)(2,1)} %shard_map.245.x_ref.refs_2_, bf16[2048,2048]{1,0:T(8,128)(2,1)} %all-gather.2.cloned.1.call-done.g0_ref.g1_ref.refs_4_, ...), custom_call_target="tpu_custom_call" | custom-call | bytes 1024 | tf_op jit(solution)/shard_map/pallas_call | solution.py:311
  195.8 4.0 add_convert_fusion.6
  208.1 12.3 %shard_map.247 = (bf16[512,2176]{1,0:T(8,128)(2,1)S(1)}, bf16[512,1536]{1,0:T(8,128)(2,1)S(1)}, bf16[512,768]{1,0:T(8,128)(2,1)S(1)}) custom-call(s32[5]{0:T(128)S(1)} %stack.233.place_ref, bf16[512,2048]{1,0:T(8,128)(2,1)} %collective-permute-done.28.x_ref.refs_3_, bf16[2048,2048]{1,0:T(8,128)(2,1)} %all-gather.2.cloned.1.call-done.g0_ref.g1_ref.refs_4_, ...), custom_call_target="tpu_custom_call" | custom-call | bytes 1024 | tf_op jit(solution)/shard_map/pallas_call | solution.py:311
  222.6 5.0 %collective-permute-done.30 = bf16[128,2176]{1,0:T(8,128)(2,1)} collective-permute-done((bf16[128,2176]{1,0:T(8,128)(2,1)}, bf16[128,2176]{1,0:T(8,128)(2,1)}, u32[]{:S(2)}, u32[]{:S(2)}) %collective-permute-start.30) | collective-permute-done | bytes 557088 | tf_op jit(solution)/shard_map/ppermute | solution.py:47
  229.8 3.5 collective-permute-start.33
  238.6 4.8 %collective-permute-done.33 = bf16[32,2176]{1,0:T(8,128)(2,1)S(1)} collective-permute-done((bf16[32,2176]{1,0:T(8,128)(2,1)S(1)}, bf16[32,2176]{1,0:T(8,128)(2,1)S(1)}, u32[]{:S(2)}, u32[]{:S(2)}) %collective-permute-start.33) | collective-permute-done | bytes 139296 | tf_op jit(solution)/shard_map/ppermute | solution.py:47
  246.2 3.5 collective-permute-start.36
  254.9 10.9 %shard_map.248 = bf16[2048,2048]{1,0:T(8,128)(2,1)S(1)} custom-call(s32[8]{0:T(128)S(1)} %stack.100.place_ref.column_ref.block_ref, bf16[512,768]{1,0:T(8,128)(2,1)} %copy-done.24, bf16[512,768]{1,0:T(8,128)(2,1)} %copy-done.25, bf16[512,768]{1,0:T(8,128)(2,1)} %copy-done.26, bf16[512,768]{1,0:T(8,128)(2,1)} %copy-done.27, bf16[768,2048]{1,0:T(8,128)(2,1)} %bitcast.60), custom_call_target="tpu_custom_call" | custom-call | bytes 1024 | tf_op jit(solution)/shard_map/pallas_call | solution.py:417
  280.6 3.7 collective-permute-done.44
  290.8 3.6 collective-permute-done.46.refs_6_
  294.4 3.6 collective-permute-done.47.refs_7_
  298.0 7.6 %shard_map.249 = (f32[256,2048]{1,0:T(8,128)S(1)}, bf16[256,2048]{1,0:T(8,128)(2,1)S(1)}, bf16[2048,128]{1,0:T(8,128)(2,1)S(1)}, bf16[512,2048]{1,0:T(8,128)(2,1)S(1)}, bf16[512,2048]{1,0:T(8,128)(2,1)S(1)}) custom-call(s32[4]{0:T(128)S(1)} %pad_add_fusion.place_ref, s32[8]{0:T(128)S(1)} %stack.100.place_ref.column_ref.block_ref, ...), custom_call_target="tpu_custom_call" | custom-call | bytes 1024 | tf_op jit(solution)/shard_map/pallas_call | solution.py:773
  308.7 13.3 %shard_map.250 = (bf16[256,2304]{1,0:T(8,128)(2,1)S(1)}, bf16[2048,1408]{1,0:T(8,128)(2,1)S(1)}) custom-call(s32[8]{0:T(128)S(1)} %stack.100.place_ref.column_ref.block_ref, bf16[256,2048]{1,0:T(8,128)(2,1)} %copy-done.43, bf16[1024,2048]{1,0:T(8,128)(2,1)} %wo_ref.3, f32[256,1152]{1,0:T(8,128)} %copy-done.42, bf16[256,1280]{1,0:T(8,128)(2,1)} %copy-done.44, ...), custom_call_target="tpu_custom_call" | custom-call | bytes 1024 | tf_op jit(solution)/shard_map/pallas_call | solution.py:645
  337.9 13.2 %shard_map.251 = f32[768,2048]{1,0:T(8,128)} custom-call(s32[16]{0:T(128)} %stack.234.place_ref, bf16[512,768]{1,0:T(8,128)(2,1)} %copy-done.24, bf16[512,768]{1,0:T(8,128)(2,1)} %copy-done.25, bf16[512,768]{1,0:T(8,128)(2,1)} %copy-done.26, bf16[512,768]{1,0:T(8,128)(2,1)} %copy-done.27, bf16[2048,2048]{1,0:T(8,128)(2,1)} %all-gather.2.cloned.1.call-done.g0_ref.g1_ref.refs_4_), custom_call_target="tpu_custom_call" | custom-call | bytes 1024 | tf_op jit(solution)/shard_map/pallas_call | solution.py:381
  354.4 7.4 %collective-permute-done.51 = bf16[64,2304]{1,0:T(8,128)(2,1)} collective-permute-done((bf16[64,2304]{1,0:T(8,128)(2,1)}, bf16[64,2304]{1,0:T(8,128)(2,1)}, u32[]{:S(2)}, u32[]{:S(2)}) %collective-permute-start.51) | collective-permute-done | bytes 294944 | tf_op jit(solution)/shard_map/ppermute | solution.py:47
  369.1 19.2 %shard_map.252 = f32[4,2048,384]{2,1,0:T(8,128)} custom-call(bf16[512,2048]{1,0:T(8,128)(2,1)} %shard_map.242.x_ref.refs_0_, bf16[512,2048]{1,0:T(8,128)(2,1)} %collective-permute-done.26.x_ref.refs_1_, bf16[512,2048]{1,0:T(8,128)(2,1)} %shard_map.245.x_ref.refs_2_, bf16[512,2048]{1,0:T(8,128)(2,1)} %collective-permute-done.28.x_ref.refs_3_, ...), custom_call_target="tpu_custom_call" | custom-call | bytes 1024 | tf_op jit(solution)/shard_map/pallas_call | solution.py:352
  396.8 5.0 %shard_map.253 = (f32[256,2048]{1,0:T(8,128)}, f32[8,512]{1,0:T(8,128)S(1)}) custom-call(s32[4]{0:T(128)S(1)} %pad_add_fusion.place_ref, s32[8]{0:T(128)S(1)} %stack.100.place_ref.column_ref.block_ref, bf16[64,2304]{1,0:T(8,128)(2,1)S(1)} %add_convert_fusion.15.refs_0_, bf16[64,2304]{1,0:T(8,128)(2,1)S(1)} %collective-permute-done.55.refs_1_, ...), custom_call_target="tpu_custom_call" | custom-call | bytes 1024 | tf_op jit(solution)/shard_map/pallas_call | solution.py:825
  401.9 10.8 %collective-permute-done.63 = bf16[64,2048]{1,0:T(8,128)(2,1)S(1)} collective-permute-done((bf16[64,2048]{1,0:T(8,128)(2,1)S(1)}, bf16[64,2048]{1,0:T(8,128)(2,1)S(1)}, u32[]{:S(2)}, u32[]{:S(2)}) %collective-permute-start.63) | collective-permute-done | bytes 262176 | tf_op jit(solution)/shard_map/ppermute | solution.py:47
  412.7 5.3 %collective-permute-done.64 = bf16[64,2048]{1,0:T(8,128)(2,1)S(1)} collective-permute-done((bf16[64,2048]{1,0:T(8,128)(2,1)S(1)}, bf16[64,2048]{1,0:T(8,128)(2,1)S(1)}, u32[]{:S(2)}, u32[]{:S(2)}) %collective-permute-start.64) | collective-permute-done | bytes 262176 | tf_op jit(solution)/shard_map/ppermute | solution.py:47
  418.0 7.3 %collective-permute-done.60.refs_2_ = bf16[128,2048]{1,0:T(8,128)(2,1)S(1)} collective-permute-done((bf16[128,2048]{1,0:T(8,128)(2,1)S(1)}, bf16[128,2048]{1,0:T(8,128)(2,1)S(1)}, u32[]{:S(2)}, u32[]{:S(2)}) %collective-permute-start.60) | collective-permute-done | bytes 524320 | tf_op jit(solution)/shard_map/ppermute | solution.py:47
  439.5 5.3 %shard_map.255 = f32[1024,2048]{1,0:T(8,128)} custom-call(s32[8]{0:T(128)S(1)} %stack.100.place_ref.column_ref.block_ref, bf16[512,2048]{1,0:T(8,128)(2,1)S(1)} %shard_map.254.near_ref, bf16[512,2048]{1,0:T(8,128)(2,1)S(1)} %copy-done.33), custom_call_target="tpu_custom_call" | custom-call | bytes 1024 | tf_op jit(solution)/shard_map/pallas_call | solution.py:851
  444.9 9.7 %collective-permute-done.71 = bf16[64,2048]{1,0:T(8,128)(2,1)} collective-permute-done((bf16[64,2048]{1,0:T(8,128)(2,1)}, bf16[64,2048]{1,0:T(8,128)(2,1)}, u32[]{:S(2)}, u32[]{:S(2)}) %collective-permute-start.71) | collective-permute-done | bytes 262176 | tf_op jit(solution)/shard_map/ppermute | solution.py:47
  (352 shorter events, 201.1 us)
Async XLA Ops:
  7.2 129.6 %all-gather.2.cloned.1.call-start = ((), (), s32[]{:S(2)}) async-start(), calls=%async_computation.2 | async-start | bytes 9437184 | tf_op jit(solution)/shard_map/all_gather | solution.py:964
  16.9 29.7 %collective-permute-start.1 = (bf16[256,1024]{1,0:T(8,128)(2,1)}, bf16[256,1024]{1,0:T(8,128)(2,1)}, u32[]{:S(2)}, u32[]{:S(2)}) collective-permute-start(bf16[256,1024]{1,0:T(8,128)(2,1)} %refs_0_.1), channel_id=1, source_target_pairs={{0,16},{4,20},{8,24},{12,28},{16,0},{20,4},{24,8},{28,12},{1,17},{... | collective-permute-start | bytes 1572872 | tf_op jit(solution)/shard_map/ppermute | solution.py:47
  19.7 26.9 %collective-permute-start.2 = (bf16[256,1024]{1,0:T(8,128)(2,1)}, bf16[256,1024]{1,0:T(8,128)(2,1)}, u32[]{:S(2)}, u32[]{:S(2)}) collective-permute-start(bf16[256,1024]{1,0:T(8,128)(2,1)} %refs_0_.1), channel_id=1, source_target_pairs={{0,24},{4,28},{8,16},{12,20},{16,8},{20,12},{24,0},{28,4},{1,25},{... | collective-permute-start | bytes 1572872 | tf_op jit(solution)/shard_map/ppermute | solution.py:47
  46.6 315.3 %reduce-scatter.3.cloned.1.call-start = ((), (), s32[]{:S(2)}) async-start(), calls=%async_computation.3 | async-start | bytes 9437184 | tf_op jit(solution)/shard_map/reduce_scatter | solution.py:1028
  105.1 22.3 %collective-permute-start.18 = (bf16[128,2048]{1,0:T(8,128)(2,1)S(1)}, bf16[128,2048]{1,0:T(8,128)(2,1)S(1)}, u32[]{:S(2)}, u32[]{:S(2)}) collective-permute-start(bf16[128,2048]{1,0:T(8,128)(2,1)S(1)} %get-tuple-element.169.refs_0_.refs_10_), channel_id=1, source_target_pairs={{0,16},{4,20},{8,24},{12,28},{16,0},{20,4},{24,8},{28,12},{1,17},{... | collective-permute-start | bytes 1572872 | tf_op jit(solution)/shard_map/ppermute | solution.py:47
  105.9 23.1 %collective-permute-start.19 = (bf16[128,2048]{1,0:T(8,128)(2,1)S(1)}, bf16[128,2048]{1,0:T(8,128)(2,1)S(1)}, u32[]{:S(2)}, u32[]{:S(2)}) collective-permute-start(bf16[128,2048]{1,0:T(8,128)(2,1)S(1)} %get-tuple-element.169.refs_0_.refs_10_), channel_id=1, source_target_pairs={{0,24},{4,28},{8,16},{12,20},{16,8},{20,12},{24,0},{28,4},{1,25},{... | collective-permute-start | bytes 1572872 | tf_op jit(solution)/shard_map/ppermute | solution.py:47
  130.5 29.3 %collective-permute-start.26 = (bf16[512,2048]{1,0:T(8,128)(2,1)}, bf16[512,2048]{1,0:T(8,128)(2,1)}, u32[]{:S(2)}, u32[]{:S(2)}) collective-permute-start(bf16[512,2048]{1,0:T(8,128)(2,1)} %shard_map.242.x_ref.refs_0_), channel_id=1, source_target_pairs={{0,4},{4,0},{8,12},{12,8},{16,20},{20,16},{24,28},{28,24},{1,5},{5... | collective-permute-start | bytes 6291464 | tf_op jit(solution)/shard_map/ppermute | solution.py:47
  133.2 40.3 %collective-permute-start.23 = (bf16[128,2048]{1,0:T(8,128)(2,1)}, bf16[128,2048]{1,0:T(8,128)(2,1)}, u32[]{:S(2)}, u32[]{:S(2)}) collective-permute-start(bf16[128,2048]{1,0:T(8,128)(2,1)} %get-tuple-element.174.refs_0_.refs_11_), channel_id=1, source_target_pairs={{0,8},{4,12},{8,0},{12,4},{16,24},{20,28},{24,16},{28,20},{1,9},{5... | collective-permute-start | bytes 1572872 | tf_op jit(solution)/shard_map/ppermute | solution.py:47
  133.9 39.6 %collective-permute-start.24 = (bf16[128,2048]{1,0:T(8,128)(2,1)}, bf16[128,2048]{1,0:T(8,128)(2,1)}, u32[]{:S(2)}, u32[]{:S(2)}) collective-permute-start(bf16[128,2048]{1,0:T(8,128)(2,1)} %get-tuple-element.174.refs_0_.refs_11_), channel_id=1, source_target_pairs={{0,16},{4,20},{8,24},{12,28},{16,0},{20,4},{24,8},{28,12},{1,17},{... | collective-permute-start | bytes 1572872 | tf_op jit(solution)/shard_map/ppermute | solution.py:47
  135.5 38.0 %collective-permute-start.25 = (bf16[128,2048]{1,0:T(8,128)(2,1)}, bf16[128,2048]{1,0:T(8,128)(2,1)}, u32[]{:S(2)}, u32[]{:S(2)}) collective-permute-start(bf16[128,2048]{1,0:T(8,128)(2,1)} %get-tuple-element.174.refs_0_.refs_11_), channel_id=1, source_target_pairs={{0,24},{4,28},{8,16},{12,20},{16,8},{20,12},{24,0},{28,4},{1,25},{... | collective-permute-start | bytes 1572872 | tf_op jit(solution)/shard_map/ppermute | solution.py:47
  173.5 22.3 %collective-permute-start.27 = (bf16[512,2176]{1,0:T(8,128)(2,1)}, bf16[512,2176]{1,0:T(8,128)(2,1)}, u32[]{:S(2)}, u32[]{:S(2)}) collective-permute-start(bf16[512,2176]{1,0:T(8,128)(2,1)} %get-tuple-element.185), channel_id=1, source_target_pairs={{0,4},{4,0},{8,12},{12,8},{16,20},{20,16},{24,28},{28,24},{1,5},{5... | collective-permute-start | bytes 6684680 | tf_op jit(solution)/shard_map/ppermute | solution.py:47
  199.9 22.7 %collective-permute-start.29 = (bf16[128,2176]{1,0:T(8,128)(2,1)}, bf16[128,2176]{1,0:T(8,128)(2,1)}, u32[]{:S(2)}, u32[]{:S(2)}) collective-permute-start(bf16[128,2176]{1,0:T(8,128)(2,1)} %get-tuple-element.338), channel_id=1, source_target_pairs={{0,8},{4,12},{8,0},{12,4},{16,24},{20,28},{24,16},{28,20},{1,9},{5... | collective-permute-start | bytes 1671176 | tf_op jit(solution)/shard_map/ppermute | solution.py:47
  200.6 27.0 %collective-permute-start.30 = (bf16[128,2176]{1,0:T(8,128)(2,1)}, bf16[128,2176]{1,0:T(8,128)(2,1)}, u32[]{:S(2)}, u32[]{:S(2)}) collective-permute-start(bf16[128,2176]{1,0:T(8,128)(2,1)} %get-tuple-element.337), channel_id=1, source_target_pairs={{0,16},{4,20},{8,24},{12,28},{16,0},{20,4},{24,8},{28,12},{1,17},{... | collective-permute-start | bytes 1671176 | tf_op jit(solution)/shard_map/ppermute | solution.py:47
  202.2 25.4 %collective-permute-start.31 = (bf16[128,2176]{1,0:T(8,128)(2,1)}, bf16[128,2176]{1,0:T(8,128)(2,1)}, u32[]{:S(2)}, u32[]{:S(2)}) collective-permute-start(bf16[128,2176]{1,0:T(8,128)(2,1)} %get-tuple-element.336), channel_id=1, source_target_pairs={{0,24},{4,28},{8,16},{12,20},{16,8},{20,12},{24,0},{28,4},{1,25},{... | collective-permute-start | bytes 1671176 | tf_op jit(solution)/shard_map/ppermute | solution.py:47
  235.1 34.2 %collective-permute-start.39 = (bf16[128,2176]{1,0:T(8,128)(2,1)}, bf16[128,2176]{1,0:T(8,128)(2,1)}, u32[]{:S(2)}, u32[]{:S(2)}) collective-permute-start(bf16[128,2176]{1,0:T(8,128)(2,1)} %get-tuple-element.335), channel_id=1, source_target_pairs={{0,8},{4,12},{8,0},{12,4},{16,24},{20,28},{24,16},{28,20},{1,9},{5... | collective-permute-start | bytes 1671176 | tf_op jit(solution)/shard_map/ppermute | solution.py:47
  236.3 33.0 %collective-permute-start.40 = (bf16[128,2176]{1,0:T(8,128)(2,1)}, bf16[128,2176]{1,0:T(8,128)(2,1)}, u32[]{:S(2)}, u32[]{:S(2)}) collective-permute-start(bf16[128,2176]{1,0:T(8,128)(2,1)} %get-tuple-element.334), channel_id=1, source_target_pairs={{0,16},{4,20},{8,24},{12,28},{16,0},{20,4},{24,8},{28,12},{1,17},{... | collective-permute-start | bytes 1671176 | tf_op jit(solution)/shard_map/ppermute | solution.py:47
  237.1 32.2 %collective-permute-start.41 = (bf16[128,2176]{1,0:T(8,128)(2,1)}, bf16[128,2176]{1,0:T(8,128)(2,1)}, u32[]{:S(2)}, u32[]{:S(2)}) collective-permute-start(bf16[128,2176]{1,0:T(8,128)(2,1)} %get-tuple-element.333), channel_id=1, source_target_pairs={{0,24},{4,28},{8,16},{12,20},{16,8},{20,12},{24,0},{28,4},{1,25},{... | collective-permute-start | bytes 1671176 | tf_op jit(solution)/shard_map/ppermute | solution.py:47
  246.2 23.1 %collective-permute-start.36 = (bf16[32,2176]{1,0:T(8,128)(2,1)S(1)}, bf16[32,2176]{1,0:T(8,128)(2,1)S(1)}, u32[]{:S(2)}, u32[]{:S(2)}) collective-permute-start(bf16[32,2176]{1,0:T(8,128)(2,1)S(1)} %add_convert_fusion.18.refs_0_), channel_id=1, source_target_pairs={{0,2},{1,3},{2,0},{3,1},{4,6},{5,7},{6,4},{7,5},{8,10},{9,11},{10,... | collective-permute-start | bytes 417800 | tf_op jit(solution)/shard_map/ppermute | solution.py:47
  269.3 175.5 %reduce-scatter.5.cloned.1.call-start = ((), (), s32[]{:S(2)}) async-start(), calls=%async_computation.4 | async-start | bytes 6488064 | tf_op jit(solution)/shard_map/reduce_scatter | solution.py:1068
  329.5 32.3 %collective-permute-start.52 = (bf16[128,2048]{1,0:T(8,128)(2,1)}, bf16[128,2048]{1,0:T(8,128)(2,1)}, u32[]{:S(2)}, u32[]{:S(2)}) collective-permute-start(bf16[128,2048]{1,0:T(8,128)(2,1)} %get-tuple-element.341), channel_id=1, source_target_pairs={{0,8},{4,12},{8,0},{12,4},{16,24},{20,28},{24,16},{28,20},{1,9},{5... | collective-permute-start | bytes 1572872 | tf_op jit(solution)/shard_map/ppermute | solution.py:47
  330.7 31.1 %collective-permute-start.53 = (bf16[128,2048]{1,0:T(8,128)(2,1)}, bf16[128,2048]{1,0:T(8,128)(2,1)}, u32[]{:S(2)}, u32[]{:S(2)}) collective-permute-start(bf16[128,2048]{1,0:T(8,128)(2,1)} %get-tuple-element.340), channel_id=1, source_target_pairs={{0,16},{4,20},{8,24},{12,28},{16,0},{20,4},{24,8},{28,12},{1,17},{... | collective-permute-start | bytes 1572872 | tf_op jit(solution)/shard_map/ppermute | solution.py:47
  331.6 30.2 %collective-permute-start.54 = (bf16[128,2048]{1,0:T(8,128)(2,1)}, bf16[128,2048]{1,0:T(8,128)(2,1)}, u32[]{:S(2)}, u32[]{:S(2)}) collective-permute-start(bf16[128,2048]{1,0:T(8,128)(2,1)} %get-tuple-element.339), channel_id=1, source_target_pairs={{0,24},{4,28},{8,16},{12,20},{16,8},{20,12},{24,0},{28,4},{1,25},{... | collective-permute-start | bytes 1572872 | tf_op jit(solution)/shard_map/ppermute | solution.py:47
  337.2 24.6 %collective-permute-start.51 = (bf16[64,2304]{1,0:T(8,128)(2,1)}, bf16[64,2304]{1,0:T(8,128)(2,1)}, u32[]{:S(2)}, u32[]{:S(2)}) collective-permute-start(bf16[64,2304]{1,0:T(8,128)(2,1)} %get-tuple-element.342), channel_id=1, source_target_pairs={{0,3},{1,2},{2,1},{3,0},{4,7},{5,6},{6,5},{7,4},{8,11},{9,10},{10,... | collective-permute-start | bytes 884744 | tf_op jit(solution)/shard_map/ppermute | solution.py:47
  363.3 26.9 %collective-permute-start.55 = (bf16[64,2304]{1,0:T(8,128)(2,1)S(1)}, bf16[64,2304]{1,0:T(8,128)(2,1)S(1)}, u32[]{:S(2)}, u32[]{:S(2)}) collective-permute-start(bf16[64,2304]{1,0:T(8,128)(2,1)S(1)} %add_convert_fusion.15.refs_0_), channel_id=1, source_target_pairs={{0,1},{1,0},{2,3},{3,2},{4,5},{5,4},{6,7},{7,6},{8,9},{9,8},{10,11... | collective-permute-start | bytes 884744 | tf_op jit(solution)/shard_map/ppermute | solution.py:47
  363.4 26.8 %collective-permute-start.56 = (bf16[64,2304]{1,0:T(8,128)(2,1)S(1)}, bf16[64,2304]{1,0:T(8,128)(2,1)S(1)}, u32[]{:S(2)}, u32[]{:S(2)}) collective-permute-start(bf16[64,2304]{1,0:T(8,128)(2,1)S(1)} %add_convert_fusion.15.refs_0_), channel_id=1, source_target_pairs={{0,2},{1,3},{2,0},{3,1},{4,6},{5,7},{6,4},{7,5},{8,10},{9,11},{10,... | collective-permute-start | bytes 884744 | tf_op jit(solution)/shard_map/ppermute | solution.py:47
  365.8 26.7 %collective-permute-start.57 = (bf16[64,2304]{1,0:T(8,128)(2,1)S(1)}, bf16[64,2304]{1,0:T(8,128)(2,1)S(1)}, u32[]{:S(2)}, u32[]{:S(2)}) collective-permute-start(bf16[64,2304]{1,0:T(8,128)(2,1)S(1)} %add_convert_fusion.15.refs_0_), channel_id=1, source_target_pairs={{0,3},{1,2},{2,1},{3,0},{4,7},{5,6},{6,5},{7,4},{8,11},{9,10},{10,... | collective-permute-start | bytes 884744 | tf_op jit(solution)/shard_map/ppermute | solution.py:47
  368.1 27.9 %collective-permute-start.62 = (bf16[64,2048]{1,0:T(8,128)(2,1)S(1)}, bf16[64,2048]{1,0:T(8,128)(2,1)S(1)}, u32[]{:S(2)}, u32[]{:S(2)}) collective-permute-start(bf16[64,2048]{1,0:T(8,128)(2,1)S(1)} %get-tuple-element.347), channel_id=1, source_target_pairs={{0,1},{1,0},{2,3},{3,2},{4,5},{5,4},{6,7},{7,6},{8,9},{9,8},{10,11... | collective-permute-start | bytes 786440 | tf_op jit(solution)/shard_map/ppermute | solution.py:47
  392.5 25.5 %collective-permute-start.59 = (bf16[128,2048]{1,0:T(8,128)(2,1)S(1)}, bf16[128,2048]{1,0:T(8,128)(2,1)S(1)}, u32[]{:S(2)}, u32[]{:S(2)}) collective-permute-start(bf16[128,2048]{1,0:T(8,128)(2,1)S(1)} %add_convert_fusion.10.refs_0_), channel_id=1, source_target_pairs={{0,8},{4,12},{8,0},{12,4},{16,24},{20,28},{24,16},{28,20},{1,9},{5... | collective-permute-start | bytes 1572872 | tf_op jit(solution)/shard_map/ppermute | solution.py:47
  393.8 31.5 %collective-permute-start.60 = (bf16[128,2048]{1,0:T(8,128)(2,1)S(1)}, bf16[128,2048]{1,0:T(8,128)(2,1)S(1)}, u32[]{:S(2)}, u32[]{:S(2)}) collective-permute-start(bf16[128,2048]{1,0:T(8,128)(2,1)S(1)} %add_convert_fusion.10.refs_0_), channel_id=1, source_target_pairs={{0,16},{4,20},{8,24},{12,28},{16,0},{20,4},{24,8},{28,12},{1,17},{... | collective-permute-start | bytes 1572872 | tf_op jit(solution)/shard_map/ppermute | solution.py:47
  394.6 30.6 %collective-permute-start.61 = (bf16[128,2048]{1,0:T(8,128)(2,1)S(1)}, bf16[128,2048]{1,0:T(8,128)(2,1)S(1)}, u32[]{:S(2)}, u32[]{:S(2)}) collective-permute-start(bf16[128,2048]{1,0:T(8,128)(2,1)S(1)} %add_convert_fusion.10.refs_0_), channel_id=1, source_target_pairs={{0,24},{4,28},{8,16},{12,20},{16,8},{20,12},{24,0},{28,4},{1,25},{... | collective-permute-start | bytes 1572872 | tf_op jit(solution)/shard_map/ppermute | solution.py:47
  396.0 22.0 %collective-permute-start.64 = (bf16[64,2048]{1,0:T(8,128)(2,1)S(1)}, bf16[64,2048]{1,0:T(8,128)(2,1)S(1)}, u32[]{:S(2)}, u32[]{:S(2)}) collective-permute-start(bf16[64,2048]{1,0:T(8,128)(2,1)S(1)} %get-tuple-element.345), channel_id=1, source_target_pairs={{0,3},{1,2},{2,1},{3,0},{4,7},{5,6},{6,5},{7,4},{8,11},{9,10},{10,... | collective-permute-start | bytes 786440 | tf_op jit(solution)/shard_map/ppermute | solution.py:47
  428.8 25.7 %collective-permute-start.71 = (bf16[64,2048]{1,0:T(8,128)(2,1)}, bf16[64,2048]{1,0:T(8,128)(2,1)}, u32[]{:S(2)}, u32[]{:S(2)}) collective-permute-start(bf16[64,2048]{1,0:T(8,128)(2,1)} %get-tuple-element.332), channel_id=1, source_target_pairs={{0,3},{1,2},{2,1},{3,0},{4,7},{5,6},{6,5},{7,4},{8,11},{9,10},{10,... | collective-permute-start | bytes 786440 | tf_op jit(solution)/shard_map/ppermute | solution.py:47
  (107 other events, 1093.8 us)
Sparse Core Ops, SparseCore 0:
  46.7 54.6 all-gather.1
  269.4 74.9 reduce-scatter.2
  348.2 68.1 reduce-scatter.4

commit v6 on v5

--- a/solution.py
+++ b/solution.py
@@ -188,13 +188,39 @@
 
 
 def expert_kernel(
-    local, place_ref, x_ref, g0_ref, g1_ref, ids0_ref, ids1_ref, router_ref, wgu_ref, wd_ref,
-    dx_ref, joined_ref, hidden_ref,
+    local,
+    place_ref,
+    x_ref,
+    g0_ref,
+    g1_ref,
+    ids0_ref,
+    ids1_ref,
+    router_ref,
+    wgu_in_ref,
+    wd_in_ref,
+    dx_ref,
+    joined_ref,
+    hidden_ref,
+    wgu_ref,
+    wd_ref,
+    arrived,
 ):
     rows = x_ref.shape[0]
     features = x_ref.shape[1]
     expert_count = router_ref.shape[1]
     hidden_count = wd_ref.shape[0]
+    group = 3
+    count = hidden_count // LANES // group
+    copies = [
+        pltpu.make_async_copy(wgu_in_ref, wgu_ref, arrived.at[0]),
+        pltpu.make_async_copy(wd_in_ref, wd_ref, arrived.at[1]),
+    ]
+
+    @pl.when(pl.program_id(0) == 0)
+    def _():
+        for copy in copies:
+            copy.start()
+
     extra = dx_ref.shape[1] - features
     base = place_ref[0]
     x = x_ref[...]
@@ -216,7 +242,11 @@
     left = lax.broadcasted_iota(jnp.int32, (rows, LANES), 1) < PAIR
     per_expert = hidden_count // local // PAIR
     gate_sum = [jnp.zeros((rows, LANES), F32) for _ in range(local)]
-    group = 3
+
+    @pl.when(pl.program_id(0) == 0)
+    def _():
+        for copy in copies:
+            copy.wait()
 
     def products(q):
         wide = group * LANES
@@ -264,7 +294,6 @@
                 left, pltpu.roll(dg, PAIR, 1), du
             ).astype(BF16)
 
-    count = hidden_count // LANES // group
     waiting = []
     for q in range(count):
         waiting.append((q, *products(q)))
@@ -294,7 +323,8 @@
     extra = -(-2 * expert_count // LANES) * LANES
     place = jnp.stack([lax.axis_index("ep") * local] + list(where)).astype(jnp.int32)
     found = lambda width, j: pl.BlockSpec((block, width), lambda i, s: (s[1 + 2 * i + j], 0))
-    resident = pl.BlockSpec(memory_space=pltpu.VMEM)
+    whole = pl.BlockSpec(router.shape, lambda i, s: (0, 0), pipeline_mode=pl.Buffered(1))
+    anywhere = pl.BlockSpec(memory_space=pl.ANY)
     by_rows = lambda width: pl.BlockSpec((tile, width), lambda i, s: (i, 0))
     in_specs = [
         by_rows(features),
@@ -302,11 +332,11 @@
         found(features, 1),
         found(TOP, 0),
         found(TOP, 1),
-        resident,
-        resident,
-        resident,
+        whole,
+        anywhere,
+        anywhere,
     ]
-    (g,) = in_hbm(g)
+    g, wgu, wd = in_hbm(g, wgu, wd)
     operands = [place, x, g, g, ids, ids, router, wgu, wd]
     return pl.pallas_call(
         functools.partial(expert_kernel, local),
@@ -319,13 +349,18 @@
                 by_rows(wgu.shape[1]),
                 by_rows(wd.shape[0]),
             ],
+            scratch_shapes=[
+                pltpu.VMEM(wgu.shape, BF16),
+                pltpu.VMEM(wd.shape, BF16),
+                pltpu.SemaphoreType.DMA((2,)),
+            ],
         ),
         out_shape=[
-            jax.ShapeDtypeStruct((tokens, features + extra), BF16),
-            jax.ShapeDtypeStruct((tokens, wgu.shape[1]), BF16),
-            jax.ShapeDtypeStruct((tokens, wd.shape[0]), BF16),
+            pltpu.HBM((tokens, features + extra), BF16),
+            pltpu.HBM((tokens, wgu.shape[1]), BF16),
+            pltpu.HBM((tokens, wd.shape[0]), BF16),
         ],
-        compiler_params=pltpu.CompilerParams(vmem_limit_bytes=20 * 1024 * 1024),
+        compiler_params=pltpu.CompilerParams(vmem_limit_bytes=32 * 1024 * 1024),
         cost_estimate=SMALL,
     )(*operands)
 
@@ -423,7 +458,7 @@
             + [pl.BlockSpec((width, features), lambda i, s: (0, 0))],
             out_specs=pl.BlockSpec((2 * block, features), lambda i, s: (s[i], 0)),
         ),
-        out_shape=jax.ShapeDtypeStruct((2 * block * count, features), BF16),
+        out_shape=pltpu.HBM((2 * block * count, features), BF16),
         compiler_params=pltpu.CompilerParams(vmem_limit_bytes=24 * 1024 * 1024),
         cost_estimate=SMALL,
     )(jnp.stack(where).astype(jnp.int32), *in_hbm(*hidden, wd))
@@ -679,7 +714,7 @@
         in_specs=in_smem() + in_vmem(len(pieces) + 2),
         out_specs=in_vmem(2),
         out_shape=[
-            jax.ShapeDtypeStruct(hidden.shape, F32),
+            pltpu.HBM(hidden.shape, F32),
             jax.ShapeDtypeStruct(hidden.shape, BF16),
         ],
         compiler_params=pltpu.CompilerParams(vmem_limit_bytes=6 * 1024 * 1024),

time: 477 us -> 468 us (0.981)
  local copies, waits for them, and re-layouts: 63.8 us -> 34 us
  Pallas kernels: 144 us -> 164 us
    unnamed x138 -> x80, local copies, waits for them, and re-layouts: 43.6 us -> 14.9 us
    pallas_call x4, Pallas kernels: 52.4 us -> 69.4 us  [run_experts(): pl.pallas_call(functools.partial(expert_kernel, local), grid_spec=pltpu.P...]
  transfers between devices with their start and end apart: 75 -> 75, of which waited for: 35 -> 37; matrix products, arithmetic and copies ran while one was open for 6% -> 7% of each run, Pallas kernels for 30% -> 35%
where the time goes in v6:
time: 468 us; the launch traced here: 463 us
  Pallas kernels  164 us (35%)
  waiting for transfers between devices  142 us (30%)
  starting transfers between devices  80 us (17%)
  local copies, waits for them, and re-layouts  34 us (7%)
  other arithmetic  26.8 us (6%)
  between operations  15.4 us (3%)
    ppermute x72, waiting for transfers between devices, swap(): return lax.ppermute(value, axis, [(i, i ^ mask) for i in range(count)])  142 us
    ppermute x72, starting transfers between devices, swap(): return lax.ppermute(value, axis, [(i, i ^ mask) for i in range(count)])  79.4 us
    pallas_call x4, Pallas kernels, run_experts(): pl.pallas_call(functools.partial(expert_kernel, local), grid_spec=pltpu.P...  69.4 us
    pallas_call x1, Pallas kernels, gate_up_product(): pl.pallas_call(gate_up_kernel, grid=(features // tile,), in_specs=[pl.Blo...  19.2 us
    unnamed x80, local copies, waits for them, and re-layouts  14.9 us
    convert_element_type x11, other arithmetic, plus(): return total.astype(values[0].dtype)  14.3 us
    pallas_call x1, Pallas kernels, attention_back(): pl.pallas_call(functools.partial(attention_back_kernel, key_heads), in_sp...  13.3 us
    pallas_call x1, Pallas kernels, down_product(): pl.pallas_call(down_kernel, grid_spec=pltpu.PrefetchScalarGridSpec(num_sc...  13.3 us
  transfers between devices with their start and end apart: 75, of which 37 were waited for; matrix products, arithmetic and copies ran while one was open for 7% of the time, Pallas kernels for 35%

profile of v6, /device:TPU:8, one launch (start us, length us, event | category | flops | bytes accessed | tf_op | source)
XLA Modules:
  0.0 462.6 jit_solution(17338177665015617643)
XLA Ops:
  35.3 11.3 %collective-permute-done.1.refs_2_ = bf16[256,1024]{1,0:T(8,128)(2,1)} collective-permute-done((bf16[256,1024]{1,0:T(8,128)(2,1)}, bf16[256,1024]{1,0:T(8,128)(2,1)}, u32[]{:S(2)}, u32[]{:S(2)}) %collective-permute-start.1) | collective-permute-done | bytes 524320 | tf_op jit(solution)/shard_map/ppermute | solution.py:47
  50.8 6.4 %copy.56 = bf16[4,256,8,384]{3,2,0,1:T(8,128)(2,1)} copy(bf16[4,256,8,384]{3,2,1,0:T(8,128)(2,1)} %bitcast.77) | data formatting | bytes 12582912 | tf_op jit(solution)/shard_map/reshape | solution.py:1009
  57.2 7.8 %shard_map.239 = (f32[256,1152]{1,0:T(8,128)S(1)}, bf16[256,1280]{1,0:T(8,128)(2,1)S(1)}, bf16[256,1024]{1,0:T(8,128)(2,1)S(1)}, f32[256,8]{1,0:T(8,128)S(1)}, b...) custom-call(bf16[256,2048]{1,0:T(8,128)(2,1)S(1)} %dynamic-slice_dynamic-update-slice_fusion.x_ref, ...), custom_call_target="tpu_custom_call" | custom-call | bytes 1024 | tf_op jit(solution)/shard_map/pallas_call | solution.py:564
  83.3 4.1 collective-permute-done.15
  87.4 9.3 %collective-permute-done.16 = bf16[32,2048]{1,0:T(8,128)(2,1)S(1)} collective-permute-done((bf16[32,2048]{1,0:T(8,128)(2,1)S(1)}, bf16[32,2048]{1,0:T(8,128)(2,1)S(1)}, u32[]{:S(2)}, u32[]{:S(2)}) %collective-permute-start.16) | collective-permute-done | bytes 131104 | tf_op jit(solution)/shard_map/ppermute | solution.py:47
  98.7 3.4 collective-permute-done.13.refs_3_
  115.3 3.4 collective-permute-done.21.refs_2_
  121.5 8.2 %collective-permute-done.19.refs_3_ = bf16[128,2048]{1,0:T(8,128)(2,1)S(1)} collective-permute-done((bf16[128,2048]{1,0:T(8,128)(2,1)S(1)}, bf16[128,2048]{1,0:T(8,128)(2,1)S(1)}, u32[]{:S(2)}, u32[]{:S(2)}) %collective-permute-start.19) | collective-permute-done | bytes 524320 | tf_op jit(solution)/shard_map/ppermute | solution.py:47
  136.6 17.6 %shard_map.244 = (bf16[512,2176]{1,0:T(8,128)(2,1)}, bf16[512,1536]{1,0:T(8,128)(2,1)}, bf16[512,768]{1,0:T(8,128)(2,1)}) custom-call(s32[5]{0:T(128)S(1)} %stack.111.place_ref, bf16[512,2048]{1,0:T(8,128)(2,1)} %shard_map.242.x_ref.refs_0_, bf16[2048,2048]{1,0:T(8,128)(2,1)} %all-gather.2.cloned.1.call-done.g0_ref.g1_ref.refs_4_, ...), custom_call_target="tpu_custom_call" | custom-call | bytes 1024 | tf_op jit(solution)/shard_map/pallas_call | solution.py:341
  154.2 17.2 %shard_map.243 = (bf16[512,2176]{1,0:T(8,128)(2,1)}, bf16[512,1536]{1,0:T(8,128)(2,1)}, bf16[512,768]{1,0:T(8,128)(2,1)}) custom-call(s32[5]{0:T(128)S(1)} %stack.106.place_ref, bf16[512,2048]{1,0:T(8,128)(2,1)} %collective-permute-done.26.x_ref.refs_1_, bf16[2048,2048]{1,0:T(8,128)(2,1)} %all-gather.2.cloned.1.call-done.g0_ref.g1_ref.refs_4_, ...), custom_call_target="tpu_custom_call" | custom-call | bytes 1024 | tf_op jit(solution)/shard_map/pallas_call | solution.py:341
  174.6 17.4 %shard_map.246 = (bf16[512,2176]{1,0:T(8,128)(2,1)}, bf16[512,1536]{1,0:T(8,128)(2,1)}, bf16[512,768]{1,0:T(8,128)(2,1)}) custom-call(s32[5]{0:T(128)S(1)} %stack.228.place_ref, bf16[512,2048]{1,0:T(8,128)(2,1)} %shard_map.245.x_ref.refs_2_, bf16[2048,2048]{1,0:T(8,128)(2,1)} %all-gather.2.cloned.1.call-done.g0_ref.g1_ref.refs_4_, ...), custom_call_target="tpu_custom_call" | custom-call | bytes 1024 | tf_op jit(solution)/shard_map/pallas_call | solution.py:341
  198.4 17.2 %shard_map.247 = (bf16[512,2176]{1,0:T(8,128)(2,1)}, bf16[512,1536]{1,0:T(8,128)(2,1)}, bf16[512,768]{1,0:T(8,128)(2,1)}) custom-call(s32[5]{0:T(128)S(1)} %stack.233.place_ref, bf16[512,2048]{1,0:T(8,128)(2,1)} %collective-permute-done.28.x_ref.refs_3_, bf16[2048,2048]{1,0:T(8,128)(2,1)} %all-gather.2.cloned.1.call-done.g0_ref.g1_ref.refs_4_, ...), custom_call_target="tpu_custom_call" | custom-call | bytes 1024 | tf_op jit(solution)/shard_map/pallas_call | solution.py:341
  215.7 6.4 %collective-permute-done.30 = bf16[128,2176]{1,0:T(8,128)(2,1)S(1)} collective-permute-done((bf16[128,2176]{1,0:T(8,128)(2,1)}, bf16[128,2176]{1,0:T(8,128)(2,1)S(1)}, u32[]{:S(2)}, u32[]{:S(2)}) %collective-permute-start.30) | collective-permute-done | bytes 557088 | tf_op jit(solution)/shard_map/ppermute | solution.py:47
  232.6 4.5 collective-permute-done.33
  243.4 3.4 collective-permute-done.35.refs_1_
  248.7 13.1 %shard_map.248 = bf16[2048,2048]{1,0:T(8,128)(2,1)} custom-call(s32[8]{0:T(128)S(1)} %stack.100.place_ref.column_ref.block_ref, bf16[512,768]{1,0:T(8,128)(2,1)} %get-tuple-element.203.upper0_ref.refs_0_, bf16[512,768]{1,0:T(8,128)(2,1)} %get-tuple-element.204.upper1_ref.refs_1_, bf16[512,768]{1,0:T(8,128)(2,1)} %get-tuple-element.205.lower0_ref.refs_2_, ...), custom_call_target="tpu_custom_call" | custom-call | bytes 1024 | tf_op jit(solution)/shard_map/pallas_call | solution.py:452
  269.3 3.4 collective-permute-done.43
  272.7 3.6 collective-permute-done.44
  283.0 3.6 collective-permute-done.46.refs_6_
  286.7 3.6 collective-permute-done.47.refs_7_
  290.2 7.3 %shard_map.249 = (f32[256,2048]{1,0:T(8,128)S(1)}, bf16[256,2048]{1,0:T(8,128)(2,1)S(1)}, bf16[2048,128]{1,0:T(8,128)(2,1)S(1)}, bf16[512,2048]{1,0:T(8,128)(2,1)S(1)}, bf16[512,2048]{1,0:T(8,128)(2,1)S(1)}) custom-call(s32[4]{0:T(128)S(1)} %pad_add_fusion.place_ref, s32[8]{0:T(128)S(1)} %stack.100.place_ref.column_ref.block_ref, ...), custom_call_target="tpu_custom_call" | custom-call | bytes 1024 | tf_op jit(solution)/shard_map/pallas_call | solution.py:808
  300.7 13.3 %shard_map.250 = (bf16[256,2304]{1,0:T(8,128)(2,1)S(1)}, bf16[2048,1408]{1,0:T(8,128)(2,1)S(1)}) custom-call(s32[8]{0:T(128)S(1)} %stack.100.place_ref.column_ref.block_ref, bf16[256,2048]{1,0:T(8,128)(2,1)} %copy-done.15, bf16[1024,2048]{1,0:T(8,128)(2,1)} %wo_ref.3, f32[256,1152]{1,0:T(8,128)} %copy-done.14, bf16[256,1280]{1,0:T(8,128)(2,1)} %copy-done.16, ...), custom_call_target="tpu_custom_call" | custom-call | bytes 1024 | tf_op jit(solution)/shard_map/pallas_call | solution.py:680
  329.9 13.3 %shard_map.251 = f32[768,2048]{1,0:T(8,128)} custom-call(s32[16]{0:T(128)} %stack.234.place_ref, bf16[512,768]{1,0:T(8,128)(2,1)} %get-tuple-element.203.upper0_ref.refs_0_, bf16[512,768]{1,0:T(8,128)(2,1)} %get-tuple-element.204.upper1_ref.refs_1_, bf16[512,768]{1,0:T(8,128)(2,1)} %get-tuple-element.205.lower0_ref.refs_2_, ...), custom_call_target="tpu_custom_call" | custom-call | bytes 1024 | tf_op jit(solution)/shard_map/pallas_call | solution.py:416
  343.2 3.2 collective-permute-done.50
  346.4 7.5 %collective-permute-done.51 = bf16[64,2304]{1,0:T(8,128)(2,1)} collective-permute-done((bf16[64,2304]{1,0:T(8,128)(2,1)}, bf16[64,2304]{1,0:T(8,128)(2,1)}, u32[]{:S(2)}, u32[]{:S(2)}) %collective-permute-start.51) | collective-permute-done | bytes 294944 | tf_op jit(solution)/shard_map/ppermute | solution.py:47
  361.7 19.2 %shard_map.252 = f32[4,2048,384]{2,1,0:T(8,128)} custom-call(bf16[512,2048]{1,0:T(8,128)(2,1)} %shard_map.242.x_ref.refs_0_, bf16[512,2048]{1,0:T(8,128)(2,1)} %collective-permute-done.26.x_ref.refs_1_, bf16[512,2048]{1,0:T(8,128)(2,1)} %shard_map.245.x_ref.refs_2_, bf16[512,2048]{1,0:T(8,128)(2,1)} %collective-permute-done.28.x_ref.refs_3_, ...), custom_call_target="tpu_custom_call" | custom-call | bytes 1024 | tf_op jit(solution)/shard_map/pallas_call | solution.py:387
  389.5 5.1 %shard_map.253 = (f32[256,2048]{1,0:T(8,128)}, f32[8,512]{1,0:T(8,128)S(1)}) custom-call(s32[4]{0:T(128)S(1)} %pad_add_fusion.place_ref, s32[8]{0:T(128)S(1)} %stack.100.place_ref.column_ref.block_ref, bf16[64,2304]{1,0:T(8,128)(2,1)S(1)} %add_convert_fusion.15.refs_0_, bf16[64,2304]{1,0:T(8,128)(2,1)S(1)} %collective-permute-done.55.refs_1_, ...), custom_call_target="tpu_custom_call" | custom-call | bytes 1024 | tf_op jit(solution)/shard_map/pallas_call | solution.py:860
  394.6 10.9 %collective-permute-done.63 = bf16[64,2048]{1,0:T(8,128)(2,1)S(1)} collective-permute-done((bf16[64,2048]{1,0:T(8,128)(2,1)S(1)}, bf16[64,2048]{1,0:T(8,128)(2,1)S(1)}, u32[]{:S(2)}, u32[]{:S(2)}) %collective-permute-start.63) | collective-permute-done | bytes 262176 | tf_op jit(solution)/shard_map/ppermute | solution.py:47
  405.6 5.3 %collective-permute-done.64 = bf16[64,2048]{1,0:T(8,128)(2,1)S(1)} collective-permute-done((bf16[64,2048]{1,0:T(8,128)(2,1)S(1)}, bf16[64,2048]{1,0:T(8,128)(2,1)S(1)}, u32[]{:S(2)}, u32[]{:S(2)}) %collective-permute-start.64) | collective-permute-done | bytes 262176 | tf_op jit(solution)/shard_map/ppermute | solution.py:47
  410.9 6.5 %collective-permute-done.61.refs_3_ = bf16[128,2048]{1,0:T(8,128)(2,1)S(1)} collective-permute-done((bf16[128,2048]{1,0:T(8,128)(2,1)S(1)}, bf16[128,2048]{1,0:T(8,128)(2,1)S(1)}, u32[]{:S(2)}, u32[]{:S(2)}) %collective-permute-start.61) | collective-permute-done | bytes 524320 | tf_op jit(solution)/shard_map/ppermute | solution.py:47
  431.8 5.1 %shard_map.255 = f32[1024,2048]{1,0:T(8,128)} custom-call(s32[8]{0:T(128)S(1)} %stack.100.place_ref.column_ref.block_ref, bf16[512,2048]{1,0:T(8,128)(2,1)S(1)} %shard_map.254.near_ref, bf16[512,2048]{1,0:T(8,128)(2,1)S(1)} %copy-done.8), custom_call_target="tpu_custom_call" | custom-call | bytes 1024 | tf_op jit(solution)/shard_map/pallas_call | solution.py:886
  439.5 7.2 %collective-permute-done.71 = bf16[64,2048]{1,0:T(8,128)(2,1)} collective-permute-done((bf16[64,2048]{1,0:T(8,128)(2,1)}, bf16[64,2048]{1,0:T(8,128)(2,1)}, u32[]{:S(2)}, u32[]{:S(2)}) %collective-permute-start.71) | collective-permute-done | bytes 262176 | tf_op jit(solution)/shard_map/ppermute | solution.py:47
  (293 shorter events, 178.7 us)
Async XLA Ops:
  7.2 129.4 %all-gather.2.cloned.1.call-start = ((), (), s32[]{:S(2)}) async-start(), calls=%async_computation.2 | async-start | bytes 9437184 | tf_op jit(solution)/shard_map/all_gather | solution.py:999
  16.9 29.7 %collective-permute-start.1 = (bf16[256,1024]{1,0:T(8,128)(2,1)}, bf16[256,1024]{1,0:T(8,128)(2,1)}, u32[]{:S(2)}, u32[]{:S(2)}) collective-permute-start(bf16[256,1024]{1,0:T(8,128)(2,1)} %refs_0_.1), channel_id=1, source_target_pairs={{0,16},{4,20},{8,24},{12,28},{16,0},{20,4},{24,8},{28,12},{1,17},{... | collective-permute-start | bytes 1572872 | tf_op jit(solution)/shard_map/ppermute | solution.py:47
  19.7 26.9 %collective-permute-start.2 = (bf16[256,1024]{1,0:T(8,128)(2,1)}, bf16[256,1024]{1,0:T(8,128)(2,1)}, u32[]{:S(2)}, u32[]{:S(2)}) collective-permute-start(bf16[256,1024]{1,0:T(8,128)(2,1)} %refs_0_.1), channel_id=1, source_target_pairs={{0,24},{4,28},{8,16},{12,20},{16,8},{20,12},{24,0},{28,4},{1,25},{... | collective-permute-start | bytes 1572872 | tf_op jit(solution)/shard_map/ppermute | solution.py:47
  46.6 307.4 %reduce-scatter.3.cloned.1.call-start = ((), (), s32[]{:S(2)}) async-start(), calls=%async_computation.3 | async-start | bytes 9437184 | tf_op jit(solution)/shard_map/reduce_scatter | solution.py:1063
  74.2 22.6 %collective-permute-start.16 = (bf16[32,2048]{1,0:T(8,128)(2,1)S(1)}, bf16[32,2048]{1,0:T(8,128)(2,1)S(1)}, u32[]{:S(2)}, u32[]{:S(2)}) collective-permute-start(bf16[32,2048]{1,0:T(8,128)(2,1)S(1)} %get-tuple-element.358), channel_id=1, source_target_pairs={{0,3},{1,2},{2,1},{3,0},{4,7},{5,6},{6,5},{7,4},{8,11},{9,10},{10,... | collective-permute-start | bytes 393224 | tf_op jit(solution)/shard_map/ppermute | solution.py:47
  106.0 23.7 %collective-permute-start.19 = (bf16[128,2048]{1,0:T(8,128)(2,1)S(1)}, bf16[128,2048]{1,0:T(8,128)(2,1)S(1)}, u32[]{:S(2)}, u32[]{:S(2)}) collective-permute-start(bf16[128,2048]{1,0:T(8,128)(2,1)S(1)} %get-tuple-element.169.refs_0_.refs_10_), channel_id=1, source_target_pairs={{0,24},{4,28},{8,16},{12,20},{16,8},{20,12},{24,0},{28,4},{1,25},{... | collective-permute-start | bytes 1572872 | tf_op jit(solution)/shard_map/ppermute | solution.py:47
  131.1 23.1 %collective-permute-start.26 = (bf16[512,2048]{1,0:T(8,128)(2,1)}, bf16[512,2048]{1,0:T(8,128)(2,1)}, u32[]{:S(2)}, u32[]{:S(2)}) collective-permute-start(bf16[512,2048]{1,0:T(8,128)(2,1)} %shard_map.242.x_ref.refs_0_), channel_id=1, source_target_pairs={{0,4},{4,0},{8,12},{12,8},{16,20},{20,16},{24,28},{28,24},{1,5},{5... | collective-permute-start | bytes 6291464 | tf_op jit(solution)/shard_map/ppermute | solution.py:47
  132.9 38.5 %collective-permute-start.23 = (bf16[128,2048]{1,0:T(8,128)(2,1)S(1)}, bf16[128,2048]{1,0:T(8,128)(2,1)S(1)}, u32[]{:S(2)}, u32[]{:S(2)}) collective-permute-start(bf16[128,2048]{1,0:T(8,128)(2,1)S(1)} %get-tuple-element.174.refs_0_.refs_11_), channel_id=1, source_target_pairs={{0,8},{4,12},{8,0},{12,4},{16,24},{20,28},{24,16},{28,20},{1,9},{5... | collective-permute-start | bytes 1572872 | tf_op jit(solution)/shard_map/ppermute | solution.py:47
  133.6 37.8 %collective-permute-start.24 = (bf16[128,2048]{1,0:T(8,128)(2,1)S(1)}, bf16[128,2048]{1,0:T(8,128)(2,1)S(1)}, u32[]{:S(2)}, u32[]{:S(2)}) collective-permute-start(bf16[128,2048]{1,0:T(8,128)(2,1)S(1)} %get-tuple-element.174.refs_0_.refs_11_), channel_id=1, source_target_pairs={{0,16},{4,20},{8,24},{12,28},{16,0},{20,4},{24,8},{28,12},{1,17},{... | collective-permute-start | bytes 1572872 | tf_op jit(solution)/shard_map/ppermute | solution.py:47
  135.2 36.2 %collective-permute-start.25 = (bf16[128,2048]{1,0:T(8,128)(2,1)S(1)}, bf16[128,2048]{1,0:T(8,128)(2,1)}, u32[]{:S(2)}, u32[]{:S(2)}) collective-permute-start(bf16[128,2048]{1,0:T(8,128)(2,1)S(1)} %get-tuple-element.174.refs_0_.refs_11_), channel_id=1, source_target_pairs={{0,24},{4,28},{8,16},{12,20},{16,8},{20,12},{24,0},{28,4},{1,25},{... | collective-permute-start | bytes 1572872 | tf_op jit(solution)/shard_map/ppermute | solution.py:47
  194.8 20.8 %collective-permute-start.29 = (bf16[128,2176]{1,0:T(8,128)(2,1)}, bf16[128,2176]{1,0:T(8,128)(2,1)S(1)}, u32[]{:S(2)}, u32[]{:S(2)}) collective-permute-start(bf16[128,2176]{1,0:T(8,128)(2,1)} %get-tuple-element.338), channel_id=1, source_target_pairs={{0,8},{4,12},{8,0},{12,4},{16,24},{20,28},{24,16},{28,20},{1,9},{5... | collective-permute-start | bytes 1671176 | tf_op jit(solution)/shard_map/ppermute | solution.py:47
  195.6 26.4 %collective-permute-start.30 = (bf16[128,2176]{1,0:T(8,128)(2,1)}, bf16[128,2176]{1,0:T(8,128)(2,1)S(1)}, u32[]{:S(2)}, u32[]{:S(2)}) collective-permute-start(bf16[128,2176]{1,0:T(8,128)(2,1)} %get-tuple-element.337), channel_id=1, source_target_pairs={{0,16},{4,20},{8,24},{12,28},{16,0},{20,4},{24,8},{28,12},{1,17},{... | collective-permute-start | bytes 1671176 | tf_op jit(solution)/shard_map/ppermute | solution.py:47
  197.2 24.9 %collective-permute-start.31 = (bf16[128,2176]{1,0:T(8,128)(2,1)}, bf16[128,2176]{1,0:T(8,128)(2,1)}, u32[]{:S(2)}, u32[]{:S(2)}) collective-permute-start(bf16[128,2176]{1,0:T(8,128)(2,1)} %get-tuple-element.336), channel_id=1, source_target_pairs={{0,24},{4,28},{8,16},{12,20},{16,8},{20,12},{24,0},{28,4},{1,25},{... | collective-permute-start | bytes 1671176 | tf_op jit(solution)/shard_map/ppermute | solution.py:47
  229.1 32.7 %collective-permute-start.39 = (bf16[128,2176]{1,0:T(8,128)(2,1)}, bf16[128,2176]{1,0:T(8,128)(2,1)S(1)}, u32[]{:S(2)}, u32[]{:S(2)}) collective-permute-start(bf16[128,2176]{1,0:T(8,128)(2,1)} %get-tuple-element.335), channel_id=1, source_target_pairs={{0,8},{4,12},{8,0},{12,4},{16,24},{20,28},{24,16},{28,20},{1,9},{5... | collective-permute-start | bytes 1671176 | tf_op jit(solution)/shard_map/ppermute | solution.py:47
  230.5 31.3 %collective-permute-start.40 = (bf16[128,2176]{1,0:T(8,128)(2,1)}, bf16[128,2176]{1,0:T(8,128)(2,1)S(1)}, u32[]{:S(2)}, u32[]{:S(2)}) collective-permute-start(bf16[128,2176]{1,0:T(8,128)(2,1)} %get-tuple-element.334), channel_id=1, source_target_pairs={{0,16},{4,20},{8,24},{12,28},{16,0},{20,4},{24,8},{28,12},{1,17},{... | collective-permute-start | bytes 1671176 | tf_op jit(solution)/shard_map/ppermute | solution.py:47
  231.1 30.7 %collective-permute-start.41 = (bf16[128,2176]{1,0:T(8,128)(2,1)}, bf16[128,2176]{1,0:T(8,128)(2,1)S(1)}, u32[]{:S(2)}, u32[]{:S(2)}) collective-permute-start(bf16[128,2176]{1,0:T(8,128)(2,1)} %get-tuple-element.333), channel_id=1, source_target_pairs={{0,24},{4,28},{8,16},{12,20},{16,8},{20,12},{24,0},{28,4},{1,25},{... | collective-permute-start | bytes 1671176 | tf_op jit(solution)/shard_map/ppermute | solution.py:47
  240.4 21.4 %collective-permute-start.36 = (bf16[32,2176]{1,0:T(8,128)(2,1)S(1)}, bf16[32,2176]{1,0:T(8,128)(2,1)S(1)}, u32[]{:S(2)}, u32[]{:S(2)}) collective-permute-start(bf16[32,2176]{1,0:T(8,128)(2,1)S(1)} %add_convert_fusion.18.refs_0_), channel_id=1, source_target_pairs={{0,2},{1,3},{2,0},{3,1},{4,6},{5,7},{6,4},{7,5},{8,10},{9,11},{10,... | collective-permute-start | bytes 417800 | tf_op jit(solution)/shard_map/ppermute | solution.py:47
  261.8 175.1 %reduce-scatter.5.cloned.1.call-start = ((), (), s32[]{:S(2)}) async-start(), calls=%async_computation.4 | async-start | bytes 6488064 | tf_op jit(solution)/shard_map/reduce_scatter | solution.py:1103
  321.6 32.3 %collective-permute-start.52 = (bf16[128,2048]{1,0:T(8,128)(2,1)}, bf16[128,2048]{1,0:T(8,128)(2,1)}, u32[]{:S(2)}, u32[]{:S(2)}) collective-permute-start(bf16[128,2048]{1,0:T(8,128)(2,1)} %get-tuple-element.341), channel_id=1, source_target_pairs={{0,8},{4,12},{8,0},{12,4},{16,24},{20,28},{24,16},{28,20},{1,9},{5... | collective-permute-start | bytes 1572872 | tf_op jit(solution)/shard_map/ppermute | solution.py:47
  323.0 30.9 %collective-permute-start.53 = (bf16[128,2048]{1,0:T(8,128)(2,1)}, bf16[128,2048]{1,0:T(8,128)(2,1)}, u32[]{:S(2)}, u32[]{:S(2)}) collective-permute-start(bf16[128,2048]{1,0:T(8,128)(2,1)} %get-tuple-element.340), channel_id=1, source_target_pairs={{0,16},{4,20},{8,24},{12,28},{16,0},{20,4},{24,8},{28,12},{1,17},{... | collective-permute-start | bytes 1572872 | tf_op jit(solution)/shard_map/ppermute | solution.py:47
  323.7 30.4 %collective-permute-start.54 = (bf16[128,2048]{1,0:T(8,128)(2,1)}, bf16[128,2048]{1,0:T(8,128)(2,1)}, u32[]{:S(2)}, u32[]{:S(2)}) collective-permute-start(bf16[128,2048]{1,0:T(8,128)(2,1)} %get-tuple-element.339), channel_id=1, source_target_pairs={{0,24},{4,28},{8,16},{12,20},{16,8},{20,12},{24,0},{28,4},{1,25},{... | collective-permute-start | bytes 1572872 | tf_op jit(solution)/shard_map/ppermute | solution.py:47
  325.1 21.3 %collective-permute-start.50 = (bf16[64,2304]{1,0:T(8,128)(2,1)}, bf16[64,2304]{1,0:T(8,128)(2,1)}, u32[]{:S(2)}, u32[]{:S(2)}) collective-permute-start(bf16[64,2304]{1,0:T(8,128)(2,1)} %get-tuple-element.343), channel_id=1, source_target_pairs={{0,2},{1,3},{2,0},{3,1},{4,6},{5,7},{6,4},{7,5},{8,10},{9,11},{10,... | collective-permute-start | bytes 884744 | tf_op jit(solution)/shard_map/ppermute | solution.py:47
  329.3 24.6 %collective-permute-start.51 = (bf16[64,2304]{1,0:T(8,128)(2,1)}, bf16[64,2304]{1,0:T(8,128)(2,1)}, u32[]{:S(2)}, u32[]{:S(2)}) collective-permute-start(bf16[64,2304]{1,0:T(8,128)(2,1)} %get-tuple-element.342), channel_id=1, source_target_pairs={{0,3},{1,2},{2,1},{3,0},{4,7},{5,6},{6,5},{7,4},{8,11},{9,10},{10,... | collective-permute-start | bytes 884744 | tf_op jit(solution)/shard_map/ppermute | solution.py:47
  355.4 27.4 %collective-permute-start.55 = (bf16[64,2304]{1,0:T(8,128)(2,1)S(1)}, bf16[64,2304]{1,0:T(8,128)(2,1)S(1)}, u32[]{:S(2)}, u32[]{:S(2)}) collective-permute-start(bf16[64,2304]{1,0:T(8,128)(2,1)S(1)} %add_convert_fusion.15.refs_0_), channel_id=1, source_target_pairs={{0,1},{1,0},{2,3},{3,2},{4,5},{5,4},{6,7},{7,6},{8,9},{9,8},{10,11... | collective-permute-start | bytes 884744 | tf_op jit(solution)/shard_map/ppermute | solution.py:47
  356.1 26.8 %collective-permute-start.56 = (bf16[64,2304]{1,0:T(8,128)(2,1)S(1)}, bf16[64,2304]{1,0:T(8,128)(2,1)S(1)}, u32[]{:S(2)}, u32[]{:S(2)}) collective-permute-start(bf16[64,2304]{1,0:T(8,128)(2,1)S(1)} %add_convert_fusion.15.refs_0_), channel_id=1, source_target_pairs={{0,2},{1,3},{2,0},{3,1},{4,6},{5,7},{6,4},{7,5},{8,10},{9,11},{10,... | collective-permute-start | bytes 884744 | tf_op jit(solution)/shard_map/ppermute | solution.py:47
  358.4 26.3 %collective-permute-start.57 = (bf16[64,2304]{1,0:T(8,128)(2,1)S(1)}, bf16[64,2304]{1,0:T(8,128)(2,1)S(1)}, u32[]{:S(2)}, u32[]{:S(2)}) collective-permute-start(bf16[64,2304]{1,0:T(8,128)(2,1)S(1)} %add_convert_fusion.15.refs_0_), channel_id=1, source_target_pairs={{0,3},{1,2},{2,1},{3,0},{4,7},{5,6},{6,5},{7,4},{8,11},{9,10},{10,... | collective-permute-start | bytes 884744 | tf_op jit(solution)/shard_map/ppermute | solution.py:47
  360.1 28.2 %collective-permute-start.62 = (bf16[64,2048]{1,0:T(8,128)(2,1)S(1)}, bf16[64,2048]{1,0:T(8,128)(2,1)S(1)}, u32[]{:S(2)}, u32[]{:S(2)}) collective-permute-start(bf16[64,2048]{1,0:T(8,128)(2,1)S(1)} %get-tuple-element.347), channel_id=1, source_target_pairs={{0,1},{1,0},{2,3},{3,2},{4,5},{5,4},{6,7},{7,6},{8,9},{9,8},{10,11... | collective-permute-start | bytes 786440 | tf_op jit(solution)/shard_map/ppermute | solution.py:47
  384.7 26.2 %collective-permute-start.59 = (bf16[128,2048]{1,0:T(8,128)(2,1)S(1)}, bf16[128,2048]{1,0:T(8,128)(2,1)S(1)}, u32[]{:S(2)}, u32[]{:S(2)}) collective-permute-start(bf16[128,2048]{1,0:T(8,128)(2,1)S(1)} %add_convert_fusion.10.refs_0_), channel_id=1, source_target_pairs={{0,8},{4,12},{8,0},{12,4},{16,24},{20,28},{24,16},{28,20},{1,9},{5... | collective-permute-start | bytes 1572872 | tf_op jit(solution)/shard_map/ppermute | solution.py:47
  385.9 24.9 %collective-permute-start.60 = (bf16[128,2048]{1,0:T(8,128)(2,1)S(1)}, bf16[128,2048]{1,0:T(8,128)(2,1)S(1)}, u32[]{:S(2)}, u32[]{:S(2)}) collective-permute-start(bf16[128,2048]{1,0:T(8,128)(2,1)S(1)} %add_convert_fusion.10.refs_0_), channel_id=1, source_target_pairs={{0,16},{4,20},{8,24},{12,28},{16,0},{20,4},{24,8},{28,12},{1,17},{... | collective-permute-start | bytes 1572872 | tf_op jit(solution)/shard_map/ppermute | solution.py:47
  386.5 30.9 %collective-permute-start.61 = (bf16[128,2048]{1,0:T(8,128)(2,1)S(1)}, bf16[128,2048]{1,0:T(8,128)(2,1)S(1)}, u32[]{:S(2)}, u32[]{:S(2)}) collective-permute-start(bf16[128,2048]{1,0:T(8,128)(2,1)S(1)} %add_convert_fusion.10.refs_0_), channel_id=1, source_target_pairs={{0,24},{4,28},{8,16},{12,20},{16,8},{20,12},{24,0},{28,4},{1,25},{... | collective-permute-start | bytes 1572872 | tf_op jit(solution)/shard_map/ppermute | solution.py:47
  388.3 22.5 %collective-permute-start.64 = (bf16[64,2048]{1,0:T(8,128)(2,1)S(1)}, bf16[64,2048]{1,0:T(8,128)(2,1)S(1)}, u32[]{:S(2)}, u32[]{:S(2)}) collective-permute-start(bf16[64,2048]{1,0:T(8,128)(2,1)S(1)} %get-tuple-element.345), channel_id=1, source_target_pairs={{0,3},{1,2},{2,1},{3,0},{4,7},{5,6},{6,5},{7,4},{8,11},{9,10},{10,... | collective-permute-start | bytes 786440 | tf_op jit(solution)/shard_map/ppermute | solution.py:47
  421.4 25.3 %collective-permute-start.71 = (bf16[64,2048]{1,0:T(8,128)(2,1)}, bf16[64,2048]{1,0:T(8,128)(2,1)}, u32[]{:S(2)}, u32[]{:S(2)}) collective-permute-start(bf16[64,2048]{1,0:T(8,128)(2,1)} %get-tuple-element.332), channel_id=1, source_target_pairs={{0,3},{1,2},{2,1},{3,0},{4,7},{5,6},{6,5},{7,4},{8,11},{9,10},{10,... | collective-permute-start | bytes 786440 | tf_op jit(solution)/shard_map/ppermute | solution.py:47
  (78 other events, 1177.7 us)
Sparse Core Ops, SparseCore 0:
  46.7 54.6 all-gather.1
  261.9 75.6 reduce-scatter.2
  341.5 67.5 reduce-scatter.4

commit v7 on v6

--- a/solution.py
+++ b/solution.py
@@ -1004,13 +1004,15 @@
         normed_rel, *weights_rel, gains, cosine, sine_table, output_weight, key_heads
     )
     (head_parts,) = join(head_parts)
+    head_parts = list(head_parts)
 
     hops = reduce_hops(head_parts[0])
     wgu = gate_up_low.transpose(1, 0, 2).reshape(features, -1)
-    hops, wgu = join(hops, wgu)
+    hops, wgu, head_parts[1] = join(hops, wgu, head_parts[1])
 
     chunk = reduce_total(head_parts[0], hops)
-    hops, hops_b = join(spread_hops(chunk), reduce_hops(head_parts[1]))
+    hops_b = reduce_hops(head_parts[1])
+    (hops,) = join(spread_hops(chunk))
 
     resid_a, routed_a = resid_and_routed([chunk] + hops, hidden_in[:rows_a], mlp_gain_full)
     chunk = reduce_total(head_parts[1], hops_b)

time: 468 us -> 466 us (level)
  waiting for transfers between devices: 142 us -> 133 us
  local copies, waits for them, and re-layouts: 34 us -> 42.6 us
    ppermute x72, waiting for transfers between devices: 142 us -> 133 us  [swap(): return lax.ppermute(value, axis, [(i, i ^ mask) for i in range(count)])]
    unnamed x80 -> x86, local copies, waits for them, and re-layouts: 14.9 us -> 23.1 us
  transfers between devices with their start and end apart: 75 -> 75, of which waited for: 37 -> 34; matrix products, arithmetic and copies ran while one was open for 7% -> 7% of each run, Pallas kernels for 35% -> 36%
where the time goes in v7:
time: 466 us; the launch traced here: 460 us
  Pallas kernels  164 us (35%)
  waiting for transfers between devices  133 us (29%)
  starting transfers between devices  77.6 us (17%)
  local copies, waits for them, and re-layouts  42.6 us (9%)
  other arithmetic  27.7 us (6%)
  between operations  15.3 us (3%)
    ppermute x72, waiting for transfers between devices, swap(): return lax.ppermute(value, axis, [(i, i ^ mask) for i in range(count)])  133 us
    ppermute x72, starting transfers between devices, swap(): return lax.ppermute(value, axis, [(i, i ^ mask) for i in range(count)])  77.1 us
    pallas_call x4, Pallas kernels, run_experts(): pl.pallas_call(functools.partial(expert_kernel, local), grid_spec=pltpu.P...  69.4 us
    unnamed x86, local copies, waits for them, and re-layouts  23.1 us
    pallas_call x1, Pallas kernels, gate_up_product(): pl.pallas_call(gate_up_kernel, grid=(features // tile,), in_specs=[pl.Blo...  19.2 us
    convert_element_type x11, other arithmetic, plus(): return total.astype(values[0].dtype)  15.2 us
    pallas_call x1, Pallas kernels, down_product(): pl.pallas_call(down_kernel, grid_spec=pltpu.PrefetchScalarGridSpec(num_sc...  13.3 us
    pallas_call x1, Pallas kernels, attention_back(): pl.pallas_call(functools.partial(attention_back_kernel, key_heads), in_sp...  13.2 us
  transfers between devices with their start and end apart: 75, of which 34 were waited for; matrix products, arithmetic and copies ran while one was open for 7% of the time, Pallas kernels for 36%

profile of v7, /device:TPU:8, one launch (start us, length us, event | category | flops | bytes accessed | tf_op | source)
XLA Modules:
  0.0 460.2 jit_solution(2911350377031240645)
XLA Ops:
  35.3 11.3 %collective-permute-done.1.refs_2_ = bf16[256,1024]{1,0:T(8,128)(2,1)} collective-permute-done((bf16[256,1024]{1,0:T(8,128)(2,1)}, bf16[256,1024]{1,0:T(8,128)(2,1)}, u32[]{:S(2)}, u32[]{:S(2)}) %collective-permute-start.1) | collective-permute-done | bytes 524320 | tf_op jit(solution)/shard_map/ppermute | solution.py:47
  50.7 4.5 collective-permute-done.7.core_ref
  59.9 7.7 %shard_map.239 = (f32[256,1152]{1,0:T(8,128)S(1)}, bf16[256,1280]{1,0:T(8,128)(2,1)S(1)}, bf16[256,1024]{1,0:T(8,128)(2,1)S(1)}, f32[256,8]{1,0:T(8,128)S(1)}, b...) custom-call(bf16[256,2048]{1,0:T(8,128)(2,1)S(1)} %dynamic-slice_dynamic-update-slice_fusion.x_ref, ...), custom_call_target="tpu_custom_call" | custom-call | bytes 1024 | tf_op jit(solution)/shard_map/pallas_call | solution.py:564
  75.3 6.7 %copy.56 = bf16[4,256,8,384]{3,2,0,1:T(8,128)(2,1)} copy(bf16[4,256,8,384]{3,2,1,0:T(8,128)(2,1)} %bitcast.77) | data formatting | bytes 12582912 | tf_op jit(solution)/shard_map/reshape | solution.py:1010
  98.2 9.2 %collective-permute-done.13.refs_3_ = bf16[32,2048]{1,0:T(8,128)(2,1)S(1)} collective-permute-done((bf16[32,2048]{1,0:T(8,128)(2,1)S(1)}, bf16[32,2048]{1,0:T(8,128)(2,1)S(1)}, u32[]{:S(2)}, u32[]{:S(2)}) %collective-permute-start.13) | collective-permute-done | bytes 131104 | tf_op jit(solution)/shard_map/ppermute | solution.py:47
  115.3 3.6 collective-permute-done.20.refs_1_
  121.1 4.3 collective-permute-done.22.refs_3_
  134.4 17.6 %shard_map.244 = (bf16[512,2176]{1,0:T(8,128)(2,1)}, bf16[512,1536]{1,0:T(8,128)(2,1)}, bf16[512,768]{1,0:T(8,128)(2,1)}) custom-call(s32[5]{0:T(128)S(1)} %stack.111.place_ref, bf16[512,2048]{1,0:T(8,128)(2,1)} %shard_map.242.x_ref.refs_0_, bf16[2048,2048]{1,0:T(8,128)(2,1)} %all-gather.2.cloned.1.call-done.g0_ref.g1_ref.refs_4_, ...), custom_call_target="tpu_custom_call" | custom-call | bytes 1024 | tf_op jit(solution)/shard_map/pallas_call | solution.py:341
  152.0 17.2 %shard_map.243 = (bf16[512,2176]{1,0:T(8,128)(2,1)}, bf16[512,1536]{1,0:T(8,128)(2,1)}, bf16[512,768]{1,0:T(8,128)(2,1)}) custom-call(s32[5]{0:T(128)S(1)} %stack.106.place_ref, bf16[512,2048]{1,0:T(8,128)(2,1)} %collective-permute-done.26.x_ref.refs_1_, bf16[2048,2048]{1,0:T(8,128)(2,1)} %all-gather.2.cloned.1.call-done.g0_ref.g1_ref.refs_4_, ...), custom_call_target="tpu_custom_call" | custom-call | bytes 1024 | tf_op jit(solution)/shard_map/pallas_call | solution.py:341
  172.5 17.4 %shard_map.246 = (bf16[512,2176]{1,0:T(8,128)(2,1)}, bf16[512,1536]{1,0:T(8,128)(2,1)}, bf16[512,768]{1,0:T(8,128)(2,1)}) custom-call(s32[5]{0:T(128)S(1)} %stack.228.place_ref, bf16[512,2048]{1,0:T(8,128)(2,1)} %shard_map.245.x_ref.refs_2_, bf16[2048,2048]{1,0:T(8,128)(2,1)} %all-gather.2.cloned.1.call-done.g0_ref.g1_ref.refs_4_, ...), custom_call_target="tpu_custom_call" | custom-call | bytes 1024 | tf_op jit(solution)/shard_map/pallas_call | solution.py:341
  196.3 17.2 %shard_map.247 = (bf16[512,2176]{1,0:T(8,128)(2,1)}, bf16[512,1536]{1,0:T(8,128)(2,1)}, bf16[512,768]{1,0:T(8,128)(2,1)}) custom-call(s32[5]{0:T(128)S(1)} %stack.233.place_ref, bf16[512,2048]{1,0:T(8,128)(2,1)} %collective-permute-done.28.x_ref.refs_3_, bf16[2048,2048]{1,0:T(8,128)(2,1)} %all-gather.2.cloned.1.call-done.g0_ref.g1_ref.refs_4_, ...), custom_call_target="tpu_custom_call" | custom-call | bytes 1024 | tf_op jit(solution)/shard_map/pallas_call | solution.py:341
  213.5 6.3 %collective-permute-done.30 = bf16[128,2176]{1,0:T(8,128)(2,1)S(1)} collective-permute-done((bf16[128,2176]{1,0:T(8,128)(2,1)}, bf16[128,2176]{1,0:T(8,128)(2,1)S(1)}, u32[]{:S(2)}, u32[]{:S(2)}) %collective-permute-start.30) | collective-permute-done | bytes 557088 | tf_op jit(solution)/shard_map/ppermute | solution.py:47
  230.4 4.2 collective-permute-done.33
  234.5 3.4 collective-permute-done.34
  240.9 3.7 collective-permute-done.35.refs_1_
  246.2 13.1 %shard_map.248 = bf16[2048,2048]{1,0:T(8,128)(2,1)} custom-call(s32[8]{0:T(128)S(1)} %stack.100.place_ref.column_ref.block_ref, bf16[512,768]{1,0:T(8,128)(2,1)} %get-tuple-element.199.upper0_ref.refs_0_, bf16[512,768]{1,0:T(8,128)(2,1)} %get-tuple-element.200.upper1_ref.refs_1_, bf16[512,768]{1,0:T(8,128)(2,1)} %get-tuple-element.201.lower0_ref.refs_2_, ...), custom_call_target="tpu_custom_call" | custom-call | bytes 1024 | tf_op jit(solution)/shard_map/pallas_call | solution.py:452
  266.8 3.7 collective-permute-done.43
  270.5 3.2 collective-permute-done.44
  280.5 4.1 collective-permute-done.46.refs_6_
  284.6 3.2 collective-permute-done.47.refs_7_
  287.8 7.5 %shard_map.249 = (f32[256,2048]{1,0:T(8,128)S(1)}, bf16[256,2048]{1,0:T(8,128)(2,1)S(1)}, bf16[2048,128]{1,0:T(8,128)(2,1)S(1)}, bf16[512,2048]{1,0:T(8,128)(2,1)S(1)}, bf16[512,2048]{1,0:T(8,128)(2,1)S(1)}) custom-call(s32[4]{0:T(128)S(1)} %pad_add_fusion.place_ref, s32[8]{0:T(128)S(1)} %stack.100.place_ref.column_ref.block_ref, ...), custom_call_target="tpu_custom_call" | custom-call | bytes 1024 | tf_op jit(solution)/shard_map/pallas_call | solution.py:808
  298.4 13.2 %shard_map.250 = (bf16[256,2304]{1,0:T(8,128)(2,1)S(1)}, bf16[2048,1408]{1,0:T(8,128)(2,1)S(1)}) custom-call(s32[8]{0:T(128)S(1)} %stack.100.place_ref.column_ref.block_ref, bf16[256,2048]{1,0:T(8,128)(2,1)} %copy-done.15, bf16[1024,2048]{1,0:T(8,128)(2,1)} %wo_ref.3, f32[256,1152]{1,0:T(8,128)} %copy-done.14, bf16[256,1280]{1,0:T(8,128)(2,1)} %copy-done.16, ...), custom_call_target="tpu_custom_call" | custom-call | bytes 1024 | tf_op jit(solution)/shard_map/pallas_call | solution.py:680
  327.8 13.3 %shard_map.251 = f32[768,2048]{1,0:T(8,128)} custom-call(s32[16]{0:T(128)} %stack.234.place_ref, bf16[512,768]{1,0:T(8,128)(2,1)} %get-tuple-element.199.upper0_ref.refs_0_, bf16[512,768]{1,0:T(8,128)(2,1)} %get-tuple-element.200.upper1_ref.refs_1_, bf16[512,768]{1,0:T(8,128)(2,1)} %get-tuple-element.201.lower0_ref.refs_2_, ...), custom_call_target="tpu_custom_call" | custom-call | bytes 1024 | tf_op jit(solution)/shard_map/pallas_call | solution.py:416
  344.1 7.5 %collective-permute-done.51 = bf16[64,2304]{1,0:T(8,128)(2,1)} collective-permute-done((bf16[64,2304]{1,0:T(8,128)(2,1)}, bf16[64,2304]{1,0:T(8,128)(2,1)}, u32[]{:S(2)}, u32[]{:S(2)}) %collective-permute-start.51) | collective-permute-done | bytes 294944 | tf_op jit(solution)/shard_map/ppermute | solution.py:47
  359.1 19.2 %shard_map.252 = f32[4,2048,384]{2,1,0:T(8,128)} custom-call(bf16[512,2048]{1,0:T(8,128)(2,1)} %shard_map.242.x_ref.refs_0_, bf16[512,2048]{1,0:T(8,128)(2,1)} %collective-permute-done.26.x_ref.refs_1_, bf16[512,2048]{1,0:T(8,128)(2,1)} %shard_map.245.x_ref.refs_2_, bf16[512,2048]{1,0:T(8,128)(2,1)} %collective-permute-done.28.x_ref.refs_3_, ...), custom_call_target="tpu_custom_call" | custom-call | bytes 1024 | tf_op jit(solution)/shard_map/pallas_call | solution.py:387
  386.9 4.8 %shard_map.253 = (f32[256,2048]{1,0:T(8,128)}, f32[8,512]{1,0:T(8,128)S(1)}) custom-call(s32[4]{0:T(128)S(1)} %pad_add_fusion.place_ref, s32[8]{0:T(128)S(1)} %stack.100.place_ref.column_ref.block_ref, bf16[64,2304]{1,0:T(8,128)(2,1)S(1)} %add_convert_fusion.15.refs_0_, bf16[64,2304]{1,0:T(8,128)(2,1)S(1)} %collective-permute-done.55.refs_1_, ...), custom_call_target="tpu_custom_call" | custom-call | bytes 1024 | tf_op jit(solution)/shard_map/pallas_call | solution.py:860
  391.7 11.3 %collective-permute-done.63 = bf16[64,2048]{1,0:T(8,128)(2,1)S(1)} collective-permute-done((bf16[64,2048]{1,0:T(8,128)(2,1)S(1)}, bf16[64,2048]{1,0:T(8,128)(2,1)S(1)}, u32[]{:S(2)}, u32[]{:S(2)}) %collective-permute-start.63) | collective-permute-done | bytes 262176 | tf_op jit(solution)/shard_map/ppermute | solution.py:47
  403.0 5.3 %collective-permute-done.64 = bf16[64,2048]{1,0:T(8,128)(2,1)S(1)} collective-permute-done((bf16[64,2048]{1,0:T(8,128)(2,1)S(1)}, bf16[64,2048]{1,0:T(8,128)(2,1)S(1)}, u32[]{:S(2)}, u32[]{:S(2)}) %collective-permute-start.64) | collective-permute-done | bytes 262176 | tf_op jit(solution)/shard_map/ppermute | solution.py:47
  408.3 6.7 %collective-permute-done.60.refs_2_ = bf16[128,2048]{1,0:T(8,128)(2,1)S(1)} collective-permute-done((bf16[128,2048]{1,0:T(8,128)(2,1)S(1)}, bf16[128,2048]{1,0:T(8,128)(2,1)S(1)}, u32[]{:S(2)}, u32[]{:S(2)}) %collective-permute-start.60) | collective-permute-done | bytes 524320 | tf_op jit(solution)/shard_map/ppermute | solution.py:47
  429.3 5.1 %shard_map.255 = f32[1024,2048]{1,0:T(8,128)} custom-call(s32[8]{0:T(128)S(1)} %stack.100.place_ref.column_ref.block_ref, bf16[512,2048]{1,0:T(8,128)(2,1)S(1)} %shard_map.254.near_ref, bf16[512,2048]{1,0:T(8,128)(2,1)S(1)} %copy-done.8), custom_call_target="tpu_custom_call" | custom-call | bytes 1024 | tf_op jit(solution)/shard_map/pallas_call | solution.py:886
  434.4 3.5 collective-permute-done.70
  437.9 6.3 %collective-permute-done.71 = bf16[64,2048]{1,0:T(8,128)(2,1)} collective-permute-done((bf16[64,2048]{1,0:T(8,128)(2,1)}, bf16[64,2048]{1,0:T(8,128)(2,1)}, u32[]{:S(2)}, u32[]{:S(2)}) %collective-permute-start.71) | collective-permute-done | bytes 262176 | tf_op jit(solution)/shard_map/ppermute | solution.py:47
  (299 shorter events, 179.7 us)
Async XLA Ops:
  7.2 127.2 %all-gather.2.cloned.1.call-start = ((), (), s32[]{:S(2)}) async-start(), calls=%async_computation.2 | async-start | bytes 9437184 | tf_op jit(solution)/shard_map/all_gather | solution.py:999
  16.9 29.7 %collective-permute-start.1 = (bf16[256,1024]{1,0:T(8,128)(2,1)}, bf16[256,1024]{1,0:T(8,128)(2,1)}, u32[]{:S(2)}, u32[]{:S(2)}) collective-permute-start(bf16[256,1024]{1,0:T(8,128)(2,1)} %refs_0_.1), channel_id=1, source_target_pairs={{0,16},{4,20},{8,24},{12,28},{16,0},{20,4},{24,8},{28,12},{1,17},{... | collective-permute-start | bytes 1572872 | tf_op jit(solution)/shard_map/ppermute | solution.py:47
  19.7 26.9 %collective-permute-start.2 = (bf16[256,1024]{1,0:T(8,128)(2,1)}, bf16[256,1024]{1,0:T(8,128)(2,1)}, u32[]{:S(2)}, u32[]{:S(2)}) collective-permute-start(bf16[256,1024]{1,0:T(8,128)(2,1)} %refs_0_.1), channel_id=1, source_target_pairs={{0,24},{4,28},{8,16},{12,20},{16,8},{20,12},{24,0},{28,4},{1,25},{... | collective-permute-start | bytes 1572872 | tf_op jit(solution)/shard_map/ppermute | solution.py:47
  46.6 305.0 %reduce-scatter.3.cloned.1.call-start = ((), (), s32[]{:S(2)}) async-start(), calls=%async_computation.3 | async-start | bytes 9437184 | tf_op jit(solution)/shard_map/reduce_scatter | solution.py:1065
  89.3 21.9 %collective-permute-start.14 = (bf16[32,2048]{1,0:T(8,128)(2,1)S(1)}, bf16[32,2048]{1,0:T(8,128)(2,1)S(1)}, u32[]{:S(2)}, u32[]{:S(2)}) collective-permute-start(bf16[32,2048]{1,0:T(8,128)(2,1)S(1)} %get-tuple-element.354), channel_id=1, source_target_pairs={{0,1},{1,0},{2,3},{3,2},{4,5},{5,4},{6,7},{7,6},{8,9},{9,8},{10,11... | collective-permute-start | bytes 393224 | tf_op jit(solution)/shard_map/ppermute | solution.py:47
  129.0 23.0 %collective-permute-start.26 = (bf16[512,2048]{1,0:T(8,128)(2,1)}, bf16[512,2048]{1,0:T(8,128)(2,1)}, u32[]{:S(2)}, u32[]{:S(2)}) collective-permute-start(bf16[512,2048]{1,0:T(8,128)(2,1)} %shard_map.242.x_ref.refs_0_), channel_id=1, source_target_pairs={{0,4},{4,0},{8,12},{12,8},{16,20},{20,16},{24,28},{28,24},{1,5},{5... | collective-permute-start | bytes 6291464 | tf_op jit(solution)/shard_map/ppermute | solution.py:47
  130.8 38.5 %collective-permute-start.23 = (bf16[128,2048]{1,0:T(8,128)(2,1)S(1)}, bf16[128,2048]{1,0:T(8,128)(2,1)S(1)}, u32[]{:S(2)}, u32[]{:S(2)}) collective-permute-start(bf16[128,2048]{1,0:T(8,128)(2,1)S(1)} %get-tuple-element.170.refs_0_.refs_11_), channel_id=1, source_target_pairs={{0,8},{4,12},{8,0},{12,4},{16,24},{20,28},{24,16},{28,20},{1,9},{5... | collective-permute-start | bytes 1572872 | tf_op jit(solution)/shard_map/ppermute | solution.py:47
  131.5 37.8 %collective-permute-start.24 = (bf16[128,2048]{1,0:T(8,128)(2,1)S(1)}, bf16[128,2048]{1,0:T(8,128)(2,1)S(1)}, u32[]{:S(2)}, u32[]{:S(2)}) collective-permute-start(bf16[128,2048]{1,0:T(8,128)(2,1)S(1)} %get-tuple-element.170.refs_0_.refs_11_), channel_id=1, source_target_pairs={{0,16},{4,20},{8,24},{12,28},{16,0},{20,4},{24,8},{28,12},{1,17},{... | collective-permute-start | bytes 1572872 | tf_op jit(solution)/shard_map/ppermute | solution.py:47
  132.9 36.4 %collective-permute-start.25 = (bf16[128,2048]{1,0:T(8,128)(2,1)S(1)}, bf16[128,2048]{1,0:T(8,128)(2,1)}, u32[]{:S(2)}, u32[]{:S(2)}) collective-permute-start(bf16[128,2048]{1,0:T(8,128)(2,1)S(1)} %get-tuple-element.170.refs_0_.refs_11_), channel_id=1, source_target_pairs={{0,24},{4,28},{8,16},{12,20},{16,8},{20,12},{24,0},{28,4},{1,25},{... | collective-permute-start | bytes 1572872 | tf_op jit(solution)/shard_map/ppermute | solution.py:47
  192.7 20.8 %collective-permute-start.29 = (bf16[128,2176]{1,0:T(8,128)(2,1)}, bf16[128,2176]{1,0:T(8,128)(2,1)S(1)}, u32[]{:S(2)}, u32[]{:S(2)}) collective-permute-start(bf16[128,2176]{1,0:T(8,128)(2,1)} %get-tuple-element.334), channel_id=1, source_target_pairs={{0,8},{4,12},{8,0},{12,4},{16,24},{20,28},{24,16},{28,20},{1,9},{5... | collective-permute-start | bytes 1671176 | tf_op jit(solution)/shard_map/ppermute | solution.py:47
  193.4 26.4 %collective-permute-start.30 = (bf16[128,2176]{1,0:T(8,128)(2,1)}, bf16[128,2176]{1,0:T(8,128)(2,1)S(1)}, u32[]{:S(2)}, u32[]{:S(2)}) collective-permute-start(bf16[128,2176]{1,0:T(8,128)(2,1)} %get-tuple-element.333), channel_id=1, source_target_pairs={{0,16},{4,20},{8,24},{12,28},{16,0},{20,4},{24,8},{28,12},{1,17},{... | collective-permute-start | bytes 1671176 | tf_op jit(solution)/shard_map/ppermute | solution.py:47
  194.8 25.0 %collective-permute-start.31 = (bf16[128,2176]{1,0:T(8,128)(2,1)}, bf16[128,2176]{1,0:T(8,128)(2,1)}, u32[]{:S(2)}, u32[]{:S(2)}) collective-permute-start(bf16[128,2176]{1,0:T(8,128)(2,1)} %get-tuple-element.332), channel_id=1, source_target_pairs={{0,24},{4,28},{8,16},{12,20},{16,8},{20,12},{24,0},{28,4},{1,25},{... | collective-permute-start | bytes 1671176 | tf_op jit(solution)/shard_map/ppermute | solution.py:47
  226.9 32.4 %collective-permute-start.39 = (bf16[128,2176]{1,0:T(8,128)(2,1)}, bf16[128,2176]{1,0:T(8,128)(2,1)S(1)}, u32[]{:S(2)}, u32[]{:S(2)}) collective-permute-start(bf16[128,2176]{1,0:T(8,128)(2,1)} %get-tuple-element.331), channel_id=1, source_target_pairs={{0,8},{4,12},{8,0},{12,4},{16,24},{20,28},{24,16},{28,20},{1,9},{5... | collective-permute-start | bytes 1671176 | tf_op jit(solution)/shard_map/ppermute | solution.py:47
  228.2 31.0 %collective-permute-start.40 = (bf16[128,2176]{1,0:T(8,128)(2,1)}, bf16[128,2176]{1,0:T(8,128)(2,1)S(1)}, u32[]{:S(2)}, u32[]{:S(2)}) collective-permute-start(bf16[128,2176]{1,0:T(8,128)(2,1)} %get-tuple-element.330), channel_id=1, source_target_pairs={{0,16},{4,20},{8,24},{12,28},{16,0},{20,4},{24,8},{28,12},{1,17},{... | collective-permute-start | bytes 1671176 | tf_op jit(solution)/shard_map/ppermute | solution.py:47
  228.9 30.4 %collective-permute-start.41 = (bf16[128,2176]{1,0:T(8,128)(2,1)}, bf16[128,2176]{1,0:T(8,128)(2,1)S(1)}, u32[]{:S(2)}, u32[]{:S(2)}) collective-permute-start(bf16[128,2176]{1,0:T(8,128)(2,1)} %get-tuple-element.329), channel_id=1, source_target_pairs={{0,24},{4,28},{8,16},{12,20},{16,8},{20,12},{24,0},{28,4},{1,25},{... | collective-permute-start | bytes 1671176 | tf_op jit(solution)/shard_map/ppermute | solution.py:47
  238.1 21.1 %collective-permute-start.36 = (bf16[32,2176]{1,0:T(8,128)(2,1)S(1)}, bf16[32,2176]{1,0:T(8,128)(2,1)S(1)}, u32[]{:S(2)}, u32[]{:S(2)}) collective-permute-start(bf16[32,2176]{1,0:T(8,128)(2,1)S(1)} %add_convert_fusion.18.refs_0_), channel_id=1, source_target_pairs={{0,2},{1,3},{2,0},{3,1},{4,6},{5,7},{6,4},{7,5},{8,10},{9,11},{10,... | collective-permute-start | bytes 417800 | tf_op jit(solution)/shard_map/ppermute | solution.py:47
  259.3 175.0 %reduce-scatter.5.cloned.1.call-start = ((), (), s32[]{:S(2)}) async-start(), calls=%async_computation.4 | async-start | bytes 6488064 | tf_op jit(solution)/shard_map/reduce_scatter | solution.py:1105
  319.3 32.3 %collective-permute-start.52 = (bf16[128,2048]{1,0:T(8,128)(2,1)}, bf16[128,2048]{1,0:T(8,128)(2,1)}, u32[]{:S(2)}, u32[]{:S(2)}) collective-permute-start(bf16[128,2048]{1,0:T(8,128)(2,1)} %get-tuple-element.337), channel_id=1, source_target_pairs={{0,8},{4,12},{8,0},{12,4},{16,24},{20,28},{24,16},{28,20},{1,9},{5... | collective-permute-start | bytes 1572872 | tf_op jit(solution)/shard_map/ppermute | solution.py:47
  320.6 31.1 %collective-permute-start.53 = (bf16[128,2048]{1,0:T(8,128)(2,1)}, bf16[128,2048]{1,0:T(8,128)(2,1)}, u32[]{:S(2)}, u32[]{:S(2)}) collective-permute-start(bf16[128,2048]{1,0:T(8,128)(2,1)} %get-tuple-element.336), channel_id=1, source_target_pairs={{0,16},{4,20},{8,24},{12,28},{16,0},{20,4},{24,8},{28,12},{1,17},{... | collective-permute-start | bytes 1572872 | tf_op jit(solution)/shard_map/ppermute | solution.py:47
  321.3 30.3 %collective-permute-start.54 = (bf16[128,2048]{1,0:T(8,128)(2,1)}, bf16[128,2048]{1,0:T(8,128)(2,1)}, u32[]{:S(2)}, u32[]{:S(2)}) collective-permute-start(bf16[128,2048]{1,0:T(8,128)(2,1)} %get-tuple-element.335), channel_id=1, source_target_pairs={{0,24},{4,28},{8,16},{12,20},{16,8},{20,12},{24,0},{28,4},{1,25},{... | collective-permute-start | bytes 1572872 | tf_op jit(solution)/shard_map/ppermute | solution.py:47
  322.8 21.3 %collective-permute-start.50 = (bf16[64,2304]{1,0:T(8,128)(2,1)}, bf16[64,2304]{1,0:T(8,128)(2,1)}, u32[]{:S(2)}, u32[]{:S(2)}) collective-permute-start(bf16[64,2304]{1,0:T(8,128)(2,1)} %get-tuple-element.339), channel_id=1, source_target_pairs={{0,2},{1,3},{2,0},{3,1},{4,6},{5,7},{6,4},{7,5},{8,10},{9,11},{10,... | collective-permute-start | bytes 884744 | tf_op jit(solution)/shard_map/ppermute | solution.py:47
  326.9 24.7 %collective-permute-start.51 = (bf16[64,2304]{1,0:T(8,128)(2,1)}, bf16[64,2304]{1,0:T(8,128)(2,1)}, u32[]{:S(2)}, u32[]{:S(2)}) collective-permute-start(bf16[64,2304]{1,0:T(8,128)(2,1)} %get-tuple-element.338), channel_id=1, source_target_pairs={{0,3},{1,2},{2,1},{3,0},{4,7},{5,6},{6,5},{7,4},{8,11},{9,10},{10,... | collective-permute-start | bytes 884744 | tf_op jit(solution)/shard_map/ppermute | solution.py:47
  353.1 27.1 %collective-permute-start.55 = (bf16[64,2304]{1,0:T(8,128)(2,1)S(1)}, bf16[64,2304]{1,0:T(8,128)(2,1)S(1)}, u32[]{:S(2)}, u32[]{:S(2)}) collective-permute-start(bf16[64,2304]{1,0:T(8,128)(2,1)S(1)} %add_convert_fusion.15.refs_0_), channel_id=1, source_target_pairs={{0,1},{1,0},{2,3},{3,2},{4,5},{5,4},{6,7},{7,6},{8,9},{9,8},{10,11... | collective-permute-start | bytes 884744 | tf_op jit(solution)/shard_map/ppermute | solution.py:47
  353.4 26.8 %collective-permute-start.56 = (bf16[64,2304]{1,0:T(8,128)(2,1)S(1)}, bf16[64,2304]{1,0:T(8,128)(2,1)S(1)}, u32[]{:S(2)}, u32[]{:S(2)}) collective-permute-start(bf16[64,2304]{1,0:T(8,128)(2,1)S(1)} %add_convert_fusion.15.refs_0_), channel_id=1, source_target_pairs={{0,2},{1,3},{2,0},{3,1},{4,6},{5,7},{6,4},{7,5},{8,10},{9,11},{10,... | collective-permute-start | bytes 884744 | tf_op jit(solution)/shard_map/ppermute | solution.py:47
  355.8 26.5 %collective-permute-start.57 = (bf16[64,2304]{1,0:T(8,128)(2,1)S(1)}, bf16[64,2304]{1,0:T(8,128)(2,1)S(1)}, u32[]{:S(2)}, u32[]{:S(2)}) collective-permute-start(bf16[64,2304]{1,0:T(8,128)(2,1)S(1)} %add_convert_fusion.15.refs_0_), channel_id=1, source_target_pairs={{0,3},{1,2},{2,1},{3,0},{4,7},{5,6},{6,5},{7,4},{8,11},{9,10},{10,... | collective-permute-start | bytes 884744 | tf_op jit(solution)/shard_map/ppermute | solution.py:47
  357.8 27.9 %collective-permute-start.62 = (bf16[64,2048]{1,0:T(8,128)(2,1)S(1)}, bf16[64,2048]{1,0:T(8,128)(2,1)S(1)}, u32[]{:S(2)}, u32[]{:S(2)}) collective-permute-start(bf16[64,2048]{1,0:T(8,128)(2,1)S(1)} %get-tuple-element.343), channel_id=1, source_target_pairs={{0,1},{1,0},{2,3},{3,2},{4,5},{5,4},{6,7},{7,6},{8,9},{9,8},{10,11... | collective-permute-start | bytes 786440 | tf_op jit(solution)/shard_map/ppermute | solution.py:47
  382.2 26.1 %collective-permute-start.59 = (bf16[128,2048]{1,0:T(8,128)(2,1)S(1)}, bf16[128,2048]{1,0:T(8,128)(2,1)S(1)}, u32[]{:S(2)}, u32[]{:S(2)}) collective-permute-start(bf16[128,2048]{1,0:T(8,128)(2,1)S(1)} %add_convert_fusion.10.refs_0_), channel_id=1, source_target_pairs={{0,8},{4,12},{8,0},{12,4},{16,24},{20,28},{24,16},{28,20},{1,9},{5... | collective-permute-start | bytes 1572872 | tf_op jit(solution)/shard_map/ppermute | solution.py:47
  383.7 31.3 %collective-permute-start.60 = (bf16[128,2048]{1,0:T(8,128)(2,1)S(1)}, bf16[128,2048]{1,0:T(8,128)(2,1)S(1)}, u32[]{:S(2)}, u32[]{:S(2)}) collective-permute-start(bf16[128,2048]{1,0:T(8,128)(2,1)S(1)} %add_convert_fusion.10.refs_0_), channel_id=1, source_target_pairs={{0,16},{4,20},{8,24},{12,28},{16,0},{20,4},{24,8},{28,12},{1,17},{... | collective-permute-start | bytes 1572872 | tf_op jit(solution)/shard_map/ppermute | solution.py:47
  384.3 30.7 %collective-permute-start.61 = (bf16[128,2048]{1,0:T(8,128)(2,1)S(1)}, bf16[128,2048]{1,0:T(8,128)(2,1)S(1)}, u32[]{:S(2)}, u32[]{:S(2)}) collective-permute-start(bf16[128,2048]{1,0:T(8,128)(2,1)S(1)} %add_convert_fusion.10.refs_0_), channel_id=1, source_target_pairs={{0,24},{4,28},{8,16},{12,20},{16,8},{20,12},{24,0},{28,4},{1,25},{... | collective-permute-start | bytes 1572872 | tf_op jit(solution)/shard_map/ppermute | solution.py:47
  385.7 22.6 %collective-permute-start.64 = (bf16[64,2048]{1,0:T(8,128)(2,1)S(1)}, bf16[64,2048]{1,0:T(8,128)(2,1)S(1)}, u32[]{:S(2)}, u32[]{:S(2)}) collective-permute-start(bf16[64,2048]{1,0:T(8,128)(2,1)S(1)} %get-tuple-element.341), channel_id=1, source_target_pairs={{0,3},{1,2},{2,1},{3,0},{4,7},{5,6},{6,5},{7,4},{8,11},{9,10},{10,... | collective-permute-start | bytes 786440 | tf_op jit(solution)/shard_map/ppermute | solution.py:47
  417.2 20.8 %collective-permute-start.70 = (bf16[64,2048]{1,0:T(8,128)(2,1)}, bf16[64,2048]{1,0:T(8,128)(2,1)}, u32[]{:S(2)}, u32[]{:S(2)}) collective-permute-start(bf16[64,2048]{1,0:T(8,128)(2,1)} %get-tuple-element.328), channel_id=1, source_target_pairs={{0,2},{1,3},{2,0},{3,1},{4,6},{5,7},{6,4},{7,5},{8,10},{9,11},{10,... | collective-permute-start | bytes 786440 | tf_op jit(solution)/shard_map/ppermute | solution.py:47
  419.7 24.6 %collective-permute-start.71 = (bf16[64,2048]{1,0:T(8,128)(2,1)}, bf16[64,2048]{1,0:T(8,128)(2,1)}, u32[]{:S(2)}, u32[]{:S(2)}) collective-permute-start(bf16[64,2048]{1,0:T(8,128)(2,1)} %get-tuple-element.328), channel_id=1, source_target_pairs={{0,3},{1,2},{2,1},{3,0},{4,7},{5,6},{6,5},{7,4},{8,11},{9,10},{10,... | collective-permute-start | bytes 786440 | tf_op jit(solution)/shard_map/ppermute | solution.py:47
  (81 other events, 1065.8 us)
Sparse Core Ops, SparseCore 0:
  46.7 54.6 all-gather.1
  259.4 75.2 reduce-scatter.2
  338.5 67.4 reduce-scatter.4

commit v8 on v7

--- a/solution.py
+++ b/solution.py
@@ -673,15 +673,15 @@
     width = low.shape[1]
     whole = width + beside.shape[1]
     shapes = [
-        ((rows, features + 2 * HEAD_SIZE), BF16),
-        ((features, whole), BF16),
+        jax.ShapeDtypeStruct((rows, features + 2 * HEAD_SIZE), BF16),
+        pltpu.HBM((features, whole), BF16),
     ]
     operands = [upstream, wo, raw, low, lse, gains, cosine, sine, x, *weights, beside]
     return pl.pallas_call(
         functools.partial(attention_back_kernel, key_heads),
         in_specs=in_smem() + in_vmem(len(operands)),
         out_specs=in_vmem(2),
-        out_shape=[jax.ShapeDtypeStruct(*v) for v in shapes],
+        out_shape=shapes,
         scratch_shapes=[pltpu.VMEM((rows, query_width), BF16), pltpu.VMEM((rows, width), BF16)],
         compiler_params=pltpu.CompilerParams(vmem_limit_bytes=40 * 1024 * 1024),
         cost_estimate=SMALL,
@@ -798,18 +798,18 @@
     wide = -(-(expert_count + 1) // LANES) * LANES
     half = mixed.shape[1] // 2
     shapes = [
-        ((rows, features), F32),
-        ((rows, features), BF16),
-        ((features, wide), BF16),
-        ((half, features), BF16),
-        ((half, features), BF16),
+        pltpu.HBM((rows, features), F32),
+        jax.ShapeDtypeStruct((rows, features), BF16),
+        jax.ShapeDtypeStruct((features, wide), BF16),
+        pltpu.HBM((half, features), BF16),
+        jax.ShapeDtypeStruct((half, features), BF16),
     ]
     operands = [*pieces, *in_hbm(*resid, *routed, ids, router, gain, upstream, mixed)]
     return pl.pallas_call(
         functools.partial(resid_back_kernel, parts),
         in_specs=in_smem() * 2 + in_vmem(len(operands)),
         out_specs=in_vmem(len(shapes)),
-        out_shape=[jax.ShapeDtypeStruct(*v) for v in shapes],
+        out_shape=shapes,
         scratch_shapes=[
             pltpu.VMEM((rows, pieces[0].shape[1]), BF16),
             pltpu.VMEM((rows, wide), BF16),

time: 466 us -> 466 us (level)
  local copies, waits for them, and re-layouts: 42.6 us -> 37.1 us
    unnamed x86 -> x84, local copies, waits for them, and re-layouts: 23.1 us -> 18.4 us
where the time goes in v8:
time: 466 us; the launch traced here: 460 us
  Pallas kernels  168 us (36%)
  waiting for transfers between devices  132 us (28%)
  starting transfers between devices  79.2 us (17%)
  local copies, waits for them, and re-layouts  37.1 us (8%)
  other arithmetic  28.3 us (6%)
  between operations  15.3 us (3%)
    ppermute x72, waiting for transfers between devices, swap(): return lax.ppermute(value, axis, [(i, i ^ mask) for i in range(count)])  132 us
    ppermute x72, starting transfers between devices, swap(): return lax.ppermute(value, axis, [(i, i ^ mask) for i in range(count)])  78.7 us
    pallas_call x4, Pallas kernels, run_experts(): pl.pallas_call(functools.partial(expert_kernel, local), grid_spec=pltpu.P...  69.4 us
    pallas_call x1, Pallas kernels, gate_up_product(): pl.pallas_call(gate_up_kernel, grid=(features // tile,), in_specs=[pl.Blo...  19.2 us
    unnamed x84, local copies, waits for them, and re-layouts  18.4 us
    convert_element_type x11, other arithmetic, plus(): return total.astype(values[0].dtype)  15.8 us
    pallas_call x1, Pallas kernels, attention_back(): pl.pallas_call(functools.partial(attention_back_kernel, key_heads), in_sp...  15.7 us
    pallas_call x1, Pallas kernels, down_product(): pl.pallas_call(down_kernel, grid_spec=pltpu.PrefetchScalarGridSpec(num_sc...  13.3 us
  transfers between devices with their start and end apart: 75, of which 34 were waited for; matrix products, arithmetic and copies ran while one was open for 7% of the time, Pallas kernels for 36%

profile of v8, /device:TPU:8, one launch (start us, length us, event | category | flops | bytes accessed | tf_op | source)
XLA Modules:
  0.0 459.8 jit_solution(2294523588130992150)
XLA Ops:
  35.3 11.3 %collective-permute-done.1.refs_2_ = bf16[256,1024]{1,0:T(8,128)(2,1)} collective-permute-done((bf16[256,1024]{1,0:T(8,128)(2,1)}, bf16[256,1024]{1,0:T(8,128)(2,1)}, u32[]{:S(2)}, u32[]{:S(2)}) %collective-permute-start.1) | collective-permute-done | bytes 524320 | tf_op jit(solution)/shard_map/ppermute | solution.py:47
  50.7 4.5 collective-permute-done.7.core_ref
  59.9 7.7 %shard_map.239 = (f32[256,1152]{1,0:T(8,128)S(1)}, bf16[256,1280]{1,0:T(8,128)(2,1)S(1)}, bf16[256,1024]{1,0:T(8,128)(2,1)S(1)}, f32[256,8]{1,0:T(8,128)S(1)}, b...) custom-call(bf16[256,2048]{1,0:T(8,128)(2,1)S(1)} %dynamic-slice_dynamic-update-slice_fusion.x_ref, ...), custom_call_target="tpu_custom_call" | custom-call | bytes 1024 | tf_op jit(solution)/shard_map/pallas_call | solution.py:564
  75.3 6.7 %copy.56 = bf16[4,256,8,384]{3,2,0,1:T(8,128)(2,1)} copy(bf16[4,256,8,384]{3,2,1,0:T(8,128)(2,1)} %bitcast.77) | data formatting | bytes 12582912 | tf_op jit(solution)/shard_map/reshape | solution.py:1010
  98.2 9.2 %collective-permute-done.13.refs_3_ = bf16[32,2048]{1,0:T(8,128)(2,1)S(1)} collective-permute-done((bf16[32,2048]{1,0:T(8,128)(2,1)S(1)}, bf16[32,2048]{1,0:T(8,128)(2,1)S(1)}, u32[]{:S(2)}, u32[]{:S(2)}) %collective-permute-start.13) | collective-permute-done | bytes 131104 | tf_op jit(solution)/shard_map/ppermute | solution.py:47
  115.4 3.6 collective-permute-done.20.refs_1_
  121.1 4.2 collective-permute-done.22.refs_3_
  134.6 17.6 %shard_map.244 = (bf16[512,2176]{1,0:T(8,128)(2,1)}, bf16[512,1536]{1,0:T(8,128)(2,1)}, bf16[512,768]{1,0:T(8,128)(2,1)}) custom-call(s32[5]{0:T(128)S(1)} %stack.111.place_ref, bf16[512,2048]{1,0:T(8,128)(2,1)} %shard_map.242.x_ref.refs_0_, bf16[2048,2048]{1,0:T(8,128)(2,1)} %all-gather.2.cloned.1.call-done.g0_ref.g1_ref.refs_4_, ...), custom_call_target="tpu_custom_call" | custom-call | bytes 1024 | tf_op jit(solution)/shard_map/pallas_call | solution.py:341
  152.2 17.2 %shard_map.243 = (bf16[512,2176]{1,0:T(8,128)(2,1)}, bf16[512,1536]{1,0:T(8,128)(2,1)}, bf16[512,768]{1,0:T(8,128)(2,1)}) custom-call(s32[5]{0:T(128)S(1)} %stack.106.place_ref, bf16[512,2048]{1,0:T(8,128)(2,1)} %collective-permute-done.26.x_ref.refs_1_, bf16[2048,2048]{1,0:T(8,128)(2,1)} %all-gather.2.cloned.1.call-done.g0_ref.g1_ref.refs_4_, ...), custom_call_target="tpu_custom_call" | custom-call | bytes 1024 | tf_op jit(solution)/shard_map/pallas_call | solution.py:341
  172.6 17.4 %shard_map.246 = (bf16[512,2176]{1,0:T(8,128)(2,1)}, bf16[512,1536]{1,0:T(8,128)(2,1)}, bf16[512,768]{1,0:T(8,128)(2,1)}) custom-call(s32[5]{0:T(128)S(1)} %stack.228.place_ref, bf16[512,2048]{1,0:T(8,128)(2,1)} %shard_map.245.x_ref.refs_2_, bf16[2048,2048]{1,0:T(8,128)(2,1)} %all-gather.2.cloned.1.call-done.g0_ref.g1_ref.refs_4_, ...), custom_call_target="tpu_custom_call" | custom-call | bytes 1024 | tf_op jit(solution)/shard_map/pallas_call | solution.py:341
  196.4 17.2 %shard_map.247 = (bf16[512,2176]{1,0:T(8,128)(2,1)}, bf16[512,1536]{1,0:T(8,128)(2,1)}, bf16[512,768]{1,0:T(8,128)(2,1)}) custom-call(s32[5]{0:T(128)S(1)} %stack.233.place_ref, bf16[512,2048]{1,0:T(8,128)(2,1)} %collective-permute-done.28.x_ref.refs_3_, bf16[2048,2048]{1,0:T(8,128)(2,1)} %all-gather.2.cloned.1.call-done.g0_ref.g1_ref.refs_4_, ...), custom_call_target="tpu_custom_call" | custom-call | bytes 1024 | tf_op jit(solution)/shard_map/pallas_call | solution.py:341
  213.6 6.3 %collective-permute-done.30 = bf16[128,2176]{1,0:T(8,128)(2,1)S(1)} collective-permute-done((bf16[128,2176]{1,0:T(8,128)(2,1)}, bf16[128,2176]{1,0:T(8,128)(2,1)S(1)}, u32[]{:S(2)}, u32[]{:S(2)}) %collective-permute-start.30) | collective-permute-done | bytes 557088 | tf_op jit(solution)/shard_map/ppermute | solution.py:47
  230.5 4.1 collective-permute-done.33
  234.6 3.5 collective-permute-done.34
  241.0 3.7 collective-permute-done.35.refs_1_
  246.2 13.1 %shard_map.248 = bf16[2048,2048]{1,0:T(8,128)(2,1)} custom-call(s32[8]{0:T(128)S(1)} %stack.100.place_ref.column_ref.block_ref, bf16[512,768]{1,0:T(8,128)(2,1)} %get-tuple-element.199.upper0_ref.refs_0_, bf16[512,768]{1,0:T(8,128)(2,1)} %get-tuple-element.200.upper1_ref.refs_1_, bf16[512,768]{1,0:T(8,128)(2,1)} %get-tuple-element.201.lower0_ref.refs_2_, ...), custom_call_target="tpu_custom_call" | custom-call | bytes 1024 | tf_op jit(solution)/shard_map/pallas_call | solution.py:452
  267.8 3.7 collective-permute-done.43
  271.5 3.2 collective-permute-done.44
  281.4 4.1 collective-permute-done.46.refs_6_
  285.6 3.2 collective-permute-done.47.refs_7_
  288.8 8.3 %shard_map.249 = (f32[256,2048]{1,0:T(8,128)}, bf16[256,2048]{1,0:T(8,128)(2,1)S(1)}, bf16[2048,128]{1,0:T(8,128)(2,1)S(1)}, bf16[512,2048]{1,0:T(8,128)(2,1)}, bf16[512,2048]{1,0:T(8,128)(2,1)S(1)}) custom-call(s32[4]{0:T(128)S(1)} %pad_add_fusion.place_ref, s32[8]{0:T(128)S(1)} %stack.100.place_ref.column_ref.block_ref, ...), custom_call_target="tpu_custom_call" | custom-call | bytes 1024 | tf_op jit(solution)/shard_map/pallas_call | solution.py:808
  298.9 15.7 %shard_map.250 = (bf16[256,2304]{1,0:T(8,128)(2,1)S(1)}, bf16[2048,1408]{1,0:T(8,128)(2,1)}) custom-call(s32[8]{0:T(128)S(1)} %stack.100.place_ref.column_ref.block_ref, bf16[256,2048]{1,0:T(8,128)(2,1)} %copy-done.13, bf16[1024,2048]{1,0:T(8,128)(2,1)} %wo_ref.3, f32[256,1152]{1,0:T(8,128)} %copy-done.12, bf16[256,1280]{1,0:T(8,128)(2,1)} %copy-done.14, ...), custom_call_target="tpu_custom_call" | custom-call | bytes 1024 | tf_op jit(solution)/shard_map/pallas_call | solution.py:680
  327.0 13.3 %shard_map.251 = f32[768,2048]{1,0:T(8,128)} custom-call(s32[16]{0:T(128)} %stack.234.place_ref, bf16[512,768]{1,0:T(8,128)(2,1)} %get-tuple-element.199.upper0_ref.refs_0_, bf16[512,768]{1,0:T(8,128)(2,1)} %get-tuple-element.200.upper1_ref.refs_1_, bf16[512,768]{1,0:T(8,128)(2,1)} %get-tuple-element.201.lower0_ref.refs_2_, ...), custom_call_target="tpu_custom_call" | custom-call | bytes 1024 | tf_op jit(solution)/shard_map/pallas_call | solution.py:416
  340.3 3.3 collective-permute-done.50
  343.6 7.8 %collective-permute-done.51 = bf16[64,2304]{1,0:T(8,128)(2,1)} collective-permute-done((bf16[64,2304]{1,0:T(8,128)(2,1)S(1)}, bf16[64,2304]{1,0:T(8,128)(2,1)}, u32[]{:S(2)}, u32[]{:S(2)}) %collective-permute-start.51) | collective-permute-done | bytes 294944 | tf_op jit(solution)/shard_map/ppermute | solution.py:47
  359.0 19.2 %shard_map.252 = f32[4,2048,384]{2,1,0:T(8,128)} custom-call(bf16[512,2048]{1,0:T(8,128)(2,1)} %shard_map.242.x_ref.refs_0_, bf16[512,2048]{1,0:T(8,128)(2,1)} %collective-permute-done.26.x_ref.refs_1_, bf16[512,2048]{1,0:T(8,128)(2,1)} %shard_map.245.x_ref.refs_2_, bf16[512,2048]{1,0:T(8,128)(2,1)} %collective-permute-done.28.x_ref.refs_3_, ...), custom_call_target="tpu_custom_call" | custom-call | bytes 1024 | tf_op jit(solution)/shard_map/pallas_call | solution.py:387
  386.9 4.9 %shard_map.253 = (f32[256,2048]{1,0:T(8,128)}, f32[8,512]{1,0:T(8,128)S(1)}) custom-call(s32[4]{0:T(128)S(1)} %pad_add_fusion.place_ref, s32[8]{0:T(128)S(1)} %stack.100.place_ref.column_ref.block_ref, bf16[64,2304]{1,0:T(8,128)(2,1)S(1)} %add_convert_fusion.15.refs_0_, bf16[64,2304]{1,0:T(8,128)(2,1)S(1)} %collective-permute-done.55.refs_1_, ...), custom_call_target="tpu_custom_call" | custom-call | bytes 1024 | tf_op jit(solution)/shard_map/pallas_call | solution.py:860
  391.8 11.1 %collective-permute-done.63 = bf16[64,2048]{1,0:T(8,128)(2,1)S(1)} collective-permute-done((bf16[64,2048]{1,0:T(8,128)(2,1)S(1)}, bf16[64,2048]{1,0:T(8,128)(2,1)S(1)}, u32[]{:S(2)}, u32[]{:S(2)}) %collective-permute-start.63) | collective-permute-done | bytes 262176 | tf_op jit(solution)/shard_map/ppermute | solution.py:47
  403.0 5.3 %collective-permute-done.64 = bf16[64,2048]{1,0:T(8,128)(2,1)S(1)} collective-permute-done((bf16[64,2048]{1,0:T(8,128)(2,1)S(1)}, bf16[64,2048]{1,0:T(8,128)(2,1)S(1)}, u32[]{:S(2)}, u32[]{:S(2)}) %collective-permute-start.64) | collective-permute-done | bytes 262176 | tf_op jit(solution)/shard_map/ppermute | solution.py:47
  408.3 6.4 %collective-permute-done.61.refs_3_ = bf16[128,2048]{1,0:T(8,128)(2,1)S(1)} collective-permute-done((bf16[128,2048]{1,0:T(8,128)(2,1)S(1)}, bf16[128,2048]{1,0:T(8,128)(2,1)S(1)}, u32[]{:S(2)}, u32[]{:S(2)}) %collective-permute-start.61) | collective-permute-done | bytes 524320 | tf_op jit(solution)/shard_map/ppermute | solution.py:47
  429.2 5.3 %shard_map.255 = f32[1024,2048]{1,0:T(8,128)} custom-call(s32[8]{0:T(128)S(1)} %stack.100.place_ref.column_ref.block_ref, bf16[512,2048]{1,0:T(8,128)(2,1)S(1)} %shard_map.254.near_ref, bf16[512,2048]{1,0:T(8,128)(2,1)S(1)} %copy-done.7), custom_call_target="tpu_custom_call" | custom-call | bytes 1024 | tf_op jit(solution)/shard_map/pallas_call | solution.py:886
  437.4 6.5 %collective-permute-done.71 = bf16[64,2048]{1,0:T(8,128)(2,1)} collective-permute-done((bf16[64,2048]{1,0:T(8,128)(2,1)}, bf16[64,2048]{1,0:T(8,128)(2,1)}, u32[]{:S(2)}, u32[]{:S(2)}) %collective-permute-start.71) | collective-permute-done | bytes 262176 | tf_op jit(solution)/shard_map/ppermute | solution.py:47
  (297 shorter events, 175.9 us)
Async XLA Ops:
  7.2 127.4 %all-gather.2.cloned.1.call-start = ((), (), s32[]{:S(2)}) async-start(), calls=%async_computation.2 | async-start | bytes 9437184 | tf_op jit(solution)/shard_map/all_gather | solution.py:999
  16.9 29.7 %collective-permute-start.1 = (bf16[256,1024]{1,0:T(8,128)(2,1)}, bf16[256,1024]{1,0:T(8,128)(2,1)}, u32[]{:S(2)}, u32[]{:S(2)}) collective-permute-start(bf16[256,1024]{1,0:T(8,128)(2,1)} %refs_0_.1), channel_id=1, source_target_pairs={{0,16},{4,20},{8,24},{12,28},{16,0},{20,4},{24,8},{28,12},{1,17},{... | collective-permute-start | bytes 1572872 | tf_op jit(solution)/shard_map/ppermute | solution.py:47
  19.7 26.9 %collective-permute-start.2 = (bf16[256,1024]{1,0:T(8,128)(2,1)}, bf16[256,1024]{1,0:T(8,128)(2,1)}, u32[]{:S(2)}, u32[]{:S(2)}) collective-permute-start(bf16[256,1024]{1,0:T(8,128)(2,1)} %refs_0_.1), channel_id=1, source_target_pairs={{0,24},{4,28},{8,16},{12,20},{16,8},{20,12},{24,0},{28,4},{1,25},{... | collective-permute-start | bytes 1572872 | tf_op jit(solution)/shard_map/ppermute | solution.py:47
  46.6 304.9 %reduce-scatter.3.cloned.1.call-start = ((), (), s32[]{:S(2)}) async-start(), calls=%async_computation.3 | async-start | bytes 9437184 | tf_op jit(solution)/shard_map/reduce_scatter | solution.py:1065
  89.3 21.9 %collective-permute-start.14 = (bf16[32,2048]{1,0:T(8,128)(2,1)S(1)}, bf16[32,2048]{1,0:T(8,128)(2,1)S(1)}, u32[]{:S(2)}, u32[]{:S(2)}) collective-permute-start(bf16[32,2048]{1,0:T(8,128)(2,1)S(1)} %get-tuple-element.354), channel_id=1, source_target_pairs={{0,1},{1,0},{2,3},{3,2},{4,5},{5,4},{6,7},{7,6},{8,9},{9,8},{10,11... | collective-permute-start | bytes 393224 | tf_op jit(solution)/shard_map/ppermute | solution.py:47
  129.2 23.1 %collective-permute-start.26 = (bf16[512,2048]{1,0:T(8,128)(2,1)}, bf16[512,2048]{1,0:T(8,128)(2,1)}, u32[]{:S(2)}, u32[]{:S(2)}) collective-permute-start(bf16[512,2048]{1,0:T(8,128)(2,1)} %shard_map.242.x_ref.refs_0_), channel_id=1, source_target_pairs={{0,4},{4,0},{8,12},{12,8},{16,20},{20,16},{24,28},{28,24},{1,5},{5... | collective-permute-start | bytes 6291464 | tf_op jit(solution)/shard_map/ppermute | solution.py:47
  130.9 38.5 %collective-permute-start.23 = (bf16[128,2048]{1,0:T(8,128)(2,1)S(1)}, bf16[128,2048]{1,0:T(8,128)(2,1)S(1)}, u32[]{:S(2)}, u32[]{:S(2)}) collective-permute-start(bf16[128,2048]{1,0:T(8,128)(2,1)S(1)} %get-tuple-element.170.refs_0_.refs_11_), channel_id=1, source_target_pairs={{0,8},{4,12},{8,0},{12,4},{16,24},{20,28},{24,16},{28,20},{1,9},{5... | collective-permute-start | bytes 1572872 | tf_op jit(solution)/shard_map/ppermute | solution.py:47
  131.6 37.9 %collective-permute-start.24 = (bf16[128,2048]{1,0:T(8,128)(2,1)S(1)}, bf16[128,2048]{1,0:T(8,128)(2,1)S(1)}, u32[]{:S(2)}, u32[]{:S(2)}) collective-permute-start(bf16[128,2048]{1,0:T(8,128)(2,1)S(1)} %get-tuple-element.170.refs_0_.refs_11_), channel_id=1, source_target_pairs={{0,16},{4,20},{8,24},{12,28},{16,0},{20,4},{24,8},{28,12},{1,17},{... | collective-permute-start | bytes 1572872 | tf_op jit(solution)/shard_map/ppermute | solution.py:47
  133.1 36.4 %collective-permute-start.25 = (bf16[128,2048]{1,0:T(8,128)(2,1)S(1)}, bf16[128,2048]{1,0:T(8,128)(2,1)}, u32[]{:S(2)}, u32[]{:S(2)}) collective-permute-start(bf16[128,2048]{1,0:T(8,128)(2,1)S(1)} %get-tuple-element.170.refs_0_.refs_11_), channel_id=1, source_target_pairs={{0,24},{4,28},{8,16},{12,20},{16,8},{20,12},{24,0},{28,4},{1,25},{... | collective-permute-start | bytes 1572872 | tf_op jit(solution)/shard_map/ppermute | solution.py:47
  192.8 20.8 %collective-permute-start.29 = (bf16[128,2176]{1,0:T(8,128)(2,1)}, bf16[128,2176]{1,0:T(8,128)(2,1)S(1)}, u32[]{:S(2)}, u32[]{:S(2)}) collective-permute-start(bf16[128,2176]{1,0:T(8,128)(2,1)} %get-tuple-element.334), channel_id=1, source_target_pairs={{0,8},{4,12},{8,0},{12,4},{16,24},{20,28},{24,16},{28,20},{1,9},{5... | collective-permute-start | bytes 1671176 | tf_op jit(solution)/shard_map/ppermute | solution.py:47
  193.4 26.4 %collective-permute-start.30 = (bf16[128,2176]{1,0:T(8,128)(2,1)}, bf16[128,2176]{1,0:T(8,128)(2,1)S(1)}, u32[]{:S(2)}, u32[]{:S(2)}) collective-permute-start(bf16[128,2176]{1,0:T(8,128)(2,1)} %get-tuple-element.333), channel_id=1, source_target_pairs={{0,16},{4,20},{8,24},{12,28},{16,0},{20,4},{24,8},{28,12},{1,17},{... | collective-permute-start | bytes 1671176 | tf_op jit(solution)/shard_map/ppermute | solution.py:47
  194.9 25.0 %collective-permute-start.31 = (bf16[128,2176]{1,0:T(8,128)(2,1)}, bf16[128,2176]{1,0:T(8,128)(2,1)}, u32[]{:S(2)}, u32[]{:S(2)}) collective-permute-start(bf16[128,2176]{1,0:T(8,128)(2,1)} %get-tuple-element.332), channel_id=1, source_target_pairs={{0,24},{4,28},{8,16},{12,20},{16,8},{20,12},{24,0},{28,4},{1,25},{... | collective-permute-start | bytes 1671176 | tf_op jit(solution)/shard_map/ppermute | solution.py:47
  227.0 32.3 %collective-permute-start.39 = (bf16[128,2176]{1,0:T(8,128)(2,1)}, bf16[128,2176]{1,0:T(8,128)(2,1)S(1)}, u32[]{:S(2)}, u32[]{:S(2)}) collective-permute-start(bf16[128,2176]{1,0:T(8,128)(2,1)} %get-tuple-element.331), channel_id=1, source_target_pairs={{0,8},{4,12},{8,0},{12,4},{16,24},{20,28},{24,16},{28,20},{1,9},{5... | collective-permute-start | bytes 1671176 | tf_op jit(solution)/shard_map/ppermute | solution.py:47
  228.4 30.9 %collective-permute-start.40 = (bf16[128,2176]{1,0:T(8,128)(2,1)}, bf16[128,2176]{1,0:T(8,128)(2,1)S(1)}, u32[]{:S(2)}, u32[]{:S(2)}) collective-permute-start(bf16[128,2176]{1,0:T(8,128)(2,1)} %get-tuple-element.330), channel_id=1, source_target_pairs={{0,16},{4,20},{8,24},{12,28},{16,0},{20,4},{24,8},{28,12},{1,17},{... | collective-permute-start | bytes 1671176 | tf_op jit(solution)/shard_map/ppermute | solution.py:47
  229.0 30.3 %collective-permute-start.41 = (bf16[128,2176]{1,0:T(8,128)(2,1)}, bf16[128,2176]{1,0:T(8,128)(2,1)S(1)}, u32[]{:S(2)}, u32[]{:S(2)}) collective-permute-start(bf16[128,2176]{1,0:T(8,128)(2,1)} %get-tuple-element.329), channel_id=1, source_target_pairs={{0,24},{4,28},{8,16},{12,20},{16,8},{20,12},{24,0},{28,4},{1,25},{... | collective-permute-start | bytes 1671176 | tf_op jit(solution)/shard_map/ppermute | solution.py:47
  238.2 21.1 %collective-permute-start.36 = (bf16[32,2176]{1,0:T(8,128)(2,1)S(1)}, bf16[32,2176]{1,0:T(8,128)(2,1)S(1)}, u32[]{:S(2)}, u32[]{:S(2)}) collective-permute-start(bf16[32,2176]{1,0:T(8,128)(2,1)S(1)} %add_convert_fusion.18.refs_0_), channel_id=1, source_target_pairs={{0,2},{1,3},{2,0},{3,1},{4,6},{5,7},{6,4},{7,5},{8,10},{9,11},{10,... | collective-permute-start | bytes 417800 | tf_op jit(solution)/shard_map/ppermute | solution.py:47
  260.1 174.4 %reduce-scatter.5.cloned.1.call-start = ((), (), s32[]{:S(2)}) async-start(), calls=%async_computation.4 | async-start | bytes 6488064 | tf_op jit(solution)/shard_map/reduce_scatter | solution.py:1105
  319.4 32.1 %collective-permute-start.52 = (bf16[128,2048]{1,0:T(8,128)(2,1)}, bf16[128,2048]{1,0:T(8,128)(2,1)}, u32[]{:S(2)}, u32[]{:S(2)}) collective-permute-start(bf16[128,2048]{1,0:T(8,128)(2,1)} %get-tuple-element.337), channel_id=1, source_target_pairs={{0,8},{4,12},{8,0},{12,4},{16,24},{20,28},{24,16},{28,20},{1,9},{5... | collective-permute-start | bytes 1572872 | tf_op jit(solution)/shard_map/ppermute | solution.py:47
  320.7 30.7 %collective-permute-start.53 = (bf16[128,2048]{1,0:T(8,128)(2,1)S(1)}, bf16[128,2048]{1,0:T(8,128)(2,1)}, u32[]{:S(2)}, u32[]{:S(2)}) collective-permute-start(bf16[128,2048]{1,0:T(8,128)(2,1)S(1)} %get-tuple-element.336), channel_id=1, source_target_pairs={{0,16},{4,20},{8,24},{12,28},{16,0},{20,4},{24,8},{28,12},{1,17},{... | collective-permute-start | bytes 1572872 | tf_op jit(solution)/shard_map/ppermute | solution.py:47
  321.4 30.1 %collective-permute-start.54 = (bf16[128,2048]{1,0:T(8,128)(2,1)S(1)}, bf16[128,2048]{1,0:T(8,128)(2,1)}, u32[]{:S(2)}, u32[]{:S(2)}) collective-permute-start(bf16[128,2048]{1,0:T(8,128)(2,1)S(1)} %get-tuple-element.335), channel_id=1, source_target_pairs={{0,24},{4,28},{8,16},{12,20},{16,8},{20,12},{24,0},{28,4},{1,25},{... | collective-permute-start | bytes 1572872 | tf_op jit(solution)/shard_map/ppermute | solution.py:47
  322.8 20.8 %collective-permute-start.50 = (bf16[64,2304]{1,0:T(8,128)(2,1)S(1)}, bf16[64,2304]{1,0:T(8,128)(2,1)}, u32[]{:S(2)}, u32[]{:S(2)}) collective-permute-start(bf16[64,2304]{1,0:T(8,128)(2,1)S(1)} %get-tuple-element.339), channel_id=1, source_target_pairs={{0,2},{1,3},{2,0},{3,1},{4,6},{5,7},{6,4},{7,5},{8,10},{9,11},{10,... | collective-permute-start | bytes 884744 | tf_op jit(solution)/shard_map/ppermute | solution.py:47
  325.7 25.7 %collective-permute-start.51 = (bf16[64,2304]{1,0:T(8,128)(2,1)S(1)}, bf16[64,2304]{1,0:T(8,128)(2,1)}, u32[]{:S(2)}, u32[]{:S(2)}) collective-permute-start(bf16[64,2304]{1,0:T(8,128)(2,1)S(1)} %get-tuple-element.338), channel_id=1, source_target_pairs={{0,3},{1,2},{2,1},{3,0},{4,7},{5,6},{6,5},{7,4},{8,11},{9,10},{10,... | collective-permute-start | bytes 884744 | tf_op jit(solution)/shard_map/ppermute | solution.py:47
  352.7 27.5 %collective-permute-start.55 = (bf16[64,2304]{1,0:T(8,128)(2,1)S(1)}, bf16[64,2304]{1,0:T(8,128)(2,1)S(1)}, u32[]{:S(2)}, u32[]{:S(2)}) collective-permute-start(bf16[64,2304]{1,0:T(8,128)(2,1)S(1)} %add_convert_fusion.15.refs_0_), channel_id=1, source_target_pairs={{0,1},{1,0},{2,3},{3,2},{4,5},{5,4},{6,7},{7,6},{8,9},{9,8},{10,11... | collective-permute-start | bytes 884744 | tf_op jit(solution)/shard_map/ppermute | solution.py:47
  353.4 26.9 %collective-permute-start.56 = (bf16[64,2304]{1,0:T(8,128)(2,1)S(1)}, bf16[64,2304]{1,0:T(8,128)(2,1)S(1)}, u32[]{:S(2)}, u32[]{:S(2)}) collective-permute-start(bf16[64,2304]{1,0:T(8,128)(2,1)S(1)} %add_convert_fusion.15.refs_0_), channel_id=1, source_target_pairs={{0,2},{1,3},{2,0},{3,1},{4,6},{5,7},{6,4},{7,5},{8,10},{9,11},{10,... | collective-permute-start | bytes 884744 | tf_op jit(solution)/shard_map/ppermute | solution.py:47
  355.7 26.3 %collective-permute-start.57 = (bf16[64,2304]{1,0:T(8,128)(2,1)S(1)}, bf16[64,2304]{1,0:T(8,128)(2,1)S(1)}, u32[]{:S(2)}, u32[]{:S(2)}) collective-permute-start(bf16[64,2304]{1,0:T(8,128)(2,1)S(1)} %add_convert_fusion.15.refs_0_), channel_id=1, source_target_pairs={{0,3},{1,2},{2,1},{3,0},{4,7},{5,6},{6,5},{7,4},{8,11},{9,10},{10,... | collective-permute-start | bytes 884744 | tf_op jit(solution)/shard_map/ppermute | solution.py:47
  357.5 28.3 %collective-permute-start.62 = (bf16[64,2048]{1,0:T(8,128)(2,1)S(1)}, bf16[64,2048]{1,0:T(8,128)(2,1)S(1)}, u32[]{:S(2)}, u32[]{:S(2)}) collective-permute-start(bf16[64,2048]{1,0:T(8,128)(2,1)S(1)} %get-tuple-element.343), channel_id=1, source_target_pairs={{0,1},{1,0},{2,3},{3,2},{4,5},{5,4},{6,7},{7,6},{8,9},{9,8},{10,11... | collective-permute-start | bytes 786440 | tf_op jit(solution)/shard_map/ppermute | solution.py:47
  382.0 26.2 %collective-permute-start.59 = (bf16[128,2048]{1,0:T(8,128)(2,1)S(1)}, bf16[128,2048]{1,0:T(8,128)(2,1)S(1)}, u32[]{:S(2)}, u32[]{:S(2)}) collective-permute-start(bf16[128,2048]{1,0:T(8,128)(2,1)S(1)} %add_convert_fusion.10.refs_0_), channel_id=1, source_target_pairs={{0,8},{4,12},{8,0},{12,4},{16,24},{20,28},{24,16},{28,20},{1,9},{5... | collective-permute-start | bytes 1572872 | tf_op jit(solution)/shard_map/ppermute | solution.py:47
  383.3 24.9 %collective-permute-start.60 = (bf16[128,2048]{1,0:T(8,128)(2,1)S(1)}, bf16[128,2048]{1,0:T(8,128)(2,1)S(1)}, u32[]{:S(2)}, u32[]{:S(2)}) collective-permute-start(bf16[128,2048]{1,0:T(8,128)(2,1)S(1)} %add_convert_fusion.10.refs_0_), channel_id=1, source_target_pairs={{0,16},{4,20},{8,24},{12,28},{16,0},{20,4},{24,8},{28,12},{1,17},{... | collective-permute-start | bytes 1572872 | tf_op jit(solution)/shard_map/ppermute | solution.py:47
  384.0 30.7 %collective-permute-start.61 = (bf16[128,2048]{1,0:T(8,128)(2,1)S(1)}, bf16[128,2048]{1,0:T(8,128)(2,1)S(1)}, u32[]{:S(2)}, u32[]{:S(2)}) collective-permute-start(bf16[128,2048]{1,0:T(8,128)(2,1)S(1)} %add_convert_fusion.10.refs_0_), channel_id=1, source_target_pairs={{0,24},{4,28},{8,16},{12,20},{16,8},{20,12},{24,0},{28,4},{1,25},{... | collective-permute-start | bytes 1572872 | tf_op jit(solution)/shard_map/ppermute | solution.py:47
  385.8 22.5 %collective-permute-start.64 = (bf16[64,2048]{1,0:T(8,128)(2,1)S(1)}, bf16[64,2048]{1,0:T(8,128)(2,1)S(1)}, u32[]{:S(2)}, u32[]{:S(2)}) collective-permute-start(bf16[64,2048]{1,0:T(8,128)(2,1)S(1)} %get-tuple-element.341), channel_id=1, source_target_pairs={{0,3},{1,2},{2,1},{3,0},{4,7},{5,6},{6,5},{7,4},{8,11},{9,10},{10,... | collective-permute-start | bytes 786440 | tf_op jit(solution)/shard_map/ppermute | solution.py:47
  416.8 20.6 %collective-permute-start.70 = (bf16[64,2048]{1,0:T(8,128)(2,1)}, bf16[64,2048]{1,0:T(8,128)(2,1)}, u32[]{:S(2)}, u32[]{:S(2)}) collective-permute-start(bf16[64,2048]{1,0:T(8,128)(2,1)} %get-tuple-element.328), channel_id=1, source_target_pairs={{0,2},{1,3},{2,0},{3,1},{4,6},{5,7},{6,4},{7,5},{8,10},{9,11},{10,... | collective-permute-start | bytes 786440 | tf_op jit(solution)/shard_map/ppermute | solution.py:47
  419.1 24.8 %collective-permute-start.71 = (bf16[64,2048]{1,0:T(8,128)(2,1)}, bf16[64,2048]{1,0:T(8,128)(2,1)}, u32[]{:S(2)}, u32[]{:S(2)}) collective-permute-start(bf16[64,2048]{1,0:T(8,128)(2,1)} %get-tuple-element.328), channel_id=1, source_target_pairs={{0,3},{1,2},{2,1},{3,0},{4,7},{5,6},{6,5},{7,4},{8,11},{9,10},{10,... | collective-permute-start | bytes 786440 | tf_op jit(solution)/shard_map/ppermute | solution.py:47
  (80 other events, 1070.5 us)
Sparse Core Ops, SparseCore 0:
  46.7 54.6 all-gather.1
  259.5 75.3 reduce-scatter.2
  338.7 67.3 reduce-scatter.4
